TPU v7x, 32 devices: a whole 2x2x4 slice. The times are simulated.
32 devices in a mesh: seq: 8 (over z, y), mp: 4 (over x, core).
Axes of the slice: x: 2, y: 2, z: 4, core: 2. Of those that a mesh axis runs over, the one named last changes fastest.
Arguments:
- ids: int32 [1024], P('seq'), may hold values from 0 to 3
- hidden_fwd: bfloat16 [1024, 1024], P('seq', 'mp'), may hold values from -8 to 8
- hidden_rc: bfloat16 [1024, 1024], P('seq', 'mp'), may hold values from -8 to 8
- embed: float32 [4, 1024], P(None, 'mp'), may hold values from -4 to 4
- ln1_gain: float32 [1024], replicated, may hold values from 0.1 to 1.9
- ln2_gain: float32 [1024], replicated, may hold values from 0.1 to 1.9
- mixing: float32 [5, 1024], replicated, may hold values from 0 to 1
- w_receptance: bfloat16 [1024, 1024], P(None, 'mp'), may hold values from -0.1875 to 0.1875
- w_key: bfloat16 [1024, 1024], P(None, 'mp'), may hold values from -0.1875 to 0.1875
- w_value: bfloat16 [1024, 1024], P(None, 'mp'), may hold values from -0.1875 to 0.1875
- decay_first_weight: bfloat16 [1024, 64], replicated, may hold values from -0.1875 to 0.1875
- decay_base: float32 [1024], P('mp'), may hold values from -11 to 1
- decay_second_weight: bfloat16 [64, 1024], P(None, 'mp'), may hold values from -0.75 to 0.75
- context_rate_first_weight: bfloat16 [1024, 64], replicated, may hold values from -0.1875 to 0.1875
- iclr_base: float32 [1024], P('mp'), may hold values from -9 to 1
- context_rate_second_weight: bfloat16 [64, 1024], P(None, 'mp'), may hold values from -0.75 to 0.75
- group_gain: float32 [1024], P('mp'), may hold values from 0.1 to 1.9
- w_output: bfloat16 [1024, 1024], P('mp'), may hold values from -0.1875 to 0.1875
- ffn_key: bfloat16 [1024, 4096], P(None, 'mp'), may hold values from -0.1875 to 0.1875
- ffn_value: bfloat16 [4096, 1024], P('mp'), may hold values from -0.09375 to 0.09375
Outputs:
- merged: bfloat16 [1024, 1024], P('seq', 'mp')
Inputs may be any that keep to these rules, and one draw needn't show every extreme that they name: `ids`: bases A, C, G, T are 0, 1, 2, 3; the complement of base c is 3 - c.
All inputs are finite; a program needn't handle non-finite values.
Results may differ from a plain program's by a relative error of at most 0.01.
Values may be sent and summed in bfloat16 or wider, within the bound.
No kernel may reach another device: no remote copies, remote signals or barrier semaphores. Data moves between devices by JAX's collectives and lax.ppermute only.
A program may use at most 64 MiB of HBM per device.

v0:
```python
import jax
import jax.numpy as jnp
from jax import lax
from jax.sharding import PartitionSpec as P

HEAD = 64
BLOCK = 128


PRECISE = lax.Precision.HIGHEST
DECAY_SCALE = 0.606531
NORM_EPS = 1e-05
GROUP_EPS = 0.00064
UNIT_EPS = 1e-06


def swapped(value, axis, apart):
    mask = 2**apart
    pairs = [(source, source ^ mask) for source in range(lax.axis_size(axis))]
    return lax.ppermute(value, axis, pairs)


def extended(array, sides, width):
    for axis, dim in sides:
        size, length = (lax.axis_size(axis), array.shape[dim])
        up = [(i, (i + 1) % size) for i in range(size - 1)]
        down = [(j, i) for i, j in up]
        last = lax.slice_in_dim(array, length - width, length, axis=dim)
        initial = lax.slice_in_dim(array, 0, width, axis=dim)
        before = lax.ppermute(last, axis, up)
        after = lax.ppermute(initial, axis, down)
        array = jnp.concatenate([before, array, after], axis=dim)
    return array


def from_behind(block, axis, distance):
    devices = range(lax.axis_size(axis))
    route = [(i - distance, i) for i in devices if i - distance in devices]
    return lax.ppermute(block, axis, route)


def layer_norm(values, gain):
    row_mean = jnp.mean(values, axis=-1, keepdims=True)
    centered = values - row_mean
    spread = jnp.mean(centered * centered, axis=-1, keepdims=True)
    return centered * lax.rsqrt(spread + NORM_EPS) * gain


def project(layer_input, weight):
    flat = layer_input.reshape(-1, layer_input.shape[-1])
    result = jnp.dot(flat, weight, preferred_element_type=jnp.float32)
    return result.reshape(layer_input.shape[:-1] + (weight.shape[1],))


def pairing(left_side, right_side, keep_mask):
    scores = jnp.einsum("lbtc,lbsc->lbts", left_side, right_side, precision=PRECISE)
    return jnp.where(keep_mask, scores, 0.0)


def square_product(left_side, right_side):
    return jnp.einsum("lbts,lbsu->lbtu", left_side, right_side, precision=PRECISE)


def unit_lower_inverse(strict_part):
    length = strict_part.shape[-1]
    power = strict_part
    inverse = jnp.eye(length, dtype=jnp.float32) + power
    reach = 2
    while reach < length:
        power = square_product(power, power)
        inverse = inverse + square_product(inverse, power)
        reach = reach * 2
    return inverse


def state_product(state_in, mapping):
    return jnp.einsum("lvk,lkj->lvj", state_in, mapping, precision=PRECISE)


def block_terms(receptance, key_vec, value_vec, unit_key, iclr_rate, log_decay):
    length = receptance.shape[2]
    width_value = value_vec.shape[3]
    totals = jnp.cumsum(log_decay, axis=2)
    earlier = totals - log_decay
    middle = totals[:, :, length // 2 : length // 2 + 1]
    final_position = totals[:, :, length - 1 : length]
    removal = -unit_key
    insertion = iclr_rate * unit_key
    left_prev = removal * jnp.exp(earlier - middle)
    left_here = receptance * jnp.exp(totals - middle)
    right_insert = insertion * jnp.exp(middle - totals)
    right_key = key_vec * jnp.exp(middle - totals)
    row_ids = lax.broadcasted_iota(jnp.int32, (length, length), 0)
    col_ids = lax.broadcasted_iota(jnp.int32, (length, length), 1)
    strict = row_ids > col_ids
    inclusive = row_ids >= col_ids
    insert_pull = pairing(left_prev, right_insert, strict)
    key_pull = pairing(left_prev, right_key, strict)
    insert_read = pairing(left_here, right_insert, inclusive)
    key_read = pairing(left_here, right_key, inclusive)
    inverse = unit_lower_inverse(insert_pull)
    start_removal = removal * jnp.exp(earlier)
    start_read = receptance * jnp.exp(totals)
    to_end = jnp.exp(final_position - totals)
    tail_insert = insertion * to_end
    tail_key = key_vec * to_end
    value_pull = jnp.einsum("lbts,lbsv->lbtv", key_pull, value_vec, precision=PRECISE)
    solved = jnp.einsum(
        "lbts,lbsv->lbtv",
        inverse,
        jnp.concatenate([value_pull, start_removal], axis=3),
        precision=PRECISE,
    )
    local_pull = solved[..., :width_value]
    start_pull = solved[..., width_value:]
    carried = jnp.einsum("lbst,lbsk->lbtk", inverse, tail_insert, precision=PRECISE)
    local_out = jnp.einsum(
        "lbts,lbsv->lbtv", insert_read, local_pull, precision=PRECISE
    ) + jnp.einsum("lbts,lbsv->lbtv", key_read, value_vec, precision=PRECISE)
    start_map = start_read + jnp.einsum(
        "lbts,lbsk->lbtk", insert_read, start_pull, precision=PRECISE
    )
    key_eye = jnp.eye(unit_key.shape[3], dtype=jnp.float32)
    transition = (
        jnp.einsum("lbtk,lbtj->lbkj", start_removal, carried, precision=PRECISE)
        + key_eye * jnp.exp(final_position)[:, :, 0, :, None]
    )
    local_end = jnp.einsum(
        "lbtv,lbtk->lbvk", local_pull, tail_insert, precision=PRECISE
    ) + jnp.einsum("lbtv,lbtk->lbvk", value_vec, tail_key, precision=PRECISE)
    return (local_out, start_map, transition, local_end)


def through_blocks(carry_pair, pieces):
    transition, local_end = pieces
    advanced = (
        state_product(carry_pair[0], transition),
        state_product(carry_pair[1], transition) + local_end,
    )
    return (advanced, carry_pair)


def on_device(
    ids,
    hidden_fwd,
    hidden_rc,
    embed,
    ln1_gain,
    ln2_gain,
    mixing,
    w_receptance,
    w_key,
    w_value,
    decay_first_weight,
    decay_base,
    decay_second_weight,
    context_rate_first_weight,
    iclr_base,
    context_rate_second_weight,
    group_gain,
    w_output,
    ffn_key,
    ffn_value,
):
    seq_rows = ids.shape[0]
    local_width = hidden_fwd.shape[1]
    local_heads = local_width // HEAD
    lanes_total = 4 * local_heads
    half_lanes = 2 * local_heads
    seq_count = lax.axis_size("seq")
    mirrored_ids = ids
    for bit_index in range(seq_count.bit_length() - 1):
        mirrored_ids = swapped(mirrored_ids, "seq", bit_index)
    letters = jnp.arange(4, dtype=jnp.int32)
    onehot_fwd = (ids[:, None] == letters[None, :]).astype(jnp.float32)
    onehot_rc = ((3 - mirrored_ids[::-1])[:, None] == letters[None, :]).astype(jnp.float32)
    strands = jnp.stack(
        [
            hidden_fwd.astype(jnp.float32) + jnp.dot(onehot_fwd, embed, precision=PRECISE),
            hidden_rc.astype(jnp.float32) + jnp.dot(onehot_rc, embed, precision=PRECISE),
        ]
    ).astype(jnp.bfloat16)
    padded = extended(strands, (("seq", 1),), 1)
    whole_rows = lax.all_gather(padded, "mp", axis=2, tiled=True)
    normed = layer_norm(whole_rows.astype(jnp.float32), ln1_gain)
    center = normed[None, :, 1:-1]
    neighbours = jnp.stack([normed[:, :-2], normed[:, 2:]])

    def mixed_input(mix_index):
        return (center + (neighbours - center) * mixing[mix_index]).astype(jnp.bfloat16)

    receptance = project(mixed_input(0), w_receptance)
    key_vec = project(mixed_input(1), w_key)
    value_vec = project(mixed_input(2), w_value)
    decay_low = jnp.tanh(project(mixed_input(3), decay_first_weight)).astype(jnp.bfloat16)
    log_decay = -DECAY_SCALE * jax.nn.sigmoid(decay_base + project(decay_low, decay_second_weight))
    iclr_low = project(mixed_input(4), context_rate_first_weight).astype(jnp.bfloat16)
    iclr_rate = jax.nn.sigmoid(iclr_base + project(iclr_low, context_rate_second_weight))

    def heads_first(array):
        lanes = array.reshape(2, 2, seq_rows, local_heads, HEAD)
        lanes = jnp.stack([lanes[0], lanes[1][:, ::-1]])
        lanes = jnp.transpose(lanes, (0, 1, 3, 2, 4))
        return lanes.reshape(lanes_total, seq_rows // BLOCK, BLOCK, HEAD)

    key_lanes = heads_first(key_vec)
    unit_key = key_lanes * lax.rsqrt(
        jnp.sum(key_lanes * key_lanes, axis=-1, keepdims=True) + UNIT_EPS
    )
    local_out, start_map, transition, local_end = block_terms(
        heads_first(receptance),
        key_lanes,
        heads_first(value_vec),
        unit_key,
        heads_first(iclr_rate),
        heads_first(log_decay),
    )
    identity = jnp.broadcast_to(jnp.eye(HEAD, dtype=jnp.float32), (lanes_total, HEAD, HEAD))
    empty_state = jnp.zeros((lanes_total, HEAD, HEAD), jnp.float32)
    (device_map, device_end), (prefix_maps, prefix_states) = lax.scan(
        through_blocks,
        (identity, empty_state),
        (jnp.moveaxis(transition, 1, 0), jnp.moveaxis(local_end, 1, 0)),
    )

    def link(step_index, state_pair):
        outgoing = state_pair[1]
        from_below = from_behind(outgoing[:half_lanes], "seq", 1)
        from_above = from_behind(outgoing[half_lanes:], "seq", -1)
        arriving = jnp.concatenate([from_below, from_above])
        return (arriving, state_product(arriving, device_map) + device_end)

    incoming, _ = lax.fori_loop(0, seq_count - 1, link, (empty_state, device_end))
    block_starts = jnp.einsum("lvk,nlkj->lnvj", incoming, prefix_maps, precision=PRECISE)
    block_starts = block_starts + jnp.moveaxis(prefix_states, 0, 1)
    wkv_lanes = local_out + jnp.einsum(
        "lbtk,lbvk->lbtv", start_map, block_starts, precision=PRECISE
    )
    wkv_out = wkv_lanes.reshape(2, 2, local_heads, seq_rows, HEAD)
    wkv_out = jnp.stack([wkv_out[0], wkv_out[1][:, :, ::-1]])
    head_mean = jnp.mean(wkv_out, axis=-1, keepdims=True)
    centered = wkv_out - head_mean
    head_spread = jnp.mean(centered * centered, axis=-1, keepdims=True)
    head_gain = group_gain.reshape(local_heads, HEAD)[None, None, :, None, :]
    grouped = centered * lax.rsqrt(head_spread + GROUP_EPS) * head_gain
    joined = jnp.transpose(grouped[0] + grouped[1], (0, 2, 1, 3)).reshape(2, seq_rows, local_width)
    joined = joined.astype(jnp.bfloat16)
    attention_part = project(joined, w_output)
    attention_whole = lax.psum(attention_part, "mp")
    residual_whole = whole_rows[:, 1:-1].astype(jnp.float32) + attention_whole
    ffn_in = layer_norm(residual_whole, ln2_gain).astype(jnp.bfloat16)
    pre_active = project(ffn_in, ffn_key)
    residual = lax.dynamic_slice_in_dim(
        residual_whole, lax.axis_index("mp") * local_width, local_width, 2
    )
    activated = jnp.square(jax.nn.relu(pre_active)).astype(jnp.bfloat16)
    ffn_local = lax.psum_scatter(
        project(activated, ffn_value).astype(jnp.bfloat16), "mp", scatter_dimension=2, tiled=True
    ).astype(jnp.float32)
    strand_out = residual + ffn_local
    rc_final = strand_out[1].astype(jnp.bfloat16)
    arrived = rc_final
    for bit_index in range(seq_count.bit_length() - 1):
        arrived = swapped(arrived, "seq", bit_index)
    return (strand_out[0] + arrived[::-1].astype(jnp.float32)).astype(jnp.bfloat16)


def solution(mesh):
    in_specs = (
        P("seq"),
        P("seq", "mp"),
        P("seq", "mp"),
        P(None, "mp"),
        P(),
        P(),
        P(),
        P(None, "mp"),
        P(None, "mp"),
        P(None, "mp"),
        P(),
        P("mp"),
        P(None, "mp"),
        P(),
        P("mp"),
        P(None, "mp"),
        P("mp"),
        P("mp", None),
        P(None, "mp"),
        P("mp", None),
    )
    out_specs = P("seq", "mp")
    return jax.shard_map(
        on_device, mesh=mesh, in_specs=in_specs, out_specs=out_specs, check_vma=False
    )
```

profile of v0, /device:TPU:0, one launch (start us, length us, event | category | flops | bytes accessed | tf_op | source)
XLA Modules:
  0.0 374.5 jit_solution(4720402621627019162)
XLA Ops:
  6.5 3.0 collective-permute-start.2
  27.0 2.9 collective-permute-done.6
  30.0 7.4 %all_gather.3 = bf16[2,130,1024]{2,1,0:T(8,128)(2,1)S(1)} all-gather(bf16[2,130,256]{2,1,0:T(8,128)(2,1)S(1)} %pad_maximum_fusion.4), channel_id=1, replica_groups=mesh['seq'=8,'mp'=4] {'mp'}, dimensions={2}, use_global_device_ids=true | all-gather | bytes 665600 | tf_op jit(solution)/shard_map/all_gather | solution.py:184
  40.8 3.1 fusion.31
  49.5 3.1 fusion.29
  63.5 4.0 %fusion.2 = (bf16[512,1024]{1,0:T(8,128)(2,1)}, bf16[512,1024]{1,0:T(8,128)(2,1)}, bf16[512,1024]{1,0:T(8,128)(2,1)S(1)}) fusion(f32[2,2,128,1024]{3,2,1,0:T(8,128)} %pad_maximum_fusion, f32[1024]{0:T(1024)S(1)} %bitcast.304, f32[2,128,1024]{2,1,0:T(8,128)} %copy-done.22, f32[1024]{0:T(1024)S(1)} %bitcast.306, f32[1024]{0:T(1024)S(1)} %bitcast.305), kind=kLoop, calls=%fused_computation.9 | loop fusion | flops 5242880 | bytes 6303744 | tf_op jit(solution)/shard_map/convert_element_type | solution.py:190
  93.2 2.9 convolution_select_fusion
  133.0 2.9 fusion.67
  137.0 133.7 %while.3 = (s32[]{:T(128)}, f32[16,64,64]{2,1,0:T(8,128)}, f32[16,64,64]{2,1,0:T(8,128)S(1)}, f32[16,64,64]{2,1,0:T(8,128)}, f32[16,64,64]{2,1,0:T(8,128)S(1)}) while((s32[]{:T(128)}, f32[16,64,64]{2,1,0:T(8,128)}, f32[16,64,64]{2,1,0:T(8,128)S(1)}, f32[16,64,64]{2,1,0:T(8,128)}, f32[16,64,64]{2,1,0:T(8,128)S(1)}) %tuple.55), condition=%wide.region_5.6_spmd.clone, body=%wide.region_4.5_spmd.sunk.clone | while | flops 50397184 | bytes 4587689 | solution.py:233
  137.7 4.8 %collective-permute-start = (f32[8,64,64]{2,1,0:T(8,128)}, f32[8,64,64]{2,1,0:T(8,128)S(1)}, u32[]{:S(2)}, u32[]{:S(2)}) collective-permute-start(f32[8,64,64]{2,1,0:T(8,128)} %get-tuple-element.147), channel_id=1, source_target_pairs={{0,4},{4,8},{8,12},{12,16},{16,20},{20,24},{24,28},{1,5},{5,9},{9,... | collective-permute-start | bytes 393224 | tf_op jit(solution)/shard_map/while/body/eval_jaxpr/ppermute | solution.py:39
  143.9 10.7 %collective-permute-done = f32[8,64,64]{2,1,0:T(8,128)S(1)} collective-permute-done((f32[8,64,64]{2,1,0:T(8,128)}, f32[8,64,64]{2,1,0:T(8,128)S(1)}, u32[]{:S(2)}, u32[]{:S(2)}) %collective-permute-start) | collective-permute-done | bytes 131104 | tf_op jit(solution)/shard_map/while/body/eval_jaxpr/ppermute | solution.py:39
  157.3 4.3 %collective-permute-start = (f32[8,64,64]{2,1,0:T(8,128)}, f32[8,64,64]{2,1,0:T(8,128)S(1)}, u32[]{:S(2)}, u32[]{:S(2)}) collective-permute-start(f32[8,64,64]{2,1,0:T(8,128)} %get-tuple-element.147), channel_id=1, source_target_pairs={{0,4},{4,8},{8,12},{12,16},{16,20},{20,24},{24,28},{1,5},{5,9},{9,... | collective-permute-start | bytes 393224 | tf_op jit(solution)/shard_map/while/body/eval_jaxpr/ppermute | solution.py:39
  162.9 9.9 %collective-permute-done = f32[8,64,64]{2,1,0:T(8,128)S(1)} collective-permute-done((f32[8,64,64]{2,1,0:T(8,128)}, f32[8,64,64]{2,1,0:T(8,128)S(1)}, u32[]{:S(2)}, u32[]{:S(2)}) %collective-permute-start) | collective-permute-done | bytes 131104 | tf_op jit(solution)/shard_map/while/body/eval_jaxpr/ppermute | solution.py:39
  175.5 4.3 %collective-permute-start = (f32[8,64,64]{2,1,0:T(8,128)}, f32[8,64,64]{2,1,0:T(8,128)S(1)}, u32[]{:S(2)}, u32[]{:S(2)}) collective-permute-start(f32[8,64,64]{2,1,0:T(8,128)} %get-tuple-element.147), channel_id=1, source_target_pairs={{0,4},{4,8},{8,12},{12,16},{16,20},{20,24},{24,28},{1,5},{5,9},{9,... | collective-permute-start | bytes 393224 | tf_op jit(solution)/shard_map/while/body/eval_jaxpr/ppermute | solution.py:39
  181.1 3.3 collective-permute-done
  184.4 5.9 %collective-permute-done.1 = f32[8,64,64]{2,1,0:T(8,128)S(1)} collective-permute-done((f32[8,64,64]{2,1,0:T(8,128)S(1)}, f32[8,64,64]{2,1,0:T(8,128)S(1)}, u32[]{:S(2)}, u32[]{:S(2)}) %collective-permute-start.1) | collective-permute-done | bytes 131104 | tf_op jit(solution)/shard_map/while/body/eval_jaxpr/ppermute | solution.py:39
  193.0 4.5 %collective-permute-start = (f32[8,64,64]{2,1,0:T(8,128)}, f32[8,64,64]{2,1,0:T(8,128)S(1)}, u32[]{:S(2)}, u32[]{:S(2)}) collective-permute-start(f32[8,64,64]{2,1,0:T(8,128)} %get-tuple-element.147), channel_id=1, source_target_pairs={{0,4},{4,8},{8,12},{12,16},{16,20},{20,24},{24,28},{1,5},{5,9},{9,... | collective-permute-start | bytes 393224 | tf_op jit(solution)/shard_map/while/body/eval_jaxpr/ppermute | solution.py:39
  198.9 3.6 collective-permute-done
  202.5 7.4 %collective-permute-done.1 = f32[8,64,64]{2,1,0:T(8,128)S(1)} collective-permute-done((f32[8,64,64]{2,1,0:T(8,128)S(1)}, f32[8,64,64]{2,1,0:T(8,128)S(1)}, u32[]{:S(2)}, u32[]{:S(2)}) %collective-permute-start.1) | collective-permute-done | bytes 131104 | tf_op jit(solution)/shard_map/while/body/eval_jaxpr/ppermute | solution.py:39
  212.6 4.5 %collective-permute-start = (f32[8,64,64]{2,1,0:T(8,128)}, f32[8,64,64]{2,1,0:T(8,128)S(1)}, u32[]{:S(2)}, u32[]{:S(2)}) collective-permute-start(f32[8,64,64]{2,1,0:T(8,128)} %get-tuple-element.147), channel_id=1, source_target_pairs={{0,4},{4,8},{8,12},{12,16},{16,20},{20,24},{24,28},{1,5},{5,9},{9,... | collective-permute-start | bytes 393224 | tf_op jit(solution)/shard_map/while/body/eval_jaxpr/ppermute | solution.py:39
  218.4 3.6 collective-permute-done
  222.0 7.4 %collective-permute-done.1 = f32[8,64,64]{2,1,0:T(8,128)S(1)} collective-permute-done((f32[8,64,64]{2,1,0:T(8,128)S(1)}, f32[8,64,64]{2,1,0:T(8,128)S(1)}, u32[]{:S(2)}, u32[]{:S(2)}) %collective-permute-start.1) | collective-permute-done | bytes 131104 | tf_op jit(solution)/shard_map/while/body/eval_jaxpr/ppermute | solution.py:39
  232.1 4.5 %collective-permute-start = (f32[8,64,64]{2,1,0:T(8,128)}, f32[8,64,64]{2,1,0:T(8,128)S(1)}, u32[]{:S(2)}, u32[]{:S(2)}) collective-permute-start(f32[8,64,64]{2,1,0:T(8,128)} %get-tuple-element.147), channel_id=1, source_target_pairs={{0,4},{4,8},{8,12},{12,16},{16,20},{20,24},{24,28},{1,5},{5,9},{9,... | collective-permute-start | bytes 393224 | tf_op jit(solution)/shard_map/while/body/eval_jaxpr/ppermute | solution.py:39
  238.0 3.6 collective-permute-done
  241.6 7.4 %collective-permute-done.1 = f32[8,64,64]{2,1,0:T(8,128)S(1)} collective-permute-done((f32[8,64,64]{2,1,0:T(8,128)S(1)}, f32[8,64,64]{2,1,0:T(8,128)S(1)}, u32[]{:S(2)}, u32[]{:S(2)}) %collective-permute-start.1) | collective-permute-done | bytes 131104 | tf_op jit(solution)/shard_map/while/body/eval_jaxpr/ppermute | solution.py:39
  251.7 4.5 %collective-permute-start = (f32[8,64,64]{2,1,0:T(8,128)}, f32[8,64,64]{2,1,0:T(8,128)S(1)}, u32[]{:S(2)}, u32[]{:S(2)}) collective-permute-start(f32[8,64,64]{2,1,0:T(8,128)} %get-tuple-element.147), channel_id=1, source_target_pairs={{0,4},{4,8},{8,12},{12,16},{16,20},{20,24},{24,28},{1,5},{5,9},{9,... | collective-permute-start | bytes 393224 | tf_op jit(solution)/shard_map/while/body/eval_jaxpr/ppermute | solution.py:39
  257.5 3.6 collective-permute-done
  261.1 7.4 %collective-permute-done.1 = f32[8,64,64]{2,1,0:T(8,128)S(1)} collective-permute-done((f32[8,64,64]{2,1,0:T(8,128)S(1)}, f32[8,64,64]{2,1,0:T(8,128)S(1)}, u32[]{:S(2)}, u32[]{:S(2)}) %collective-permute-start.1) | collective-permute-done | bytes 131104 | tf_op jit(solution)/shard_map/while/body/eval_jaxpr/ppermute | solution.py:39
  272.8 3.9 %convolution_add_fusion.7 = f32[16,128,64]{1,2,0:T(8,128)S(1)} fusion(f32[16,128,128]{2,1,0:T(8,128)} %convolution_select_fusion.3, f32[16,1,128,128]{2,3,0,1:T(8,128)} %copy-done.11, f32[16,128,64]{1,2,0:T(8,128)} %bitcast.283, f32[16,1,128,64]{2,3,0,1:T(8,128)} %copy-done.7), kind=kOutput, calls=%fused_computation.36 | convolution fusion | flops 201588736 | bytes 3145728 | tf_op jit(solution)/shard_map/lbts,lbsk->lbtk/dot_general | solution.py:120
  283.1 39.5 %all-reduce.2.cloned.1.call-done = f32[2,128,1024]{2,1,0:T(8,128)} async-done(((f32[2,128,1024]{2,1,0:T(8,128)}), f32[2,128,1024]{2,1,0:T(8,128)}) %all-reduce.2.cloned.1.call-update) | async-done | bytes 1048592 | tf_op jit(solution)/shard_map/psum | solution.py:249
  325.4 4.1 %fusion.15 = bf16[2,128,1024]{2,1,0:T(8,128)(2,1)} fusion(bf16[1024,1024]{1,0:T(8,128)(2,1)S(1)} %copy-done, bf16[1024,1024]{1,0:T(8,128)(2,1)} %param.40, f32[2,128,1024]{2,1,0:T(8,128)} %copy-done.12, f32[1024]{0:T(1024)S(1)} %copy-done.38, f32[2,128]{1,0:T(2,128)S(1)} %add_rsqrt_fusion.2, f32[2,128]{1,0:T(2,128)S(1)} %broadcast_multiply_fusion.2), kind=kOutput, calls=%fused_computation.34 | convolution fusion | flops 1075838976 | bytes 5773312 | tf_op jit(solution)/shard_map/dot_general | solution.py:51
  329.5 22.2 %reduce-scatter.2.cloned.1.call-done = bf16[2,128,256]{2,1,0:T(8,128)(2,1)} async-done(((bf16[2,128,1024]{2,1,0:T(8,128)(2,1)}), bf16[2,128,256]{2,1,0:T(8,128)(2,1)}) %reduce-scatter.2.cloned.1.call-update) | async-done | bytes 131088 | tf_op jit(solution)/shard_map/reduce_scatter | solution.py:257
  (256 shorter events, 154.9 us)
Async XLA Ops:
  6.5 318.8 %copy-start = (bf16[1024,1024]{1,0:T(8,128)(2,1)S(1)}, bf16[1024,1024]{1,0:T(8,128)(2,1)}, u32[]{:S(2)}) copy-start(bf16[1024,1024]{1,0:T(8,128)(2,1)} %param.41) | copy-start | bytes 6291460
  6.5 31.6 %copy-start.35 = (f32[1024]{0:T(1024)S(1)}, f32[1024]{0:T(1024)}, u32[]{:S(2)}) copy-start(f32[1024]{0:T(1024)} %param.26) | copy-start | bytes 12292
  6.5 316.1 %all-reduce.2.cloned.1.call-start = ((), (), s32[]{:S(2)}) async-start(), calls=%async_computation.1 | async-start | bytes 2097152 | tf_op jit(solution)/shard_map/psum | solution.py:249
  6.5 5.7 %collective-permute-start.2 = (s32[128]{0:T(128)}, s32[128]{0:T(128)S(1)}, u32[]{:S(2)}, u32[]{:S(2)}) collective-permute-start(s32[128]{0:T(128)} %param.22), channel_id=1, source_target_pairs={{0,4},{4,0},{8,12},{12,8},{16,20},{20,16},{24,28},{28,24},{1,5},{5... | collective-permute-start | bytes 1544 | tf_op jit(solution)/shard_map/ppermute | solution.py:20
  12.2 3.6 collective-permute-start.3
  15.8 4.4 %collective-permute-start.4 = (s32[128]{0:T(128)S(1)}, s32[128]{0:T(128)S(1)}, u32[]{:S(2)}, u32[]{:S(2)}) collective-permute-start(s32[128]{0:T(128)S(1)} %collective-permute-done.3), channel_id=1, source_target_pairs={{0,16},{4,20},{8,24},{12,28},{16,0},{20,4},{24,8},{28,12},{1,17},{... | collective-permute-start | bytes 1544 | tf_op jit(solution)/shard_map/ppermute | solution.py:20
  21.5 5.5 %collective-permute-start.5 = (bf16[2,1,256]{2,1,0:T(2,128)(2,1)S(1)}, bf16[2,1,256]{2,1,0:T(2,128)(2,1)S(1)}, u32[]{:S(2)}, u32[]{:S(2)}) collective-permute-start(bf16[2,1,256]{2,1,0:T(2,128)(2,1)S(1)} %get-tuple-element.100), channel_id=1, source_target_pairs={{0,4},{4,8},{8,12},{12,16},{16,20},{20,24},{24,28},{1,5},{5,9},{9,... | collective-permute-start | bytes 3080 | tf_op jit(solution)/shard_map/ppermute | solution.py:30
  24.3 5.6 %collective-permute-start.6 = (bf16[2,1,256]{2,1,0:T(2,128)(2,1)S(1)}, bf16[2,1,256]{2,1,0:T(2,128)(2,1)S(1)}, u32[]{:S(2)}, u32[]{:S(2)}) collective-permute-start(bf16[2,1,256]{2,1,0:T(2,128)(2,1)S(1)} %get-tuple-element.101), channel_id=1, source_target_pairs={{4,0},{8,4},{12,8},{16,12},{20,16},{24,20},{28,24},{5,1},{9,5},{13... | collective-permute-start | bytes 3080 | tf_op jit(solution)/shard_map/ppermute | solution.py:31
  38.8 10.7 %copy-start.22 = (f32[2,128,1024]{2,1,0:T(8,128)}, f32[2,128,1024]{2,1,0:T(8,128)S(1)}, u32[]{:S(2)}) copy-start(f32[2,128,1024]{2,1,0:T(8,128)S(1)} %get-tuple-element.78) | copy-start | bytes 3145732
  56.8 29.5 %copy-start.9 = (f32[2,2,128,4,64]{2,4,3,1,0:T(8,128)}, f32[2,2,128,4,64]{2,4,3,1,0:T(8,128)S(1)}, u32[]{:S(2)}) copy-start(f32[2,2,128,4,64]{2,4,3,1,0:T(8,128)S(1)} %get-tuple-element.107) | copy-start | bytes 1572868
  62.1 24.2 %copy-start.7 = (f32[16,1,128,64]{2,3,0,1:T(8,128)}, f32[16,1,128,64]{2,3,0,1:T(8,128)S(1)}, u32[]{:S(2)}) copy-start(f32[16,1,128,64]{2,3,0,1:T(8,128)S(1)} %copy.115) | copy-start | bytes 1572868
  88.5 24.8 %copy-start.13 = (f32[16,128,64]{1,2,0:T(8,128)}, f32[16,128,64]{1,2,0:T(8,128)S(1)}, u32[]{:S(2)}) copy-start(f32[16,128,64]{1,2,0:T(8,128)S(1)} %get-tuple-element.74) | copy-start | bytes 1572868
  137.7 16.8 %collective-permute-start = (f32[8,64,64]{2,1,0:T(8,128)}, f32[8,64,64]{2,1,0:T(8,128)S(1)}, u32[]{:S(2)}, u32[]{:S(2)}) collective-permute-start(f32[8,64,64]{2,1,0:T(8,128)} %get-tuple-element.147), channel_id=1, source_target_pairs={{0,4},{4,8},{8,12},{12,16},{16,20},{20,24},{24,28},{1,5},{5,9},{9,... | collective-permute-start | bytes 393224 | tf_op jit(solution)/shard_map/while/body/eval_jaxpr/ppermute | solution.py:39
  142.6 12.0 %collective-permute-start.1 = (f32[8,64,64]{2,1,0:T(8,128)S(1)}, f32[8,64,64]{2,1,0:T(8,128)S(1)}, u32[]{:S(2)}, u32[]{:S(2)}) collective-permute-start(f32[8,64,64]{2,1,0:T(8,128)S(1)} %get-tuple-element.148), channel_id=1, source_target_pairs={{4,0},{8,4},{12,8},{16,12},{20,16},{24,20},{28,24},{5,1},{9,5},{13... | collective-permute-start | bytes 393224 | tf_op jit(solution)/shard_map/while/body/eval_jaxpr/ppermute | solution.py:39
  157.3 15.5 %collective-permute-start = (f32[8,64,64]{2,1,0:T(8,128)}, f32[8,64,64]{2,1,0:T(8,128)S(1)}, u32[]{:S(2)}, u32[]{:S(2)}) collective-permute-start(f32[8,64,64]{2,1,0:T(8,128)} %get-tuple-element.147), channel_id=1, source_target_pairs={{0,4},{4,8},{8,12},{12,16},{16,20},{20,24},{24,28},{1,5},{5,9},{9,... | collective-permute-start | bytes 393224 | tf_op jit(solution)/shard_map/while/body/eval_jaxpr/ppermute | solution.py:39
  161.6 11.2 %collective-permute-start.1 = (f32[8,64,64]{2,1,0:T(8,128)S(1)}, f32[8,64,64]{2,1,0:T(8,128)S(1)}, u32[]{:S(2)}, u32[]{:S(2)}) collective-permute-start(f32[8,64,64]{2,1,0:T(8,128)S(1)} %get-tuple-element.148), channel_id=1, source_target_pairs={{4,0},{8,4},{12,8},{16,12},{20,16},{24,20},{28,24},{5,1},{9,5},{13... | collective-permute-start | bytes 393224 | tf_op jit(solution)/shard_map/while/body/eval_jaxpr/ppermute | solution.py:39
  175.5 8.9 %collective-permute-start = (f32[8,64,64]{2,1,0:T(8,128)}, f32[8,64,64]{2,1,0:T(8,128)S(1)}, u32[]{:S(2)}, u32[]{:S(2)}) collective-permute-start(f32[8,64,64]{2,1,0:T(8,128)} %get-tuple-element.147), channel_id=1, source_target_pairs={{0,4},{4,8},{8,12},{12,16},{16,20},{20,24},{24,28},{1,5},{5,9},{9,... | collective-permute-start | bytes 393224 | tf_op jit(solution)/shard_map/while/body/eval_jaxpr/ppermute | solution.py:39
  179.8 10.6 %collective-permute-start.1 = (f32[8,64,64]{2,1,0:T(8,128)S(1)}, f32[8,64,64]{2,1,0:T(8,128)S(1)}, u32[]{:S(2)}, u32[]{:S(2)}) collective-permute-start(f32[8,64,64]{2,1,0:T(8,128)S(1)} %get-tuple-element.148), channel_id=1, source_target_pairs={{4,0},{8,4},{12,8},{16,12},{20,16},{24,20},{28,24},{5,1},{9,5},{13... | collective-permute-start | bytes 393224 | tf_op jit(solution)/shard_map/while/body/eval_jaxpr/ppermute | solution.py:39
  193.0 9.4 %collective-permute-start = (f32[8,64,64]{2,1,0:T(8,128)}, f32[8,64,64]{2,1,0:T(8,128)S(1)}, u32[]{:S(2)}, u32[]{:S(2)}) collective-permute-start(f32[8,64,64]{2,1,0:T(8,128)} %get-tuple-element.147), channel_id=1, source_target_pairs={{0,4},{4,8},{8,12},{12,16},{16,20},{20,24},{24,28},{1,5},{5,9},{9,... | collective-permute-start | bytes 393224 | tf_op jit(solution)/shard_map/while/body/eval_jaxpr/ppermute | solution.py:39
  197.6 12.3 %collective-permute-start.1 = (f32[8,64,64]{2,1,0:T(8,128)S(1)}, f32[8,64,64]{2,1,0:T(8,128)S(1)}, u32[]{:S(2)}, u32[]{:S(2)}) collective-permute-start(f32[8,64,64]{2,1,0:T(8,128)S(1)} %get-tuple-element.148), channel_id=1, source_target_pairs={{4,0},{8,4},{12,8},{16,12},{20,16},{24,20},{28,24},{5,1},{9,5},{13... | collective-permute-start | bytes 393224 | tf_op jit(solution)/shard_map/while/body/eval_jaxpr/ppermute | solution.py:39
  212.6 9.4 %collective-permute-start = (f32[8,64,64]{2,1,0:T(8,128)}, f32[8,64,64]{2,1,0:T(8,128)S(1)}, u32[]{:S(2)}, u32[]{:S(2)}) collective-permute-start(f32[8,64,64]{2,1,0:T(8,128)} %get-tuple-element.147), channel_id=1, source_target_pairs={{0,4},{4,8},{8,12},{12,16},{16,20},{20,24},{24,28},{1,5},{5,9},{9,... | collective-permute-start | bytes 393224 | tf_op jit(solution)/shard_map/while/body/eval_jaxpr/ppermute | solution.py:39
  217.1 12.3 %collective-permute-start.1 = (f32[8,64,64]{2,1,0:T(8,128)S(1)}, f32[8,64,64]{2,1,0:T(8,128)S(1)}, u32[]{:S(2)}, u32[]{:S(2)}) collective-permute-start(f32[8,64,64]{2,1,0:T(8,128)S(1)} %get-tuple-element.148), channel_id=1, source_target_pairs={{4,0},{8,4},{12,8},{16,12},{20,16},{24,20},{28,24},{5,1},{9,5},{13... | collective-permute-start | bytes 393224 | tf_op jit(solution)/shard_map/while/body/eval_jaxpr/ppermute | solution.py:39
  232.1 9.4 %collective-permute-start = (f32[8,64,64]{2,1,0:T(8,128)}, f32[8,64,64]{2,1,0:T(8,128)S(1)}, u32[]{:S(2)}, u32[]{:S(2)}) collective-permute-start(f32[8,64,64]{2,1,0:T(8,128)} %get-tuple-element.147), channel_id=1, source_target_pairs={{0,4},{4,8},{8,12},{12,16},{16,20},{20,24},{24,28},{1,5},{5,9},{9,... | collective-permute-start | bytes 393224 | tf_op jit(solution)/shard_map/while/body/eval_jaxpr/ppermute | solution.py:39
  236.7 12.3 %collective-permute-start.1 = (f32[8,64,64]{2,1,0:T(8,128)S(1)}, f32[8,64,64]{2,1,0:T(8,128)S(1)}, u32[]{:S(2)}, u32[]{:S(2)}) collective-permute-start(f32[8,64,64]{2,1,0:T(8,128)S(1)} %get-tuple-element.148), channel_id=1, source_target_pairs={{4,0},{8,4},{12,8},{16,12},{20,16},{24,20},{28,24},{5,1},{9,5},{13... | collective-permute-start | bytes 393224 | tf_op jit(solution)/shard_map/while/body/eval_jaxpr/ppermute | solution.py:39
  251.7 9.4 %collective-permute-start = (f32[8,64,64]{2,1,0:T(8,128)}, f32[8,64,64]{2,1,0:T(8,128)S(1)}, u32[]{:S(2)}, u32[]{:S(2)}) collective-permute-start(f32[8,64,64]{2,1,0:T(8,128)} %get-tuple-element.147), channel_id=1, source_target_pairs={{0,4},{4,8},{8,12},{12,16},{16,20},{20,24},{24,28},{1,5},{5,9},{9,... | collective-permute-start | bytes 393224 | tf_op jit(solution)/shard_map/while/body/eval_jaxpr/ppermute | solution.py:39
  256.2 12.3 %collective-permute-start.1 = (f32[8,64,64]{2,1,0:T(8,128)S(1)}, f32[8,64,64]{2,1,0:T(8,128)S(1)}, u32[]{:S(2)}, u32[]{:S(2)}) collective-permute-start(f32[8,64,64]{2,1,0:T(8,128)S(1)} %get-tuple-element.148), channel_id=1, source_target_pairs={{4,0},{8,4},{12,8},{16,12},{20,16},{24,20},{28,24},{5,1},{9,5},{13... | collective-permute-start | bytes 393224 | tf_op jit(solution)/shard_map/while/body/eval_jaxpr/ppermute | solution.py:39
  280.6 42.1 %copy-start.3 = (bf16[2,130,1024]{2,1,0:T(8,128)(2,1)S(1)}, bf16[2,130,1024]{2,1,0:T(8,128)(2,1)}, u32[]{:S(2)}) copy-start(bf16[2,130,1024]{2,1,0:T(8,128)(2,1)} %copy-done.2) | copy-start | bytes 1597444
  283.1 42.3 %copy-start.38 = (f32[1024]{0:T(1024)S(1)}, f32[1024]{0:T(1024)}, u32[]{:S(2)}) copy-start(f32[1024]{0:T(1024)} %param.27) | copy-start | bytes 12292
  283.1 68.6 %reduce-scatter.2.cloned.1.call-start = ((), (), s32[]{:S(2)}) async-start(), calls=%async_computation.2 | async-start | bytes 655360 | tf_op jit(solution)/shard_map/reduce_scatter | solution.py:257
  352.7 4.3 %collective-permute-start.7 = (bf16[128,256]{1,0:T(8,128)(2,1)S(1)}, bf16[128,256]{1,0:T(8,128)(2,1)S(1)}, u32[]{:S(2)}, u32[]{:S(2)}) collective-permute-start(bf16[128,256]{1,0:T(8,128)(2,1)S(1)} %fusion.83), channel_id=1, source_target_pairs={{0,4},{4,0},{8,12},{12,8},{16,20},{20,16},{24,28},{28,24},{1,5},{5... | collective-permute-start | bytes 196616 | tf_op jit(solution)/shard_map/ppermute | solution.py:20
  357.0 4.3 %collective-permute-start.8 = (bf16[128,256]{1,0:T(8,128)(2,1)S(1)}, bf16[128,256]{1,0:T(8,128)(2,1)S(1)}, u32[]{:S(2)}, u32[]{:S(2)}) collective-permute-start(bf16[128,256]{1,0:T(8,128)(2,1)S(1)} %collective-permute-done.7), channel_id=1, source_target_pairs={{0,8},{4,12},{8,0},{12,4},{16,24},{20,28},{24,16},{28,20},{1,9},{5... | collective-permute-start | bytes 196616 | tf_op jit(solution)/shard_map/ppermute | solution.py:20
  361.3 5.2 %collective-permute-start.9 = (bf16[128,256]{1,0:T(8,128)(2,1)S(1)}, bf16[128,256]{1,0:T(8,128)(2,1)S(1)}, u32[]{:S(2)}, u32[]{:S(2)}) collective-permute-start(bf16[128,256]{1,0:T(8,128)(2,1)S(1)} %collective-permute-done.8), channel_id=1, source_target_pairs={{0,16},{4,20},{8,24},{12,28},{16,0},{20,4},{24,8},{28,12},{1,17},{... | collective-permute-start | bytes 196616 | tf_op jit(solution)/shard_map/ppermute | solution.py:20
  (39 other events, 109.0 us)
Sparse Core Ops, SparseCore 0:
  283.2 39.4 all-reduce.1
  329.6 22.0 reduce-scatter.1
where the time goes:
time: 382 us; the launch traced here: 374 us
  waiting for transfers between devices  150 us (39%)
  matrix products  77.3 us (20%)
  starting transfers between devices  57.4 us (15%)
  local copies, waits for them, and re-layouts  45.6 us (12%)
  other arithmetic  21 us (5%)
  between operations  14.7 us (4%)
  blocking collectives  7.35 us (2%)
    ppermute x14, waiting for transfers between devices, from_behind(): return lax.ppermute(block, axis, route)  73.7 us
    ppermute x14, starting transfers between devices, from_behind(): return lax.ppermute(block, axis, route)  40.6 us
    psum x1, waiting for transfers between devices, on_device(): attention_whole = lax.psum(attention_part, 'mp')  39.5 us
    reduce_scatter x1, waiting for transfers between devices, on_device(): lax.psum_scatter(project(activated, ffn_value).astype(jnp.bfloat16), 'mp'...  22.2 us
    slice x18, local copies, waits for them, and re-layouts, heads_first(): lanes = jnp.stack([lanes[0], lanes[1][:, ::-1]])  17.6 us
    dot_general x9, matrix products, state_product(): return jnp.einsum('lvk,lkj->lvj', state_in, mapping, precision=PRECISE)  15.9 us
    dot_general x12, matrix products, square_product(): jnp.einsum('lbts,lbsu->lbtu', left_side, right_side, precision=PRECISE)  14.3 us
    dot_general x7, matrix products, project(): result = jnp.dot(flat, weight, preferred_element_type=jnp.float32)  14 us
  transfers between devices with their start and end apart: 24, of which 20 were waited for; matrix products, arithmetic and copies ran while one was open for 1% of the time, Pallas kernels for 0%

commit v1 on v0

v1 whole, which is shorter than its diff:
```python
import functools

import jax
import jax.numpy as jnp
from jax import lax
from jax.experimental import pallas as pl
from jax.experimental.pallas import tpu as pltpu
from jax.sharding import PartitionSpec as P

HEAD = 64
DECAY_SCALE = 0.606531
NORM_EPS = 1e-05
GROUP_EPS = 0.00064
UNIT_EPS = 1e-06
RADIX = 4
F32 = jnp.float32
BF16 = jnp.bfloat16
VMEM_BYTES = 40 * 1024 * 1024


def mm(left, right):
    return jnp.dot(left, right, preferred_element_type=F32)


def mm_rows(left, right):
    return lax.dot_general(left, right, (((1,), (1,)), ((), ())), preferred_element_type=F32)


def mm_cols(left, right):
    return lax.dot_general(left, right, (((0,), (0,)), ((), ())), preferred_element_type=F32)


def halves(value):
    high = value.astype(BF16)
    return high, (value - high.astype(F32)).astype(BF16)


def head_sum(value, ones):
    high, low = halves(value)
    return mm(high, ones) + mm(low, ones)


def ids_of(shape, dim):
    return lax.broadcasted_iota(jnp.int32, shape, dim)


def block_ones(width):
    same = ids_of((width, width), 0) // HEAD == ids_of((width, width), 1) // HEAD
    return same


def spread(packed, same_head):
    tiled = jnp.concatenate([packed] * (packed.shape[1] // HEAD), axis=0)
    return jnp.where(same_head, tiled, jnp.zeros_like(tiled))


def layer_norm(values, gain):
    row_mean = jnp.mean(values, axis=-1, keepdims=True)
    centered = values - row_mean
    variance = jnp.mean(centered * centered, axis=-1, keepdims=True)
    return centered * lax.rsqrt(variance + NORM_EPS) * gain


def strands_kernel(ids_ref, fwd_ref, rc_ref, embed_ref, out_ref):
    rows = fwd_ref.shape[0]
    ids = ids_ref[...]
    letters = ids_of((embed_ref.shape[0], rows), 0)
    embed = embed_ref[...]

    def looked_up(values):
        onehot = (values == letters).astype(F32)
        return lax.dot_general(
            onehot,
            embed,
            (((0,), (0,)), ((), ())),
            precision=lax.Precision.HIGHEST,
            preferred_element_type=F32,
        )

    out_ref[0] = (fwd_ref[...].astype(F32) + looked_up(ids)).astype(BF16)
    flip = (ids_of((rows, rows), 0) + ids_of((rows, rows), 1) == rows - 1).astype(F32)
    turned = mm(flip.astype(BF16), rc_ref[...])
    out_ref[1] = (turned + looked_up(3 - ids)).astype(BF16)


def inverse_of(pulls, rows):
    row_ids, col_ids = ids_of((rows, rows), 0), ids_of((rows, rows), 1)
    eye = (row_ids == col_ids).astype(F32)
    size = 1
    inverses = None
    while size < rows:
        within = (row_ids // (2 * size) == col_ids // (2 * size)) & (row_ids // size != col_ids // size)
        parts = [jnp.where(within, pull, 0.0) for pull in pulls]
        if size == 1:
            inverses = [eye + part for part in parts]
        else:
            lows = [inverse.astype(BF16) for inverse in inverses]
            products = [mm(part.astype(BF16), low).astype(BF16) for part, low in zip(parts, lows)]
            inverses = [inverse + mm(low, product) for inverse, low, product in zip(inverses, lows, products)]
        size *= 2
    return inverses


def chunk_kernel(
    x_ref,
    before_ref,
    after_ref,
    gain_ref,
    mixing_ref,
    w_r_ref,
    w_k_ref,
    w_v_ref,
    w_d1_ref,
    d_base_ref,
    w_d2_ref,
    w_c1_ref,
    c_base_ref,
    w_c2_ref,
    local_ref,
    map_ref,
    up_ref,
    down_ref,
    normed,
    mixed,
    r_buf,
    k_buf,
    v_buf,
    d_buf,
    a_buf,
):
    strands, rows, _ = x_ref.shape
    width = w_r_ref.shape[1]
    heads = width // HEAD
    pad = 8
    gain = gain_ref[...]
    before = layer_norm(before_ref[...].astype(F32), gain)
    after = layer_norm(after_ref[...].astype(F32), gain)
    for s in range(strands):
        normed[s, pad : pad + rows, :] = layer_norm(x_ref[s].astype(F32), gain)
        normed[s, pad - 1 : pad, :] = before[s : s + 1]
        normed[s, pad + rows : pad + rows + 1, :] = after[s : s + 1]

    def mix(index):
        weight = mixing_ref[index : index + 1, :]
        for s in range(strands):
            center = normed[s, pad : pad + rows, :]
            for d in range(2):
                shift = pad - 1 + 2 * d
                neighbour = normed[s, shift : shift + rows, :]
                start = (d * strands + s) * rows
                mixed[start : start + rows, :] = (center + (neighbour - center) * weight).astype(BF16)
        return mixed[...]

    groups = 2 * strands
    shape = (groups, rows, width)
    r_buf[...] = mm(mix(0), w_r_ref[...]).reshape(shape)
    k_buf[...] = mm(mix(1), w_k_ref[...]).reshape(shape)
    v_buf[...] = mm(mix(2), w_v_ref[...]).reshape(shape)
    decay_low = jnp.tanh(mm(mix(3), w_d1_ref[...])).astype(BF16)
    d_buf[...] = (-DECAY_SCALE * jax.nn.sigmoid(d_base_ref[...] + mm(decay_low, w_d2_ref[...]))).reshape(shape)
    rate_low = mm(mix(4), w_c1_ref[...]).astype(BF16)
    a_buf[...] = jax.nn.sigmoid(c_base_ref[...] + mm(rate_low, w_c2_ref[...])).reshape(shape)

    def group(g):
        d = g // strands
        sign = 1 - 2 * d
        order = (ids_of((rows, rows), 0) - ids_of((rows, rows), 1)) * sign
        strict, inclusive = order > 0, order >= 0
        same = block_ones(width)
        ones = same.astype(F32).astype(BF16)
        lane_head = ids_of((1, width), 1) // HEAD

        def of_heads(value):
            return jnp.concatenate(
                [jnp.where(lane_head == h, value, 0.0).astype(BF16) for h in range(heads)], axis=0
            )

        receptance, key, value = r_buf[g], k_buf[g], v_buf[g]
        log_decay, rate = d_buf[g], a_buf[g]
        unit = key * lax.rsqrt(head_sum(key * key, ones) + UNIT_EPS)
        tri = inclusive.astype(F32).astype(BF16)
        high, low = halves(log_decay)
        totals = mm(tri, high) + mm(tri, low)
        middle = totals[rows // 2 : rows // 2 + 1]
        final = jnp.where(d == 0, totals[rows - 1 : rows], totals[0:1])
        here = jnp.exp(totals - middle)
        there = jnp.exp(middle - totals)
        left_prev = -unit * jnp.exp(totals - log_decay - middle)
        left_here = receptance * here
        right_insert = rate * unit * there
        right_key = key * there
        from_start = jnp.exp(middle)
        to_end = jnp.exp(final - middle)
        left = jnp.concatenate([left_prev, left_here], axis=0).astype(BF16)
        insert_pulls, key_pulls, insert_reads, key_reads = [], [], [], []
        for h in range(heads):
            mask = lane_head == h
            right = jnp.concatenate(
                [jnp.where(mask, right_insert, 0.0), jnp.where(mask, right_key, 0.0)], axis=0
            ).astype(BF16)
            scores = mm_rows(left, right)
            insert_pulls.append(jnp.where(strict, scores[:rows, :rows], 0.0))
            key_pulls.append(jnp.where(strict, scores[:rows, rows:], 0.0).astype(BF16))
            insert_reads.append(jnp.where(inclusive, scores[rows:, :rows], 0.0).astype(BF16))
            key_reads.append(jnp.where(inclusive, scores[rows:, rows:], 0.0).astype(BF16))
        values = of_heads(value)
        value_pull = mm(jnp.concatenate(key_pulls, axis=1), values)
        inverses = inverse_of(insert_pulls, rows)
        inverse = jnp.concatenate([item.astype(BF16) for item in inverses], axis=1)
        local_pull = mm(inverse, of_heads(value_pull))
        start_pull = mm(inverse, of_heads(left_prev * from_start))
        insert_read = jnp.concatenate(insert_reads, axis=1)
        key_read = jnp.concatenate(key_reads, axis=1)
        local_ref[g] = mm(insert_read, of_heads(local_pull)) + mm(key_read, values)
        map_ref[g] = (left_here * from_start + mm(insert_read, of_heads(start_pull))).astype(BF16)
        tail_insert = (right_insert * to_end).astype(BF16)
        tail_key = (right_key * to_end).astype(BF16)
        ends = mm_cols(tail_insert, local_pull.astype(BF16)) + mm_cols(tail_key, value.astype(BF16))
        maps = mm_cols(tail_insert, start_pull.astype(BF16))
        ends = jnp.where(same, ends, 0.0)
        maps = jnp.where(same, maps, 0.0)
        end = sum(ends[h * HEAD : (h + 1) * HEAD] for h in range(heads))
        across = sum(maps[h * HEAD : (h + 1) * HEAD] for h in range(heads))
        diagonal = ids_of((HEAD, width), 0) == ids_of((HEAD, width), 1) % HEAD
        across = across + jnp.where(diagonal, jnp.exp(final), 0.0)
        return jnp.concatenate([end, across], axis=0).astype(BF16)

    def up_group(s, carry):
        up_ref[s] = group(s)
        return carry

    def down_group(s, carry):
        down_ref[s] = group(s + strands)
        return carry

    lax.fori_loop(0, strands, up_group, 0)
    lax.fori_loop(0, strands, down_group, 0)


def composed(later, earlier, same_head, state_only=False):
    across = later[HEAD:].astype(BF16)
    state = mm(across, spread(earlier[:HEAD].astype(BF16), same_head)) + later[:HEAD].astype(F32)
    if state_only:
        return state
    return jnp.concatenate([state, mm(across, spread(earlier[HEAD:].astype(BF16), same_head))], axis=0)


def window_of(received, same_head, state_only):
    total = received[-1].astype(F32)
    for item in reversed(received[:-1]):
        total = composed(item, total, same_head, state_only)
    return total


def advance_kernel(has_window, count, state_only, *refs):
    taken = 1 + int(has_window) + count
    for d in range(2):
        ins = refs[d * taken : (d + 1) * taken]
        window_ref, current_ref = refs[2 * taken + 2 * d : 2 * taken + 2 * d + 2]
        same_head = block_ones(ins[0].shape[2])
        for s in range(ins[0].shape[0]):
            parts = [ref[s] for ref in ins]
            window = window_of(parts[taken - count :], same_head, False)
            current_ref[s] = composed(parts[0], window, same_head, state_only).astype(BF16)
            if has_window:
                window = composed(parts[1], window, same_head)
            window_ref[s] = window


def finish_kernel(has_window, count, state_only, *refs):
    taken = int(has_window) + count
    local_ref, map_ref, gain_ref, out_ref = refs[2 * taken :]
    strands, _, width = out_ref.shape
    same_head = block_ones(width)
    ones = same_head.astype(F32).astype(BF16)
    gain = gain_ref[...]
    for s in range(strands):
        joined = 0.0
        for d in range(2):
            parts = [ref[s] for ref in refs[d * taken : (d + 1) * taken]]
            state = window_of(parts[int(has_window) :], same_head, state_only)[:HEAD]
            if has_window:
                state = composed(parts[0], state, same_head, True)
            g = d * strands + s
            wkv = local_ref[g] + mm(map_ref[g], spread(state.astype(BF16), same_head))
            centered = wkv - head_sum(wkv, ones) * (1.0 / HEAD)
            variance = head_sum(centered * centered, ones) * (1.0 / HEAD)
            joined = joined + centered * lax.rsqrt(variance + GROUP_EPS)
        out_ref[s] = (joined * gain).astype(BF16)


def mix_kernel(index_ref, joined_ref, x_ref, w_ref, gain_ref, up_ref, down_ref, own_ref, *rest):
    *sent_refs, partial, total = rest
    strands, rows, _ = x_ref.shape
    width = own_ref.shape[1]
    gain = gain_ref[...]
    joined = jnp.concatenate([joined_ref[s] for s in range(strands)], axis=0)
    attention = mm(joined, w_ref[...])
    residuals = [x_ref[s].astype(F32) + attention[s * rows : (s + 1) * rows] for s in range(strands)]
    inner = jnp.concatenate([layer_norm(item, gain).astype(BF16) for item in residuals], axis=0)
    active = jnp.square(jnp.maximum(mm(inner, up_ref[...]), 0.0)).astype(BF16).astype(F32)
    added = sum(active[s * rows : (s + 1) * rows] for s in range(strands)).astype(BF16)
    partial[...] = mm(added, down_ref[...])
    total[...] = sum(residuals)

    def part(ref, which):
        return ref[:, pl.ds(pl.multiple_of(which * width, width), width)]

    me = index_ref[0]
    own_ref[...] = part(total, me) + part(partial, me)
    size = len(sent_refs) + 1
    for step, ref in enumerate(sent_refs):
        ref[...] = part(partial, lax.rem(me + step + 1, size)).astype(BF16)


def call(kernel, out_shape, scratch=(), **kwargs):
    return pl.pallas_call(
        kernel,
        out_shape=out_shape,
        scratch_shapes=list(scratch),
        compiler_params=pltpu.CompilerParams(vmem_limit_bytes=VMEM_BYTES),
        **kwargs,
    )


def shifted(value, axis, distance):
    devices = range(lax.axis_size(axis))
    return lax.ppermute(value, axis, [(i, i + distance) for i in devices if i + distance in devices])


def on_device(
    ids,
    hidden_fwd,
    hidden_rc,
    embed,
    ln1_gain,
    ln2_gain,
    mixing,
    w_receptance,
    w_key,
    w_value,
    decay_first_weight,
    decay_base,
    decay_second_weight,
    context_rate_first_weight,
    iclr_base,
    context_rate_second_weight,
    group_gain,
    w_output,
    ffn_key,
    ffn_value,
):
    rows, width = hidden_fwd.shape
    seq_count, mp_count = lax.axis_size("seq"), lax.axis_size("mp")
    strands, full = 2, ffn_key.shape[0]
    struct = jax.ShapeDtypeStruct

    mirror = [(i, seq_count - 1 - i) for i in range(seq_count)]
    rc_here = lax.ppermute(hidden_rc, "seq", mirror)
    local = call(strands_kernel, struct((strands, rows, width), BF16))(
        ids.reshape(1, rows), hidden_fwd, rc_here, embed
    )
    whole = lax.all_gather(local, "mp", axis=2, tiled=True)
    before = shifted(whole[:, rows - 1], "seq", 1)
    after = shifted(whole[:, 0], "seq", -1)
    w_output_whole = lax.all_gather(w_output, "mp", axis=0, tiled=True)

    groups = 2 * strands
    state_shape = (strands, 2 * HEAD, width)
    lanes = pltpu.VMEM((groups, rows, width), F32)
    local_out, start_map, up, down = call(
        chunk_kernel,
        (
            struct((groups, rows, width), F32),
            struct((groups, rows, width), BF16),
            struct(state_shape, BF16),
            struct(state_shape, BF16),
        ),
        scratch=[
            pltpu.VMEM((strands, rows + 16, full), F32),
            pltpu.VMEM((groups * rows, full), BF16),
            lanes,
            lanes,
            lanes,
            lanes,
            lanes,
        ],
    )(
        whole,
        before,
        after,
        ln1_gain.reshape(1, full),
        mixing,
        w_receptance,
        w_key,
        w_value,
        decay_first_weight,
        decay_base.reshape(1, width),
        decay_second_weight,
        context_rate_first_weight,
        iclr_base.reshape(1, width),
        context_rate_second_weight,
    )

    currents, windows = [up, down], [None, None]
    distance = 1
    while True:
        steps = [step for step in range(1, RADIX) if step * distance < seq_count]
        received = [
            [shifted(current, "seq", sign * step * distance) for step in steps]
            for current, sign in zip(currents, (1, -1))
        ]
        has_window = windows[0] is not None
        reach = distance * RADIX
        if reach >= seq_count:
            break
        state_only = 2 * reach >= seq_count
        current_struct = struct((strands, HEAD, width) if state_only else state_shape, BF16)
        operands = []
        for d in range(2):
            operands += [currents[d]] + ([windows[d]] if has_window else []) + received[d]
        outs = call(
            functools.partial(advance_kernel, has_window, len(steps), state_only),
            (struct(state_shape, F32), current_struct) * 2,
        )(*operands)
        windows, currents = [outs[0], outs[2]], [outs[1], outs[3]]
        distance = reach

    operands = []
    for d in range(2):
        operands += ([windows[d]] if has_window else []) + received[d]
    joined = call(
        functools.partial(finish_kernel, has_window, len(steps), len(steps) == 1),
        struct((strands, rows, width), BF16),
    )(*operands, local_out, start_map, group_gain.reshape(1, width))
    joined_whole = lax.all_gather(joined, "mp", axis=2, tiled=True)

    position = lax.axis_index("mp").astype(jnp.int32).reshape(1)
    vmem = pl.BlockSpec(memory_space=pltpu.VMEM)
    own, *sent = call(
        mix_kernel,
        (struct((rows, width), F32),) + (struct((rows, width), BF16),) * (mp_count - 1),
        scratch=[pltpu.VMEM((rows, full), F32), pltpu.VMEM((rows, full), F32)],
        in_specs=[pl.BlockSpec(memory_space=pltpu.SMEM)] + [vmem] * 6,
    )(position, joined_whole, whole, w_output_whole, ln2_gain.reshape(1, full), ffn_key, ffn_value)
    merged = own
    for step, item in enumerate(sent):
        pairs = [(i, (i + step + 1) % mp_count) for i in range(mp_count)]
        merged = merged + lax.ppermute(item, "mp", pairs).astype(F32)
    return merged.astype(BF16)


def solution(mesh):
    in_specs = (
        P("seq"),
        P("seq", "mp"),
        P("seq", "mp"),
        P(None, "mp"),
        P(),
        P(),
        P(),
        P(None, "mp"),
        P(None, "mp"),
        P(None, "mp"),
        P(),
        P("mp"),
        P(None, "mp"),
        P(),
        P("mp"),
        P(None, "mp"),
        P("mp"),
        P("mp", None),
        P(None, "mp"),
        P("mp", None),
    )
    out_specs = P("seq", "mp")
    return jax.shard_map(
        on_device, mesh=mesh, in_specs=in_specs, out_specs=out_specs, check_vma=False
    )
```

time: 382 us -> 125 us (0.33)
  the two profiles are of different devices: /device:TPU:0 before, /device:TPU:21 now
where the time goes in v1:
time: 125 us
  starting transfers between devices  34.3 us (27%)
  blocking collectives  23.5 us (19%)
  Pallas kernels  20.7 us (17%)
  waiting for transfers between devices  16.6 us (13%)
  local copies, waits for them, and re-layouts  15.2 us (12%)
  between operations  13.6 us (11%)
    ppermute x10, starting transfers between devices, shifted(): lax.ppermute(value, axis, [(i, i + distance) for i in devices if i + dist...  32.5 us
    unnamed x46, local copies, waits for them, and re-layouts  15.2 us
    pallas_call x1, Pallas kernels, on_device(): call(chunk_kernel, (struct((groups, rows, width), F32), struct((groups, r...  14.6 us
    all_gather x1, blocking collectives, on_device(): joined_whole = lax.all_gather(joined, 'mp', axis=2, tiled=True)  12.1 us
    all_gather x1, blocking collectives, on_device(): whole = lax.all_gather(local, 'mp', axis=2, tiled=True)  11.4 us
    ppermute x10, waiting for transfers between devices, shifted(): lax.ppermute(value, axis, [(i, i + distance) for i in devices if i + dist...  8.04 us
    ppermute x1, waiting for transfers between devices, on_device(): rc_here = lax.ppermute(hidden_rc, 'seq', mirror)  4.11 us
    ppermute x3, waiting for transfers between devices, on_device(): merged = merged + lax.ppermute(item, 'mp', pairs).astype(F32)  3.75 us
  transfers between devices with their start and end apart: 15, of which 8 were waited for; matrix products, arithmetic and copies ran while one was open for 2% of the time, Pallas kernels for 15%

profile of v1, /device:TPU:21, one launch (start us, length us, event | category | flops | bytes accessed | tf_op | source)
XLA Modules:
  0.0 124.6 jit_solution(3277753014523097433)
XLA Ops:
  7.4 4.1 %collective-permute-done.rc_ref = bf16[128,256]{1,0:T(8,128)(2,1)S(1)} collective-permute-done((bf16[128,256]{1,0:T(8,128)(2,1)}, bf16[128,256]{1,0:T(8,128)(2,1)S(1)}, u32[]{:S(2)}, u32[]{:S(2)}) %collective-permute-start) | collective-permute-done | bytes 65568 | tf_op jit(solution)/shard_map/ppermute | solution.py:359
  11.6 0.8 copy-done.10
  14.2 11.4 %all_gather.9.x_ref = bf16[2,128,1024]{2,1,0:T(8,128)(2,1)S(1)} all-gather(bf16[2,128,256]{2,1,0:T(8,128)(2,1)S(1)} %shard_map.190), channel_id=1, replica_groups=mesh['seq'=8,'mp'=4] {'mp'}, dimensions={2}, use_global_device_ids=true | all-gather | bytes 655360 | tf_op jit(solution)/shard_map/all_gather | solution.py:363
  25.6 5.4 %collective-permute-start.1 = (bf16[2,1024]{1,0:T(2,128)(2,1)S(1)}, bf16[2,1024]{1,0:T(2,128)(2,1)S(1)}, u32[]{:S(2)}, u32[]{:S(2)}) collective-permute-start(bf16[2,1024]{1,0:T(2,128)(2,1)S(1)} %bitcast.19), channel_id=1, source_target_pairs={{0,4},{4,8},{8,12},{12,16},{16,20},{20,24},{24,28},{1,5},{5,9},{9,... | collective-permute-start | bytes 12296 | tf_op jit(solution)/shard_map/ppermute | solution.py:328
  31.1 1.9 %collective-permute-start.2 = (bf16[2,1024]{1,0:T(2,128)(2,1)S(1)}, bf16[2,1024]{1,0:T(2,128)(2,1)S(1)}, u32[]{:S(2)}, u32[]{:S(2)}) collective-permute-start(bf16[2,1024]{1,0:T(2,128)(2,1)S(1)} %bitcast.20), channel_id=1, source_target_pairs={{4,0},{8,4},{12,8},{16,12},{20,16},{24,20},{28,24},{5,1},{9,5},{13... | collective-permute-start | bytes 12296 | tf_op jit(solution)/shard_map/ppermute | solution.py:328
  33.0 1.1 copy.23.w_d1_ref
  34.1 1.1 copy.24.w_c1_ref
  35.2 1.1 collective-permute-done.2.after_ref
  36.3 0.7 copy-done.11
  37.1 0.8 copy-done.12
  37.8 0.8 copy-done.13
  40.6 14.6 %shard_map.191 = (f32[4,128,256]{2,1,0:T(8,128)S(1)}, bf16[4,128,256]{2,1,0:T(8,128)(2,1)S(1)}, bf16[2,128,256]{2,1,0:T(8,128)(2,1)S(1)}, bf16[2,128,256]{2,1,0:T(8,128)(2,1)S(1)}) custom-call(bf16[2,128,1024]{2,1,0:T(8,128)(2,1)S(1)} %all_gather.9.x_ref, bf16[2,1024]{1,0:T(2,128)(2,1)S(1)} %collective-permute-done.1.before_ref, ...), custom_call_target="tpu_custom_call" | custom-call | tf_op jit(solution)/shard_map/pallas_call | solution.py:371
  55.3 3.3 %collective-permute-start.3 = (bf16[2,128,256]{2,1,0:T(8,128)(2,1)S(1)}, bf16[2,128,256]{2,1,0:T(8,128)(2,1)S(1)}, u32[]{:S(2)}, u32[]{:S(2)}) collective-permute-start(bf16[2,128,256]{2,1,0:T(8,128)(2,1)S(1)} %get-tuple-element.17.refs_0_), channel_id=1, source_target_pairs={{0,4},{4,8},{8,12},{12,16},{16,20},{20,24},{24,28},{1,5},{5,9},{9,... | collective-permute-start | bytes 393224 | tf_op jit(solution)/shard_map/ppermute | solution.py:328
  58.6 1.9 %collective-permute-start.4 = (bf16[2,128,256]{2,1,0:T(8,128)(2,1)S(1)}, bf16[2,128,256]{2,1,0:T(8,128)(2,1)S(1)}, u32[]{:S(2)}, u32[]{:S(2)}) collective-permute-start(bf16[2,128,256]{2,1,0:T(8,128)(2,1)S(1)} %get-tuple-element.17.refs_0_), channel_id=1, source_target_pairs={{0,8},{4,12},{8,16},{12,20},{16,24},{20,28},{1,9},{5,13},{9,17},{1... | collective-permute-start | bytes 393224 | tf_op jit(solution)/shard_map/ppermute | solution.py:328
  60.5 1.3 %collective-permute-start.5 = (bf16[2,128,256]{2,1,0:T(8,128)(2,1)S(1)}, bf16[2,128,256]{2,1,0:T(8,128)(2,1)S(1)}, u32[]{:S(2)}, u32[]{:S(2)}) collective-permute-start(bf16[2,128,256]{2,1,0:T(8,128)(2,1)S(1)} %get-tuple-element.17.refs_0_), channel_id=1, source_target_pairs={{0,12},{4,16},{8,20},{12,24},{16,28},{1,13},{5,17},{9,21},{13,25},... | collective-permute-start | bytes 393224 | tf_op jit(solution)/shard_map/ppermute | solution.py:328
  61.8 3.2 %collective-permute-start.6 = (bf16[2,128,256]{2,1,0:T(8,128)(2,1)S(1)}, bf16[2,128,256]{2,1,0:T(8,128)(2,1)S(1)}, u32[]{:S(2)}, u32[]{:S(2)}) collective-permute-start(bf16[2,128,256]{2,1,0:T(8,128)(2,1)S(1)} %get-tuple-element.18.refs_4_), channel_id=1, source_target_pairs={{4,0},{8,4},{12,8},{16,12},{20,16},{24,20},{28,24},{5,1},{9,5},{13... | collective-permute-start | bytes 393224 | tf_op jit(solution)/shard_map/ppermute | solution.py:328
  65.0 3.9 %collective-permute-start.7 = (bf16[2,128,256]{2,1,0:T(8,128)(2,1)S(1)}, bf16[2,128,256]{2,1,0:T(8,128)(2,1)S(1)}, u32[]{:S(2)}, u32[]{:S(2)}) collective-permute-start(bf16[2,128,256]{2,1,0:T(8,128)(2,1)S(1)} %get-tuple-element.18.refs_4_), channel_id=1, source_target_pairs={{8,0},{12,4},{16,8},{20,12},{24,16},{28,20},{9,1},{13,5},{17,9},{2... | collective-permute-start | bytes 393224 | tf_op jit(solution)/shard_map/ppermute | solution.py:328
  68.9 3.2 %collective-permute-start.8 = (bf16[2,128,256]{2,1,0:T(8,128)(2,1)S(1)}, bf16[2,128,256]{2,1,0:T(8,128)(2,1)S(1)}, u32[]{:S(2)}, u32[]{:S(2)}) collective-permute-start(bf16[2,128,256]{2,1,0:T(8,128)(2,1)S(1)} %get-tuple-element.18.refs_4_), channel_id=1, source_target_pairs={{12,0},{16,4},{20,8},{24,12},{28,16},{13,1},{17,5},{21,9},{25,13},... | collective-permute-start | bytes 393224 | tf_op jit(solution)/shard_map/ppermute | solution.py:328
  72.2 2.1 %collective-permute-done.8.refs_7_ = bf16[2,128,256]{2,1,0:T(8,128)(2,1)S(1)} collective-permute-done((bf16[2,128,256]{2,1,0:T(8,128)(2,1)S(1)}, bf16[2,128,256]{2,1,0:T(8,128)(2,1)S(1)}, u32[]{:S(2)}, u32[]{:S(2)}) %collective-permute-start.8) | collective-permute-done | bytes 131104 | tf_op jit(solution)/shard_map/ppermute | solution.py:328
  74.2 1.9 %shard_map.192 = (f32[2,128,256]{2,1,0:T(8,128)S(1)}, bf16[2,64,256]{2,1,0:T(8,128)(2,1)}, f32[2,128,256]{2,1,0:T(8,128)S(1)}, bf16[2,64,256]{2,1,0:T(8,128)(2,1)}) custom-call(bf16[2,128,256]{2,1,0:T(8,128)(2,1)S(1)} %get-tuple-element.17.refs_0_, bf16[2,128,256]{2,1,0:T(8,128)(2,1)S(1)} %collective-permute-done.3.refs_1_, ...), custom_call_target="tpu_custom_call" | custom-call | tf_op jit(solution)/shard_map/pallas_call | solution.py:422
  77.5 7.1 %collective-permute-start.10 = (bf16[2,64,256]{2,1,0:T(8,128)(2,1)}, bf16[2,64,256]{2,1,0:T(8,128)(2,1)S(1)}, u32[]{:S(2)}, u32[]{:S(2)}) collective-permute-start(bf16[2,64,256]{2,1,0:T(8,128)(2,1)} %get-tuple-element.22), channel_id=1, source_target_pairs={{16,0},{20,4},{24,8},{28,12},{17,1},{21,5},{25,9},{29,13},{18,2},{... | collective-permute-start | bytes 196616 | tf_op jit(solution)/shard_map/ppermute | solution.py:328
  84.7 1.3 %collective-permute-start.9 = (bf16[2,64,256]{2,1,0:T(8,128)(2,1)}, bf16[2,64,256]{2,1,0:T(8,128)(2,1)S(1)}, u32[]{:S(2)}, u32[]{:S(2)}) collective-permute-start(bf16[2,64,256]{2,1,0:T(8,128)(2,1)} %get-tuple-element.20), channel_id=1, source_target_pairs={{0,16},{4,20},{8,24},{12,28},{1,17},{5,21},{9,25},{13,29},{2,18},{... | collective-permute-start | bytes 196616 | tf_op jit(solution)/shard_map/ppermute | solution.py:328
  86.3 4.5 %collective-permute-done.9.refs_1_ = bf16[2,64,256]{2,1,0:T(8,128)(2,1)S(1)} collective-permute-done((bf16[2,64,256]{2,1,0:T(8,128)(2,1)}, bf16[2,64,256]{2,1,0:T(8,128)(2,1)S(1)}, u32[]{:S(2)}, u32[]{:S(2)}) %collective-permute-start.9) | collective-permute-done | bytes 65568 | tf_op jit(solution)/shard_map/ppermute | solution.py:328
  90.8 0.9 copy-done.7
  91.7 0.9 copy-done.9
  92.7 1.7 %shard_map.193 = bf16[2,128,256]{2,1,0:T(8,128)(2,1)S(1)} custom-call(f32[2,128,256]{2,1,0:T(8,128)S(1)} %copy-done.7, bf16[2,64,256]{2,1,0:T(8,128)(2,1)S(1)} %collective-permute-done.9.refs_1_, f32[2,128,256]{2,1,0:T(8,128)S(1)} %copy-done.9, bf16[2,64,256]{2,1,0:T(8,128)(2,1)S(1)} %collective-permute-done.10.refs_3_, ...), custom_call_target="tpu_custom_call" | custom-call | tf_op jit(solution)/shard_map/pallas_call | solution.py:432
  94.4 12.1 %all_gather.10.joined_ref = bf16[2,128,1024]{2,1,0:T(8,128)(2,1)S(1)} all-gather(bf16[2,128,256]{2,1,0:T(8,128)(2,1)S(1)} %shard_map.193), channel_id=1, replica_groups=mesh['seq'=8,'mp'=4] {'mp'}, dimensions={2}, use_global_device_ids=true | all-gather | bytes 655360 | tf_op jit(solution)/shard_map/all_gather | solution.py:436
  106.5 1.6 %copy-done.1 = bf16[1024,1024]{1,0:T(8,128)(2,1)S(1)} copy-done((bf16[1024,1024]{1,0:T(8,128)(2,1)S(1)}, bf16[1024,1024]{1,0:T(8,128)(2,1)}, u32[]{:S(2)}) %copy-start.1) | copy-done | bytes 2097176
  108.1 1.6 %copy-done.2 = bf16[1024,1024]{1,0:T(8,128)(2,1)S(1)} copy-done((bf16[1024,1024]{1,0:T(8,128)(2,1)S(1)}, bf16[1024,1024]{1,0:T(8,128)(2,1)}, u32[]{:S(2)}) %copy-start.2) | copy-done | bytes 2097176
  109.7 2.0 %shard_map.194 = (f32[128,256]{1,0:T(8,128)S(1)}, bf16[128,256]{1,0:T(8,128)(2,1)S(1)}, bf16[128,256]{1,0:T(8,128)(2,1)S(1)}, bf16[128,256]{1,0:T(8,128)(2,1)S(1)}) custom-call(s32[1]{0:T(128)} %bitcast.index_ref, bf16[2,128,1024]{2,1,0:T(8,128)(2,1)S(1)} %all_gather.10.joined_ref, bf16[2,128,1024]{2,1,0:T(8,128)(2,1)S(1)} %all_gather.9.x_ref, ...), custom_call_target="tpu_custom_call" | custom-call | tf_op jit(solution)/shard_map/pallas_call | solution.py:440
  112.4 0.9 collective-permute-start.12
  113.7 2.8 %collective-permute-done.12 = bf16[128,256]{1,0:T(8,128)(2,1)S(1)} collective-permute-done((bf16[128,256]{1,0:T(8,128)(2,1)S(1)}, bf16[128,256]{1,0:T(8,128)(2,1)S(1)}, u32[]{:S(2)}, u32[]{:S(2)}) %collective-permute-start.12) | collective-permute-done | bytes 65568 | tf_op jit(solution)/shard_map/ppermute | solution.py:449
  (54 shorter events, 8.8 us)
Async XLA Ops:
  6.5 29.8 %copy-start.3 = (bf16[1024,256]{1,0:T(8,128)(2,1)S(1)}, bf16[1024,256]{1,0:T(8,128)(2,1)}, u32[]{:S(2)}) copy-start(bf16[1024,256]{1,0:T(8,128)(2,1)} %w_r_ref.1) | copy-start | bytes 1572868
  6.5 29.8 %copy-start.4 = (bf16[1024,256]{1,0:T(8,128)(2,1)S(1)}, bf16[1024,256]{1,0:T(8,128)(2,1)}, u32[]{:S(2)}) copy-start(bf16[1024,256]{1,0:T(8,128)(2,1)} %w_k_ref.1) | copy-start | bytes 1572868
  6.5 29.8 %copy-start.5 = (bf16[1024,256]{1,0:T(8,128)(2,1)S(1)}, bf16[1024,256]{1,0:T(8,128)(2,1)}, u32[]{:S(2)}) copy-start(bf16[1024,256]{1,0:T(8,128)(2,1)} %w_v_ref.1) | copy-start | bytes 1572868
  6.5 100.0 %all-gather.2.cloned.1.call-start = ((), (), s32[]{:S(2)}) async-start(), calls=%async_computation | async-start | bytes 2621440 | tf_op jit(solution)/shard_map/all_gather | solution.py:366
  7.3 4.3 %collective-permute-start = (bf16[128,256]{1,0:T(8,128)(2,1)}, bf16[128,256]{1,0:T(8,128)(2,1)S(1)}, u32[]{:S(2)}, u32[]{:S(2)}) collective-permute-start(bf16[128,256]{1,0:T(8,128)(2,1)} %param.22), channel_id=1, source_target_pairs={{0,28},{4,24},{8,20},{12,16},{16,12},{20,8},{24,4},{28,0},{1,29},{... | collective-permute-start | bytes 196616 | tf_op jit(solution)/shard_map/ppermute | solution.py:359
  11.6 0.8 copy-start.10
  12.4 0.7 copy-start.15
  25.6 9.6 %collective-permute-start.1 = (bf16[2,1024]{1,0:T(2,128)(2,1)S(1)}, bf16[2,1024]{1,0:T(2,128)(2,1)S(1)}, u32[]{:S(2)}, u32[]{:S(2)}) collective-permute-start(bf16[2,1024]{1,0:T(2,128)(2,1)S(1)} %bitcast.19), channel_id=1, source_target_pairs={{0,4},{4,8},{8,12},{12,16},{16,20},{20,24},{24,28},{1,5},{5,9},{9,... | collective-permute-start | bytes 12296 | tf_op jit(solution)/shard_map/ppermute | solution.py:328
  31.1 5.3 %collective-permute-start.2 = (bf16[2,1024]{1,0:T(2,128)(2,1)S(1)}, bf16[2,1024]{1,0:T(2,128)(2,1)S(1)}, u32[]{:S(2)}, u32[]{:S(2)}) collective-permute-start(bf16[2,1024]{1,0:T(2,128)(2,1)S(1)} %bitcast.20), channel_id=1, source_target_pairs={{4,0},{8,4},{12,8},{16,12},{20,16},{24,20},{28,24},{5,1},{9,5},{13... | collective-permute-start | bytes 12296 | tf_op jit(solution)/shard_map/ppermute | solution.py:328
  34.1 56.7 %copy-start.19 = (f32[256]{0:T(256)S(1)}, f32[256]{0:T(256)}, u32[]{:S(2)}) copy-start(f32[256]{0:T(256)} %param.36) | copy-start | bytes 3076
  36.3 0.8 copy-start.11
  37.1 0.8 copy-start.12
  37.8 0.8 copy-start.13
  40.6 65.9 %copy-start.14 = (f32[1024]{0:T(1024)S(1)}, f32[1024]{0:T(1024)}, u32[]{:S(2)}) copy-start(f32[1024]{0:T(1024)} %param.25) | copy-start | bytes 12292
  55.3 51.2 %copy-start = (bf16[1024,1024]{1,0:T(8,128)(2,1)S(1)}, bf16[1024,1024]{1,0:T(8,128)(2,1)}, u32[]{:S(2)}) copy-start(bf16[1024,1024]{1,0:T(8,128)(2,1)} %up_ref.1) | copy-start | bytes 6291460
  55.3 13.6 %collective-permute-start.3 = (bf16[2,128,256]{2,1,0:T(8,128)(2,1)S(1)}, bf16[2,128,256]{2,1,0:T(8,128)(2,1)S(1)}, u32[]{:S(2)}, u32[]{:S(2)}) collective-permute-start(bf16[2,128,256]{2,1,0:T(8,128)(2,1)S(1)} %get-tuple-element.17.refs_0_), channel_id=1, source_target_pairs={{0,4},{4,8},{8,12},{12,16},{16,20},{20,24},{24,28},{1,5},{5,9},{9,... | collective-permute-start | bytes 393224 | tf_op jit(solution)/shard_map/ppermute | solution.py:328
  58.6 13.5 %collective-permute-start.4 = (bf16[2,128,256]{2,1,0:T(8,128)(2,1)S(1)}, bf16[2,128,256]{2,1,0:T(8,128)(2,1)S(1)}, u32[]{:S(2)}, u32[]{:S(2)}) collective-permute-start(bf16[2,128,256]{2,1,0:T(8,128)(2,1)S(1)} %get-tuple-element.17.refs_0_), channel_id=1, source_target_pairs={{0,8},{4,12},{8,16},{12,20},{16,24},{20,28},{1,9},{5,13},{9,17},{1... | collective-permute-start | bytes 393224 | tf_op jit(solution)/shard_map/ppermute | solution.py:328
  60.5 11.6 %collective-permute-start.5 = (bf16[2,128,256]{2,1,0:T(8,128)(2,1)S(1)}, bf16[2,128,256]{2,1,0:T(8,128)(2,1)S(1)}, u32[]{:S(2)}, u32[]{:S(2)}) collective-permute-start(bf16[2,128,256]{2,1,0:T(8,128)(2,1)S(1)} %get-tuple-element.17.refs_0_), channel_id=1, source_target_pairs={{0,12},{4,16},{8,20},{12,24},{16,28},{1,13},{5,17},{9,21},{13,25},... | collective-permute-start | bytes 393224 | tf_op jit(solution)/shard_map/ppermute | solution.py:328
  61.8 10.3 %collective-permute-start.6 = (bf16[2,128,256]{2,1,0:T(8,128)(2,1)S(1)}, bf16[2,128,256]{2,1,0:T(8,128)(2,1)S(1)}, u32[]{:S(2)}, u32[]{:S(2)}) collective-permute-start(bf16[2,128,256]{2,1,0:T(8,128)(2,1)S(1)} %get-tuple-element.18.refs_4_), channel_id=1, source_target_pairs={{4,0},{8,4},{12,8},{16,12},{20,16},{24,20},{28,24},{5,1},{9,5},{13... | collective-permute-start | bytes 393224 | tf_op jit(solution)/shard_map/ppermute | solution.py:328
  65.0 7.1 %collective-permute-start.7 = (bf16[2,128,256]{2,1,0:T(8,128)(2,1)S(1)}, bf16[2,128,256]{2,1,0:T(8,128)(2,1)S(1)}, u32[]{:S(2)}, u32[]{:S(2)}) collective-permute-start(bf16[2,128,256]{2,1,0:T(8,128)(2,1)S(1)} %get-tuple-element.18.refs_4_), channel_id=1, source_target_pairs={{8,0},{12,4},{16,8},{20,12},{24,16},{28,20},{9,1},{13,5},{17,9},{2... | collective-permute-start | bytes 393224 | tf_op jit(solution)/shard_map/ppermute | solution.py:328
  68.9 5.3 %collective-permute-start.8 = (bf16[2,128,256]{2,1,0:T(8,128)(2,1)S(1)}, bf16[2,128,256]{2,1,0:T(8,128)(2,1)S(1)}, u32[]{:S(2)}, u32[]{:S(2)}) collective-permute-start(bf16[2,128,256]{2,1,0:T(8,128)(2,1)S(1)} %get-tuple-element.18.refs_4_), channel_id=1, source_target_pairs={{12,0},{16,4},{20,8},{24,12},{28,16},{13,1},{17,5},{21,9},{25,13},... | collective-permute-start | bytes 393224 | tf_op jit(solution)/shard_map/ppermute | solution.py:328
  76.1 0.7 copy-start.6
  76.8 0.7 copy-start.8
  77.5 8.8 %collective-permute-start.10 = (bf16[2,64,256]{2,1,0:T(8,128)(2,1)}, bf16[2,64,256]{2,1,0:T(8,128)(2,1)S(1)}, u32[]{:S(2)}, u32[]{:S(2)}) collective-permute-start(bf16[2,64,256]{2,1,0:T(8,128)(2,1)} %get-tuple-element.22), channel_id=1, source_target_pairs={{16,0},{20,4},{24,8},{28,12},{17,1},{21,5},{25,9},{29,13},{18,2},{... | collective-permute-start | bytes 196616 | tf_op jit(solution)/shard_map/ppermute | solution.py:328
  84.7 6.1 %collective-permute-start.9 = (bf16[2,64,256]{2,1,0:T(8,128)(2,1)}, bf16[2,64,256]{2,1,0:T(8,128)(2,1)S(1)}, u32[]{:S(2)}, u32[]{:S(2)}) collective-permute-start(bf16[2,64,256]{2,1,0:T(8,128)(2,1)} %get-tuple-element.20), channel_id=1, source_target_pairs={{0,16},{4,20},{8,24},{12,28},{1,17},{5,21},{9,25},{13,29},{2,18},{... | collective-permute-start | bytes 196616 | tf_op jit(solution)/shard_map/ppermute | solution.py:328
  90.8 1.0 copy-start.7
  91.7 0.9 copy-start.9
  106.5 1.6 %copy-start.1 = (bf16[1024,1024]{1,0:T(8,128)(2,1)S(1)}, bf16[1024,1024]{1,0:T(8,128)(2,1)}, u32[]{:S(2)}) copy-start(bf16[1024,1024]{1,0:T(8,128)(2,1)} %down_ref.1) | copy-start | bytes 6291460
  108.1 1.6 %copy-start.2 = (bf16[1024,1024]{1,0:T(8,128)(2,1)S(1)}, bf16[1024,1024]{1,0:T(8,128)(2,1)}, u32[]{:S(2)}) copy-start(bf16[1024,1024]{1,0:T(8,128)(2,1)} %all-gather.2.cloned.1.call-done.w_ref) | copy-start | bytes 6291460
  111.8 2.0 %collective-permute-start.11 = (bf16[128,256]{1,0:T(8,128)(2,1)S(1)}, bf16[128,256]{1,0:T(8,128)(2,1)S(1)}, u32[]{:S(2)}, u32[]{:S(2)}) collective-permute-start(bf16[128,256]{1,0:T(8,128)(2,1)S(1)} %get-tuple-element.26), channel_id=1, source_target_pairs={{0,1},{1,2},{2,3},{3,0},{4,5},{5,6},{6,7},{7,4},{8,9},{9,10},{10,1... | collective-permute-start | bytes 196616 | tf_op jit(solution)/shard_map/ppermute | solution.py:449
  112.4 4.1 %collective-permute-start.12 = (bf16[128,256]{1,0:T(8,128)(2,1)S(1)}, bf16[128,256]{1,0:T(8,128)(2,1)S(1)}, u32[]{:S(2)}, u32[]{:S(2)}) collective-permute-start(bf16[128,256]{1,0:T(8,128)(2,1)S(1)} %get-tuple-element.27), channel_id=1, source_target_pairs={{0,2},{1,3},{2,0},{3,1},{4,6},{5,7},{6,4},{7,5},{8,10},{9,11},{10,... | collective-permute-start | bytes 196616 | tf_op jit(solution)/shard_map/ppermute | solution.py:449
  113.3 3.8 %collective-permute-start.13 = (bf16[128,256]{1,0:T(8,128)(2,1)S(1)}, bf16[128,256]{1,0:T(8,128)(2,1)S(1)}, u32[]{:S(2)}, u32[]{:S(2)}) collective-permute-start(bf16[128,256]{1,0:T(8,128)(2,1)S(1)} %get-tuple-element.28), channel_id=1, source_target_pairs={{0,3},{1,0},{2,1},{3,2},{4,7},{5,4},{6,5},{7,6},{8,11},{9,8},{10,9... | collective-permute-start | bytes 196616 | tf_op jit(solution)/shard_map/ppermute | solution.py:449
  (4 other events, 2.7 us)
Sparse Core Ops, SparseCore 0:
  8.9 25.8 all-gather.1

commit v2 on v1

v2 whole, which is shorter than its diff:
```python
import functools

import jax
import jax.numpy as jnp
from jax import lax
from jax.experimental import pallas as pl
from jax.experimental.pallas import tpu as pltpu
from jax.sharding import PartitionSpec as P

HEAD = 64
DECAY_SCALE = 0.606531
NORM_EPS = 1e-05
GROUP_EPS = 0.00064
UNIT_EPS = 1e-06
RADIX = 4
F32 = jnp.float32
BF16 = jnp.bfloat16
VMEM_BYTES = 32 * 1024 * 1024
VMEM_SPEC = pl.BlockSpec(memory_space=pltpu.VMEM)
SMEM_SPEC = pl.BlockSpec(memory_space=pltpu.SMEM)
ANY_SPEC = pl.BlockSpec(memory_space=pl.ANY)


def mm(left, right):
    return jnp.dot(left, right, preferred_element_type=F32)


def mm_rows(left, right):
    return lax.dot_general(left, right, (((1,), (1,)), ((), ())), preferred_element_type=F32)


def mm_cols(left, right):
    return lax.dot_general(left, right, (((0,), (0,)), ((), ())), preferred_element_type=F32)


def halves(value):
    high = value.astype(BF16)
    return high, (value - high.astype(F32)).astype(BF16)


def head_sum(value, ones):
    high, low = halves(value)
    return mm(high, ones) + mm(low, ones)


def ids_of(shape, dim):
    return lax.broadcasted_iota(jnp.int32, shape, dim)


def block_ones(width):
    same = ids_of((width, width), 0) // HEAD == ids_of((width, width), 1) // HEAD
    return same


def spread(packed, same_head):
    tiled = jnp.concatenate([packed] * (packed.shape[1] // HEAD), axis=0)
    return jnp.where(same_head, tiled, jnp.zeros_like(tiled))


def layer_norm(values, gain):
    row_mean = jnp.mean(values, axis=-1, keepdims=True)
    centered = values - row_mean
    variance = jnp.mean(centered * centered, axis=-1, keepdims=True)
    return centered * lax.rsqrt(variance + NORM_EPS) * gain


def strands_kernel(*refs):
    ins, out_ref, locals_, sems = refs[:4], refs[4], refs[5:9], refs[9]
    arrived(copied(ins, locals_, sems))
    ids_ref, fwd_ref, rc_ref, embed_ref = locals_
    rows = fwd_ref.shape[0]
    ids = ids_ref[...]
    letters = ids_of((embed_ref.shape[0], rows), 0)
    embed = embed_ref[...]

    def looked_up(values):
        onehot = (values == letters).astype(F32)
        return lax.dot_general(
            onehot,
            embed,
            (((0,), (0,)), ((), ())),
            precision=lax.Precision.HIGHEST,
            preferred_element_type=F32,
        )

    out_ref[0] = (fwd_ref[...].astype(F32) + looked_up(ids)).astype(BF16)
    flip = (ids_of((rows, rows), 0) + ids_of((rows, rows), 1) == rows - 1).astype(F32)
    turned = mm(flip.astype(BF16), rc_ref[...])
    out_ref[1] = (turned + looked_up(3 - ids)).astype(BF16)


def inverse_of(pulls, rows):
    row_ids, col_ids = ids_of((rows, rows), 0), ids_of((rows, rows), 1)
    eye = (row_ids == col_ids).astype(F32)
    size = 1
    inverses = None
    while size < rows:
        within = (row_ids // (2 * size) == col_ids // (2 * size)) & (row_ids // size != col_ids // size)
        parts = [jnp.where(within, pull, 0.0) for pull in pulls]
        if size == 1:
            inverses = [eye + part for part in parts]
        else:
            lows = [inverse.astype(BF16) for inverse in inverses]
            products = [mm(part.astype(BF16), low).astype(BF16) for part, low in zip(parts, lows)]
            inverses = [inverse + mm(low, product) for inverse, low, product in zip(inverses, lows, products)]
        size *= 2
    return inverses


def copied(sources, targets, sems):
    copies = [pltpu.make_async_copy(src, dst, sems.at[i]) for i, (src, dst) in enumerate(zip(sources, targets))]
    for item in copies:
        item.start()
    return copies


def arrived(copies):
    for item in copies:
        item.wait()


def gates(decay_mix, rate_mix, d_base, w_d2, c_base, w_c2, w_d1, w_c1):
    decay_low = jnp.tanh(mm_rows(decay_mix, w_d1)).astype(BF16)
    log_decay = -DECAY_SCALE * jax.nn.sigmoid(d_base + mm(decay_low, w_d2))
    rate_low = mm_rows(rate_mix, w_c1).astype(BF16)
    return log_decay, jax.nn.sigmoid(c_base + mm(rate_low, w_c2))


def project_kernel(x_ref, w_r_ref, w_k_ref, w_v_ref, *refs):
    smalls, refs = refs[:8], refs[8:]
    outs, edge_ref = refs[:5], refs[5]
    normed, mixed = refs[6:8]
    locals_, sems = refs[8:16], refs[16]
    gain_ref, mixing_ref, w_d1, w_c1, d_base, w_d2, c_base, w_c2 = locals_
    copies = copied(smalls, locals_, sems)
    strands, rows, _ = x_ref.shape
    width = w_r_ref.shape[1]
    pad = 8
    arrived(copies[:2])
    gain = gain_ref[...]
    for s in range(strands):
        values = layer_norm(x_ref[s].astype(F32), gain)
        normed[s, pad : pad + rows, :] = values
        normed[s, pad - 1 : pad, :] = jnp.zeros_like(values[:1])
        normed[s, pad + rows : pad + rows + 1, :] = jnp.zeros_like(values[:1])
        edge_ref[s : s + 1, :] = values[:1]
        edge_ref[strands + s : strands + s + 1, :] = values[rows - 1 :]

    def mix(index):
        weight = mixing_ref[index : index + 1, :]
        for s in range(strands):
            center = normed[s, pad : pad + rows, :]
            for d in range(2):
                shift = pad - 1 + 2 * d
                neighbour = normed[s, shift : shift + rows, :]
                start = (d * strands + s) * rows
                mixed[start : start + rows, :] = (center + (neighbour - center) * weight).astype(BF16)
        return mixed[...]

    shape = (2 * strands, rows, width)
    for index, w_ref in enumerate((w_r_ref, w_k_ref, w_v_ref)):
        outs[index][...] = mm(mix(index), w_ref[...]).reshape(shape)
    arrived(copies[2:])
    log_decay, rate = gates(
        mix(3), mix(4), d_base[...], w_d2[...], c_base[...], w_c2[...], w_d1[...], w_c1[...]
    )
    outs[3][...] = log_decay.reshape(shape)
    outs[4][...] = rate.reshape(shape)


def masked_heads(value, lane_head, heads):
    return jnp.concatenate([jnp.where(lane_head == h, value, 0.0).astype(BF16) for h in range(heads)], axis=0)


def chunk_kernel(first, direction_ref, *refs):
    lanes, refs = refs[:5], refs[5:]
    if first:
        before_ref, after_ref, edge_ref, w_r_ref, w_k_ref, w_v_ref = refs[:6]
        smalls, refs = refs[6:14], refs[14:]
    else:
        edges_ref, refs = refs[0], refs[1:]
    state_ref, here_ref, insert_ref, key_ref, value_ref, pull_ref, start_ref, read_ref = refs[:8]
    refs = refs[8:]
    if first:
        edges_ref, refs = refs[0], refs[1:]
    r_buf, k_buf, v_buf, d_buf, a_buf = refs[:5]
    sems, refs = refs[5], refs[6:]
    strands, rows, width = r_buf.shape
    heads = width // HEAD
    d = direction_ref[0]
    copies = copied([ref.at[pl.ds(d * strands, strands)] for ref in lanes], (r_buf, k_buf, v_buf, d_buf, a_buf), sems)
    if first:
        locals_, small_sems = refs[:8], refs[8]
        small_copies = copied(smalls, locals_, small_sems)
        gain_ref, mixing_ref, w_d1, w_c1, d_base, w_d2, c_base, w_c2 = locals_
        arrived(small_copies)
        gain = gain_ref[...]
        center = edge_ref[...]
        halo = jnp.concatenate([before_ref[...], after_ref[...]], axis=0).astype(F32)
        change = layer_norm(halo, gain) - center

        def mix(index):
            return (center + change * mixing_ref[index : index + 1, :]).astype(BF16)

        for index, w_ref in enumerate((w_r_ref, w_k_ref, w_v_ref)):
            edges_ref[index] = mm(mix(index), w_ref[...])
        log_decay, rate = gates(
            mix(3), mix(4), d_base[...], w_d2[...], c_base[...], w_c2[...], w_d1[...], w_c1[...]
        )
        edges_ref[3] = log_decay
        edges_ref[4] = rate
    arrived(copies)
    edge_row = d * (rows - 1)
    at_edge = ids_of((rows, width), 0) == edge_row
    order = (ids_of((rows, rows), 0) - ids_of((rows, rows), 1)) * (1 - 2 * d)
    strict, inclusive = order > 0, order >= 0
    same = block_ones(width)
    ones = same.astype(F32).astype(BF16)
    lane_head = ids_of((1, width), 1) // HEAD
    tri = inclusive.astype(F32).astype(BF16)

    def of_heads(value):
        return masked_heads(value, lane_head, heads)

    def group(s, carry):
        def lane(index, buf):
            return jnp.where(at_edge, edges_ref[index, pl.ds(d * strands + s, 1), :], buf[s])

        receptance, key, value = lane(0, r_buf), lane(1, k_buf), lane(2, v_buf)
        log_decay, rate = lane(3, d_buf), lane(4, a_buf)
        unit = key * lax.rsqrt(head_sum(key * key, ones) + UNIT_EPS)
        high, low = halves(log_decay)
        totals = mm(tri, high) + mm(tri, low)
        middle = totals[rows // 2 : rows // 2 + 1]
        final = jnp.where(d == 0, totals[rows - 1 : rows], totals[0:1])
        there = jnp.exp(middle - totals)
        left_prev = -unit * jnp.exp(totals - log_decay - middle)
        left_here = receptance * jnp.exp(totals - middle)
        right_insert = rate * unit * there
        right_key = key * there
        from_start = jnp.exp(middle)
        to_end = jnp.exp(final - middle)
        left = left_prev.astype(BF16)
        insert_pulls, key_pulls = [], []
        for h in range(heads):
            mask = lane_head == h
            right = jnp.concatenate(
                [jnp.where(mask, right_insert, 0.0), jnp.where(mask, right_key, 0.0)], axis=0
            ).astype(BF16)
            scores = mm_rows(left, right)
            insert_pulls.append(jnp.where(strict, scores[:, :rows], 0.0))
            key_pulls.append(jnp.where(strict, scores[:, rows:], 0.0).astype(BF16))
        value_pull = mm(jnp.concatenate(key_pulls, axis=1), of_heads(value))
        inverses = inverse_of(insert_pulls, rows)
        inverse = jnp.concatenate([item.astype(BF16) for item in inverses], axis=1)
        local_pull = mm(inverse, of_heads(value_pull)).astype(BF16)
        start_pull = mm(inverse, of_heads(left_prev * from_start)).astype(BF16)
        value = value.astype(BF16)
        here_ref[s] = left_here.astype(BF16)
        insert_ref[s] = right_insert.astype(BF16)
        key_ref[s] = right_key.astype(BF16)
        value_ref[s] = value
        pull_ref[s] = local_pull
        start_ref[s] = start_pull
        read_ref[s] = (left_here * from_start).astype(BF16)
        tail_insert = (right_insert * to_end).astype(BF16)
        tail_key = (right_key * to_end).astype(BF16)
        ends = mm_cols(tail_insert, local_pull) + mm_cols(tail_key, value)
        maps = mm_cols(tail_insert, start_pull)
        ends = jnp.where(same, ends, 0.0)
        maps = jnp.where(same, maps, 0.0)
        end = sum(ends[h * HEAD : (h + 1) * HEAD] for h in range(heads))
        across = sum(maps[h * HEAD : (h + 1) * HEAD] for h in range(heads))
        diagonal = ids_of((HEAD, width), 0) == ids_of((HEAD, width), 1) % HEAD
        across = across + jnp.where(diagonal, jnp.exp(final), 0.0)
        state_ref[s] = jnp.concatenate([end, across], axis=0).astype(BF16)
        return carry

    lax.fori_loop(0, strands, group, 0)


def read_kernel(*refs):
    direction_ref, refs = refs[0], refs[1:]
    roles, (local_ref, map_ref) = (refs[:7], refs[7:14]), refs[14:]
    strands, rows, width = roles[0][0].shape
    heads = width // HEAD
    lane_head = ids_of((1, width), 1) // HEAD
    for role, (here_ref, insert_ref, key_ref, value_ref, pull_ref, start_ref, read_ref) in enumerate(roles):
        sign = (1 - 2 * direction_ref[0]) * (1 - 2 * role)
        inclusive = (ids_of((rows, rows), 0) - ids_of((rows, rows), 1)) * sign >= 0

        def group(s, carry):
            here, insert, key = here_ref[s], insert_ref[s], key_ref[s]
            reads = []
            for source in (insert, key):
                scores = mm_rows(here, masked_heads(source, lane_head, heads))
                parts = [scores[:, h * rows : (h + 1) * rows] for h in range(heads)]
                reads.append(jnp.concatenate([jnp.where(inclusive, p, 0.0).astype(BF16) for p in parts], axis=1))
            pull, start, value = [
                masked_heads(ref[s], lane_head, heads) for ref in (pull_ref, start_ref, value_ref)
            ]
            g = role * strands + s
            local_ref[g] = mm(reads[0], pull) + mm(reads[1], value)
            map_ref[g] = (read_ref[s].astype(F32) + mm(reads[0], start)).astype(BF16)
            return carry

        lax.fori_loop(0, strands, group, 0)


def composed(later, earlier, same_head, state_only=False):
    across = later[HEAD:].astype(BF16)
    state = mm(across, spread(earlier[:HEAD].astype(BF16), same_head)) + later[:HEAD].astype(F32)
    if state_only:
        return state
    return jnp.concatenate([state, mm(across, spread(earlier[HEAD:].astype(BF16), same_head))], axis=0)


def window_of(received, same_head, state_only):
    total = received[-1].astype(F32)
    for item in reversed(received[:-1]):
        total = composed(item, total, same_head, state_only)
    return total


def pair_kernel(keep_ref, from_ref, pair_ref, state_ref):
    same_head = block_ones(keep_ref.shape[2])
    for s in range(keep_ref.shape[0]):
        pair = composed(keep_ref[s], from_ref[s], same_head).astype(BF16)
        pair_ref[s] = pair
        state_ref[s] = pair[:HEAD]


def advance_kernel(has_window, *refs):
    *ins, window_ref, current_ref, state_ref = refs
    same_head = block_ones(ins[0].shape[2])
    for s in range(ins[0].shape[0]):
        parts = [ref[s] for ref in ins]
        window = window_of(parts[1 + int(has_window) :], same_head, False)
        current = composed(parts[0], window, same_head).astype(BF16)
        current_ref[s] = current
        state_ref[s] = current[:HEAD]
        if has_window:
            window = composed(parts[1], window, same_head)
        window_ref[s] = window


def entry_kernel(has_window, *refs):
    *ins, entry_ref = refs
    same_head = block_ones(entry_ref.shape[2])
    for s in range(entry_ref.shape[0]):
        parts = [ref[s] for ref in ins]
        entry = window_of(parts[int(has_window) :], same_head, True)[:HEAD]
        if has_window:
            entry = composed(parts[0], entry, same_head, True)
        entry_ref[s] = entry.astype(BF16)


def finish_kernel(entry_ref, from_ref, other_ref, local_ref, map_ref, gain_ref, out_ref):
    strands, _, width = out_ref.shape
    same_head = block_ones(width)
    ones = same_head.astype(F32).astype(BF16)
    gain = gain_ref[...]
    for s in range(strands):
        kept = composed(from_ref[s], entry_ref[s], same_head, True).astype(BF16)
        joined = 0.0
        for role, state in enumerate((other_ref[s], kept)):
            g = role * strands + s
            wkv = local_ref[g] + mm(map_ref[g], spread(state, same_head))
            centered = wkv - head_sum(wkv, ones) * (1.0 / HEAD)
            variance = head_sum(centered * centered, ones) * (1.0 / HEAD)
            joined = joined + centered * lax.rsqrt(variance + GROUP_EPS)
        out_ref[s] = (joined * gain).astype(BF16)


def mix_kernel(index_ref, joined_ref, x_ref, w_ref, gain_ref, up_hbm, down_hbm, own_ref, *rest):
    *sent_refs, partial, total, up_ref, down_ref, sems = rest
    copies = copied((up_hbm, down_hbm), (up_ref, down_ref), sems)
    strands, rows, _ = x_ref.shape
    width = own_ref.shape[1]
    gain = gain_ref[...]
    joined = jnp.concatenate([joined_ref[s] for s in range(strands)], axis=0)
    attention = mm(joined, w_ref[...])
    residuals = [x_ref[s].astype(F32) + attention[s * rows : (s + 1) * rows] for s in range(strands)]
    inner = jnp.concatenate([layer_norm(item, gain).astype(BF16) for item in residuals], axis=0)
    copies[0].wait()
    active = jnp.square(jnp.maximum(mm(inner, up_ref[...]), 0.0)).astype(BF16).astype(F32)
    added = sum(active[s * rows : (s + 1) * rows] for s in range(strands)).astype(BF16)
    copies[1].wait()
    partial[...] = mm(added, down_ref[...])
    total[...] = sum(residuals)

    def part(ref, which):
        return ref[:, pl.ds(pl.multiple_of(which * width, width), width)]

    me = index_ref[0]
    own_ref[...] = part(total, me) + part(partial, me)
    size = len(sent_refs) + 1
    for step, ref in enumerate(sent_refs):
        ref[...] = part(partial, lax.rem(me + step + 1, size)).astype(BF16)


def call(kernel, out_shape, scratch=(), **kwargs):
    return pl.pallas_call(
        kernel,
        out_shape=out_shape,
        scratch_shapes=list(scratch),
        compiler_params=pltpu.CompilerParams(vmem_limit_bytes=VMEM_BYTES),
        **kwargs,
    )


def shifted(value, axis, distance):
    devices = range(lax.axis_size(axis))
    return lax.ppermute(value, axis, [(i, i + distance) for i in devices if i + distance in devices])


def on_device(
    ids,
    hidden_fwd,
    hidden_rc,
    embed,
    ln1_gain,
    ln2_gain,
    mixing,
    w_receptance,
    w_key,
    w_value,
    decay_first_weight,
    decay_base,
    decay_second_weight,
    context_rate_first_weight,
    iclr_base,
    context_rate_second_weight,
    group_gain,
    w_output,
    ffn_key,
    ffn_value,
):
    rows, width = hidden_fwd.shape
    seq_count, mp_count = lax.axis_size("seq"), lax.axis_size("mp")
    strands, full = 2, ffn_key.shape[0]
    struct = jax.ShapeDtypeStruct

    mirror = [(i, seq_count - 1 - i) for i in range(seq_count)]
    rc_here = lax.ppermute(hidden_rc, "seq", mirror)
    firsts = (ids.reshape(1, rows), hidden_fwd, rc_here, embed)
    local = call(
        strands_kernel,
        struct((strands, rows, width), BF16),
        scratch=[pltpu.VMEM(item.shape, item.dtype) for item in firsts] + [pltpu.SemaphoreType.DMA((4,))],
        in_specs=[ANY_SPEC] * 4,
    )(*firsts)
    whole = lax.all_gather(local, "mp", axis=2, tiled=True)
    before = shifted(whole[:, rows - 1], "seq", 1)
    after = shifted(whole[:, 0], "seq", -1)
    w_output_whole = lax.all_gather(w_output, "mp", axis=0, tiled=True)

    groups = 2 * strands
    f32_lanes, bf16_lanes = struct((groups, rows, width), F32), struct((strands, rows, width), BF16)
    state_struct = struct((strands, 2 * HEAD, width), BF16)
    entry_struct = struct((strands, HEAD, width), BF16)
    smalls = (
        ln1_gain.reshape(1, full),
        mixing,
        decay_first_weight.T,
        context_rate_first_weight.T,
        decay_base.reshape(1, width),
        decay_second_weight,
        iclr_base.reshape(1, width),
        context_rate_second_weight,
    )
    small_scratch = [pltpu.VMEM(item.shape, item.dtype) for item in smalls] + [pltpu.SemaphoreType.DMA((8,))]
    *lanes, edge = call(
        project_kernel,
        (f32_lanes,) * 5 + (struct((groups, full), F32),),
        scratch=[
            pltpu.VMEM((strands, rows + 16, full), F32),
            pltpu.VMEM((groups * rows, full), BF16),
        ]
        + small_scratch,
        in_specs=[VMEM_SPEC] * 4 + [ANY_SPEC] * 8,
    )(whole, w_receptance, w_key, w_value, *smalls)

    parity = (lax.axis_index("seq") % 2).astype(jnp.int32).reshape(1)
    lane_scratch = [pltpu.VMEM((strands, rows, width), F32)] * 5 + [pltpu.SemaphoreType.DMA((5,))]
    sent, *sent_parts, edges = call(
        functools.partial(chunk_kernel, True),
        (state_struct,) + (bf16_lanes,) * 7 + (struct((5, groups, width), F32),),
        scratch=lane_scratch + small_scratch,
        in_specs=[SMEM_SPEC] + [ANY_SPEC] * 5 + [VMEM_SPEC] * 6 + [ANY_SPEC] * 8,
    )(parity, *lanes, before, after, edge, w_receptance, w_key, w_value, *smalls)
    partner = [(i, i ^ 1) for i in range(seq_count)]
    from_partner = lax.ppermute(sent, "seq", partner)
    kept, *kept_parts = call(
        functools.partial(chunk_kernel, False),
        (state_struct,) + (bf16_lanes,) * 7,
        scratch=lane_scratch,
        in_specs=[SMEM_SPEC] + [ANY_SPEC] * 5 + [VMEM_SPEC],
    )(1 - parity, *lanes, edges)

    def onward(value, pairs):
        route = [(i, i + 2 * pairs if i % 2 else i - 2 * pairs) for i in range(seq_count)]
        return lax.ppermute(value, "seq", [(i, j) for i, j in route if 0 <= j < seq_count])

    current, state = call(pair_kernel, (state_struct, entry_struct))(kept, from_partner)
    window = []
    distance, count = 1, seq_count // 2
    while True:
        steps = [step for step in range(1, RADIX) if step * distance < count]
        last = distance * RADIX >= count
        received = [
            onward(state if last and step == steps[-1] else current, step * distance) for step in steps
        ]
        if last:
            break
        wide, current, state = call(
            functools.partial(advance_kernel, bool(window)),
            (struct(state_struct.shape, F32), state_struct, entry_struct),
        )(current, *window, *received)
        window = [wide]
        distance *= RADIX
    local_out, start_map = call(
        read_kernel,
        (f32_lanes, struct(f32_lanes.shape, BF16)),
        in_specs=[SMEM_SPEC] + [VMEM_SPEC] * 14,
    )(parity, *sent_parts, *kept_parts)
    entry = call(functools.partial(entry_kernel, bool(window)), entry_struct)(*window, *received)
    other = lax.ppermute(entry, "seq", partner)
    joined = call(finish_kernel, bf16_lanes)(
        entry, from_partner, other, local_out, start_map, group_gain.reshape(1, width)
    )
    joined_whole = lax.all_gather(joined, "mp", axis=2, tiled=True)

    position = lax.axis_index("mp").astype(jnp.int32).reshape(1)
    own, *sent = call(
        mix_kernel,
        (struct((rows, width), F32),) + (struct((rows, width), BF16),) * (mp_count - 1),
        scratch=[
            pltpu.VMEM((rows, full), F32),
            pltpu.VMEM((rows, full), F32),
            pltpu.VMEM(ffn_key.shape, BF16),
            pltpu.VMEM(ffn_value.shape, BF16),
            pltpu.SemaphoreType.DMA((2,)),
        ],
        in_specs=[SMEM_SPEC] + [VMEM_SPEC] * 4 + [ANY_SPEC] * 2,
    )(position, joined_whole, whole, w_output_whole, ln2_gain.reshape(1, full), ffn_key, ffn_value)
    merged = own
    for step, item in enumerate(sent):
        pairs = [(i, (i + step + 1) % mp_count) for i in range(mp_count)]
        merged = merged + lax.ppermute(item, "mp", pairs).astype(F32)
    return merged.astype(BF16)


def solution(mesh):
    in_specs = (
        P("seq"),
        P("seq", "mp"),
        P("seq", "mp"),
        P(None, "mp"),
        P(),
        P(),
        P(),
        P(None, "mp"),
        P(None, "mp"),
        P(None, "mp"),
        P(),
        P("mp"),
        P(None, "mp"),
        P(),
        P("mp"),
        P(None, "mp"),
        P("mp"),
        P("mp", None),
        P(None, "mp"),
        P("mp", None),
    )
    out_specs = P("seq", "mp")
    return jax.shard_map(
        on_device, mesh=mesh, in_specs=in_specs, out_specs=out_specs, check_vma=False
    )
```

time: 125 us -> 118 us (0.944)
  the two profiles are of different devices: /device:TPU:21 before, /device:TPU:0 now
where the time goes in v2:
time: 118 us; the launch traced here: 117 us
  local copies, waits for them, and re-layouts  24.1 us (20%)
  Pallas kernels  23.7 us (20%)
  starting transfers between devices  19.8 us (17%)
  waiting for transfers between devices  17.9 us (15%)
  blocking collectives  17.3 us (15%)
  between operations  13.7 us (12%)
    unnamed x78, local copies, waits for them, and re-layouts  24.1 us
    ppermute x3, waiting for transfers between devices, onward(): lax.ppermute(value, 'seq', [(i, j) for i, j in route if 0 <= j < seq_count])  10.6 us
    all_gather x1, blocking collectives, on_device(): whole = lax.all_gather(local, 'mp', axis=2, tiled=True)  10.2 us
    all_gather x1, blocking collectives, on_device(): joined_whole = lax.all_gather(joined, 'mp', axis=2, tiled=True)  7.1 us
    pallas_call x1, Pallas kernels, on_device(): call(functools.partial(chunk_kernel, True), (state_struct,) + (bf16_lanes...  6.91 us
    ppermute x1, starting transfers between devices, on_device(): rc_here = lax.ppermute(hidden_rc, 'seq', mirror)  6.07 us
    pallas_call x1, Pallas kernels, on_device(): call(functools.partial(chunk_kernel, False), (state_struct,) + (bf16_lane...  5.52 us
    ppermute x2, starting transfers between devices, shifted(): lax.ppermute(value, axis, [(i, i + distance) for i in devices if i + dist...  4.89 us
  transfers between devices with their start and end apart: 12, of which 6 were waited for; matrix products, arithmetic and copies ran while one was open for 0% of the time, Pallas kernels for 18%

profile of v2, /device:TPU:0, one launch (start us, length us, event | category | flops | bytes accessed | tf_op | source)
XLA Modules:
  0.0 117.2 jit_solution(9394144491763521951)
XLA Ops:
  7.3 6.1 %collective-permute-start = (bf16[128,256]{1,0:T(8,128)(2,1)}, bf16[128,256]{1,0:T(8,128)(2,1)S(1)}, u32[]{:S(2)}, u32[]{:S(2)}) collective-permute-start(bf16[128,256]{1,0:T(8,128)(2,1)} %param.22), channel_id=1, source_target_pairs={{0,28},{4,24},{8,20},{12,16},{16,12},{20,8},{24,4},{28,0},{1,29},{... | collective-permute-start | bytes 196616 | tf_op jit(solution)/shard_map/ppermute | solution.py:445
  13.3 2.5 %collective-permute-done.refs_2_ = bf16[128,256]{1,0:T(8,128)(2,1)S(1)} collective-permute-done((bf16[128,256]{1,0:T(8,128)(2,1)}, bf16[128,256]{1,0:T(8,128)(2,1)S(1)}, u32[]{:S(2)}, u32[]{:S(2)}) %collective-permute-start) | collective-permute-done | bytes 65568 | tf_op jit(solution)/shard_map/ppermute | solution.py:445
  18.6 10.2 %all_gather.9.x_ref = bf16[2,128,1024]{2,1,0:T(8,128)(2,1)S(1)} all-gather(bf16[2,128,256]{2,1,0:T(8,128)(2,1)S(1)} %shard_map.190), channel_id=1, replica_groups=mesh['seq'=8,'mp'=4] {'mp'}, dimensions={2}, use_global_device_ids=true | all-gather | bytes 655360 | tf_op jit(solution)/shard_map/all_gather | solution.py:453
  28.8 3.6 %collective-permute-start.1 = (bf16[2,1024]{1,0:T(2,128)(2,1)S(1)}, bf16[2,1024]{1,0:T(2,128)(2,1)S(1)}, u32[]{:S(2)}, u32[]{:S(2)}) collective-permute-start(bf16[2,1024]{1,0:T(2,128)(2,1)S(1)} %bitcast.29), channel_id=1, source_target_pairs={{0,4},{4,8},{8,12},{12,16},{16,20},{20,24},{24,28},{1,5},{5,9},{9,... | collective-permute-start | bytes 12296 | tf_op jit(solution)/shard_map/ppermute | solution.py:414
  32.5 1.3 %collective-permute-start.2 = (bf16[2,1024]{1,0:T(2,128)(2,1)S(1)}, bf16[2,1024]{1,0:T(2,128)(2,1)S(1)}, u32[]{:S(2)}, u32[]{:S(2)}) collective-permute-start(bf16[2,1024]{1,0:T(2,128)(2,1)S(1)} %bitcast.30), channel_id=1, source_target_pairs={{4,0},{8,4},{12,8},{16,12},{20,16},{24,20},{28,24},{5,1},{9,5},{13... | collective-permute-start | bytes 12296 | tf_op jit(solution)/shard_map/ppermute | solution.py:414
  33.8 1.0 copy-done.3
  34.8 1.0 copy-done.4
  35.9 1.1 copy-done.5
  36.9 0.9 copy-done.6
  37.8 0.9 copy-done.7
  43.0 4.1 %shard_map.191 = (f32[4,128,256]{2,1,0:T(8,128)S(1)}, f32[4,128,256]{2,1,0:T(8,128)S(1)}, f32[4,128,256]{2,1,0:T(8,128)S(1)}, f32[4,128,256]{2,1,0:T(8,128)S(1)}...) custom-call(bf16[2,128,1024]{2,1,0:T(8,128)(2,1)S(1)} %all_gather.9.x_ref, bf16[1024,256]{1,0:T(8,128)(2,1)S(1)} %copy-done.3, ...), custom_call_target="tpu_custom_call" | custom-call | tf_op jit(solution)/shard_map/pallas_call | solution.py:473
  47.2 6.9 %shard_map.192 = (bf16[2,128,256]{2,1,0:T(8,128)(2,1)S(1)}, bf16[2,128,256]{2,1,0:T(8,128)(2,1)S(1)}, bf16[2,128,256]{2,1,0:T(8,128)(2,1)S(1)}, bf16[2,128,256]{...) custom-call(s32[1]{0:T(128)} %bitcast.1.direction_ref.refs_0_, ...), custom_call_target="tpu_custom_call" | custom-call | tf_op jit(solution)/shard_map/pallas_call | solution.py:486
  54.1 2.7 %collective-permute-start.3 = (bf16[2,128,256]{2,1,0:T(8,128)(2,1)S(1)}, bf16[2,128,256]{2,1,0:T(8,128)(2,1)S(1)}, u32[]{:S(2)}, u32[]{:S(2)}) collective-permute-start(bf16[2,128,256]{2,1,0:T(8,128)(2,1)S(1)} %get-tuple-element.44), channel_id=1, source_target_pairs={{0,4},{4,0},{8,12},{12,8},{16,20},{20,16},{24,28},{28,24},{1,5},{5... | collective-permute-start | bytes 393224 | tf_op jit(solution)/shard_map/ppermute | solution.py:493
  56.8 5.5 %shard_map.193 = (bf16[2,128,256]{2,1,0:T(8,128)(2,1)S(1)}, bf16[2,128,256]{2,1,0:T(8,128)(2,1)S(1)}, bf16[2,128,256]{2,1,0:T(8,128)(2,1)S(1)}, bf16[2,128,256]{...) custom-call(s32[1]{0:T(128)S(6)} %sub.3.direction_ref, ...), custom_call_target="tpu_custom_call" | custom-call | tf_op jit(solution)/shard_map/pallas_call | solution.py:494
  63.9 1.4 %collective-permute-start.4 = (bf16[2,128,256]{2,1,0:T(8,128)(2,1)S(1)}, bf16[2,128,256]{2,1,0:T(8,128)(2,1)S(1)}, u32[]{:S(2)}, u32[]{:S(2)}) collective-permute-start(bf16[2,128,256]{2,1,0:T(8,128)(2,1)S(1)} %get-tuple-element.45), channel_id=1, source_target_pairs={{4,12},{8,0},{12,20},{16,8},{20,28},{24,16},{5,13},{9,1},{13,21},{... | collective-permute-start | bytes 393224 | tf_op jit(solution)/shard_map/ppermute | solution.py:503
  65.3 1.3 %collective-permute-start.5 = (bf16[2,128,256]{2,1,0:T(8,128)(2,1)S(1)}, bf16[2,128,256]{2,1,0:T(8,128)(2,1)S(1)}, u32[]{:S(2)}, u32[]{:S(2)}) collective-permute-start(bf16[2,128,256]{2,1,0:T(8,128)(2,1)S(1)} %get-tuple-element.45), channel_id=1, source_target_pairs={{4,20},{12,28},{16,0},{24,8},{5,21},{13,29},{17,1},{25,9},{6,22},{... | collective-permute-start | bytes 393224 | tf_op jit(solution)/shard_map/ppermute | solution.py:503
  66.6 1.3 %collective-permute-start.6 = (bf16[2,64,256]{2,1,0:T(8,128)(2,1)S(1)}, bf16[2,64,256]{2,1,0:T(8,128)(2,1)S(1)}, u32[]{:S(2)}, u32[]{:S(2)}) collective-permute-start(bf16[2,64,256]{2,1,0:T(8,128)(2,1)S(1)} %get-tuple-element.46), channel_id=1, source_target_pairs={{4,28},{24,0},{5,29},{25,1},{6,30},{26,2},{7,31},{27,3}} | collective-permute-start | bytes 196616 | tf_op jit(solution)/shard_map/ppermute | solution.py:503
  67.9 9.0 %collective-permute-done.6.refs_2_ = bf16[2,64,256]{2,1,0:T(8,128)(2,1)S(1)} collective-permute-done((bf16[2,64,256]{2,1,0:T(8,128)(2,1)S(1)}, bf16[2,64,256]{2,1,0:T(8,128)(2,1)S(1)}, u32[]{:S(2)}, u32[]{:S(2)}) %collective-permute-start.6) | collective-permute-done | bytes 65568 | tf_op jit(solution)/shard_map/ppermute | solution.py:503
  77.0 1.6 %collective-permute-done.5.refs_1_ = bf16[2,128,256]{2,1,0:T(8,128)(2,1)S(1)} collective-permute-done((bf16[2,128,256]{2,1,0:T(8,128)(2,1)S(1)}, bf16[2,128,256]{2,1,0:T(8,128)(2,1)S(1)}, u32[]{:S(2)}, u32[]{:S(2)}) %collective-permute-start.5) | collective-permute-done | bytes 131104 | tf_op jit(solution)/shard_map/ppermute | solution.py:503
  80.0 0.9 copy-done.15
  80.9 0.9 copy-done.17
  81.8 0.9 copy-done.19
  82.7 0.9 copy-done.21
  87.3 2.1 %shard_map.196 = (f32[4,128,256]{2,1,0:T(8,128)S(1)}, bf16[4,128,256]{2,1,0:T(8,128)(2,1)S(1)}) custom-call(s32[1]{0:T(128)} %bitcast.1.direction_ref.refs_0_, bf16[2,128,256]{2,1,0:T(8,128)(2,1)S(1)} %get-tuple-element.47.refs_1_, bf16[2,128,256]{2,1,0:T(8,128)(2,1)S(1)} %get-tuple-element.48.refs_2_, bf16[2,128,256]{2,1,0:T(8,128)(2,1)S(1)} %get-tuple-element.49.refs_3_, ...), custom_call_target="tpu_custom_call" | custom-call | tf_op jit(solution)/shard_map/pallas_call | solution.py:522
  89.4 1.3 %shard_map.197 = bf16[2,128,256]{2,1,0:T(8,128)(2,1)S(1)} custom-call(bf16[2,64,256]{2,1,0:T(8,128)(2,1)S(1)} %shard_map.195.entry_ref, bf16[2,128,256]{2,1,0:T(8,128)(2,1)S(1)} %collective-permute-done.3.from_ref, bf16[2,64,256]{2,1,0:T(8,128)(2,1)S(1)} %collective-permute-done.7.other_ref, f32[4,128,256]{2,1,0:T(8,128)S(1)} %get-tuple-element.61.local_ref, ...), custom_call_target="tpu_custom_call" | custom-call | tf_op jit(solution)/shard_map/pallas_call | solution.py:529
  90.7 7.1 %all_gather.10.joined_ref = bf16[2,128,1024]{2,1,0:T(8,128)(2,1)S(1)} all-gather(bf16[2,128,256]{2,1,0:T(8,128)(2,1)S(1)} %shard_map.197), channel_id=1, replica_groups=mesh['seq'=8,'mp'=4] {'mp'}, dimensions={2}, use_global_device_ids=true | all-gather | bytes 655360 | tf_op jit(solution)/shard_map/all_gather | solution.py:532
  97.8 1.6 %copy-done.1 = bf16[1024,1024]{1,0:T(8,128)(2,1)S(1)} copy-done((bf16[1024,1024]{1,0:T(8,128)(2,1)S(1)}, bf16[1024,1024]{1,0:T(8,128)(2,1)}, u32[]{:S(2)}) %copy-start.1) | copy-done | bytes 2097176
  99.4 1.6 %copy-done.2 = bf16[1024,1024]{1,0:T(8,128)(2,1)S(1)} copy-done((bf16[1024,1024]{1,0:T(8,128)(2,1)S(1)}, bf16[1024,1024]{1,0:T(8,128)(2,1)}, u32[]{:S(2)}) %copy-start.2) | copy-done | bytes 2097176
  101.0 2.6 %shard_map.198 = (f32[128,256]{1,0:T(8,128)S(1)}, bf16[128,256]{1,0:T(8,128)(2,1)S(1)}, bf16[128,256]{1,0:T(8,128)(2,1)S(1)}, bf16[128,256]{1,0:T(8,128)(2,1)S(1)}) custom-call(s32[1]{0:T(128)} %bitcast.index_ref, bf16[2,128,1024]{2,1,0:T(8,128)(2,1)S(1)} %all_gather.10.joined_ref, bf16[2,128,1024]{2,1,0:T(8,128)(2,1)S(1)} %all_gather.9.x_ref, ...), custom_call_target="tpu_custom_call" | custom-call | tf_op jit(solution)/shard_map/pallas_call | solution.py:535
  104.4 1.2 %collective-permute-start.9 = (bf16[128,256]{1,0:T(8,128)(2,1)S(1)}, bf16[128,256]{1,0:T(8,128)(2,1)S(1)}, u32[]{:S(2)}, u32[]{:S(2)}) collective-permute-start(bf16[128,256]{1,0:T(8,128)(2,1)S(1)} %get-tuple-element.65), channel_id=1, source_target_pairs={{0,2},{1,3},{2,0},{3,1},{4,6},{5,7},{6,4},{7,5},{8,10},{9,11},{10,... | collective-permute-start | bytes 196616 | tf_op jit(solution)/shard_map/ppermute | solution.py:550
  106.3 2.5 %collective-permute-done.8 = bf16[128,256]{1,0:T(8,128)(2,1)S(1)} collective-permute-done((bf16[128,256]{1,0:T(8,128)(2,1)S(1)}, bf16[128,256]{1,0:T(8,128)(2,1)S(1)}, u32[]{:S(2)}, u32[]{:S(2)}) %collective-permute-start.8) | collective-permute-done | bytes 65568 | tf_op jit(solution)/shard_map/ppermute | solution.py:550
  108.8 0.9 collective-permute-done.9
  (84 shorter events, 16.6 us)
Async XLA Ops:
  6.5 40.6 %copy-start.11 = (bf16[64,256]{1,0:T(8,128)(2,1)S(1)}, bf16[64,256]{1,0:T(8,128)(2,1)}, u32[]{:S(2)}) copy-start(bf16[64,256]{1,0:T(8,128)(2,1)} %refs_18_.1) | copy-start | bytes 98308
  6.5 91.3 %all-gather.2.cloned.1.call-start = ((), (), s32[]{:S(2)}) async-start(), calls=%async_computation | async-start | bytes 2621440 | tf_op jit(solution)/shard_map/all_gather | solution.py:456
  7.3 8.5 %collective-permute-start = (bf16[128,256]{1,0:T(8,128)(2,1)}, bf16[128,256]{1,0:T(8,128)(2,1)S(1)}, u32[]{:S(2)}, u32[]{:S(2)}) collective-permute-start(bf16[128,256]{1,0:T(8,128)(2,1)} %param.22), channel_id=1, source_target_pairs={{0,28},{4,24},{8,20},{12,16},{16,12},{20,8},{24,4},{28,0},{1,29},{... | collective-permute-start | bytes 196616 | tf_op jit(solution)/shard_map/ppermute | solution.py:445
  28.8 18.3 %collective-permute-start.1 = (bf16[2,1024]{1,0:T(2,128)(2,1)S(1)}, bf16[2,1024]{1,0:T(2,128)(2,1)S(1)}, u32[]{:S(2)}, u32[]{:S(2)}) collective-permute-start(bf16[2,1024]{1,0:T(2,128)(2,1)S(1)} %bitcast.29), channel_id=1, source_target_pairs={{0,4},{4,8},{8,12},{12,16},{16,20},{20,24},{24,28},{1,5},{5,9},{9,... | collective-permute-start | bytes 12296 | tf_op jit(solution)/shard_map/ppermute | solution.py:414
  32.5 14.7 %collective-permute-start.2 = (bf16[2,1024]{1,0:T(2,128)(2,1)S(1)}, bf16[2,1024]{1,0:T(2,128)(2,1)S(1)}, u32[]{:S(2)}, u32[]{:S(2)}) collective-permute-start(bf16[2,1024]{1,0:T(2,128)(2,1)S(1)} %bitcast.30), channel_id=1, source_target_pairs={{4,0},{8,4},{12,8},{16,12},{20,16},{24,20},{28,24},{5,1},{9,5},{13... | collective-permute-start | bytes 12296 | tf_op jit(solution)/shard_map/ppermute | solution.py:414
  33.8 1.0 copy-start.3
  34.8 1.0 copy-start.4
  35.9 1.1 copy-start.5
  54.1 24.9 %copy-start.12 = (bf16[2,128,256]{2,1,0:T(8,128)(2,1)}, bf16[2,128,256]{2,1,0:T(8,128)(2,1)S(1)}, u32[]{:S(2)}) copy-start(bf16[2,128,256]{2,1,0:T(8,128)(2,1)S(1)} %get-tuple-element.52.refs_6_) | copy-start | bytes 393220
  54.1 24.9 %copy-start.14 = (bf16[2,128,256]{2,1,0:T(8,128)(2,1)}, bf16[2,128,256]{2,1,0:T(8,128)(2,1)S(1)}, u32[]{:S(2)}) copy-start(bf16[2,128,256]{2,1,0:T(8,128)(2,1)S(1)} %get-tuple-element.53.refs_7_) | copy-start | bytes 393220
  54.1 9.6 %collective-permute-start.3 = (bf16[2,128,256]{2,1,0:T(8,128)(2,1)S(1)}, bf16[2,128,256]{2,1,0:T(8,128)(2,1)S(1)}, u32[]{:S(2)}, u32[]{:S(2)}) collective-permute-start(bf16[2,128,256]{2,1,0:T(8,128)(2,1)S(1)} %get-tuple-element.44), channel_id=1, source_target_pairs={{0,4},{4,0},{8,12},{12,8},{16,20},{20,16},{24,28},{28,24},{1,5},{5... | collective-permute-start | bytes 393224 | tf_op jit(solution)/shard_map/ppermute | solution.py:493
  56.8 32.6 %copy-start.36 = (f32[256]{0:T(256)S(1)}, f32[256]{0:T(256)}, u32[]{:S(2)}) copy-start(f32[256]{0:T(256)} %param.36) | copy-start | bytes 3076
  63.6 15.3 %copy-start.16 = (bf16[2,128,256]{2,1,0:T(8,128)(2,1)}, bf16[2,128,256]{2,1,0:T(8,128)(2,1)S(1)}, u32[]{:S(2)}) copy-start(bf16[2,128,256]{2,1,0:T(8,128)(2,1)S(1)} %get-tuple-element.54.refs_8_) | copy-start | bytes 393220
  63.6 15.4 %copy-start.18 = (bf16[2,128,256]{2,1,0:T(8,128)(2,1)}, bf16[2,128,256]{2,1,0:T(8,128)(2,1)S(1)}, u32[]{:S(2)}) copy-start(bf16[2,128,256]{2,1,0:T(8,128)(2,1)S(1)} %get-tuple-element.55.refs_9_) | copy-start | bytes 393220
  63.6 15.4 %copy-start.20 = (bf16[2,128,256]{2,1,0:T(8,128)(2,1)}, bf16[2,128,256]{2,1,0:T(8,128)(2,1)S(1)}, u32[]{:S(2)}) copy-start(bf16[2,128,256]{2,1,0:T(8,128)(2,1)S(1)} %get-tuple-element.56.refs_10_) | copy-start | bytes 393220
  63.6 15.4 %copy-start.22 = (bf16[2,128,256]{2,1,0:T(8,128)(2,1)}, bf16[2,128,256]{2,1,0:T(8,128)(2,1)S(1)}, u32[]{:S(2)}) copy-start(bf16[2,128,256]{2,1,0:T(8,128)(2,1)S(1)} %get-tuple-element.57.refs_11_) | copy-start | bytes 393220
  63.7 15.4 %copy-start.24 = (bf16[2,128,256]{2,1,0:T(8,128)(2,1)}, bf16[2,128,256]{2,1,0:T(8,128)(2,1)S(1)}, u32[]{:S(2)}) copy-start(bf16[2,128,256]{2,1,0:T(8,128)(2,1)S(1)} %get-tuple-element.58.refs_12_) | copy-start | bytes 393220
  63.7 34.1 %copy-start.32 = (f32[1024]{0:T(1024)S(1)}, f32[1024]{0:T(1024)}, u32[]{:S(2)}) copy-start(f32[1024]{0:T(1024)} %param.25) | copy-start | bytes 12292
  63.9 33.9 %copy-start = (bf16[1024,1024]{1,0:T(8,128)(2,1)S(1)}, bf16[1024,1024]{1,0:T(8,128)(2,1)}, u32[]{:S(2)}) copy-start(bf16[1024,1024]{1,0:T(8,128)(2,1)} %up_hbm.1) | copy-start | bytes 6291460
  63.9 13.0 %collective-permute-start.4 = (bf16[2,128,256]{2,1,0:T(8,128)(2,1)S(1)}, bf16[2,128,256]{2,1,0:T(8,128)(2,1)S(1)}, u32[]{:S(2)}, u32[]{:S(2)}) collective-permute-start(bf16[2,128,256]{2,1,0:T(8,128)(2,1)S(1)} %get-tuple-element.45), channel_id=1, source_target_pairs={{4,12},{8,0},{12,20},{16,8},{20,28},{24,16},{5,13},{9,1},{13,21},{... | collective-permute-start | bytes 393224 | tf_op jit(solution)/shard_map/ppermute | solution.py:503
  65.3 13.2 %collective-permute-start.5 = (bf16[2,128,256]{2,1,0:T(8,128)(2,1)S(1)}, bf16[2,128,256]{2,1,0:T(8,128)(2,1)S(1)}, u32[]{:S(2)}, u32[]{:S(2)}) collective-permute-start(bf16[2,128,256]{2,1,0:T(8,128)(2,1)S(1)} %get-tuple-element.45), channel_id=1, source_target_pairs={{4,20},{12,28},{16,0},{24,8},{5,21},{13,29},{17,1},{25,9},{6,22},{... | collective-permute-start | bytes 393224 | tf_op jit(solution)/shard_map/ppermute | solution.py:503
  66.6 10.3 %collective-permute-start.6 = (bf16[2,64,256]{2,1,0:T(8,128)(2,1)S(1)}, bf16[2,64,256]{2,1,0:T(8,128)(2,1)S(1)}, u32[]{:S(2)}, u32[]{:S(2)}) collective-permute-start(bf16[2,64,256]{2,1,0:T(8,128)(2,1)S(1)} %get-tuple-element.46), channel_id=1, source_target_pairs={{4,28},{24,0},{5,29},{25,1},{6,30},{26,2},{7,31},{27,3}} | collective-permute-start | bytes 196616 | tf_op jit(solution)/shard_map/ppermute | solution.py:503
  79.0 10.3 %collective-permute-start.7 = (bf16[2,64,256]{2,1,0:T(8,128)(2,1)S(1)}, bf16[2,64,256]{2,1,0:T(8,128)(2,1)S(1)}, u32[]{:S(2)}, u32[]{:S(2)}) collective-permute-start(bf16[2,64,256]{2,1,0:T(8,128)(2,1)S(1)} %shard_map.195.entry_ref), channel_id=1, source_target_pairs={{0,4},{4,0},{8,12},{12,8},{16,20},{20,16},{24,28},{28,24},{1,5},{5... | collective-permute-start | bytes 196616 | tf_op jit(solution)/shard_map/ppermute | solution.py:528
  79.1 0.9 copy-start.13
  80.0 0.9 copy-start.15
  80.9 0.9 copy-start.17
  81.8 0.9 copy-start.19
  97.8 1.6 %copy-start.1 = (bf16[1024,1024]{1,0:T(8,128)(2,1)S(1)}, bf16[1024,1024]{1,0:T(8,128)(2,1)}, u32[]{:S(2)}) copy-start(bf16[1024,1024]{1,0:T(8,128)(2,1)} %down_hbm.1) | copy-start | bytes 6291460
  99.4 1.6 %copy-start.2 = (bf16[1024,1024]{1,0:T(8,128)(2,1)S(1)}, bf16[1024,1024]{1,0:T(8,128)(2,1)}, u32[]{:S(2)}) copy-start(bf16[1024,1024]{1,0:T(8,128)(2,1)} %all-gather.2.cloned.1.call-done.w_ref) | copy-start | bytes 6291460
  103.6 2.7 %collective-permute-start.10 = (bf16[128,256]{1,0:T(8,128)(2,1)S(1)}, bf16[128,256]{1,0:T(8,128)(2,1)S(1)}, u32[]{:S(2)}, u32[]{:S(2)}) collective-permute-start(bf16[128,256]{1,0:T(8,128)(2,1)S(1)} %get-tuple-element.66), channel_id=1, source_target_pairs={{0,3},{1,0},{2,1},{3,2},{4,7},{5,4},{6,5},{7,6},{8,11},{9,8},{10,9... | collective-permute-start | bytes 196616 | tf_op jit(solution)/shard_map/ppermute | solution.py:550
  104.4 4.4 %collective-permute-start.8 = (bf16[128,256]{1,0:T(8,128)(2,1)S(1)}, bf16[128,256]{1,0:T(8,128)(2,1)S(1)}, u32[]{:S(2)}, u32[]{:S(2)}) collective-permute-start(bf16[128,256]{1,0:T(8,128)(2,1)S(1)} %get-tuple-element.64), channel_id=1, source_target_pairs={{0,1},{1,2},{2,3},{3,0},{4,5},{5,6},{6,7},{7,4},{8,9},{9,10},{10,1... | collective-permute-start | bytes 196616 | tf_op jit(solution)/shard_map/ppermute | solution.py:550
  104.4 5.3 %collective-permute-start.9 = (bf16[128,256]{1,0:T(8,128)(2,1)S(1)}, bf16[128,256]{1,0:T(8,128)(2,1)S(1)}, u32[]{:S(2)}, u32[]{:S(2)}) collective-permute-start(bf16[128,256]{1,0:T(8,128)(2,1)S(1)} %get-tuple-element.65), channel_id=1, source_target_pairs={{0,2},{1,3},{2,0},{3,1},{4,6},{5,7},{6,4},{7,5},{8,10},{9,11},{10,... | collective-permute-start | bytes 196616 | tf_op jit(solution)/shard_map/ppermute | solution.py:550
  (18 other events, 14.1 us)
Sparse Core Ops, SparseCore 0:
  8.9 28.0 all-gather.1

commit v3 on v2

--- a/solution.py
+++ b/solution.py
@@ -15,10 +15,10 @@
 RADIX = 4
 F32 = jnp.float32
 BF16 = jnp.bfloat16
-VMEM_BYTES = 32 * 1024 * 1024
+MIB = 1024 * 1024
 VMEM_SPEC = pl.BlockSpec(memory_space=pltpu.VMEM)
 SMEM_SPEC = pl.BlockSpec(memory_space=pltpu.SMEM)
-ANY_SPEC = pl.BlockSpec(memory_space=pl.ANY)
+HBM_SPEC = pl.BlockSpec(memory_space=pltpu.HBM)
 
 
 def mm(left, right):
@@ -65,9 +65,9 @@
 
 
 def strands_kernel(*refs):
-    ins, out_ref, locals_, sems = refs[:4], refs[4], refs[5:9], refs[9]
+    rc_ref, ins, out_ref, locals_, sems = refs[0], refs[1:4], refs[4], refs[5:8], refs[8]
     arrived(copied(ins, locals_, sems))
-    ids_ref, fwd_ref, rc_ref, embed_ref = locals_
+    ids_ref, fwd_ref, embed_ref = locals_
     rows = fwd_ref.shape[0]
     ids = ids_ref[...]
     letters = ids_of((embed_ref.shape[0], rows), 0)
@@ -126,13 +126,13 @@
     return log_decay, jax.nn.sigmoid(c_base + mm(rate_low, w_c2))
 
 
-def project_kernel(x_ref, w_r_ref, w_k_ref, w_v_ref, *refs):
-    smalls, refs = refs[:8], refs[8:]
+def project_kernel(x_ref, *refs):
+    params, refs = refs[:11], refs[11:]
     outs, edge_ref = refs[:5], refs[5]
     normed, mixed = refs[6:8]
-    locals_, sems = refs[8:16], refs[16]
-    gain_ref, mixing_ref, w_d1, w_c1, d_base, w_d2, c_base, w_c2 = locals_
-    copies = copied(smalls, locals_, sems)
+    locals_, sems = refs[8:19], refs[19]
+    gain_ref, mixing_ref, w_r_ref, w_k_ref, w_v_ref, w_d1, w_c1, d_base, w_d2, c_base, w_c2 = locals_
+    copies = copied(params, locals_, sems)
     strands, rows, _ = x_ref.shape
     width = w_r_ref.shape[1]
     pad = 8
@@ -159,8 +159,9 @@
 
     shape = (2 * strands, rows, width)
     for index, w_ref in enumerate((w_r_ref, w_k_ref, w_v_ref)):
+        copies[2 + index].wait()
         outs[index][...] = mm(mix(index), w_ref[...]).reshape(shape)
-    arrived(copies[2:])
+    arrived(copies[5:])
     log_decay, rate = gates(
         mix(3), mix(4), d_base[...], w_d2[...], c_base[...], w_c2[...], w_d1[...], w_c1[...]
     )
@@ -175,25 +176,18 @@
 def chunk_kernel(first, direction_ref, *refs):
     lanes, refs = refs[:5], refs[5:]
     if first:
-        before_ref, after_ref, edge_ref, w_r_ref, w_k_ref, w_v_ref = refs[:6]
-        smalls, refs = refs[6:14], refs[14:]
+        before_ref, after_ref, edge_ref = refs[:3]
+        params, refs = refs[3:14], refs[14:]
+        state_ref, parts_ref, edges_ref = refs[:3]
+        locals_, sems = refs[3:14], refs[14]
     else:
-        edges_ref, refs = refs[0], refs[1:]
-    state_ref, here_ref, insert_ref, key_ref, value_ref, pull_ref, start_ref, read_ref = refs[:8]
-    refs = refs[8:]
-    if first:
-        edges_ref, refs = refs[0], refs[1:]
-    r_buf, k_buf, v_buf, d_buf, a_buf = refs[:5]
-    sems, refs = refs[5], refs[6:]
-    strands, rows, width = r_buf.shape
+        edges_ref, state_ref, parts_ref = refs
+    strands, _, rows, width = parts_ref.shape
     heads = width // HEAD
     d = direction_ref[0]
-    copies = copied([ref.at[pl.ds(d * strands, strands)] for ref in lanes], (r_buf, k_buf, v_buf, d_buf, a_buf), sems)
     if first:
-        locals_, small_sems = refs[:8], refs[8]
-        small_copies = copied(smalls, locals_, small_sems)
-        gain_ref, mixing_ref, w_d1, w_c1, d_base, w_d2, c_base, w_c2 = locals_
-        arrived(small_copies)
+        arrived(copied(params, locals_, sems))
+        gain_ref, mixing_ref, w_r_ref, w_k_ref, w_v_ref, w_d1, w_c1, d_base, w_d2, c_base, w_c2 = locals_
         gain = gain_ref[...]
         center = edge_ref[...]
         halo = jnp.concatenate([before_ref[...], after_ref[...]], axis=0).astype(F32)
@@ -209,7 +203,6 @@
         )
         edges_ref[3] = log_decay
         edges_ref[4] = rate
-    arrived(copies)
     edge_row = d * (rows - 1)
     at_edge = ids_of((rows, width), 0) == edge_row
     order = (ids_of((rows, rows), 0) - ids_of((rows, rows), 1)) * (1 - 2 * d)
@@ -223,11 +216,12 @@
         return masked_heads(value, lane_head, heads)
 
     def group(s, carry):
-        def lane(index, buf):
-            return jnp.where(at_edge, edges_ref[index, pl.ds(d * strands + s, 1), :], buf[s])
-
-        receptance, key, value = lane(0, r_buf), lane(1, k_buf), lane(2, v_buf)
-        log_decay, rate = lane(3, d_buf), lane(4, a_buf)
+        g = d * strands + s
+
+        def lane(index, ref):
+            return jnp.where(at_edge, edges_ref[index, pl.ds(g, 1), :], ref[g])
+
+        receptance, key, value, log_decay, rate = [lane(index, ref) for index, ref in enumerate(lanes)]
         unit = key * lax.rsqrt(head_sum(key * key, ones) + UNIT_EPS)
         high, low = halves(log_decay)
         totals = mm(tri, high) + mm(tri, low)
@@ -256,13 +250,13 @@
         local_pull = mm(inverse, of_heads(value_pull)).astype(BF16)
         start_pull = mm(inverse, of_heads(left_prev * from_start)).astype(BF16)
         value = value.astype(BF16)
-        here_ref[s] = left_here.astype(BF16)
-        insert_ref[s] = right_insert.astype(BF16)
-        key_ref[s] = right_key.astype(BF16)
-        value_ref[s] = value
-        pull_ref[s] = local_pull
-        start_ref[s] = start_pull
-        read_ref[s] = (left_here * from_start).astype(BF16)
+        parts_ref[s, 0] = left_here.astype(BF16)
+        parts_ref[s, 1] = right_insert.astype(BF16)
+        parts_ref[s, 2] = right_key.astype(BF16)
+        parts_ref[s, 3] = value
+        parts_ref[s, 4] = local_pull
+        parts_ref[s, 5] = start_pull
+        parts_ref[s, 6] = (left_here * from_start).astype(BF16)
         tail_insert = (right_insert * to_end).astype(BF16)
         tail_key = (right_key * to_end).astype(BF16)
         ends = mm_cols(tail_insert, local_pull) + mm_cols(tail_key, value)
@@ -279,29 +273,27 @@
     lax.fori_loop(0, strands, group, 0)
 
 
-def read_kernel(*refs):
-    direction_ref, refs = refs[0], refs[1:]
-    roles, (local_ref, map_ref) = (refs[:7], refs[7:14]), refs[14:]
-    strands, rows, width = roles[0][0].shape
+def read_kernel(direction_ref, sent_ref, kept_ref, local_ref, map_ref):
+    strands, _, rows, width = sent_ref.shape
     heads = width // HEAD
     lane_head = ids_of((1, width), 1) // HEAD
-    for role, (here_ref, insert_ref, key_ref, value_ref, pull_ref, start_ref, read_ref) in enumerate(roles):
+    for role, parts_ref in enumerate((sent_ref, kept_ref)):
         sign = (1 - 2 * direction_ref[0]) * (1 - 2 * role)
         inclusive = (ids_of((rows, rows), 0) - ids_of((rows, rows), 1)) * sign >= 0
 
         def group(s, carry):
-            here, insert, key = here_ref[s], insert_ref[s], key_ref[s]
+            here, insert, key, value, pull, start, read = [parts_ref[s, i] for i in range(7)]
             reads = []
             for source in (insert, key):
                 scores = mm_rows(here, masked_heads(source, lane_head, heads))
                 parts = [scores[:, h * rows : (h + 1) * rows] for h in range(heads)]
                 reads.append(jnp.concatenate([jnp.where(inclusive, p, 0.0).astype(BF16) for p in parts], axis=1))
             pull, start, value = [
-                masked_heads(ref[s], lane_head, heads) for ref in (pull_ref, start_ref, value_ref)
+                masked_heads(item, lane_head, heads) for item in (pull, start, value)
             ]
             g = role * strands + s
             local_ref[g] = mm(reads[0], pull) + mm(reads[1], value)
-            map_ref[g] = (read_ref[s].astype(F32) + mm(reads[0], start)).astype(BF16)
+            map_ref[g] = (read.astype(F32) + mm(reads[0], start)).astype(BF16)
             return carry
 
         lax.fori_loop(0, strands, group, 0)
@@ -399,12 +391,12 @@
         ref[...] = part(partial, lax.rem(me + step + 1, size)).astype(BF16)
 
 
-def call(kernel, out_shape, scratch=(), **kwargs):
+def call(kernel, out_shape, scratch=(), mib=12, **kwargs):
     return pl.pallas_call(
         kernel,
         out_shape=out_shape,
         scratch_shapes=list(scratch),
-        compiler_params=pltpu.CompilerParams(vmem_limit_bytes=VMEM_BYTES),
+        compiler_params=pltpu.CompilerParams(vmem_limit_bytes=mib * MIB),
         **kwargs,
     )
 
@@ -443,25 +435,30 @@
 
     mirror = [(i, seq_count - 1 - i) for i in range(seq_count)]
     rc_here = lax.ppermute(hidden_rc, "seq", mirror)
-    firsts = (ids.reshape(1, rows), hidden_fwd, rc_here, embed)
+    firsts = (ids.reshape(1, rows), hidden_fwd, embed)
     local = call(
         strands_kernel,
         struct((strands, rows, width), BF16),
-        scratch=[pltpu.VMEM(item.shape, item.dtype) for item in firsts] + [pltpu.SemaphoreType.DMA((4,))],
-        in_specs=[ANY_SPEC] * 4,
-    )(*firsts)
+        scratch=[pltpu.VMEM(item.shape, item.dtype) for item in firsts] + [pltpu.SemaphoreType.DMA((3,))],
+        in_specs=[VMEM_SPEC] + [HBM_SPEC] * 3,
+    )(rc_here, *firsts)
     whole = lax.all_gather(local, "mp", axis=2, tiled=True)
     before = shifted(whole[:, rows - 1], "seq", 1)
     after = shifted(whole[:, 0], "seq", -1)
+    w_output, _ = lax.optimization_barrier((w_output, whole))
     w_output_whole = lax.all_gather(w_output, "mp", axis=0, tiled=True)
 
     groups = 2 * strands
     f32_lanes, bf16_lanes = struct((groups, rows, width), F32), struct((strands, rows, width), BF16)
+    parts_struct = struct((strands, 7, rows, width), BF16)
     state_struct = struct((strands, 2 * HEAD, width), BF16)
     entry_struct = struct((strands, HEAD, width), BF16)
-    smalls = (
+    params = (
         ln1_gain.reshape(1, full),
         mixing,
+        w_receptance,
+        w_key,
+        w_value,
         decay_first_weight.T,
         context_rate_first_weight.T,
         decay_base.reshape(1, width),
@@ -469,7 +466,8 @@
         iclr_base.reshape(1, width),
         context_rate_second_weight,
     )
-    small_scratch = [pltpu.VMEM(item.shape, item.dtype) for item in smalls] + [pltpu.SemaphoreType.DMA((8,))]
+    param_scratch = [pltpu.VMEM(item.shape, item.dtype) for item in params]
+    param_scratch += [pltpu.SemaphoreType.DMA((len(params),))]
     *lanes, edge = call(
         project_kernel,
         (f32_lanes,) * 5 + (struct((groups, full), F32),),
@@ -477,25 +475,23 @@
             pltpu.VMEM((strands, rows + 16, full), F32),
             pltpu.VMEM((groups * rows, full), BF16),
         ]
-        + small_scratch,
-        in_specs=[VMEM_SPEC] * 4 + [ANY_SPEC] * 8,
-    )(whole, w_receptance, w_key, w_value, *smalls)
+        + param_scratch,
+        in_specs=[VMEM_SPEC] + [HBM_SPEC] * len(params),
+    )(whole, *params)
 
     parity = (lax.axis_index("seq") % 2).astype(jnp.int32).reshape(1)
-    lane_scratch = [pltpu.VMEM((strands, rows, width), F32)] * 5 + [pltpu.SemaphoreType.DMA((5,))]
-    sent, *sent_parts, edges = call(
+    sent, sent_parts, edges = call(
         functools.partial(chunk_kernel, True),
-        (state_struct,) + (bf16_lanes,) * 7 + (struct((5, groups, width), F32),),
-        scratch=lane_scratch + small_scratch,
-        in_specs=[SMEM_SPEC] + [ANY_SPEC] * 5 + [VMEM_SPEC] * 6 + [ANY_SPEC] * 8,
-    )(parity, *lanes, before, after, edge, w_receptance, w_key, w_value, *smalls)
+        (state_struct, parts_struct, struct((5, groups, width), F32)),
+        scratch=param_scratch,
+        in_specs=[SMEM_SPEC] + [VMEM_SPEC] * 8 + [HBM_SPEC] * len(params),
+    )(parity, *lanes, before, after, edge, *params)
     partner = [(i, i ^ 1) for i in range(seq_count)]
     from_partner = lax.ppermute(sent, "seq", partner)
-    kept, *kept_parts = call(
+    kept, kept_parts = call(
         functools.partial(chunk_kernel, False),
-        (state_struct,) + (bf16_lanes,) * 7,
-        scratch=lane_scratch,
-        in_specs=[SMEM_SPEC] + [ANY_SPEC] * 5 + [VMEM_SPEC],
+        (state_struct, parts_struct),
+        in_specs=[SMEM_SPEC] + [VMEM_SPEC] * 6,
     )(1 - parity, *lanes, edges)
 
     def onward(value, pairs):
@@ -522,8 +518,9 @@
     local_out, start_map = call(
         read_kernel,
         (f32_lanes, struct(f32_lanes.shape, BF16)),
-        in_specs=[SMEM_SPEC] + [VMEM_SPEC] * 14,
-    )(parity, *sent_parts, *kept_parts)
+        in_specs=[SMEM_SPEC] + [VMEM_SPEC] * 2,
+    )(parity, sent_parts, kept_parts)
+    received, local_out, start_map = lax.optimization_barrier((received, local_out, start_map))
     entry = call(functools.partial(entry_kernel, bool(window)), entry_struct)(*window, *received)
     other = lax.ppermute(entry, "seq", partner)
     joined = call(finish_kernel, bf16_lanes)(
@@ -542,7 +539,8 @@
             pltpu.VMEM(ffn_value.shape, BF16),
             pltpu.SemaphoreType.DMA((2,)),
         ],
-        in_specs=[SMEM_SPEC] + [VMEM_SPEC] * 4 + [ANY_SPEC] * 2,
+        mib=24,
+        in_specs=[SMEM_SPEC] + [VMEM_SPEC] * 4 + [HBM_SPEC] * 2,
     )(position, joined_whole, whole, w_output_whole, ln2_gain.reshape(1, full), ffn_key, ffn_value)
     merged = own
     for step, item in enumerate(sent):

time: 118 us -> 109 us (0.924)
  local copies, waits for them, and re-layouts: 24.1 us -> 14.8 us
  blocking collectives: 17.3 us -> 14 us
  waiting for transfers between devices: 17.9 us -> 19.6 us
  Pallas kernels: 23.7 us -> 25.4 us
    unnamed x78 -> x52, local copies, waits for them, and re-layouts: 24.1 us -> 14.8 us
    ppermute x1, waiting for transfers between devices: 0.01 us -> 4.58 us  [on_device(): other = lax.ppermute(entry, 'seq', partner)]
    all_gather x1, blocking collectives: 10.2 us -> 7.34 us  [on_device(): whole = lax.all_gather(local, 'mp', axis=2, tiled=True)]
    ppermute x3, waiting for transfers between devices: 10.6 us -> 8.49 us  [onward(): lax.ppermute(value, 'seq', [(i, j) for i, j in route if 0 <= j < seq_count])]
  transfers between devices with their start and end apart: 12 -> 12, of which waited for: 6 -> 7; matrix products, arithmetic and copies ran while one was open for 0% -> 0% of each run, Pallas kernels for 18% -> 21%
where the time goes in v3:
time: 109 us; the launch traced here: 108 us
  Pallas kernels  25.4 us (23%)
  starting transfers between devices  19.6 us (18%)
  waiting for transfers between devices  19.6 us (18%)
  local copies, waits for them, and re-layouts  14.8 us (14%)
  blocking collectives  14 us (13%)
  between operations  13.7 us (13%)
    unnamed x52, local copies, waits for them, and re-layouts  14.8 us
    ppermute x3, waiting for transfers between devices, onward(): lax.ppermute(value, 'seq', [(i, j) for i, j in route if 0 <= j < seq_count])  8.49 us
    all_gather x1, blocking collectives, on_device(): whole = lax.all_gather(local, 'mp', axis=2, tiled=True)  7.34 us
    pallas_call x1, Pallas kernels, on_device(): call(functools.partial(chunk_kernel, True), (state_struct, parts_struct,...  6.89 us
    all_gather x1, blocking collectives, on_device(): joined_whole = lax.all_gather(joined, 'mp', axis=2, tiled=True)  6.69 us
    ppermute x1, starting transfers between devices, on_device(): rc_here = lax.ppermute(hidden_rc, 'seq', mirror)  6.07 us
    pallas_call x1, Pallas kernels, on_device(): call(functools.partial(chunk_kernel, False), (state_struct, parts_struct)...  5.41 us
    ppermute x2, starting transfers between devices, shifted(): lax.ppermute(value, axis, [(i, i + distance) for i in devices if i + dist...  4.71 us
  transfers between devices with their start and end apart: 12, of which 7 were waited for; matrix products, arithmetic and copies ran while one was open for 0% of the time, Pallas kernels for 21%

profile of v3, /device:TPU:0, one launch (start us, length us, event | category | flops | bytes accessed | tf_op | source)
XLA Modules:
  0.0 107.7 jit_solution(9288222345834734286)
XLA Ops:
  6.6 6.1 %collective-permute-start = (bf16[128,256]{1,0:T(8,128)(2,1)}, bf16[128,256]{1,0:T(8,128)(2,1)S(1)}, u32[]{:S(2)}, u32[]{:S(2)}) collective-permute-start(bf16[128,256]{1,0:T(8,128)(2,1)} %param.22), channel_id=1, source_target_pairs={{0,28},{4,24},{8,20},{12,16},{16,12},{20,8},{24,4},{28,0},{1,29},{... | collective-permute-start | bytes 196616 | tf_op jit(solution)/shard_map/ppermute | solution.py:437
  12.7 2.5 %collective-permute-done.refs_0_ = bf16[128,256]{1,0:T(8,128)(2,1)S(1)} collective-permute-done((bf16[128,256]{1,0:T(8,128)(2,1)}, bf16[128,256]{1,0:T(8,128)(2,1)S(1)}, u32[]{:S(2)}, u32[]{:S(2)}) %collective-permute-start) | collective-permute-done | bytes 65568 | tf_op jit(solution)/shard_map/ppermute | solution.py:437
  17.9 7.3 %all_gather.9.x_ref = bf16[2,128,1024]{2,1,0:T(8,128)(2,1)S(1)} all-gather(bf16[2,128,256]{2,1,0:T(8,128)(2,1)S(1)} %shard_map.190), channel_id=1, replica_groups=mesh['seq'=8,'mp'=4] {'mp'}, dimensions={2}, use_global_device_ids=true | all-gather | bytes 655360 | tf_op jit(solution)/shard_map/all_gather | solution.py:445
  25.3 3.4 %collective-permute-start.1 = (bf16[2,1024]{1,0:T(2,128)(2,1)S(1)}, bf16[2,1024]{1,0:T(2,128)(2,1)S(1)}, u32[]{:S(2)}, u32[]{:S(2)}) collective-permute-start(bf16[2,1024]{1,0:T(2,128)(2,1)S(1)} %bitcast.29), channel_id=1, source_target_pairs={{0,4},{4,8},{8,12},{12,16},{16,20},{20,24},{24,28},{1,5},{5,9},{9,... | collective-permute-start | bytes 12296 | tf_op jit(solution)/shard_map/ppermute | solution.py:406
  28.7 1.3 %collective-permute-start.2 = (bf16[2,1024]{1,0:T(2,128)(2,1)S(1)}, bf16[2,1024]{1,0:T(2,128)(2,1)S(1)}, u32[]{:S(2)}, u32[]{:S(2)}) collective-permute-start(bf16[2,1024]{1,0:T(2,128)(2,1)S(1)} %bitcast.30), channel_id=1, source_target_pairs={{4,0},{8,4},{12,8},{16,12},{20,16},{24,20},{28,24},{5,1},{9,5},{13... | collective-permute-start | bytes 12296 | tf_op jit(solution)/shard_map/ppermute | solution.py:406
  30.0 1.0 copy-done.3
  31.1 1.1 copy-done.5
  32.1 1.1 %copy-done.6 = bf16[1024,256]{1,0:T(8,128)(2,1)S(1)} copy-done((bf16[1024,256]{1,0:T(8,128)(2,1)S(1)}, bf16[1024,256]{1,0:T(8,128)(2,1)}, u32[]{:S(2)}) %copy-start.6) | copy-done | bytes 524312
  33.2 0.9 copy-done.7
  34.2 0.9 copy-done.9
  39.4 4.5 %shard_map.191 = (f32[4,128,256]{2,1,0:T(8,128)S(1)}, f32[4,128,256]{2,1,0:T(8,128)S(1)}, f32[4,128,256]{2,1,0:T(8,128)S(1)}, f32[4,128,256]{2,1,0:T(8,128)S(1)}...) custom-call(bf16[2,128,1024]{2,1,0:T(8,128)(2,1)S(1)} %all_gather.9.x_ref, f32[1,1024]{1,0:T(1,128)S(1)} %bitcast.20, ...), custom_call_target="tpu_custom_call" | custom-call | tf_op jit(solution)/shard_map/pallas_call | solution.py:471
  43.9 6.9 %shard_map.192 = (bf16[2,128,256]{2,1,0:T(8,128)(2,1)S(1)}, bf16[2,7,128,256]{3,2,1,0:T(8,128)(2,1)S(1)}, f32[5,4,256]{2,1,0:T(4,128)S(1)}) custom-call(s32[1]{0:T(128)} %bitcast.1.direction_ref, f32[4,128,256]{2,1,0:T(8,128)S(1)} %get-tuple-element.30.refs_0_, f32[4,128,256]{2,1,0:T(8,128)S(1)} %get-tuple-element.31.refs_1_, ...), custom_call_target="tpu_custom_call" | custom-call | tf_op jit(solution)/shard_map/pallas_call | solution.py:483
  50.8 2.7 %collective-permute-start.3 = (bf16[2,128,256]{2,1,0:T(8,128)(2,1)S(1)}, bf16[2,128,256]{2,1,0:T(8,128)(2,1)S(1)}, u32[]{:S(2)}, u32[]{:S(2)}) collective-permute-start(bf16[2,128,256]{2,1,0:T(8,128)(2,1)S(1)} %get-tuple-element.38), channel_id=1, source_target_pairs={{0,4},{4,0},{8,12},{12,8},{16,20},{20,16},{24,28},{28,24},{1,5},{5... | collective-permute-start | bytes 393224 | tf_op jit(solution)/shard_map/ppermute | solution.py:490
  53.5 5.4 %shard_map.193 = (bf16[2,128,256]{2,1,0:T(8,128)(2,1)S(1)}, bf16[2,7,128,256]{3,2,1,0:T(8,128)(2,1)S(1)}) custom-call(s32[1]{0:T(128)S(6)} %sub.3.direction_ref, f32[4,128,256]{2,1,0:T(8,128)S(1)} %get-tuple-element.30.refs_0_, f32[4,128,256]{2,1,0:T(8,128)S(1)} %get-tuple-element.31.refs_1_, f32[4,128,256]{2,1,0:T(8,128)S(1)} %get-tuple-element.32.refs_2_, ...), custom_call_target="tpu_custom_call" | custom-call | tf_op jit(solution)/shard_map/pallas_call | solution.py:491
  59.2 1.4 %collective-permute-start.4 = (bf16[2,128,256]{2,1,0:T(8,128)(2,1)S(1)}, bf16[2,128,256]{2,1,0:T(8,128)(2,1)S(1)}, u32[]{:S(2)}, u32[]{:S(2)}) collective-permute-start(bf16[2,128,256]{2,1,0:T(8,128)(2,1)S(1)} %get-tuple-element.39), channel_id=1, source_target_pairs={{4,12},{8,0},{12,20},{16,8},{20,28},{24,16},{5,13},{9,1},{13,21},{... | collective-permute-start | bytes 393224 | tf_op jit(solution)/shard_map/ppermute | solution.py:499
  60.6 1.3 %collective-permute-start.5 = (bf16[2,128,256]{2,1,0:T(8,128)(2,1)S(1)}, bf16[2,128,256]{2,1,0:T(8,128)(2,1)S(1)}, u32[]{:S(2)}, u32[]{:S(2)}) collective-permute-start(bf16[2,128,256]{2,1,0:T(8,128)(2,1)S(1)} %get-tuple-element.39), channel_id=1, source_target_pairs={{4,20},{12,28},{16,0},{24,8},{5,21},{13,29},{17,1},{25,9},{6,22},{... | collective-permute-start | bytes 393224 | tf_op jit(solution)/shard_map/ppermute | solution.py:499
  61.9 1.3 %collective-permute-start.6 = (bf16[2,64,256]{2,1,0:T(8,128)(2,1)S(1)}, bf16[2,64,256]{2,1,0:T(8,128)(2,1)S(1)}, u32[]{:S(2)}, u32[]{:S(2)}) collective-permute-start(bf16[2,64,256]{2,1,0:T(8,128)(2,1)S(1)} %get-tuple-element.40), channel_id=1, source_target_pairs={{4,28},{24,0},{5,29},{25,1},{6,30},{26,2},{7,31},{27,3}} | collective-permute-start | bytes 196616 | tf_op jit(solution)/shard_map/ppermute | solution.py:499
  63.2 2.1 %shard_map.195 = (f32[4,128,256]{2,1,0:T(8,128)S(1)}, bf16[4,128,256]{2,1,0:T(8,128)(2,1)S(1)}) custom-call(s32[1]{0:T(128)} %bitcast.1.direction_ref, bf16[2,7,128,256]{3,2,1,0:T(8,128)(2,1)S(1)} %get-tuple-element.41.sent_ref, bf16[2,7,128,256]{3,2,1,0:T(8,128)(2,1)S(1)} %get-tuple-element.42.kept_ref), custom_call_target="tpu_custom_call" | custom-call | tf_op jit(solution)/shard_map/pallas_call | solution.py:518
  65.3 7.0 %collective-permute-done.6.refs_2_ = bf16[2,64,256]{2,1,0:T(8,128)(2,1)S(1)} collective-permute-done((bf16[2,64,256]{2,1,0:T(8,128)(2,1)S(1)}, bf16[2,64,256]{2,1,0:T(8,128)(2,1)S(1)}, u32[]{:S(2)}, u32[]{:S(2)}) %collective-permute-start.6) | collective-permute-done | bytes 65568 | tf_op jit(solution)/shard_map/ppermute | solution.py:499
  72.3 1.5 %collective-permute-done.5.refs_1_ = bf16[2,128,256]{2,1,0:T(8,128)(2,1)S(1)} collective-permute-done((bf16[2,128,256]{2,1,0:T(8,128)(2,1)S(1)}, bf16[2,128,256]{2,1,0:T(8,128)(2,1)S(1)}, u32[]{:S(2)}, u32[]{:S(2)}) %collective-permute-start.5) | collective-permute-done | bytes 131104 | tf_op jit(solution)/shard_map/ppermute | solution.py:499
  73.8 1.0 shard_map.196.entry_ref
  74.8 4.6 %collective-permute-done.7.other_ref = bf16[2,64,256]{2,1,0:T(8,128)(2,1)} collective-permute-done((bf16[2,64,256]{2,1,0:T(8,128)(2,1)}, bf16[2,64,256]{2,1,0:T(8,128)(2,1)}, u32[]{:S(2)}, u32[]{:S(2)}) %collective-permute-start.7) | collective-permute-done | bytes 65568 | tf_op jit(solution)/shard_map/ppermute | solution.py:525
  79.4 2.2 %shard_map.197 = bf16[2,128,256]{2,1,0:T(8,128)(2,1)S(1)} custom-call(bf16[2,64,256]{2,1,0:T(8,128)(2,1)} %shard_map.196.entry_ref, bf16[2,128,256]{2,1,0:T(8,128)(2,1)S(1)} %collective-permute-done.3.from_ref, bf16[2,64,256]{2,1,0:T(8,128)(2,1)} %collective-permute-done.7.other_ref, f32[4,128,256]{2,1,0:T(8,128)S(1)} %get-tuple-element.48.local_ref, ...), custom_call_target="tpu_custom_call" | custom-call | tf_op jit(solution)/shard_map/pallas_call | solution.py:526
  81.6 6.7 %all_gather.10.joined_ref = bf16[2,128,1024]{2,1,0:T(8,128)(2,1)S(1)} all-gather(bf16[2,128,256]{2,1,0:T(8,128)(2,1)S(1)} %shard_map.197), channel_id=1, replica_groups=mesh['seq'=8,'mp'=4] {'mp'}, dimensions={2}, use_global_device_ids=true | all-gather | bytes 655360 | tf_op jit(solution)/shard_map/all_gather | solution.py:529
  88.3 1.6 %copy-done.1 = bf16[1024,1024]{1,0:T(8,128)(2,1)S(1)} copy-done((bf16[1024,1024]{1,0:T(8,128)(2,1)S(1)}, bf16[1024,1024]{1,0:T(8,128)(2,1)}, u32[]{:S(2)}) %copy-start.1) | copy-done | bytes 2097176
  89.9 1.6 %copy-done.2 = bf16[1024,1024]{1,0:T(8,128)(2,1)S(1)} copy-done((bf16[1024,1024]{1,0:T(8,128)(2,1)S(1)}, bf16[1024,1024]{1,0:T(8,128)(2,1)}, u32[]{:S(2)}) %copy-start.2) | copy-done | bytes 2097176
  91.5 2.6 %shard_map.198 = (f32[128,256]{1,0:T(8,128)S(1)}, bf16[128,256]{1,0:T(8,128)(2,1)S(1)}, bf16[128,256]{1,0:T(8,128)(2,1)S(1)}, bf16[128,256]{1,0:T(8,128)(2,1)S(1)}) custom-call(s32[1]{0:T(128)} %bitcast.index_ref, bf16[2,128,1024]{2,1,0:T(8,128)(2,1)S(1)} %all_gather.10.joined_ref, bf16[2,128,1024]{2,1,0:T(8,128)(2,1)S(1)} %all_gather.9.x_ref, ...), custom_call_target="tpu_custom_call" | custom-call | tf_op jit(solution)/shard_map/pallas_call | solution.py:532
  94.1 1.2 %collective-permute-start.10 = (bf16[128,256]{1,0:T(8,128)(2,1)S(1)}, bf16[128,256]{1,0:T(8,128)(2,1)S(1)}, u32[]{:S(2)}, u32[]{:S(2)}) collective-permute-start(bf16[128,256]{1,0:T(8,128)(2,1)S(1)} %get-tuple-element.54), channel_id=1, source_target_pairs={{0,3},{1,0},{2,1},{3,2},{4,7},{5,4},{6,5},{7,6},{8,11},{9,8},{10,9... | collective-permute-start | bytes 196616 | tf_op jit(solution)/shard_map/ppermute | solution.py:548
  95.3 0.9 collective-permute-start.9
  96.1 1.4 %collective-permute-done.10 = bf16[128,256]{1,0:T(8,128)(2,1)S(1)} collective-permute-done((bf16[128,256]{1,0:T(8,128)(2,1)S(1)}, bf16[128,256]{1,0:T(8,128)(2,1)S(1)}, u32[]{:S(2)}, u32[]{:S(2)}) %collective-permute-start.10) | collective-permute-done | bytes 65568 | tf_op jit(solution)/shard_map/ppermute | solution.py:548
  97.5 1.8 %collective-permute-done.8 = bf16[128,256]{1,0:T(8,128)(2,1)S(1)} collective-permute-done((bf16[128,256]{1,0:T(8,128)(2,1)S(1)}, bf16[128,256]{1,0:T(8,128)(2,1)S(1)}, u32[]{:S(2)}, u32[]{:S(2)}) %collective-permute-start.8) | collective-permute-done | bytes 65568 | tf_op jit(solution)/shard_map/ppermute | solution.py:548
  99.3 0.9 collective-permute-done.9
  (58 shorter events, 8.1 us)
Async XLA Ops:
  6.5 37.3 %copy-start.8 = (bf16[1024,64]{0,1:T(8,128)(2,1)S(1)}, bf16[1024,64]{0,1:T(8,128)(2,1)}, u32[]{:S(2)}) copy-start(bf16[1024,64]{0,1:T(8,128)(2,1)} %param.30) | copy-start | bytes 393220
  6.5 37.4 %copy-start.10 = (bf16[1024,64]{0,1:T(8,128)(2,1)S(1)}, bf16[1024,64]{0,1:T(8,128)(2,1)}, u32[]{:S(2)}) copy-start(bf16[1024,64]{0,1:T(8,128)(2,1)} %param.33) | copy-start | bytes 393220
  6.5 37.4 %copy-start.4 = (bf16[1024,256]{1,0:T(8,128)(2,1)S(1)}, bf16[1024,256]{1,0:T(8,128)(2,1)}, u32[]{:S(2)}) copy-start(bf16[1024,256]{1,0:T(8,128)(2,1)} %refs_10_.3) | copy-start | bytes 1572868
  6.5 37.4 %copy-start.14 = (bf16[64,256]{1,0:T(8,128)(2,1)S(1)}, bf16[64,256]{1,0:T(8,128)(2,1)}, u32[]{:S(2)}) copy-start(bf16[64,256]{1,0:T(8,128)(2,1)} %refs_18_.1) | copy-start | bytes 98308
  6.5 81.8 %all-gather.2.cloned.1.call-start = ((), (), s32[]{:S(2)}) async-start(), calls=%async_computation | async-start | bytes 2621440 | tf_op jit(solution)/shard_map/all_gather | solution.py:449
  6.6 8.5 %collective-permute-start = (bf16[128,256]{1,0:T(8,128)(2,1)}, bf16[128,256]{1,0:T(8,128)(2,1)S(1)}, u32[]{:S(2)}, u32[]{:S(2)}) collective-permute-start(bf16[128,256]{1,0:T(8,128)(2,1)} %param.22), channel_id=1, source_target_pairs={{0,28},{4,24},{8,20},{12,16},{16,12},{20,8},{24,4},{28,0},{1,29},{... | collective-permute-start | bytes 196616 | tf_op jit(solution)/shard_map/ppermute | solution.py:437
  15.1 0.8 copy-start.15
  17.3 26.6 %copy-start.20 = (f32[256]{0:T(256)S(1)}, f32[256]{0:T(256)}, u32[]{:S(2)}) copy-start(f32[256]{0:T(256)} %param.31) | copy-start | bytes 3076
  17.3 26.6 %copy-start.22 = (f32[256]{0:T(256)S(1)}, f32[256]{0:T(256)}, u32[]{:S(2)}) copy-start(f32[256]{0:T(256)} %param.34) | copy-start | bytes 3076
  25.3 18.6 %collective-permute-start.1 = (bf16[2,1024]{1,0:T(2,128)(2,1)S(1)}, bf16[2,1024]{1,0:T(2,128)(2,1)S(1)}, u32[]{:S(2)}, u32[]{:S(2)}) collective-permute-start(bf16[2,1024]{1,0:T(2,128)(2,1)S(1)} %bitcast.29), channel_id=1, source_target_pairs={{0,4},{4,8},{8,12},{12,16},{16,20},{20,24},{24,28},{1,5},{5,9},{9,... | collective-permute-start | bytes 12296 | tf_op jit(solution)/shard_map/ppermute | solution.py:406
  28.7 15.2 %collective-permute-start.2 = (bf16[2,1024]{1,0:T(2,128)(2,1)S(1)}, bf16[2,1024]{1,0:T(2,128)(2,1)S(1)}, u32[]{:S(2)}, u32[]{:S(2)}) collective-permute-start(bf16[2,1024]{1,0:T(2,128)(2,1)S(1)} %bitcast.30), channel_id=1, source_target_pairs={{4,0},{8,4},{12,8},{16,12},{20,16},{24,20},{28,24},{5,1},{9,5},{13... | collective-permute-start | bytes 12296 | tf_op jit(solution)/shard_map/ppermute | solution.py:406
  30.0 1.0 copy-start.3
  31.1 1.1 copy-start.5
  32.1 1.1 %copy-start.6 = (bf16[1024,256]{1,0:T(8,128)(2,1)S(1)}, bf16[1024,256]{1,0:T(8,128)(2,1)}, u32[]{:S(2)}) copy-start(bf16[1024,256]{1,0:T(8,128)(2,1)} %refs_12_.1) | copy-start | bytes 1572868
  33.2 0.9 copy-start.7
  34.1 0.9 copy-start.9
  35.1 0.8 copy-start.11
  35.8 0.8 copy-start.12
  36.6 0.8 copy-start.13
  50.8 8.1 %collective-permute-start.3 = (bf16[2,128,256]{2,1,0:T(8,128)(2,1)S(1)}, bf16[2,128,256]{2,1,0:T(8,128)(2,1)S(1)}, u32[]{:S(2)}, u32[]{:S(2)}) collective-permute-start(bf16[2,128,256]{2,1,0:T(8,128)(2,1)S(1)} %get-tuple-element.38), channel_id=1, source_target_pairs={{0,4},{4,0},{8,12},{12,8},{16,20},{20,16},{24,28},{28,24},{1,5},{5... | collective-permute-start | bytes 393224 | tf_op jit(solution)/shard_map/ppermute | solution.py:490
  53.5 25.9 %copy-start.23 = (f32[256]{0:T(256)S(1)}, f32[256]{0:T(256)}, u32[]{:S(2)}) copy-start(f32[256]{0:T(256)} %param.36) | copy-start | bytes 3076
  59.2 29.1 %copy-start = (bf16[1024,1024]{1,0:T(8,128)(2,1)S(1)}, bf16[1024,1024]{1,0:T(8,128)(2,1)}, u32[]{:S(2)}) copy-start(bf16[1024,1024]{1,0:T(8,128)(2,1)} %up_hbm.1) | copy-start | bytes 6291460
  59.2 29.1 %copy-start.17 = (f32[1024]{0:T(1024)S(1)}, f32[1024]{0:T(1024)}, u32[]{:S(2)}) copy-start(f32[1024]{0:T(1024)} %param.25) | copy-start | bytes 12292
  59.2 13.1 %collective-permute-start.4 = (bf16[2,128,256]{2,1,0:T(8,128)(2,1)S(1)}, bf16[2,128,256]{2,1,0:T(8,128)(2,1)S(1)}, u32[]{:S(2)}, u32[]{:S(2)}) collective-permute-start(bf16[2,128,256]{2,1,0:T(8,128)(2,1)S(1)} %get-tuple-element.39), channel_id=1, source_target_pairs={{4,12},{8,0},{12,20},{16,8},{20,28},{24,16},{5,13},{9,1},{13,21},{... | collective-permute-start | bytes 393224 | tf_op jit(solution)/shard_map/ppermute | solution.py:499
  60.6 13.2 %collective-permute-start.5 = (bf16[2,128,256]{2,1,0:T(8,128)(2,1)S(1)}, bf16[2,128,256]{2,1,0:T(8,128)(2,1)S(1)}, u32[]{:S(2)}, u32[]{:S(2)}) collective-permute-start(bf16[2,128,256]{2,1,0:T(8,128)(2,1)S(1)} %get-tuple-element.39), channel_id=1, source_target_pairs={{4,20},{12,28},{16,0},{24,8},{5,21},{13,29},{17,1},{25,9},{6,22},{... | collective-permute-start | bytes 393224 | tf_op jit(solution)/shard_map/ppermute | solution.py:499
  61.9 10.4 %collective-permute-start.6 = (bf16[2,64,256]{2,1,0:T(8,128)(2,1)S(1)}, bf16[2,64,256]{2,1,0:T(8,128)(2,1)S(1)}, u32[]{:S(2)}, u32[]{:S(2)}) collective-permute-start(bf16[2,64,256]{2,1,0:T(8,128)(2,1)S(1)} %get-tuple-element.40), channel_id=1, source_target_pairs={{4,28},{24,0},{5,29},{25,1},{6,30},{26,2},{7,31},{27,3}} | collective-permute-start | bytes 196616 | tf_op jit(solution)/shard_map/ppermute | solution.py:499
  74.8 4.6 %collective-permute-start.7 = (bf16[2,64,256]{2,1,0:T(8,128)(2,1)}, bf16[2,64,256]{2,1,0:T(8,128)(2,1)}, u32[]{:S(2)}, u32[]{:S(2)}) collective-permute-start(bf16[2,64,256]{2,1,0:T(8,128)(2,1)} %shard_map.196.entry_ref), channel_id=1, source_target_pairs={{0,4},{4,0},{8,12},{12,8},{16,20},{20,16},{24,28},{28,24},{1,5},{5... | collective-permute-start | bytes 196616 | tf_op jit(solution)/shard_map/ppermute | solution.py:525
  88.3 1.6 %copy-start.1 = (bf16[1024,1024]{1,0:T(8,128)(2,1)S(1)}, bf16[1024,1024]{1,0:T(8,128)(2,1)}, u32[]{:S(2)}) copy-start(bf16[1024,1024]{1,0:T(8,128)(2,1)} %down_hbm.1) | copy-start | bytes 6291460
  89.9 1.6 %copy-start.2 = (bf16[1024,1024]{1,0:T(8,128)(2,1)S(1)}, bf16[1024,1024]{1,0:T(8,128)(2,1)}, u32[]{:S(2)}) copy-start(bf16[1024,1024]{1,0:T(8,128)(2,1)} %all-gather.2.cloned.1.call-done.w_ref) | copy-start | bytes 6291460
  94.1 3.4 %collective-permute-start.10 = (bf16[128,256]{1,0:T(8,128)(2,1)S(1)}, bf16[128,256]{1,0:T(8,128)(2,1)S(1)}, u32[]{:S(2)}, u32[]{:S(2)}) collective-permute-start(bf16[128,256]{1,0:T(8,128)(2,1)S(1)} %get-tuple-element.54), channel_id=1, source_target_pairs={{0,3},{1,0},{2,1},{3,2},{4,7},{5,4},{6,5},{7,6},{8,11},{9,8},{10,9... | collective-permute-start | bytes 196616 | tf_op jit(solution)/shard_map/ppermute | solution.py:548
  95.3 4.0 %collective-permute-start.8 = (bf16[128,256]{1,0:T(8,128)(2,1)S(1)}, bf16[128,256]{1,0:T(8,128)(2,1)S(1)}, u32[]{:S(2)}, u32[]{:S(2)}) collective-permute-start(bf16[128,256]{1,0:T(8,128)(2,1)S(1)} %get-tuple-element.52), channel_id=1, source_target_pairs={{0,1},{1,2},{2,3},{3,0},{4,5},{5,6},{6,7},{7,4},{8,9},{9,10},{10,1... | collective-permute-start | bytes 196616 | tf_op jit(solution)/shard_map/ppermute | solution.py:548
  95.3 4.9 %collective-permute-start.9 = (bf16[128,256]{1,0:T(8,128)(2,1)S(1)}, bf16[128,256]{1,0:T(8,128)(2,1)S(1)}, u32[]{:S(2)}, u32[]{:S(2)}) collective-permute-start(bf16[128,256]{1,0:T(8,128)(2,1)S(1)} %get-tuple-element.53), channel_id=1, source_target_pairs={{0,2},{1,3},{2,0},{3,1},{4,6},{5,7},{6,4},{7,5},{8,10},{9,11},{10,... | collective-permute-start | bytes 196616 | tf_op jit(solution)/shard_map/ppermute | solution.py:548
  (5 other events, 3.4 us)
Sparse Core Ops, SparseCore 0:
  25.3 23.2 all-gather.1

commit v4 on v3

--- a/solution.py
+++ b/solution.py
@@ -18,7 +18,6 @@
 MIB = 1024 * 1024
 VMEM_SPEC = pl.BlockSpec(memory_space=pltpu.VMEM)
 SMEM_SPEC = pl.BlockSpec(memory_space=pltpu.SMEM)
-HBM_SPEC = pl.BlockSpec(memory_space=pltpu.HBM)
 
 
 def mm(left, right):
@@ -64,10 +63,7 @@
     return centered * lax.rsqrt(variance + NORM_EPS) * gain
 
 
-def strands_kernel(*refs):
-    rc_ref, ins, out_ref, locals_, sems = refs[0], refs[1:4], refs[4], refs[5:8], refs[8]
-    arrived(copied(ins, locals_, sems))
-    ids_ref, fwd_ref, embed_ref = locals_
+def embed_kernel(ids_ref, fwd_ref, embed_ref, strand_ref, other_ref):
     rows = fwd_ref.shape[0]
     ids = ids_ref[...]
     letters = ids_of((embed_ref.shape[0], rows), 0)
@@ -83,10 +79,15 @@
             preferred_element_type=F32,
         )
 
-    out_ref[0] = (fwd_ref[...].astype(F32) + looked_up(ids)).astype(BF16)
+    strand_ref[...] = (fwd_ref[...].astype(F32) + looked_up(ids)).astype(BF16)
+    other_ref[...] = looked_up(3 - ids)
+
+
+def strands_kernel(rc_ref, strand_ref, other_ref, out_ref):
+    rows = rc_ref.shape[0]
+    out_ref[0] = strand_ref[...]
     flip = (ids_of((rows, rows), 0) + ids_of((rows, rows), 1) == rows - 1).astype(F32)
-    turned = mm(flip.astype(BF16), rc_ref[...])
-    out_ref[1] = (turned + looked_up(3 - ids)).astype(BF16)
+    out_ref[1] = (mm(flip.astype(BF16), rc_ref[...]) + other_ref[...]).astype(BF16)
 
 
 def inverse_of(pulls, rows):
@@ -107,36 +108,22 @@
     return inverses
 
 
-def copied(sources, targets, sems):
-    copies = [pltpu.make_async_copy(src, dst, sems.at[i]) for i, (src, dst) in enumerate(zip(sources, targets))]
-    for item in copies:
-        item.start()
-    return copies
-
-
-def arrived(copies):
-    for item in copies:
-        item.wait()
-
-
-def gates(decay_mix, rate_mix, d_base, w_d2, c_base, w_c2, w_d1, w_c1):
-    decay_low = jnp.tanh(mm_rows(decay_mix, w_d1)).astype(BF16)
-    log_decay = -DECAY_SCALE * jax.nn.sigmoid(d_base + mm(decay_low, w_d2))
-    rate_low = mm_rows(rate_mix, w_c1).astype(BF16)
-    return log_decay, jax.nn.sigmoid(c_base + mm(rate_low, w_c2))
+def project_all(mix, params):
+    w_r, w_k, w_v, w_d1, w_c1, w_d2, w_c2, d_base, c_base = params
+    for index, weight in enumerate((w_r, w_k, w_v)):
+        yield mm(mix(index), weight[...])
+    decay_low = jnp.tanh(mm_rows(mix(3), w_d1[...])).astype(BF16)
+    yield -DECAY_SCALE * jax.nn.sigmoid(d_base[...] + mm(decay_low, w_d2[...]))
+    rate_low = mm_rows(mix(4), w_c1[...]).astype(BF16)
+    yield jax.nn.sigmoid(c_base[...] + mm(rate_low, w_c2[...]))
 
 
 def project_kernel(x_ref, *refs):
-    params, refs = refs[:11], refs[11:]
-    outs, edge_ref = refs[:5], refs[5]
-    normed, mixed = refs[6:8]
-    locals_, sems = refs[8:19], refs[19]
-    gain_ref, mixing_ref, w_r_ref, w_k_ref, w_v_ref, w_d1, w_c1, d_base, w_d2, c_base, w_c2 = locals_
-    copies = copied(params, locals_, sems)
+    (gain_ref, mixing_ref), params = refs[:2], refs[2:11]
+    outs, edge_ref, (normed, mixed) = refs[11:16], refs[16], refs[17:]
     strands, rows, _ = x_ref.shape
-    width = w_r_ref.shape[1]
+    width = outs[0].shape[2]
     pad = 8
-    arrived(copies[:2])
     gain = gain_ref[...]
     for s in range(strands):
         values = layer_norm(x_ref[s].astype(F32), gain)
@@ -158,15 +145,8 @@
         return mixed[...]
 
     shape = (2 * strands, rows, width)
-    for index, w_ref in enumerate((w_r_ref, w_k_ref, w_v_ref)):
-        copies[2 + index].wait()
-        outs[index][...] = mm(mix(index), w_ref[...]).reshape(shape)
-    arrived(copies[5:])
-    log_decay, rate = gates(
-        mix(3), mix(4), d_base[...], w_d2[...], c_base[...], w_c2[...], w_d1[...], w_c1[...]
-    )
-    outs[3][...] = log_decay.reshape(shape)
-    outs[4][...] = rate.reshape(shape)
+    for out_ref, result in zip(outs, project_all(mix, params)):
+        out_ref[...] = result.reshape(shape)
 
 
 def masked_heads(value, lane_head, heads):
@@ -176,33 +156,22 @@
 def chunk_kernel(first, direction_ref, *refs):
     lanes, refs = refs[:5], refs[5:]
     if first:
-        before_ref, after_ref, edge_ref = refs[:3]
-        params, refs = refs[3:14], refs[14:]
-        state_ref, parts_ref, edges_ref = refs[:3]
-        locals_, sems = refs[3:14], refs[14]
+        before_ref, after_ref, edge_ref, gain_ref, mixing_ref, *params, state_ref, parts_ref, edges_ref = refs
     else:
         edges_ref, state_ref, parts_ref = refs
     strands, _, rows, width = parts_ref.shape
     heads = width // HEAD
     d = direction_ref[0]
     if first:
-        arrived(copied(params, locals_, sems))
-        gain_ref, mixing_ref, w_r_ref, w_k_ref, w_v_ref, w_d1, w_c1, d_base, w_d2, c_base, w_c2 = locals_
-        gain = gain_ref[...]
         center = edge_ref[...]
         halo = jnp.concatenate([before_ref[...], after_ref[...]], axis=0).astype(F32)
-        change = layer_norm(halo, gain) - center
+        change = layer_norm(halo, gain_ref[...]) - center
 
         def mix(index):
             return (center + change * mixing_ref[index : index + 1, :]).astype(BF16)
 
-        for index, w_ref in enumerate((w_r_ref, w_k_ref, w_v_ref)):
-            edges_ref[index] = mm(mix(index), w_ref[...])
-        log_decay, rate = gates(
-            mix(3), mix(4), d_base[...], w_d2[...], c_base[...], w_c2[...], w_d1[...], w_c1[...]
-        )
-        edges_ref[3] = log_decay
-        edges_ref[4] = rate
+        for index, result in enumerate(project_all(mix, params)):
+            edges_ref[index] = result
     edge_row = d * (rows - 1)
     at_edge = ids_of((rows, width), 0) == edge_row
     order = (ids_of((rows, rows), 0) - ids_of((rows, rows), 1)) * (1 - 2 * d)
@@ -364,9 +333,8 @@
         out_ref[s] = (joined * gain).astype(BF16)
 
 
-def mix_kernel(index_ref, joined_ref, x_ref, w_ref, gain_ref, up_hbm, down_hbm, own_ref, *rest):
-    *sent_refs, partial, total, up_ref, down_ref, sems = rest
-    copies = copied((up_hbm, down_hbm), (up_ref, down_ref), sems)
+def mix_kernel(index_ref, joined_ref, x_ref, w_ref, up_ref, down_ref, gain_ref, own_ref, *rest):
+    *sent_refs, partial, total = rest
     strands, rows, _ = x_ref.shape
     width = own_ref.shape[1]
     gain = gain_ref[...]
@@ -374,10 +342,8 @@
     attention = mm(joined, w_ref[...])
     residuals = [x_ref[s].astype(F32) + attention[s * rows : (s + 1) * rows] for s in range(strands)]
     inner = jnp.concatenate([layer_norm(item, gain).astype(BF16) for item in residuals], axis=0)
-    copies[0].wait()
     active = jnp.square(jnp.maximum(mm(inner, up_ref[...]), 0.0)).astype(BF16).astype(F32)
     added = sum(active[s * rows : (s + 1) * rows] for s in range(strands)).astype(BF16)
-    copies[1].wait()
     partial[...] = mm(added, down_ref[...])
     total[...] = sum(residuals)
 
@@ -391,11 +357,12 @@
         ref[...] = part(partial, lax.rem(me + step + 1, size)).astype(BF16)
 
 
-def call(kernel, out_shape, scratch=(), mib=12, **kwargs):
+def call(kernel, out_shape, scratch=(), mib=12, us=2, **kwargs):
     return pl.pallas_call(
         kernel,
         out_shape=out_shape,
         scratch_shapes=list(scratch),
+        cost_estimate=pl.CostEstimate(flops=us * 10**9, bytes_accessed=us * 10**6, transcendentals=0),
         compiler_params=pltpu.CompilerParams(vmem_limit_bytes=mib * MIB),
         **kwargs,
     )
@@ -435,24 +402,6 @@
 
     mirror = [(i, seq_count - 1 - i) for i in range(seq_count)]
     rc_here = lax.ppermute(hidden_rc, "seq", mirror)
-    firsts = (ids.reshape(1, rows), hidden_fwd, embed)
-    local = call(
-        strands_kernel,
-        struct((strands, rows, width), BF16),
-        scratch=[pltpu.VMEM(item.shape, item.dtype) for item in firsts] + [pltpu.SemaphoreType.DMA((3,))],
-        in_specs=[VMEM_SPEC] + [HBM_SPEC] * 3,
-    )(rc_here, *firsts)
-    whole = lax.all_gather(local, "mp", axis=2, tiled=True)
-    before = shifted(whole[:, rows - 1], "seq", 1)
-    after = shifted(whole[:, 0], "seq", -1)
-    w_output, _ = lax.optimization_barrier((w_output, whole))
-    w_output_whole = lax.all_gather(w_output, "mp", axis=0, tiled=True)
-
-    groups = 2 * strands
-    f32_lanes, bf16_lanes = struct((groups, rows, width), F32), struct((strands, rows, width), BF16)
-    parts_struct = struct((strands, 7, rows, width), BF16)
-    state_struct = struct((strands, 2 * HEAD, width), BF16)
-    entry_struct = struct((strands, HEAD, width), BF16)
     params = (
         ln1_gain.reshape(1, full),
         mixing,
@@ -461,30 +410,41 @@
         w_value,
         decay_first_weight.T,
         context_rate_first_weight.T,
+        decay_second_weight,
+        context_rate_second_weight,
         decay_base.reshape(1, width),
-        decay_second_weight,
         iclr_base.reshape(1, width),
-        context_rate_second_weight,
     )
-    param_scratch = [pltpu.VMEM(item.shape, item.dtype) for item in params]
-    param_scratch += [pltpu.SemaphoreType.DMA((len(params),))]
+    strand, other = call(
+        embed_kernel, (struct((rows, width), BF16), struct((rows, width), F32)), us=10
+    )(ids.reshape(1, rows), hidden_fwd, embed)
+    rc_here, strand, other = lax.optimization_barrier((rc_here, strand, other))
+    local = call(strands_kernel, struct((strands, rows, width), BF16), us=10)(rc_here, strand, other)
+    whole = lax.all_gather(local, "mp", axis=2, tiled=True)
+    before = shifted(whole[:, rows - 1], "seq", 1)
+    after = shifted(whole[:, 0], "seq", -1)
+    w_output, _ = lax.optimization_barrier((w_output, whole))
+    w_output_whole = lax.all_gather(w_output, "mp", axis=0, tiled=True)
+
+    groups = 2 * strands
+    f32_lanes, bf16_lanes = struct((groups, rows, width), F32), struct((strands, rows, width), BF16)
+    parts_struct = struct((strands, 7, rows, width), BF16)
+    state_struct = struct((strands, 2 * HEAD, width), BF16)
+    entry_struct = struct((strands, HEAD, width), BF16)
     *lanes, edge = call(
         project_kernel,
         (f32_lanes,) * 5 + (struct((groups, full), F32),),
         scratch=[
             pltpu.VMEM((strands, rows + 16, full), F32),
             pltpu.VMEM((groups * rows, full), BF16),
-        ]
-        + param_scratch,
-        in_specs=[VMEM_SPEC] + [HBM_SPEC] * len(params),
+        ],
     )(whole, *params)
 
     parity = (lax.axis_index("seq") % 2).astype(jnp.int32).reshape(1)
     sent, sent_parts, edges = call(
         functools.partial(chunk_kernel, True),
         (state_struct, parts_struct, struct((5, groups, width), F32)),
-        scratch=param_scratch,
-        in_specs=[SMEM_SPEC] + [VMEM_SPEC] * 8 + [HBM_SPEC] * len(params),
+        in_specs=[SMEM_SPEC] + [VMEM_SPEC] * (8 + len(params)),
     )(parity, *lanes, before, after, edge, *params)
     partner = [(i, i ^ 1) for i in range(seq_count)]
     from_partner = lax.ppermute(sent, "seq", partner)
@@ -515,12 +475,15 @@
         )(current, *window, *received)
         window = [wide]
         distance *= RADIX
+    sent_parts, kept_parts, _ = lax.optimization_barrier((sent_parts, kept_parts, current))
     local_out, start_map = call(
         read_kernel,
         (f32_lanes, struct(f32_lanes.shape, BF16)),
         in_specs=[SMEM_SPEC] + [VMEM_SPEC] * 2,
     )(parity, sent_parts, kept_parts)
-    received, local_out, start_map = lax.optimization_barrier((received, local_out, start_map))
+    received, local_out, start_map, w_output_whole = lax.optimization_barrier(
+        (received, local_out, start_map, w_output_whole)
+    )
     entry = call(functools.partial(entry_kernel, bool(window)), entry_struct)(*window, *received)
     other = lax.ppermute(entry, "seq", partner)
     joined = call(finish_kernel, bf16_lanes)(
@@ -535,13 +498,10 @@
         scratch=[
             pltpu.VMEM((rows, full), F32),
             pltpu.VMEM((rows, full), F32),
-            pltpu.VMEM(ffn_key.shape, BF16),
-            pltpu.VMEM(ffn_value.shape, BF16),
-            pltpu.SemaphoreType.DMA((2,)),
         ],
         mib=24,
-        in_specs=[SMEM_SPEC] + [VMEM_SPEC] * 4 + [HBM_SPEC] * 2,
-    )(position, joined_whole, whole, w_output_whole, ln2_gain.reshape(1, full), ffn_key, ffn_value)
+        in_specs=[SMEM_SPEC] + [VMEM_SPEC] * 6,
+    )(position, joined_whole, whole, w_output_whole, ffn_key, ffn_value, ln2_gain.reshape(1, full))
     merged = own
     for step, item in enumerate(sent):
         pairs = [(i, (i + step + 1) % mp_count) for i in range(mp_count)]

time: 109 us -> 89.1 us (0.82)
  local copies, waits for them, and re-layouts: 14.8 us -> 2.3 us
  Pallas kernels: 25.4 us -> 21.7 us
  waiting for transfers between devices: 19.6 us -> 17.5 us
    unnamed x52 -> x40, local copies, waits for them, and re-layouts: 14.8 us -> 2.28 us
    ppermute x1, waiting for transfers between devices: 2.46 us -> 0.01 us  [on_device(): rc_here = lax.ppermute(hidden_rc, 'seq', mirror)]
  transfers between devices with their start and end apart: 12 -> 12, of which waited for: 7 -> 7; matrix products, arithmetic and copies ran while one was open for 0% -> 0% of each run, Pallas kernels for 21% -> 20%
where the time goes in v4:
time: 89.1 us; the launch traced here: 88.8 us
  Pallas kernels  21.7 us (24%)
  starting transfers between devices  18.9 us (21%)
  waiting for transfers between devices  17.5 us (20%)
  blocking collectives  14 us (16%)
  between operations  13.8 us (15%)
  local copies, waits for them, and re-layouts  2.3 us (3%)
    ppermute x3, waiting for transfers between devices, onward(): lax.ppermute(value, 'seq', [(i, j) for i, j in route if 0 <= j < seq_count])  8.61 us
    all_gather x1, blocking collectives, on_device(): whole = lax.all_gather(local, 'mp', axis=2, tiled=True)  7.3 us
    all_gather x1, blocking collectives, on_device(): joined_whole = lax.all_gather(joined, 'mp', axis=2, tiled=True)  6.65 us
    pallas_call x1, Pallas kernels, on_device(): call(functools.partial(chunk_kernel, True), (state_struct, parts_struct,...  6.16 us
    ppermute x1, starting transfers between devices, on_device(): rc_here = lax.ppermute(hidden_rc, 'seq', mirror)  6 us
    pallas_call x1, Pallas kernels, on_device(): call(functools.partial(chunk_kernel, False), (state_struct, parts_struct)...  5.41 us
    ppermute x2, starting transfers between devices, shifted(): lax.ppermute(value, axis, [(i, i + distance) for i in devices if i + dist...  4.68 us
    ppermute x1, waiting for transfers between devices, on_device(): other = lax.ppermute(entry, 'seq', partner)  4.25 us
  transfers between devices with their start and end apart: 12, of which 7 were waited for; matrix products, arithmetic and copies ran while one was open for 0% of the time, Pallas kernels for 20%

profile of v4, /device:TPU:0, one launch (start us, length us, event | category | flops | bytes accessed | tf_op | source)
XLA Modules:
  0.0 88.8 jit_solution(14391740216450538923)
XLA Ops:
  6.5 6.0 %collective-permute-start = (bf16[128,256]{1,0:T(8,128)(2,1)}, bf16[128,256]{1,0:T(8,128)(2,1)S(1)}, u32[]{:S(2)}, u32[]{:S(2)}) collective-permute-start(bf16[128,256]{1,0:T(8,128)(2,1)} %param.22), channel_id=1, source_target_pairs={{0,28},{4,24},{8,20},{12,16},{16,12},{20,8},{24,4},{28,0},{1,29},{... | collective-permute-start | bytes 196616 | tf_op jit(solution)/shard_map/ppermute | solution.py:404
  12.5 0.8 copy-done.8
  13.4 0.7 copy-done.12
  14.1 0.7 copy-done.18
  14.7 0.4 shard_map.190
  15.3 0.1 shard_map.191
  15.4 7.3 %all_gather.9.x_ref = bf16[2,128,1024]{2,1,0:T(8,128)(2,1)S(1)} all-gather(bf16[2,128,256]{2,1,0:T(8,128)(2,1)S(1)} %shard_map.191), channel_id=1, replica_groups=mesh['seq'=8,'mp'=4] {'mp'}, dimensions={2}, use_global_device_ids=true | all-gather | bytes 655360 | tf_op jit(solution)/shard_map/all_gather | solution.py:423
  22.8 3.4 %collective-permute-start.1 = (bf16[2,1024]{1,0:T(2,128)(2,1)S(1)}, bf16[2,1024]{1,0:T(2,128)(2,1)S(1)}, u32[]{:S(2)}, u32[]{:S(2)}) collective-permute-start(bf16[2,1024]{1,0:T(2,128)(2,1)S(1)} %bitcast.29), channel_id=1, source_target_pairs={{0,4},{4,8},{8,12},{12,16},{16,20},{20,24},{24,28},{1,5},{5,9},{9,... | collective-permute-start | bytes 12296 | tf_op jit(solution)/shard_map/ppermute | solution.py:373
  26.2 1.3 %collective-permute-start.2 = (bf16[2,1024]{1,0:T(2,128)(2,1)S(1)}, bf16[2,1024]{1,0:T(2,128)(2,1)S(1)}, u32[]{:S(2)}, u32[]{:S(2)}) collective-permute-start(bf16[2,1024]{1,0:T(2,128)(2,1)S(1)} %bitcast.30), channel_id=1, source_target_pairs={{4,0},{8,4},{12,8},{16,12},{20,16},{24,20},{28,24},{5,1},{9,5},{13... | collective-permute-start | bytes 12296 | tf_op jit(solution)/shard_map/ppermute | solution.py:373
  27.6 3.5 %shard_map.192 = (f32[4,128,256]{2,1,0:T(8,128)S(1)}, f32[4,128,256]{2,1,0:T(8,128)S(1)}, f32[4,128,256]{2,1,0:T(8,128)S(1)}, f32[4,128,256]{2,1,0:T(8,128)S(1)}...) custom-call(bf16[2,128,1024]{2,1,0:T(8,128)(2,1)S(1)} %all_gather.9.x_ref, f32[1,1024]{1,0:T(1,128)S(1)} %bitcast.20, ...), custom_call_target="tpu_custom_call" | custom-call | flops 2000000000 | bytes 2000000 | tf_op jit(solution)/shard_map/pallas_call | solution.py:434
  31.2 0.6 collective-permute-done.2.refs_6_
  31.7 6.2 %shard_map.193 = (bf16[2,128,256]{2,1,0:T(8,128)(2,1)S(1)}, bf16[2,7,128,256]{3,2,1,0:T(8,128)(2,1)S(1)}, f32[5,4,256]{2,1,0:T(4,128)S(1)}) custom-call(s32[1]{0:T(128)} %bitcast.1.direction_ref, f32[4,128,256]{2,1,0:T(8,128)S(1)} %get-tuple-element.43.refs_0_, f32[4,128,256]{2,1,0:T(8,128)S(1)} %get-tuple-element.44.refs_1_, ...), custom_call_target="tpu_custom_call" | custom-call | flops 2000000000 | bytes 2000000 | tf_op jit(solution)/shard_map/pallas_call | solution.py:444
  37.9 2.2 %collective-permute-start.3 = (bf16[2,128,256]{2,1,0:T(8,128)(2,1)S(1)}, bf16[2,128,256]{2,1,0:T(8,128)(2,1)S(1)}, u32[]{:S(2)}, u32[]{:S(2)}) collective-permute-start(bf16[2,128,256]{2,1,0:T(8,128)(2,1)S(1)} %get-tuple-element.51), channel_id=1, source_target_pairs={{0,4},{4,0},{8,12},{12,8},{16,20},{20,16},{24,28},{28,24},{1,5},{5... | collective-permute-start | bytes 393224 | tf_op jit(solution)/shard_map/ppermute | solution.py:450
  40.1 5.4 %shard_map.194 = (bf16[2,128,256]{2,1,0:T(8,128)(2,1)S(1)}, bf16[2,7,128,256]{3,2,1,0:T(8,128)(2,1)S(1)}) custom-call(s32[1]{0:T(128)S(6)} %sub.3.direction_ref, f32[4,128,256]{2,1,0:T(8,128)S(1)} %get-tuple-element.43.refs_0_, f32[4,128,256]{2,1,0:T(8,128)S(1)} %get-tuple-element.44.refs_1_, f32[4,128,256]{2,1,0:T(8,128)S(1)} %get-tuple-element.45.refs_2_, ...), custom_call_target="tpu_custom_call" | custom-call | flops 2000000000 | bytes 2000000 | tf_op jit(solution)/shard_map/pallas_call | solution.py:451
  45.5 0.2 shard_map.195
  45.7 1.3 %collective-permute-start.4 = (bf16[2,128,256]{2,1,0:T(8,128)(2,1)S(1)}, bf16[2,128,256]{2,1,0:T(8,128)(2,1)S(1)}, u32[]{:S(2)}, u32[]{:S(2)}) collective-permute-start(bf16[2,128,256]{2,1,0:T(8,128)(2,1)S(1)} %get-tuple-element.52), channel_id=1, source_target_pairs={{4,12},{8,0},{12,20},{16,8},{20,28},{24,16},{5,13},{9,1},{13,21},{... | collective-permute-start | bytes 393224 | tf_op jit(solution)/shard_map/ppermute | solution.py:459
  47.0 1.3 %collective-permute-start.5 = (bf16[2,128,256]{2,1,0:T(8,128)(2,1)S(1)}, bf16[2,128,256]{2,1,0:T(8,128)(2,1)S(1)}, u32[]{:S(2)}, u32[]{:S(2)}) collective-permute-start(bf16[2,128,256]{2,1,0:T(8,128)(2,1)S(1)} %get-tuple-element.52), channel_id=1, source_target_pairs={{4,20},{12,28},{16,0},{24,8},{5,21},{13,29},{17,1},{25,9},{6,22},{... | collective-permute-start | bytes 393224 | tf_op jit(solution)/shard_map/ppermute | solution.py:459
  48.3 1.3 %collective-permute-start.6 = (bf16[2,64,256]{2,1,0:T(8,128)(2,1)S(1)}, bf16[2,64,256]{2,1,0:T(8,128)(2,1)S(1)}, u32[]{:S(2)}, u32[]{:S(2)}) collective-permute-start(bf16[2,64,256]{2,1,0:T(8,128)(2,1)S(1)} %get-tuple-element.53), channel_id=1, source_target_pairs={{4,28},{24,0},{5,29},{25,1},{6,30},{26,2},{7,31},{27,3}} | collective-permute-start | bytes 196616 | tf_op jit(solution)/shard_map/ppermute | solution.py:459
  49.6 2.1 %shard_map.196 = (f32[4,128,256]{2,1,0:T(8,128)S(1)}, bf16[4,128,256]{2,1,0:T(8,128)(2,1)S(1)}) custom-call(s32[1]{0:T(128)} %bitcast.1.direction_ref, bf16[2,7,128,256]{3,2,1,0:T(8,128)(2,1)S(1)} %get-tuple-element.56.sent_ref, bf16[2,7,128,256]{3,2,1,0:T(8,128)(2,1)S(1)} %get-tuple-element.57.kept_ref), custom_call_target="tpu_custom_call" | custom-call | flops 2000000000 | bytes 2000000 | tf_op jit(solution)/shard_map/pallas_call | solution.py:479
  51.7 7.5 %collective-permute-done.6.refs_2_ = bf16[2,64,256]{2,1,0:T(8,128)(2,1)S(1)} collective-permute-done((bf16[2,64,256]{2,1,0:T(8,128)(2,1)S(1)}, bf16[2,64,256]{2,1,0:T(8,128)(2,1)S(1)}, u32[]{:S(2)}, u32[]{:S(2)}) %collective-permute-start.6) | collective-permute-done | bytes 65568 | tf_op jit(solution)/shard_map/ppermute | solution.py:459
  59.2 1.1 %collective-permute-done.5.refs_1_ = bf16[2,128,256]{2,1,0:T(8,128)(2,1)S(1)} collective-permute-done((bf16[2,128,256]{2,1,0:T(8,128)(2,1)S(1)}, bf16[2,128,256]{2,1,0:T(8,128)(2,1)S(1)}, u32[]{:S(2)}, u32[]{:S(2)}) %collective-permute-start.5) | collective-permute-done | bytes 131104 | tf_op jit(solution)/shard_map/ppermute | solution.py:459
  60.3 0.4 shard_map.197.entry_ref
  60.8 4.3 %collective-permute-done.7.other_ref = bf16[2,64,256]{2,1,0:T(8,128)(2,1)S(1)} collective-permute-done((bf16[2,64,256]{2,1,0:T(8,128)(2,1)S(1)}, bf16[2,64,256]{2,1,0:T(8,128)(2,1)S(1)}, u32[]{:S(2)}, u32[]{:S(2)}) %collective-permute-start.7) | collective-permute-done | bytes 65568 | tf_op jit(solution)/shard_map/ppermute | solution.py:488
  65.1 1.3 %shard_map.198 = bf16[2,128,256]{2,1,0:T(8,128)(2,1)S(1)} custom-call(bf16[2,64,256]{2,1,0:T(8,128)(2,1)S(1)} %shard_map.197.entry_ref, bf16[2,128,256]{2,1,0:T(8,128)(2,1)S(1)} %collective-permute-done.3.from_ref, bf16[2,64,256]{2,1,0:T(8,128)(2,1)S(1)} %collective-permute-done.7.other_ref, f32[4,128,256]{2,1,0:T(8,128)S(1)} %get-tuple-element.64.local_ref, ...), custom_call_target="tpu_custom_call" | custom-call | flops 2000000000 | bytes 2000000 | tf_op jit(solution)/shard_map/pallas_call | solution.py:489
  66.4 6.7 %all_gather.11.joined_ref = bf16[2,128,1024]{2,1,0:T(8,128)(2,1)S(1)} all-gather(bf16[2,128,256]{2,1,0:T(8,128)(2,1)S(1)} %shard_map.198), channel_id=1, replica_groups=mesh['seq'=8,'mp'=4] {'mp'}, dimensions={2}, use_global_device_ids=true | all-gather | bytes 655360 | tf_op jit(solution)/shard_map/all_gather | solution.py:492
  73.1 2.1 %shard_map.199 = (f32[128,256]{1,0:T(8,128)S(1)}, bf16[128,256]{1,0:T(8,128)(2,1)S(1)}, bf16[128,256]{1,0:T(8,128)(2,1)S(1)}, bf16[128,256]{1,0:T(8,128)(2,1)S(1)}) custom-call(s32[1]{0:T(128)} %bitcast.index_ref, bf16[2,128,1024]{2,1,0:T(8,128)(2,1)S(1)} %all_gather.11.joined_ref, bf16[2,128,1024]{2,1,0:T(8,128)(2,1)S(1)} %all_gather.9.x_ref, ...), custom_call_target="tpu_custom_call" | custom-call | flops 2000000000 | bytes 2000000 | tf_op jit(solution)/shard_map/pallas_call | solution.py:495
  75.2 1.2 %collective-permute-start.10 = (bf16[128,256]{1,0:T(8,128)(2,1)S(1)}, bf16[128,256]{1,0:T(8,128)(2,1)S(1)}, u32[]{:S(2)}, u32[]{:S(2)}) collective-permute-start(bf16[128,256]{1,0:T(8,128)(2,1)S(1)} %get-tuple-element.70), channel_id=1, source_target_pairs={{0,3},{1,0},{2,1},{3,2},{4,7},{5,4},{6,5},{7,6},{8,11},{9,8},{10,9... | collective-permute-start | bytes 196616 | tf_op jit(solution)/shard_map/ppermute | solution.py:508
  76.4 0.9 collective-permute-start.9
  77.2 1.4 %collective-permute-done.10 = bf16[128,256]{1,0:T(8,128)(2,1)S(1)} collective-permute-done((bf16[128,256]{1,0:T(8,128)(2,1)S(1)}, bf16[128,256]{1,0:T(8,128)(2,1)S(1)}, u32[]{:S(2)}, u32[]{:S(2)}) %collective-permute-start.10) | collective-permute-done | bytes 65568 | tf_op jit(solution)/shard_map/ppermute | solution.py:508
  78.6 1.8 %collective-permute-done.8 = bf16[128,256]{1,0:T(8,128)(2,1)S(1)} collective-permute-done((bf16[128,256]{1,0:T(8,128)(2,1)S(1)}, bf16[128,256]{1,0:T(8,128)(2,1)S(1)}, u32[]{:S(2)}, u32[]{:S(2)}) %collective-permute-start.8) | collective-permute-done | bytes 65568 | tf_op jit(solution)/shard_map/ppermute | solution.py:508
  80.4 0.9 %collective-permute-done.9 = bf16[128,256]{1,0:T(8,128)(2,1)S(1)} collective-permute-done((bf16[128,256]{1,0:T(8,128)(2,1)S(1)}, bf16[128,256]{1,0:T(8,128)(2,1)S(1)}, u32[]{:S(2)}, u32[]{:S(2)}) %collective-permute-start.9) | collective-permute-done | bytes 65568 | tf_op jit(solution)/shard_map/ppermute | solution.py:508
  81.3 0.7 add_convert_fusion
  (47 shorter events, 0.2 us)
Async XLA Ops:
  6.5 53.8 %all-gather.2.cloned.1.call-start = ((), (), s32[]{:S(2)}) async-start(), calls=%async_computation | async-start | bytes 2621440 | tf_op jit(solution)/shard_map/all_gather | solution.py:427
  6.5 8.6 %collective-permute-start = (bf16[128,256]{1,0:T(8,128)(2,1)}, bf16[128,256]{1,0:T(8,128)(2,1)S(1)}, u32[]{:S(2)}, u32[]{:S(2)}) collective-permute-start(bf16[128,256]{1,0:T(8,128)(2,1)} %param.22), channel_id=1, source_target_pairs={{0,28},{4,24},{8,20},{12,16},{16,12},{20,8},{24,4},{28,0},{1,29},{... | collective-permute-start | bytes 196616 | tf_op jit(solution)/shard_map/ppermute | solution.py:404
  12.5 0.8 copy-start.8
  13.4 0.7 copy-start.12
  14.1 0.7 copy-start.18
  15.2 12.4 %copy-start.3 = (bf16[1024,256]{1,0:T(8,128)(2,1)S(1)}, bf16[1024,256]{1,0:T(8,128)(2,1)}, u32[]{:S(2)}) copy-start(bf16[1024,256]{1,0:T(8,128)(2,1)} %refs_10_.1) | copy-start | bytes 1572868
  15.2 12.4 %copy-start.4 = (bf16[1024,256]{1,0:T(8,128)(2,1)S(1)}, bf16[1024,256]{1,0:T(8,128)(2,1)}, u32[]{:S(2)}) copy-start(bf16[1024,256]{1,0:T(8,128)(2,1)} %refs_11_.1) | copy-start | bytes 1572868
  15.2 12.4 %copy-start.5 = (bf16[1024,256]{1,0:T(8,128)(2,1)S(1)}, bf16[1024,256]{1,0:T(8,128)(2,1)}, u32[]{:S(2)}) copy-start(bf16[1024,256]{1,0:T(8,128)(2,1)} %refs_12_.1) | copy-start | bytes 1572868
  15.2 12.4 %copy-start.6 = (bf16[1024,64]{0,1:T(8,128)(2,1)S(1)}, bf16[1024,64]{0,1:T(8,128)(2,1)}, u32[]{:S(2)}) copy-start(bf16[1024,64]{0,1:T(8,128)(2,1)} %param.30) | copy-start | bytes 393220
  15.2 12.4 %copy-start.7 = (bf16[1024,64]{0,1:T(8,128)(2,1)S(1)}, bf16[1024,64]{0,1:T(8,128)(2,1)}, u32[]{:S(2)}) copy-start(bf16[1024,64]{0,1:T(8,128)(2,1)} %param.33) | copy-start | bytes 393220
  15.2 12.4 %copy-start.9 = (f32[5,1024]{1,0:T(8,128)S(1)}, f32[5,1024]{1,0:T(8,128)}, u32[]{:S(2)}) copy-start(f32[5,1024]{1,0:T(8,128)} %refs_9_.1) | copy-start | bytes 61444
  15.2 12.4 %copy-start.10 = (bf16[64,256]{1,0:T(8,128)(2,1)S(1)}, bf16[64,256]{1,0:T(8,128)(2,1)}, u32[]{:S(2)}) copy-start(bf16[64,256]{1,0:T(8,128)(2,1)} %refs_15_.1) | copy-start | bytes 98308
  15.2 12.4 %copy-start.11 = (bf16[64,256]{1,0:T(8,128)(2,1)S(1)}, bf16[64,256]{1,0:T(8,128)(2,1)}, u32[]{:S(2)}) copy-start(bf16[64,256]{1,0:T(8,128)(2,1)} %refs_16_.1) | copy-start | bytes 98308
  15.3 12.4 %copy-start.13 = (f32[1024]{0:T(1024)S(1)}, f32[1024]{0:T(1024)}, u32[]{:S(2)}) copy-start(f32[1024]{0:T(1024)} %param.24) | copy-start | bytes 12292
  15.3 12.4 %copy-start.15 = (f32[256]{0:T(256)S(1)}, f32[256]{0:T(256)}, u32[]{:S(2)}) copy-start(f32[256]{0:T(256)} %param.31) | copy-start | bytes 3076
  15.3 12.4 %copy-start.16 = (f32[256]{0:T(256)S(1)}, f32[256]{0:T(256)}, u32[]{:S(2)}) copy-start(f32[256]{0:T(256)} %param.34) | copy-start | bytes 3076
  22.8 8.3 %collective-permute-start.1 = (bf16[2,1024]{1,0:T(2,128)(2,1)S(1)}, bf16[2,1024]{1,0:T(2,128)(2,1)S(1)}, u32[]{:S(2)}, u32[]{:S(2)}) collective-permute-start(bf16[2,1024]{1,0:T(2,128)(2,1)S(1)} %bitcast.29), channel_id=1, source_target_pairs={{0,4},{4,8},{8,12},{12,16},{16,20},{20,24},{24,28},{1,5},{5,9},{9,... | collective-permute-start | bytes 12296 | tf_op jit(solution)/shard_map/ppermute | solution.py:373
  26.2 5.5 %collective-permute-start.2 = (bf16[2,1024]{1,0:T(2,128)(2,1)S(1)}, bf16[2,1024]{1,0:T(2,128)(2,1)S(1)}, u32[]{:S(2)}, u32[]{:S(2)}) collective-permute-start(bf16[2,1024]{1,0:T(2,128)(2,1)S(1)} %bitcast.30), channel_id=1, source_target_pairs={{4,0},{8,4},{12,8},{16,12},{20,16},{24,20},{28,24},{5,1},{9,5},{13... | collective-permute-start | bytes 12296 | tf_op jit(solution)/shard_map/ppermute | solution.py:373
  37.9 7.6 %collective-permute-start.3 = (bf16[2,128,256]{2,1,0:T(8,128)(2,1)S(1)}, bf16[2,128,256]{2,1,0:T(8,128)(2,1)S(1)}, u32[]{:S(2)}, u32[]{:S(2)}) collective-permute-start(bf16[2,128,256]{2,1,0:T(8,128)(2,1)S(1)} %get-tuple-element.51), channel_id=1, source_target_pairs={{0,4},{4,0},{8,12},{12,8},{16,20},{20,16},{24,28},{28,24},{1,5},{5... | collective-permute-start | bytes 393224 | tf_op jit(solution)/shard_map/ppermute | solution.py:450
  45.7 13.5 %collective-permute-start.4 = (bf16[2,128,256]{2,1,0:T(8,128)(2,1)S(1)}, bf16[2,128,256]{2,1,0:T(8,128)(2,1)S(1)}, u32[]{:S(2)}, u32[]{:S(2)}) collective-permute-start(bf16[2,128,256]{2,1,0:T(8,128)(2,1)S(1)} %get-tuple-element.52), channel_id=1, source_target_pairs={{4,12},{8,0},{12,20},{16,8},{20,28},{24,16},{5,13},{9,1},{13,21},{... | collective-permute-start | bytes 393224 | tf_op jit(solution)/shard_map/ppermute | solution.py:459
  47.0 13.3 %collective-permute-start.5 = (bf16[2,128,256]{2,1,0:T(8,128)(2,1)S(1)}, bf16[2,128,256]{2,1,0:T(8,128)(2,1)S(1)}, u32[]{:S(2)}, u32[]{:S(2)}) collective-permute-start(bf16[2,128,256]{2,1,0:T(8,128)(2,1)S(1)} %get-tuple-element.52), channel_id=1, source_target_pairs={{4,20},{12,28},{16,0},{24,8},{5,21},{13,29},{17,1},{25,9},{6,22},{... | collective-permute-start | bytes 393224 | tf_op jit(solution)/shard_map/ppermute | solution.py:459
  48.3 10.9 %collective-permute-start.6 = (bf16[2,64,256]{2,1,0:T(8,128)(2,1)S(1)}, bf16[2,64,256]{2,1,0:T(8,128)(2,1)S(1)}, u32[]{:S(2)}, u32[]{:S(2)}) collective-permute-start(bf16[2,64,256]{2,1,0:T(8,128)(2,1)S(1)} %get-tuple-element.53), channel_id=1, source_target_pairs={{4,28},{24,0},{5,29},{25,1},{6,30},{26,2},{7,31},{27,3}} | collective-permute-start | bytes 196616 | tf_op jit(solution)/shard_map/ppermute | solution.py:459
  60.3 4.7 %copy-start.17 = (f32[256]{0:T(256)S(1)}, f32[256]{0:T(256)}, u32[]{:S(2)}) copy-start(f32[256]{0:T(256)} %param.36) | copy-start | bytes 3076
  60.7 4.3 %collective-permute-start.7 = (bf16[2,64,256]{2,1,0:T(8,128)(2,1)S(1)}, bf16[2,64,256]{2,1,0:T(8,128)(2,1)S(1)}, u32[]{:S(2)}, u32[]{:S(2)}) collective-permute-start(bf16[2,64,256]{2,1,0:T(8,128)(2,1)S(1)} %shard_map.197.entry_ref), channel_id=1, source_target_pairs={{0,4},{4,0},{8,12},{12,8},{16,20},{20,16},{24,28},{28,24},{1,5},{5... | collective-permute-start | bytes 196616 | tf_op jit(solution)/shard_map/ppermute | solution.py:488
  65.0 8.0 %copy-start = (bf16[1024,1024]{1,0:T(8,128)(2,1)S(1)}, bf16[1024,1024]{1,0:T(8,128)(2,1)}, u32[]{:S(2)}) copy-start(bf16[1024,1024]{1,0:T(8,128)(2,1)} %up_ref.1) | copy-start | bytes 6291460
  65.0 8.0 %copy-start.1 = (bf16[1024,1024]{1,0:T(8,128)(2,1)S(1)}, bf16[1024,1024]{1,0:T(8,128)(2,1)}, u32[]{:S(2)}) copy-start(bf16[1024,1024]{1,0:T(8,128)(2,1)} %down_ref.1) | copy-start | bytes 6291460
  65.0 8.0 %copy-start.2 = (bf16[1024,1024]{1,0:T(8,128)(2,1)S(1)}, bf16[1024,1024]{1,0:T(8,128)(2,1)}, u32[]{:S(2)}) copy-start(bf16[1024,1024]{1,0:T(8,128)(2,1)} %all-gather.2.cloned.1.call-done.w_ref) | copy-start | bytes 6291460
  65.0 8.0 %copy-start.14 = (f32[1024]{0:T(1024)S(1)}, f32[1024]{0:T(1024)}, u32[]{:S(2)}) copy-start(f32[1024]{0:T(1024)} %param.25) | copy-start | bytes 12292
  75.2 3.4 %collective-permute-start.10 = (bf16[128,256]{1,0:T(8,128)(2,1)S(1)}, bf16[128,256]{1,0:T(8,128)(2,1)S(1)}, u32[]{:S(2)}, u32[]{:S(2)}) collective-permute-start(bf16[128,256]{1,0:T(8,128)(2,1)S(1)} %get-tuple-element.70), channel_id=1, source_target_pairs={{0,3},{1,0},{2,1},{3,2},{4,7},{5,4},{6,5},{7,6},{8,11},{9,8},{10,9... | collective-permute-start | bytes 196616 | tf_op jit(solution)/shard_map/ppermute | solution.py:508
  76.4 4.0 %collective-permute-start.8 = (bf16[128,256]{1,0:T(8,128)(2,1)S(1)}, bf16[128,256]{1,0:T(8,128)(2,1)S(1)}, u32[]{:S(2)}, u32[]{:S(2)}) collective-permute-start(bf16[128,256]{1,0:T(8,128)(2,1)S(1)} %get-tuple-element.68), channel_id=1, source_target_pairs={{0,1},{1,2},{2,3},{3,0},{4,5},{5,6},{6,7},{7,4},{8,9},{9,10},{10,1... | collective-permute-start | bytes 196616 | tf_op jit(solution)/shard_map/ppermute | solution.py:508
  76.4 4.9 %collective-permute-start.9 = (bf16[128,256]{1,0:T(8,128)(2,1)S(1)}, bf16[128,256]{1,0:T(8,128)(2,1)S(1)}, u32[]{:S(2)}, u32[]{:S(2)}) collective-permute-start(bf16[128,256]{1,0:T(8,128)(2,1)S(1)} %get-tuple-element.69), channel_id=1, source_target_pairs={{0,2},{1,3},{2,0},{3,1},{4,6},{5,7},{6,4},{7,5},{8,10},{9,11},{10,... | collective-permute-start | bytes 196616 | tf_op jit(solution)/shard_map/ppermute | solution.py:508
Sparse Core Ops, SparseCore 0:
  22.9 23.1 all-gather.1

commit v5 on v4

--- a/solution.py
+++ b/solution.py
@@ -184,7 +184,7 @@
     def of_heads(value):
         return masked_heads(value, lane_head, heads)
 
-    def group(s, carry):
+    def prepared(s):
         g = d * strands + s
 
         def lane(index, ref):
@@ -214,32 +214,34 @@
             insert_pulls.append(jnp.where(strict, scores[:, :rows], 0.0))
             key_pulls.append(jnp.where(strict, scores[:, rows:], 0.0).astype(BF16))
         value_pull = mm(jnp.concatenate(key_pulls, axis=1), of_heads(value))
-        inverses = inverse_of(insert_pulls, rows)
-        inverse = jnp.concatenate([item.astype(BF16) for item in inverses], axis=1)
-        local_pull = mm(inverse, of_heads(value_pull)).astype(BF16)
-        start_pull = mm(inverse, of_heads(left_prev * from_start)).astype(BF16)
         value = value.astype(BF16)
         parts_ref[s, 0] = left_here.astype(BF16)
         parts_ref[s, 1] = right_insert.astype(BF16)
         parts_ref[s, 2] = right_key.astype(BF16)
         parts_ref[s, 3] = value
-        parts_ref[s, 4] = local_pull
-        parts_ref[s, 5] = start_pull
         parts_ref[s, 6] = (left_here * from_start).astype(BF16)
         tail_insert = (right_insert * to_end).astype(BF16)
         tail_key = (right_key * to_end).astype(BF16)
-        ends = mm_cols(tail_insert, local_pull) + mm_cols(tail_key, value)
-        maps = mm_cols(tail_insert, start_pull)
-        ends = jnp.where(same, ends, 0.0)
-        maps = jnp.where(same, maps, 0.0)
+        solved_for = jnp.concatenate([of_heads(value_pull), of_heads(left_prev * from_start)], axis=1)
+        end = mm_cols(tail_key, value)
+        return insert_pulls, (solved_for, tail_insert, end, jnp.exp(final))
+
+    prepared_all = [prepared(s) for s in range(strands)]
+    inverses = inverse_of([pull for pulls, _ in prepared_all for pull in pulls], rows)
+    for s, (_, (solved_for, tail_insert, end, kept)) in enumerate(prepared_all):
+        own = inverses[s * heads : (s + 1) * heads]
+        inverse = jnp.concatenate([item.astype(BF16) for item in own], axis=1)
+        solved = mm(inverse, solved_for).astype(BF16)
+        parts_ref[s, 4] = solved[:, :width]
+        parts_ref[s, 5] = solved[:, width:]
+        added = mm_cols(tail_insert, solved)
+        ends = jnp.where(same, end + added[:, :width], 0.0)
+        maps = jnp.where(same, added[:, width:], 0.0)
         end = sum(ends[h * HEAD : (h + 1) * HEAD] for h in range(heads))
         across = sum(maps[h * HEAD : (h + 1) * HEAD] for h in range(heads))
         diagonal = ids_of((HEAD, width), 0) == ids_of((HEAD, width), 1) % HEAD
-        across = across + jnp.where(diagonal, jnp.exp(final), 0.0)
+        across = across + jnp.where(diagonal, kept, 0.0)
         state_ref[s] = jnp.concatenate([end, across], axis=0).astype(BF16)
-        return carry
-
-    lax.fori_loop(0, strands, group, 0)
 
 
 def read_kernel(direction_ref, sent_ref, kept_ref, local_ref, map_ref):

time: 89.1 us -> 85.6 us (0.961)
  Pallas kernels: 21.7 us -> 18.2 us
    pallas_call x1, Pallas kernels: 5.41 us -> 3.62 us  [on_device(): call(functools.partial(chunk_kernel, False), (state_struct, parts_struct)...]
    pallas_call x1, Pallas kernels: 6.16 us -> 4.44 us  [on_device(): call(functools.partial(chunk_kernel, True), (state_struct, parts_struct,...]
  transfers between devices with their start and end apart: 12 -> 12, of which waited for: 7 -> 7; matrix products, arithmetic and copies ran while one was open for 0% -> 0% of each run, Pallas kernels for 20% -> 17%
where the time goes in v5:
time: 85.6 us; the launch traced here: 85.3 us
  starting transfers between devices  19 us (22%)
  Pallas kernels  18.2 us (21%)
  waiting for transfers between devices  17.4 us (20%)
  blocking collectives  13.9 us (16%)
  between operations  13.8 us (16%)
  local copies, waits for them, and re-layouts  2.3 us (3%)
    ppermute x3, waiting for transfers between devices, onward(): lax.ppermute(value, 'seq', [(i, j) for i, j in route if 0 <= j < seq_count])  8.48 us
    all_gather x1, blocking collectives, on_device(): whole = lax.all_gather(local, 'mp', axis=2, tiled=True)  7.3 us
    all_gather x1, blocking collectives, on_device(): joined_whole = lax.all_gather(joined, 'mp', axis=2, tiled=True)  6.64 us
    ppermute x1, starting transfers between devices, on_device(): rc_here = lax.ppermute(hidden_rc, 'seq', mirror)  6 us
    ppermute x2, starting transfers between devices, shifted(): lax.ppermute(value, axis, [(i, i + distance) for i in devices if i + dist...  4.68 us
    pallas_call x1, Pallas kernels, on_device(): call(functools.partial(chunk_kernel, True), (state_struct, parts_struct,...  4.44 us
    ppermute x1, waiting for transfers between devices, on_device(): other = lax.ppermute(entry, 'seq', partner)  4.25 us
    ppermute x3, waiting for transfers between devices, on_device(): merged = merged + lax.ppermute(item, 'mp', pairs).astype(F32)  4.09 us
  transfers between devices with their start and end apart: 12, of which 7 were waited for; matrix products, arithmetic and copies ran while one was open for 0% of the time, Pallas kernels for 17%

profile of v5, /device:TPU:0, one launch (start us, length us, event | category | flops | bytes accessed | tf_op | source)
XLA Modules:
  0.0 85.3 jit_solution(9643912666519127420)
XLA Ops:
  6.5 6.0 %collective-permute-start = (bf16[128,256]{1,0:T(8,128)(2,1)}, bf16[128,256]{1,0:T(8,128)(2,1)S(1)}, u32[]{:S(2)}, u32[]{:S(2)}) collective-permute-start(bf16[128,256]{1,0:T(8,128)(2,1)} %param.22), channel_id=1, source_target_pairs={{0,28},{4,24},{8,20},{12,16},{16,12},{20,8},{24,4},{28,0},{1,29},{... | collective-permute-start | bytes 196616 | tf_op jit(solution)/shard_map/ppermute | solution.py:406
  12.5 0.8 copy-done.8
  13.4 0.7 copy-done.12
  14.1 0.7 copy-done.18
  14.7 0.4 shard_map.190
  15.3 0.1 shard_map.191
  15.4 7.3 %all_gather.9.x_ref = bf16[2,128,1024]{2,1,0:T(8,128)(2,1)S(1)} all-gather(bf16[2,128,256]{2,1,0:T(8,128)(2,1)S(1)} %shard_map.191), channel_id=1, replica_groups=mesh['seq'=8,'mp'=4] {'mp'}, dimensions={2}, use_global_device_ids=true | all-gather | bytes 655360 | tf_op jit(solution)/shard_map/all_gather | solution.py:425
  22.8 3.4 %collective-permute-start.1 = (bf16[2,1024]{1,0:T(2,128)(2,1)S(1)}, bf16[2,1024]{1,0:T(2,128)(2,1)S(1)}, u32[]{:S(2)}, u32[]{:S(2)}) collective-permute-start(bf16[2,1024]{1,0:T(2,128)(2,1)S(1)} %bitcast.29), channel_id=1, source_target_pairs={{0,4},{4,8},{8,12},{12,16},{16,20},{20,24},{24,28},{1,5},{5,9},{9,... | collective-permute-start | bytes 12296 | tf_op jit(solution)/shard_map/ppermute | solution.py:375
  26.2 1.3 %collective-permute-start.2 = (bf16[2,1024]{1,0:T(2,128)(2,1)S(1)}, bf16[2,1024]{1,0:T(2,128)(2,1)S(1)}, u32[]{:S(2)}, u32[]{:S(2)}) collective-permute-start(bf16[2,1024]{1,0:T(2,128)(2,1)S(1)} %bitcast.30), channel_id=1, source_target_pairs={{4,0},{8,4},{12,8},{16,12},{20,16},{24,20},{28,24},{5,1},{9,5},{13... | collective-permute-start | bytes 12296 | tf_op jit(solution)/shard_map/ppermute | solution.py:375
  27.6 3.5 %shard_map.192 = (f32[4,128,256]{2,1,0:T(8,128)S(1)}, f32[4,128,256]{2,1,0:T(8,128)S(1)}, f32[4,128,256]{2,1,0:T(8,128)S(1)}, f32[4,128,256]{2,1,0:T(8,128)S(1)}...) custom-call(bf16[2,128,1024]{2,1,0:T(8,128)(2,1)S(1)} %all_gather.9.x_ref, f32[1,1024]{1,0:T(1,128)S(1)} %bitcast.20, ...), custom_call_target="tpu_custom_call" | custom-call | flops 2000000000 | bytes 2000000 | tf_op jit(solution)/shard_map/pallas_call | solution.py:436
  31.2 0.6 collective-permute-done.2.refs_6_
  31.7 4.4 %shard_map.193 = (bf16[2,128,256]{2,1,0:T(8,128)(2,1)S(1)}, bf16[2,7,128,256]{3,2,1,0:T(8,128)(2,1)S(1)}, f32[5,4,256]{2,1,0:T(4,128)S(1)}) custom-call(s32[1]{0:T(128)} %bitcast.1.direction_ref, f32[4,128,256]{2,1,0:T(8,128)S(1)} %get-tuple-element.43.refs_0_, f32[4,128,256]{2,1,0:T(8,128)S(1)} %get-tuple-element.44.refs_1_, ...), custom_call_target="tpu_custom_call" | custom-call | flops 2000000000 | bytes 2000000 | tf_op jit(solution)/shard_map/pallas_call | solution.py:446
  36.2 2.2 %collective-permute-start.3 = (bf16[2,128,256]{2,1,0:T(8,128)(2,1)S(1)}, bf16[2,128,256]{2,1,0:T(8,128)(2,1)S(1)}, u32[]{:S(2)}, u32[]{:S(2)}) collective-permute-start(bf16[2,128,256]{2,1,0:T(8,128)(2,1)S(1)} %get-tuple-element.51), channel_id=1, source_target_pairs={{0,4},{4,0},{8,12},{12,8},{16,20},{20,16},{24,28},{28,24},{1,5},{5... | collective-permute-start | bytes 393224 | tf_op jit(solution)/shard_map/ppermute | solution.py:452
  38.3 3.6 %shard_map.194 = (bf16[2,128,256]{2,1,0:T(8,128)(2,1)S(1)}, bf16[2,7,128,256]{3,2,1,0:T(8,128)(2,1)S(1)}) custom-call(s32[1]{0:T(128)S(6)} %sub.3.direction_ref, f32[4,128,256]{2,1,0:T(8,128)S(1)} %get-tuple-element.43.refs_0_, f32[4,128,256]{2,1,0:T(8,128)S(1)} %get-tuple-element.44.refs_1_, f32[4,128,256]{2,1,0:T(8,128)S(1)} %get-tuple-element.45.refs_2_, ...), custom_call_target="tpu_custom_call" | custom-call | flops 2000000000 | bytes 2000000 | tf_op jit(solution)/shard_map/pallas_call | solution.py:453
  42.0 0.2 shard_map.195
  42.2 1.3 %collective-permute-start.4 = (bf16[2,128,256]{2,1,0:T(8,128)(2,1)S(1)}, bf16[2,128,256]{2,1,0:T(8,128)(2,1)S(1)}, u32[]{:S(2)}, u32[]{:S(2)}) collective-permute-start(bf16[2,128,256]{2,1,0:T(8,128)(2,1)S(1)} %get-tuple-element.52), channel_id=1, source_target_pairs={{4,12},{8,0},{12,20},{16,8},{20,28},{24,16},{5,13},{9,1},{13,21},{... | collective-permute-start | bytes 393224 | tf_op jit(solution)/shard_map/ppermute | solution.py:461
  43.5 1.3 %collective-permute-start.5 = (bf16[2,128,256]{2,1,0:T(8,128)(2,1)S(1)}, bf16[2,128,256]{2,1,0:T(8,128)(2,1)S(1)}, u32[]{:S(2)}, u32[]{:S(2)}) collective-permute-start(bf16[2,128,256]{2,1,0:T(8,128)(2,1)S(1)} %get-tuple-element.52), channel_id=1, source_target_pairs={{4,20},{12,28},{16,0},{24,8},{5,21},{13,29},{17,1},{25,9},{6,22},{... | collective-permute-start | bytes 393224 | tf_op jit(solution)/shard_map/ppermute | solution.py:461
  44.8 1.5 %collective-permute-start.6 = (bf16[2,64,256]{2,1,0:T(8,128)(2,1)S(1)}, bf16[2,64,256]{2,1,0:T(8,128)(2,1)S(1)}, u32[]{:S(2)}, u32[]{:S(2)}) collective-permute-start(bf16[2,64,256]{2,1,0:T(8,128)(2,1)S(1)} %get-tuple-element.53), channel_id=1, source_target_pairs={{4,28},{24,0},{5,29},{25,1},{6,30},{26,2},{7,31},{27,3}} | collective-permute-start | bytes 196616 | tf_op jit(solution)/shard_map/ppermute | solution.py:461
  46.3 2.1 %shard_map.196 = (f32[4,128,256]{2,1,0:T(8,128)S(1)}, bf16[4,128,256]{2,1,0:T(8,128)(2,1)S(1)}) custom-call(s32[1]{0:T(128)} %bitcast.1.direction_ref, bf16[2,7,128,256]{3,2,1,0:T(8,128)(2,1)S(1)} %get-tuple-element.56.sent_ref, bf16[2,7,128,256]{3,2,1,0:T(8,128)(2,1)S(1)} %get-tuple-element.57.kept_ref), custom_call_target="tpu_custom_call" | custom-call | flops 2000000000 | bytes 2000000 | tf_op jit(solution)/shard_map/pallas_call | solution.py:481
  48.4 7.4 %collective-permute-done.6.refs_2_ = bf16[2,64,256]{2,1,0:T(8,128)(2,1)S(1)} collective-permute-done((bf16[2,64,256]{2,1,0:T(8,128)(2,1)S(1)}, bf16[2,64,256]{2,1,0:T(8,128)(2,1)S(1)}, u32[]{:S(2)}, u32[]{:S(2)}) %collective-permute-start.6) | collective-permute-done | bytes 65568 | tf_op jit(solution)/shard_map/ppermute | solution.py:461
  55.7 1.1 %collective-permute-done.5.refs_1_ = bf16[2,128,256]{2,1,0:T(8,128)(2,1)S(1)} collective-permute-done((bf16[2,128,256]{2,1,0:T(8,128)(2,1)S(1)}, bf16[2,128,256]{2,1,0:T(8,128)(2,1)S(1)}, u32[]{:S(2)}, u32[]{:S(2)}) %collective-permute-start.5) | collective-permute-done | bytes 131104 | tf_op jit(solution)/shard_map/ppermute | solution.py:461
  56.9 0.4 shard_map.197.entry_ref
  57.3 4.3 %collective-permute-done.7.other_ref = bf16[2,64,256]{2,1,0:T(8,128)(2,1)S(1)} collective-permute-done((bf16[2,64,256]{2,1,0:T(8,128)(2,1)S(1)}, bf16[2,64,256]{2,1,0:T(8,128)(2,1)S(1)}, u32[]{:S(2)}, u32[]{:S(2)}) %collective-permute-start.7) | collective-permute-done | bytes 65568 | tf_op jit(solution)/shard_map/ppermute | solution.py:490
  61.6 1.3 %shard_map.198 = bf16[2,128,256]{2,1,0:T(8,128)(2,1)S(1)} custom-call(bf16[2,64,256]{2,1,0:T(8,128)(2,1)S(1)} %shard_map.197.entry_ref, bf16[2,128,256]{2,1,0:T(8,128)(2,1)S(1)} %collective-permute-done.3.from_ref, bf16[2,64,256]{2,1,0:T(8,128)(2,1)S(1)} %collective-permute-done.7.other_ref, f32[4,128,256]{2,1,0:T(8,128)S(1)} %get-tuple-element.64.local_ref, ...), custom_call_target="tpu_custom_call" | custom-call | flops 2000000000 | bytes 2000000 | tf_op jit(solution)/shard_map/pallas_call | solution.py:491
  62.9 6.6 %all_gather.11.joined_ref = bf16[2,128,1024]{2,1,0:T(8,128)(2,1)S(1)} all-gather(bf16[2,128,256]{2,1,0:T(8,128)(2,1)S(1)} %shard_map.198), channel_id=1, replica_groups=mesh['seq'=8,'mp'=4] {'mp'}, dimensions={2}, use_global_device_ids=true | all-gather | bytes 655360 | tf_op jit(solution)/shard_map/all_gather | solution.py:494
  69.6 2.1 %shard_map.199 = (f32[128,256]{1,0:T(8,128)S(1)}, bf16[128,256]{1,0:T(8,128)(2,1)S(1)}, bf16[128,256]{1,0:T(8,128)(2,1)S(1)}, bf16[128,256]{1,0:T(8,128)(2,1)S(1)}) custom-call(s32[1]{0:T(128)} %bitcast.index_ref, bf16[2,128,1024]{2,1,0:T(8,128)(2,1)S(1)} %all_gather.11.joined_ref, bf16[2,128,1024]{2,1,0:T(8,128)(2,1)S(1)} %all_gather.9.x_ref, ...), custom_call_target="tpu_custom_call" | custom-call | flops 2000000000 | bytes 2000000 | tf_op jit(solution)/shard_map/pallas_call | solution.py:497
  71.7 1.2 %collective-permute-start.10 = (bf16[128,256]{1,0:T(8,128)(2,1)S(1)}, bf16[128,256]{1,0:T(8,128)(2,1)S(1)}, u32[]{:S(2)}, u32[]{:S(2)}) collective-permute-start(bf16[128,256]{1,0:T(8,128)(2,1)S(1)} %get-tuple-element.70), channel_id=1, source_target_pairs={{0,3},{1,0},{2,1},{3,2},{4,7},{5,4},{6,5},{7,6},{8,11},{9,8},{10,9... | collective-permute-start | bytes 196616 | tf_op jit(solution)/shard_map/ppermute | solution.py:510
  72.9 0.9 %collective-permute-start.9 = (bf16[128,256]{1,0:T(8,128)(2,1)S(1)}, bf16[128,256]{1,0:T(8,128)(2,1)S(1)}, u32[]{:S(2)}, u32[]{:S(2)}) collective-permute-start(bf16[128,256]{1,0:T(8,128)(2,1)S(1)} %get-tuple-element.69), channel_id=1, source_target_pairs={{0,2},{1,3},{2,0},{3,1},{4,6},{5,7},{6,4},{7,5},{8,10},{9,11},{10,... | collective-permute-start | bytes 196616 | tf_op jit(solution)/shard_map/ppermute | solution.py:510
  73.7 1.4 %collective-permute-done.10 = bf16[128,256]{1,0:T(8,128)(2,1)S(1)} collective-permute-done((bf16[128,256]{1,0:T(8,128)(2,1)S(1)}, bf16[128,256]{1,0:T(8,128)(2,1)S(1)}, u32[]{:S(2)}, u32[]{:S(2)}) %collective-permute-start.10) | collective-permute-done | bytes 65568 | tf_op jit(solution)/shard_map/ppermute | solution.py:510
  75.1 1.8 %collective-permute-done.8 = bf16[128,256]{1,0:T(8,128)(2,1)S(1)} collective-permute-done((bf16[128,256]{1,0:T(8,128)(2,1)S(1)}, bf16[128,256]{1,0:T(8,128)(2,1)S(1)}, u32[]{:S(2)}, u32[]{:S(2)}) %collective-permute-start.8) | collective-permute-done | bytes 65568 | tf_op jit(solution)/shard_map/ppermute | solution.py:510
  76.9 1.0 %collective-permute-done.9 = bf16[128,256]{1,0:T(8,128)(2,1)S(1)} collective-permute-done((bf16[128,256]{1,0:T(8,128)(2,1)S(1)}, bf16[128,256]{1,0:T(8,128)(2,1)S(1)}, u32[]{:S(2)}, u32[]{:S(2)}) %collective-permute-start.9) | collective-permute-done | bytes 65568 | tf_op jit(solution)/shard_map/ppermute | solution.py:510
  77.8 0.7 add_convert_fusion
  (47 shorter events, 0.2 us)
Async XLA Ops:
  6.5 50.3 %all-gather.2.cloned.1.call-start = ((), (), s32[]{:S(2)}) async-start(), calls=%async_computation | async-start | bytes 2621440 | tf_op jit(solution)/shard_map/all_gather | solution.py:429
  6.5 8.6 %collective-permute-start = (bf16[128,256]{1,0:T(8,128)(2,1)}, bf16[128,256]{1,0:T(8,128)(2,1)S(1)}, u32[]{:S(2)}, u32[]{:S(2)}) collective-permute-start(bf16[128,256]{1,0:T(8,128)(2,1)} %param.22), channel_id=1, source_target_pairs={{0,28},{4,24},{8,20},{12,16},{16,12},{20,8},{24,4},{28,0},{1,29},{... | collective-permute-start | bytes 196616 | tf_op jit(solution)/shard_map/ppermute | solution.py:406
  12.5 0.8 copy-start.8
  13.4 0.7 copy-start.12
  14.1 0.7 copy-start.18
  15.2 12.4 %copy-start.3 = (bf16[1024,256]{1,0:T(8,128)(2,1)S(1)}, bf16[1024,256]{1,0:T(8,128)(2,1)}, u32[]{:S(2)}) copy-start(bf16[1024,256]{1,0:T(8,128)(2,1)} %refs_10_.1) | copy-start | bytes 1572868
  15.2 12.4 %copy-start.4 = (bf16[1024,256]{1,0:T(8,128)(2,1)S(1)}, bf16[1024,256]{1,0:T(8,128)(2,1)}, u32[]{:S(2)}) copy-start(bf16[1024,256]{1,0:T(8,128)(2,1)} %refs_11_.1) | copy-start | bytes 1572868
  15.2 12.4 %copy-start.5 = (bf16[1024,256]{1,0:T(8,128)(2,1)S(1)}, bf16[1024,256]{1,0:T(8,128)(2,1)}, u32[]{:S(2)}) copy-start(bf16[1024,256]{1,0:T(8,128)(2,1)} %refs_12_.1) | copy-start | bytes 1572868
  15.2 12.4 %copy-start.6 = (bf16[1024,64]{0,1:T(8,128)(2,1)S(1)}, bf16[1024,64]{0,1:T(8,128)(2,1)}, u32[]{:S(2)}) copy-start(bf16[1024,64]{0,1:T(8,128)(2,1)} %param.30) | copy-start | bytes 393220
  15.2 12.4 %copy-start.7 = (bf16[1024,64]{0,1:T(8,128)(2,1)S(1)}, bf16[1024,64]{0,1:T(8,128)(2,1)}, u32[]{:S(2)}) copy-start(bf16[1024,64]{0,1:T(8,128)(2,1)} %param.33) | copy-start | bytes 393220
  15.2 12.4 %copy-start.9 = (f32[5,1024]{1,0:T(8,128)S(1)}, f32[5,1024]{1,0:T(8,128)}, u32[]{:S(2)}) copy-start(f32[5,1024]{1,0:T(8,128)} %refs_9_.1) | copy-start | bytes 61444
  15.2 12.4 %copy-start.10 = (bf16[64,256]{1,0:T(8,128)(2,1)S(1)}, bf16[64,256]{1,0:T(8,128)(2,1)}, u32[]{:S(2)}) copy-start(bf16[64,256]{1,0:T(8,128)(2,1)} %refs_15_.1) | copy-start | bytes 98308
  15.2 12.4 %copy-start.11 = (bf16[64,256]{1,0:T(8,128)(2,1)S(1)}, bf16[64,256]{1,0:T(8,128)(2,1)}, u32[]{:S(2)}) copy-start(bf16[64,256]{1,0:T(8,128)(2,1)} %refs_16_.1) | copy-start | bytes 98308
  15.3 12.4 %copy-start.13 = (f32[1024]{0:T(1024)S(1)}, f32[1024]{0:T(1024)}, u32[]{:S(2)}) copy-start(f32[1024]{0:T(1024)} %param.24) | copy-start | bytes 12292
  15.3 12.4 %copy-start.15 = (f32[256]{0:T(256)S(1)}, f32[256]{0:T(256)}, u32[]{:S(2)}) copy-start(f32[256]{0:T(256)} %param.31) | copy-start | bytes 3076
  15.3 12.4 %copy-start.16 = (f32[256]{0:T(256)S(1)}, f32[256]{0:T(256)}, u32[]{:S(2)}) copy-start(f32[256]{0:T(256)} %param.34) | copy-start | bytes 3076
  22.8 8.3 %collective-permute-start.1 = (bf16[2,1024]{1,0:T(2,128)(2,1)S(1)}, bf16[2,1024]{1,0:T(2,128)(2,1)S(1)}, u32[]{:S(2)}, u32[]{:S(2)}) collective-permute-start(bf16[2,1024]{1,0:T(2,128)(2,1)S(1)} %bitcast.29), channel_id=1, source_target_pairs={{0,4},{4,8},{8,12},{12,16},{16,20},{20,24},{24,28},{1,5},{5,9},{9,... | collective-permute-start | bytes 12296 | tf_op jit(solution)/shard_map/ppermute | solution.py:375
  26.2 5.5 %collective-permute-start.2 = (bf16[2,1024]{1,0:T(2,128)(2,1)S(1)}, bf16[2,1024]{1,0:T(2,128)(2,1)S(1)}, u32[]{:S(2)}, u32[]{:S(2)}) collective-permute-start(bf16[2,1024]{1,0:T(2,128)(2,1)S(1)} %bitcast.30), channel_id=1, source_target_pairs={{4,0},{8,4},{12,8},{16,12},{20,16},{24,20},{28,24},{5,1},{9,5},{13... | collective-permute-start | bytes 12296 | tf_op jit(solution)/shard_map/ppermute | solution.py:375
  36.2 5.8 %collective-permute-start.3 = (bf16[2,128,256]{2,1,0:T(8,128)(2,1)S(1)}, bf16[2,128,256]{2,1,0:T(8,128)(2,1)S(1)}, u32[]{:S(2)}, u32[]{:S(2)}) collective-permute-start(bf16[2,128,256]{2,1,0:T(8,128)(2,1)S(1)} %get-tuple-element.51), channel_id=1, source_target_pairs={{0,4},{4,0},{8,12},{12,8},{16,20},{20,16},{24,28},{28,24},{1,5},{5... | collective-permute-start | bytes 393224 | tf_op jit(solution)/shard_map/ppermute | solution.py:452
  42.2 13.5 %collective-permute-start.4 = (bf16[2,128,256]{2,1,0:T(8,128)(2,1)S(1)}, bf16[2,128,256]{2,1,0:T(8,128)(2,1)S(1)}, u32[]{:S(2)}, u32[]{:S(2)}) collective-permute-start(bf16[2,128,256]{2,1,0:T(8,128)(2,1)S(1)} %get-tuple-element.52), channel_id=1, source_target_pairs={{4,12},{8,0},{12,20},{16,8},{20,28},{24,16},{5,13},{9,1},{13,21},{... | collective-permute-start | bytes 393224 | tf_op jit(solution)/shard_map/ppermute | solution.py:461
  43.5 13.4 %collective-permute-start.5 = (bf16[2,128,256]{2,1,0:T(8,128)(2,1)S(1)}, bf16[2,128,256]{2,1,0:T(8,128)(2,1)S(1)}, u32[]{:S(2)}, u32[]{:S(2)}) collective-permute-start(bf16[2,128,256]{2,1,0:T(8,128)(2,1)S(1)} %get-tuple-element.52), channel_id=1, source_target_pairs={{4,20},{12,28},{16,0},{24,8},{5,21},{13,29},{17,1},{25,9},{6,22},{... | collective-permute-start | bytes 393224 | tf_op jit(solution)/shard_map/ppermute | solution.py:461
  44.8 10.9 %collective-permute-start.6 = (bf16[2,64,256]{2,1,0:T(8,128)(2,1)S(1)}, bf16[2,64,256]{2,1,0:T(8,128)(2,1)S(1)}, u32[]{:S(2)}, u32[]{:S(2)}) collective-permute-start(bf16[2,64,256]{2,1,0:T(8,128)(2,1)S(1)} %get-tuple-element.53), channel_id=1, source_target_pairs={{4,28},{24,0},{5,29},{25,1},{6,30},{26,2},{7,31},{27,3}} | collective-permute-start | bytes 196616 | tf_op jit(solution)/shard_map/ppermute | solution.py:461
  56.9 4.7 %copy-start.17 = (f32[256]{0:T(256)S(1)}, f32[256]{0:T(256)}, u32[]{:S(2)}) copy-start(f32[256]{0:T(256)} %param.36) | copy-start | bytes 3076
  57.2 4.3 %collective-permute-start.7 = (bf16[2,64,256]{2,1,0:T(8,128)(2,1)S(1)}, bf16[2,64,256]{2,1,0:T(8,128)(2,1)S(1)}, u32[]{:S(2)}, u32[]{:S(2)}) collective-permute-start(bf16[2,64,256]{2,1,0:T(8,128)(2,1)S(1)} %shard_map.197.entry_ref), channel_id=1, source_target_pairs={{0,4},{4,0},{8,12},{12,8},{16,20},{20,16},{24,28},{28,24},{1,5},{5... | collective-permute-start | bytes 196616 | tf_op jit(solution)/shard_map/ppermute | solution.py:490
  61.6 8.0 %copy-start = (bf16[1024,1024]{1,0:T(8,128)(2,1)S(1)}, bf16[1024,1024]{1,0:T(8,128)(2,1)}, u32[]{:S(2)}) copy-start(bf16[1024,1024]{1,0:T(8,128)(2,1)} %up_ref.1) | copy-start | bytes 6291460
  61.6 8.0 %copy-start.1 = (bf16[1024,1024]{1,0:T(8,128)(2,1)S(1)}, bf16[1024,1024]{1,0:T(8,128)(2,1)}, u32[]{:S(2)}) copy-start(bf16[1024,1024]{1,0:T(8,128)(2,1)} %down_ref.1) | copy-start | bytes 6291460
  61.6 8.0 %copy-start.2 = (bf16[1024,1024]{1,0:T(8,128)(2,1)S(1)}, bf16[1024,1024]{1,0:T(8,128)(2,1)}, u32[]{:S(2)}) copy-start(bf16[1024,1024]{1,0:T(8,128)(2,1)} %all-gather.2.cloned.1.call-done.w_ref) | copy-start | bytes 6291460
  61.6 8.0 %copy-start.14 = (f32[1024]{0:T(1024)S(1)}, f32[1024]{0:T(1024)}, u32[]{:S(2)}) copy-start(f32[1024]{0:T(1024)} %param.25) | copy-start | bytes 12292
  71.7 3.4 %collective-permute-start.10 = (bf16[128,256]{1,0:T(8,128)(2,1)S(1)}, bf16[128,256]{1,0:T(8,128)(2,1)S(1)}, u32[]{:S(2)}, u32[]{:S(2)}) collective-permute-start(bf16[128,256]{1,0:T(8,128)(2,1)S(1)} %get-tuple-element.70), channel_id=1, source_target_pairs={{0,3},{1,0},{2,1},{3,2},{4,7},{5,4},{6,5},{7,6},{8,11},{9,8},{10,9... | collective-permute-start | bytes 196616 | tf_op jit(solution)/shard_map/ppermute | solution.py:510
  72.9 4.0 %collective-permute-start.8 = (bf16[128,256]{1,0:T(8,128)(2,1)S(1)}, bf16[128,256]{1,0:T(8,128)(2,1)S(1)}, u32[]{:S(2)}, u32[]{:S(2)}) collective-permute-start(bf16[128,256]{1,0:T(8,128)(2,1)S(1)} %get-tuple-element.68), channel_id=1, source_target_pairs={{0,1},{1,2},{2,3},{3,0},{4,5},{5,6},{6,7},{7,4},{8,9},{9,10},{10,1... | collective-permute-start | bytes 196616 | tf_op jit(solution)/shard_map/ppermute | solution.py:510
  72.9 4.9 %collective-permute-start.9 = (bf16[128,256]{1,0:T(8,128)(2,1)S(1)}, bf16[128,256]{1,0:T(8,128)(2,1)S(1)}, u32[]{:S(2)}, u32[]{:S(2)}) collective-permute-start(bf16[128,256]{1,0:T(8,128)(2,1)S(1)} %get-tuple-element.69), channel_id=1, source_target_pairs={{0,2},{1,3},{2,0},{3,1},{4,6},{5,7},{6,4},{7,5},{8,10},{9,11},{10,... | collective-permute-start | bytes 196616 | tf_op jit(solution)/shard_map/ppermute | solution.py:510
Sparse Core Ops, SparseCore 0:
  22.9 23.1 all-gather.1

commit v6 on v5

--- a/solution.py
+++ b/solution.py
@@ -12,7 +12,6 @@
 NORM_EPS = 1e-05
 GROUP_EPS = 0.00064
 UNIT_EPS = 1e-06
-RADIX = 4
 F32 = jnp.float32
 BF16 = jnp.bfloat16
 MIB = 1024 * 1024
@@ -156,7 +155,7 @@
 def chunk_kernel(first, direction_ref, *refs):
     lanes, refs = refs[:5], refs[5:]
     if first:
-        before_ref, after_ref, edge_ref, gain_ref, mixing_ref, *params, state_ref, parts_ref, edges_ref = refs
+        partner_ref, beyond_ref, edge_ref, gain_ref, mixing_ref, *params, state_ref, parts_ref, edges_ref = refs
     else:
         edges_ref, state_ref, parts_ref = refs
     strands, _, rows, width = parts_ref.shape
@@ -164,7 +163,9 @@
     d = direction_ref[0]
     if first:
         center = edge_ref[...]
-        halo = jnp.concatenate([before_ref[...], after_ref[...]], axis=0).astype(F32)
+        near, far = partner_ref[...].astype(F32), beyond_ref[...].astype(F32)
+        odd = d == 1
+        halo = jnp.concatenate([jnp.where(odd, near, far), jnp.where(odd, far, near)], axis=0)
         change = layer_norm(halo, gain_ref[...]) - center
 
         def mix(index):
@@ -278,13 +279,6 @@
     return jnp.concatenate([state, mm(across, spread(earlier[HEAD:].astype(BF16), same_head))], axis=0)
 
 
-def window_of(received, same_head, state_only):
-    total = received[-1].astype(F32)
-    for item in reversed(received[:-1]):
-        total = composed(item, total, same_head, state_only)
-    return total
-
-
 def pair_kernel(keep_ref, from_ref, pair_ref, state_ref):
     same_head = block_ones(keep_ref.shape[2])
     for s in range(keep_ref.shape[0]):
@@ -293,29 +287,32 @@
         state_ref[s] = pair[:HEAD]
 
 
-def advance_kernel(has_window, *refs):
-    *ins, window_ref, current_ref, state_ref = refs
-    same_head = block_ones(ins[0].shape[2])
-    for s in range(ins[0].shape[0]):
-        parts = [ref[s] for ref in ins]
-        window = window_of(parts[1 + int(has_window) :], same_head, False)
-        current = composed(parts[0], window, same_head).astype(BF16)
-        current_ref[s] = current
-        state_ref[s] = current[:HEAD]
-        if has_window:
-            window = composed(parts[1], window, same_head)
-        window_ref[s] = window
-
-
-def entry_kernel(has_window, *refs):
-    *ins, entry_ref = refs
+def advance_kernel(has_prefix, later_ref, total_ref, from_ref, *refs):
+    *prefix_ref, wide_ref, next_ref, state_ref = refs
+    same_head = block_ones(total_ref.shape[2])
+    later = later_ref[0] == 1
+    shape = total_ref.shape[1:]
+    within = (ids_of(shape, 0) - HEAD) == ids_of(shape, 1) % HEAD
+    for s in range(total_ref.shape[0]):
+        own, other = total_ref[s], from_ref[s]
+        total = composed(jnp.where(later, own, other), jnp.where(later, other, own), same_head).astype(BF16)
+        next_ref[s] = total
+        state_ref[s] = total[:HEAD]
+        ahead = jnp.where(later, other.astype(F32), within.astype(F32))
+        if has_prefix:
+            ahead = composed(prefix_ref[0][s], ahead, same_head)
+        wide_ref[s] = ahead
+
+
+def entry_kernel(has_prefix, later_ref, from_ref, *refs):
+    *prefix_ref, entry_ref = refs
     same_head = block_ones(entry_ref.shape[2])
     for s in range(entry_ref.shape[0]):
-        parts = [ref[s] for ref in ins]
-        entry = window_of(parts[int(has_window) :], same_head, True)[:HEAD]
-        if has_window:
-            entry = composed(parts[0], entry, same_head, True)
-        entry_ref[s] = entry.astype(BF16)
+        other = from_ref[s]
+        ahead = jnp.where(later_ref[0] == 1, other, jnp.zeros_like(other))
+        if has_prefix:
+            ahead = composed(prefix_ref[0][s], ahead, same_head, True)
+        entry_ref[s] = ahead.astype(BF16)
 
 
 def finish_kernel(entry_ref, from_ref, other_ref, local_ref, map_ref, gain_ref, out_ref):
@@ -335,13 +332,18 @@
         out_ref[s] = (joined * gain).astype(BF16)
 
 
-def mix_kernel(index_ref, joined_ref, x_ref, w_ref, up_ref, down_ref, gain_ref, own_ref, *rest):
-    *sent_refs, partial, total = rest
+def mix_kernel(blocks, index_ref, joined_ref, x_ref, *refs):
+    w_refs, (up_ref, down_ref, gain_ref, own_ref) = refs[:blocks], refs[blocks : blocks + 4]
+    *sent_refs, partial, total = refs[blocks + 4 :]
     strands, rows, _ = x_ref.shape
     width = own_ref.shape[1]
     gain = gain_ref[...]
-    joined = jnp.concatenate([joined_ref[s] for s in range(strands)], axis=0)
-    attention = mm(joined, w_ref[...])
+    me = index_ref[0]
+    attention = 0.0
+    for step, w_ref in enumerate(w_refs):
+        start = pl.multiple_of((me ^ step) * width, width)
+        joined = jnp.concatenate([joined_ref[s, :, pl.ds(start, width)] for s in range(strands)], axis=0)
+        attention = attention + mm(joined, w_ref[...])
     residuals = [x_ref[s].astype(F32) + attention[s * rows : (s + 1) * rows] for s in range(strands)]
     inner = jnp.concatenate([layer_norm(item, gain).astype(BF16) for item in residuals], axis=0)
     active = jnp.square(jnp.maximum(mm(inner, up_ref[...]), 0.0)).astype(BF16).astype(F32)
@@ -352,11 +354,9 @@
     def part(ref, which):
         return ref[:, pl.ds(pl.multiple_of(which * width, width), width)]
 
-    me = index_ref[0]
     own_ref[...] = part(total, me) + part(partial, me)
-    size = len(sent_refs) + 1
     for step, ref in enumerate(sent_refs):
-        ref[...] = part(partial, lax.rem(me + step + 1, size)).astype(BF16)
+        ref[...] = part(partial, me ^ (step + 1)).astype(BF16)
 
 
 def call(kernel, out_shape, scratch=(), mib=12, us=2, **kwargs):
@@ -370,9 +370,8 @@
     )
 
 
-def shifted(value, axis, distance):
-    devices = range(lax.axis_size(axis))
-    return lax.ppermute(value, axis, [(i, i + distance) for i in devices if i + distance in devices])
+def swapped(value, axis, mask):
+    return lax.ppermute(value, axis, [(i, i ^ mask) for i in range(lax.axis_size(axis))])
 
 
 def on_device(
@@ -423,10 +422,17 @@
     rc_here, strand, other = lax.optimization_barrier((rc_here, strand, other))
     local = call(strands_kernel, struct((strands, rows, width), BF16), us=10)(rc_here, strand, other)
     whole = lax.all_gather(local, "mp", axis=2, tiled=True)
-    before = shifted(whole[:, rows - 1], "seq", 1)
-    after = shifted(whole[:, 0], "seq", -1)
-    w_output, _ = lax.optimization_barrier((w_output, whole))
-    w_output_whole = lax.all_gather(w_output, "mp", axis=0, tiled=True)
+    place = lax.axis_index("seq").astype(jnp.int32)
+    parity = place % 2
+    first, last = whole[:, 0], whole[:, rows - 1]
+    near = lax.ppermute(jnp.where(parity == 1, first, last), "seq", [(i, i ^ 1) for i in range(seq_count)])
+    bridges = [(i, i + 1) for i in range(1, seq_count - 1, 2)]
+    bridges += [(j, i) for i, j in bridges]
+    far = lax.ppermute(jnp.where(parity == 1, last, first), "seq", bridges)
+    parity = parity.reshape(1)
+    w_output_held, _ = lax.optimization_barrier((w_output, whole))
+    w_across = swapped(w_output_held, "mp", 2)
+    w_beside = swapped(w_output_held, "mp", 1)
 
     groups = 2 * strands
     f32_lanes, bf16_lanes = struct((groups, rows, width), F32), struct((strands, rows, width), BF16)
@@ -442,72 +448,71 @@
         ],
     )(whole, *params)
 
-    parity = (lax.axis_index("seq") % 2).astype(jnp.int32).reshape(1)
     sent, sent_parts, edges = call(
         functools.partial(chunk_kernel, True),
         (state_struct, parts_struct, struct((5, groups, width), F32)),
         in_specs=[SMEM_SPEC] + [VMEM_SPEC] * (8 + len(params)),
-    )(parity, *lanes, before, after, edge, *params)
-    partner = [(i, i ^ 1) for i in range(seq_count)]
-    from_partner = lax.ppermute(sent, "seq", partner)
+    )(parity, *lanes, near, far, edge, *params)
+    from_partner = swapped(sent, "seq", 1)
     kept, kept_parts = call(
         functools.partial(chunk_kernel, False),
         (state_struct, parts_struct),
         in_specs=[SMEM_SPEC] + [VMEM_SPEC] * 6,
     )(1 - parity, *lanes, edges)
 
-    def onward(value, pairs):
-        route = [(i, i + 2 * pairs if i % 2 else i - 2 * pairs) for i in range(seq_count)]
-        return lax.ppermute(value, "seq", [(i, j) for i, j in route if 0 <= j < seq_count])
-
-    current, state = call(pair_kernel, (state_struct, entry_struct))(kept, from_partner)
-    window = []
-    distance, count = 1, seq_count // 2
-    while True:
-        steps = [step for step in range(1, RADIX) if step * distance < count]
-        last = distance * RADIX >= count
-        received = [
-            onward(state if last and step == steps[-1] else current, step * distance) for step in steps
-        ]
-        if last:
+    total, state = call(pair_kernel, (state_struct, entry_struct))(kept, from_partner)
+    paired = total
+    w_across, _ = lax.optimization_barrier((w_across, total))
+    w_opposite = swapped(w_across, "mp", 1)
+    prefix = []
+    bits = range(1, seq_count.bit_length() - 1)
+    for bit in bits:
+        later = ((place >> bit) % 2 == place % 2).astype(jnp.int32).reshape(1)
+        if bit == bits[-1]:
+            received = swapped(state, "seq", 1 << bit)
             break
-        wide, current, state = call(
-            functools.partial(advance_kernel, bool(window)),
+        arriving = swapped(total, "seq", 1 << bit)
+        wide, total, state = call(
+            functools.partial(advance_kernel, bool(prefix)),
             (struct(state_struct.shape, F32), state_struct, entry_struct),
-        )(current, *window, *received)
-        window = [wide]
-        distance *= RADIX
-    sent_parts, kept_parts, _ = lax.optimization_barrier((sent_parts, kept_parts, current))
+            in_specs=[SMEM_SPEC] + [VMEM_SPEC] * (2 + len(prefix)),
+        )(later, total, arriving, *prefix)
+        prefix = [wide]
+    sent_parts, kept_parts, _ = lax.optimization_barrier((sent_parts, kept_parts, paired))
     local_out, start_map = call(
         read_kernel,
         (f32_lanes, struct(f32_lanes.shape, BF16)),
         in_specs=[SMEM_SPEC] + [VMEM_SPEC] * 2,
     )(parity, sent_parts, kept_parts)
-    received, local_out, start_map, w_output_whole = lax.optimization_barrier(
-        (received, local_out, start_map, w_output_whole)
+    received, local_out, start_map, w_opposite = lax.optimization_barrier(
+        (received, local_out, start_map, w_opposite)
     )
-    entry = call(functools.partial(entry_kernel, bool(window)), entry_struct)(*window, *received)
-    other = lax.ppermute(entry, "seq", partner)
+    entry = call(
+        functools.partial(entry_kernel, bool(prefix)),
+        entry_struct,
+        in_specs=[SMEM_SPEC] + [VMEM_SPEC] * (1 + len(prefix)),
+    )(later, received, *prefix)
+    other = swapped(entry, "seq", 1)
     joined = call(finish_kernel, bf16_lanes)(
         entry, from_partner, other, local_out, start_map, group_gain.reshape(1, width)
     )
     joined_whole = lax.all_gather(joined, "mp", axis=2, tiled=True)
 
+    w_blocks = (w_output, w_beside, w_across, w_opposite)
     position = lax.axis_index("mp").astype(jnp.int32).reshape(1)
     own, *sent = call(
-        mix_kernel,
+        functools.partial(mix_kernel, mp_count),
         (struct((rows, width), F32),) + (struct((rows, width), BF16),) * (mp_count - 1),
         scratch=[
             pltpu.VMEM((rows, full), F32),
             pltpu.VMEM((rows, full), F32),
         ],
         mib=24,
-        in_specs=[SMEM_SPEC] + [VMEM_SPEC] * 6,
-    )(position, joined_whole, whole, w_output_whole, ffn_key, ffn_value, ln2_gain.reshape(1, full))
+        in_specs=[SMEM_SPEC] + [VMEM_SPEC] * (5 + mp_count),
+    )(position, joined_whole, whole, *w_blocks, ffn_key, ffn_value, ln2_gain.reshape(1, full))
     merged = own
     for step, item in enumerate(sent):
-        pairs = [(i, (i + step + 1) % mp_count) for i in range(mp_count)]
-        merged = merged + lax.ppermute(item, "mp", pairs).astype(F32)
+        merged = merged + swapped(item, "mp", step + 1).astype(F32)
     return merged.astype(BF16)
 
 

time: 85.6 us -> 71.4 us (0.83)
  between operations: 13.8 us -> 0.35 us
  waiting for transfers between devices: 17.4 us -> 11.9 us
  local copies, waits for them, and re-layouts: 2.3 us -> 3.96 us
  starting transfers between devices: 19 us -> 20.5 us
  Pallas kernels: 18.2 us -> 19.6 us
    ppermute x10 -> x12, waiting for transfers between devices: 17.4 us -> 11.9 us  [the longest x10 11.9 us: swapped(): lax.ppermute(value, axis, [(i, i ^ mask) for i in range(lax.axis_size(axi...]
    unnamed x40 -> x52, local copies, waits for them, and re-layouts: 2.28 us -> 3.96 us
    ppermute x10 -> x12, starting transfers between devices: 13 us -> 14.4 us  [the longest x10 12.3 us: swapped(): lax.ppermute(value, axis, [(i, i ^ mask) for i in range(lax.axis_size(axi...]
    pallas_call x2 -> x3, Pallas kernels: 2.47 us -> 3.09 us  [the longest x1 2.04 us: on_device(): call(functools.partial(mix_kernel, mp_count), (struct((rows, width), F32)...]
  transfers between devices with their start and end apart: 12 -> 13, of which waited for: 7 -> 5; matrix products, arithmetic and copies ran while one was open for 0% -> 0% of each run, Pallas kernels for 17% -> 25%
where the time goes in v6:
time: 71.4 us; the launch traced here: 71.1 us
  starting transfers between devices  20.5 us (29%)
  Pallas kernels  19.6 us (27%)
  blocking collectives  14.2 us (20%)
  waiting for transfers between devices  11.9 us (17%)
  local copies, waits for them, and re-layouts  3.96 us (6%)
    ppermute x10, starting transfers between devices, swapped(): lax.ppermute(value, axis, [(i, i ^ mask) for i in range(lax.axis_size(axi...  12.3 us
    ppermute x10, waiting for transfers between devices, swapped(): lax.ppermute(value, axis, [(i, i ^ mask) for i in range(lax.axis_size(axi...  11.9 us
    all_gather x1, blocking collectives, on_device(): whole = lax.all_gather(local, 'mp', axis=2, tiled=True)  7.3 us
    all_gather x1, blocking collectives, on_device(): joined_whole = lax.all_gather(joined, 'mp', axis=2, tiled=True)  6.88 us
    ppermute x1, starting transfers between devices, on_device(): rc_here = lax.ppermute(hidden_rc, 'seq', mirror)  6 us
    pallas_call x1, Pallas kernels, on_device(): call(functools.partial(chunk_kernel, True), (state_struct, parts_struct,...  4.47 us
    unnamed x52, local copies, waits for them, and re-layouts  3.96 us
    pallas_call x1, Pallas kernels, on_device(): call(functools.partial(chunk_kernel, False), (state_struct, parts_struct)...  3.63 us
  transfers between devices with their start and end apart: 13, of which 5 were waited for; matrix products, arithmetic and copies ran while one was open for 0% of the time, Pallas kernels for 25%

profile of v6, /device:TPU:0, one launch (start us, length us, event | category | flops | bytes accessed | tf_op | source)
XLA Modules:
  0.0 71.1 jit_solution(3862738073199404185)
XLA Ops:
  0.0 6.0 %collective-permute-start = (bf16[128,256]{1,0:T(8,128)(2,1)}, bf16[128,256]{1,0:T(8,128)(2,1)S(1)}, u32[]{:S(2)}, u32[]{:S(2)}) collective-permute-start(bf16[128,256]{1,0:T(8,128)(2,1)} %param.22), channel_id=1, source_target_pairs={{0,28},{4,24},{8,20},{12,16},{16,12},{20,8},{24,4},{28,0},{1,29},{... | collective-permute-start | bytes 196616 | tf_op jit(solution)/shard_map/ppermute | solution.py:405
  6.0 0.8 %copy-done.8 = bf16[128,256]{1,0:T(8,128)(2,1)S(1)} copy-done((bf16[128,256]{1,0:T(8,128)(2,1)S(1)}, bf16[128,256]{1,0:T(8,128)(2,1)}, u32[]{:S(2)}) %copy-start.8) | copy-done | bytes 65560
  6.8 0.7 copy-done.12
  7.5 0.7 copy-done.18
  8.9 7.3 %all_gather.6.x_ref = bf16[2,128,1024]{2,1,0:T(8,128)(2,1)S(1)} all-gather(bf16[2,128,256]{2,1,0:T(8,128)(2,1)S(1)} %shard_map.191), channel_id=1, replica_groups=mesh['seq'=8,'mp'=4] {'mp'}, dimensions={2}, use_global_device_ids=true | all-gather | bytes 655360 | tf_op jit(solution)/shard_map/all_gather | solution.py:424
  16.3 1.5 %collective-permute-start.1 = (bf16[2,1024]{1,0:T(2,128)(2,1)S(1)}, bf16[2,1024]{1,0:T(2,128)(2,1)S(1)}, u32[]{:S(2)}, u32[]{:S(2)}) collective-permute-start(bf16[2,1024]{1,0:T(2,128)(2,1)S(1)} %bitcast.31), channel_id=1, source_target_pairs={{0,4},{4,0},{8,12},{12,8},{16,20},{20,16},{24,28},{28,24},{1,5},{5... | collective-permute-start | bytes 12296 | tf_op jit(solution)/shard_map/ppermute | solution.py:428
  17.8 0.6 collective-permute-start.2
  18.5 0.9 %collective-permute-start.6 = (bf16[256,1024]{1,0:T(8,128)(2,1)S(1)}, bf16[256,1024]{1,0:T(8,128)(2,1)S(1)}, u32[]{:S(2)}, u32[]{:S(2)}) collective-permute-start(bf16[256,1024]{1,0:T(8,128)(2,1)S(1)} %copy-done.5), channel_id=1, source_target_pairs={{0,2},{1,3},{2,0},{3,1},{4,6},{5,7},{6,4},{7,5},{8,10},{9,11},{10,... | collective-permute-start | bytes 1572872 | tf_op jit(solution)/shard_map/ppermute | solution.py:374
  19.5 3.6 %shard_map.192 = (f32[4,128,256]{2,1,0:T(8,128)S(1)}, f32[4,128,256]{2,1,0:T(8,128)S(1)}, f32[4,128,256]{2,1,0:T(8,128)S(1)}, f32[4,128,256]{2,1,0:T(8,128)S(1)}...) custom-call(bf16[2,128,1024]{2,1,0:T(8,128)(2,1)S(1)} %all_gather.6.x_ref, f32[1,1024]{1,0:T(1,128)S(1)} %bitcast.22, ...), custom_call_target="tpu_custom_call" | custom-call | flops 2000000000 | bytes 2000000 | tf_op jit(solution)/shard_map/pallas_call | solution.py:442
  23.0 4.5 %shard_map.193 = (bf16[2,128,256]{2,1,0:T(8,128)(2,1)S(1)}, bf16[2,7,128,256]{3,2,1,0:T(8,128)(2,1)S(1)}, f32[5,4,256]{2,1,0:T(4,128)S(1)}) custom-call(s32[1]{0:T(128)} %bitcast.3.direction_ref, f32[4,128,256]{2,1,0:T(8,128)S(1)} %get-tuple-element.43.refs_0_, f32[4,128,256]{2,1,0:T(8,128)S(1)} %get-tuple-element.44.refs_1_, ...), custom_call_target="tpu_custom_call" | custom-call | flops 2000000000 | bytes 2000000 | tf_op jit(solution)/shard_map/pallas_call | solution.py:451
  27.5 3.6 %collective-permute-start.3 = (bf16[2,128,256]{2,1,0:T(8,128)(2,1)S(1)}, bf16[2,128,256]{2,1,0:T(8,128)(2,1)S(1)}, u32[]{:S(2)}, u32[]{:S(2)}) collective-permute-start(bf16[2,128,256]{2,1,0:T(8,128)(2,1)S(1)} %get-tuple-element.51), channel_id=1, source_target_pairs={{0,4},{4,0},{8,12},{12,8},{16,20},{20,16},{24,28},{28,24},{1,5},{5... | collective-permute-start | bytes 393224 | tf_op jit(solution)/shard_map/ppermute | solution.py:374
  31.1 3.6 %shard_map.194 = (bf16[2,128,256]{2,1,0:T(8,128)(2,1)S(1)}, bf16[2,7,128,256]{3,2,1,0:T(8,128)(2,1)S(1)}) custom-call(s32[1]{0:T(128)S(6)} %sub.3.direction_ref, f32[4,128,256]{2,1,0:T(8,128)S(1)} %get-tuple-element.43.refs_0_, f32[4,128,256]{2,1,0:T(8,128)S(1)} %get-tuple-element.44.refs_1_, f32[4,128,256]{2,1,0:T(8,128)S(1)} %get-tuple-element.45.refs_2_, ...), custom_call_target="tpu_custom_call" | custom-call | flops 2000000000 | bytes 2000000 | tf_op jit(solution)/shard_map/pallas_call | solution.py:457
  34.8 0.9 %shard_map.195 = (bf16[2,128,256]{2,1,0:T(8,128)(2,1)S(1)}, bf16[2,64,256]{2,1,0:T(8,128)(2,1)}) custom-call(bf16[2,128,256]{2,1,0:T(8,128)(2,1)S(1)} %get-tuple-element.50.keep_ref, bf16[2,128,256]{2,1,0:T(8,128)(2,1)S(1)} %collective-permute-done.3.from_ref), custom_call_target="tpu_custom_call" | custom-call | flops 2000000000 | bytes 2000000 | tf_op jit(solution)/shard_map/pallas_call | solution.py:463
  35.7 1.0 %collective-permute-start.4 = (bf16[2,128,256]{2,1,0:T(8,128)(2,1)S(1)}, bf16[2,128,256]{2,1,0:T(8,128)(2,1)S(1)}, u32[]{:S(2)}, u32[]{:S(2)}) collective-permute-start(bf16[2,128,256]{2,1,0:T(8,128)(2,1)S(1)} %get-tuple-element.52.total_ref), channel_id=1, source_target_pairs={{0,8},{4,12},{8,0},{12,4},{16,24},{20,28},{24,16},{28,20},{1,9},{5... | collective-permute-start | bytes 393224 | tf_op jit(solution)/shard_map/ppermute | solution.py:374
  36.9 4.7 %collective-permute-done.4.from_ref = bf16[2,128,256]{2,1,0:T(8,128)(2,1)S(1)} collective-permute-done((bf16[2,128,256]{2,1,0:T(8,128)(2,1)S(1)}, bf16[2,128,256]{2,1,0:T(8,128)(2,1)S(1)}, u32[]{:S(2)}, u32[]{:S(2)}) %collective-permute-start.4) | collective-permute-done | bytes 131104 | tf_op jit(solution)/shard_map/ppermute | solution.py:374
  41.6 0.9 %shard_map.196 = (f32[2,128,256]{2,1,0:T(8,128)S(1)}, bf16[2,128,256]{2,1,0:T(8,128)(2,1)}, bf16[2,64,256]{2,1,0:T(8,128)(2,1)S(1)}) custom-call(s32[1]{0:T(128)} %bitcast.2.later_ref, bf16[2,128,256]{2,1,0:T(8,128)(2,1)S(1)} %get-tuple-element.52.total_ref, bf16[2,128,256]{2,1,0:T(8,128)(2,1)S(1)} %collective-permute-done.4.from_ref), custom_call_target="tpu_custom_call" | custom-call | flops 2000000000 | bytes 2000000 | tf_op jit(solution)/shard_map/pallas_call | solution.py:475
  42.5 3.3 %collective-permute-start.5 = (bf16[2,64,256]{2,1,0:T(8,128)(2,1)S(1)}, bf16[2,64,256]{2,1,0:T(8,128)(2,1)S(1)}, u32[]{:S(2)}, u32[]{:S(2)}) collective-permute-start(bf16[2,64,256]{2,1,0:T(8,128)(2,1)S(1)} %get-tuple-element.53), channel_id=1, source_target_pairs={{0,16},{4,20},{8,24},{12,28},{16,0},{20,4},{24,8},{28,12},{1,17},{... | collective-permute-start | bytes 196616 | tf_op jit(solution)/shard_map/ppermute | solution.py:374
  45.8 2.1 %shard_map.197 = (f32[4,128,256]{2,1,0:T(8,128)S(1)}, bf16[4,128,256]{2,1,0:T(8,128)(2,1)S(1)}) custom-call(s32[1]{0:T(128)} %bitcast.3.direction_ref, bf16[2,7,128,256]{3,2,1,0:T(8,128)(2,1)S(1)} %copy-done.20, bf16[2,7,128,256]{3,2,1,0:T(8,128)(2,1)S(1)} %copy-done.22), custom_call_target="tpu_custom_call" | custom-call | flops 2000000000 | bytes 2000000 | tf_op jit(solution)/shard_map/pallas_call | solution.py:482
  47.9 0.7 copy-done.23
  48.7 0.4 collective-permute-done.5.from_ref
  49.3 1.3 %collective-permute-start.8 = (bf16[2,64,256]{2,1,0:T(8,128)(2,1)S(1)}, bf16[2,64,256]{2,1,0:T(8,128)(2,1)S(1)}, u32[]{:S(2)}, u32[]{:S(2)}) collective-permute-start(bf16[2,64,256]{2,1,0:T(8,128)(2,1)S(1)} %shard_map.198.entry_ref), channel_id=1, source_target_pairs={{0,4},{4,0},{8,12},{12,8},{16,20},{20,16},{24,28},{28,24},{1,5},{5... | collective-permute-start | bytes 196616 | tf_op jit(solution)/shard_map/ppermute | solution.py:374
  50.6 3.0 %collective-permute-done.8.other_ref = bf16[2,64,256]{2,1,0:T(8,128)(2,1)S(1)} collective-permute-done((bf16[2,64,256]{2,1,0:T(8,128)(2,1)S(1)}, bf16[2,64,256]{2,1,0:T(8,128)(2,1)S(1)}, u32[]{:S(2)}, u32[]{:S(2)}) %collective-permute-start.8) | collective-permute-done | bytes 65568 | tf_op jit(solution)/shard_map/ppermute | solution.py:374
  53.6 0.9 %copy-done.24 = bf16[4,128,256]{2,1,0:T(8,128)(2,1)S(1)} copy-done((bf16[4,128,256]{2,1,0:T(8,128)(2,1)S(1)}, bf16[4,128,256]{2,1,0:T(8,128)(2,1)}, u32[]{:S(2)}) %copy-start.24) | copy-done | bytes 262168
  54.6 1.3 %shard_map.199 = bf16[2,128,256]{2,1,0:T(8,128)(2,1)S(1)} custom-call(bf16[2,64,256]{2,1,0:T(8,128)(2,1)S(1)} %shard_map.198.entry_ref, bf16[2,128,256]{2,1,0:T(8,128)(2,1)S(1)} %collective-permute-done.3.from_ref, bf16[2,64,256]{2,1,0:T(8,128)(2,1)S(1)} %collective-permute-done.8.other_ref, f32[4,128,256]{2,1,0:T(8,128)S(1)} %get-tuple-element.64.local_ref, ...), custom_call_target="tpu_custom_call" | custom-call | flops 2000000000 | bytes 2000000 | tf_op jit(solution)/shard_map/pallas_call | solution.py:496
  55.9 6.9 %all_gather.7.joined_ref = bf16[2,128,1024]{2,1,0:T(8,128)(2,1)S(1)} all-gather(bf16[2,128,256]{2,1,0:T(8,128)(2,1)S(1)} %shard_map.199), channel_id=1, replica_groups=mesh['seq'=8,'mp'=4] {'mp'}, dimensions={2}, use_global_device_ids=true | all-gather | bytes 655360 | tf_op jit(solution)/shard_map/all_gather | solution.py:499
  62.8 2.0 %shard_map.200 = (f32[128,256]{1,0:T(8,128)S(1)}, bf16[128,256]{1,0:T(8,128)(2,1)S(1)}, bf16[128,256]{1,0:T(8,128)(2,1)S(1)}, bf16[128,256]{1,0:T(8,128)(2,1)S(1)}) custom-call(s32[1]{0:T(128)} %bitcast.index_ref, bf16[2,128,1024]{2,1,0:T(8,128)(2,1)S(1)} %all_gather.7.joined_ref, bf16[2,128,1024]{2,1,0:T(8,128)(2,1)S(1)} %all_gather.6.x_ref, ...), custom_call_target="tpu_custom_call" | custom-call | flops 2000000000 | bytes 2000000 | tf_op jit(solution)/shard_map/pallas_call | solution.py:503
  64.8 0.4 collective-permute-start.10
  65.3 0.8 %collective-permute-start.11 = (bf16[128,256]{1,0:T(8,128)(2,1)S(1)}, bf16[128,256]{1,0:T(8,128)(2,1)S(1)}, u32[]{:S(2)}, u32[]{:S(2)}) collective-permute-start(bf16[128,256]{1,0:T(8,128)(2,1)S(1)} %get-tuple-element.69), channel_id=1, source_target_pairs={{0,2},{1,3},{2,0},{3,1},{4,6},{5,7},{6,4},{7,5},{8,10},{9,11},{10,... | collective-permute-start | bytes 196616 | tf_op jit(solution)/shard_map/ppermute | solution.py:374
  66.1 0.7 collective-permute-start.12
  66.8 3.2 %collective-permute-done.11 = bf16[128,256]{1,0:T(8,128)(2,1)S(1)} collective-permute-done((bf16[128,256]{1,0:T(8,128)(2,1)S(1)}, bf16[128,256]{1,0:T(8,128)(2,1)S(1)}, u32[]{:S(2)}, u32[]{:S(2)}) %collective-permute-start.11) | collective-permute-done | bytes 65568 | tf_op jit(solution)/shard_map/ppermute | solution.py:374
  70.0 0.5 collective-permute-done.12
  70.5 0.7 add_convert_fusion
  (61 shorter events, 1.1 us)
Async XLA Ops:
  0.0 8.6 %collective-permute-start = (bf16[128,256]{1,0:T(8,128)(2,1)}, bf16[128,256]{1,0:T(8,128)(2,1)S(1)}, u32[]{:S(2)}, u32[]{:S(2)}) collective-permute-start(bf16[128,256]{1,0:T(8,128)(2,1)} %param.22), channel_id=1, source_target_pairs={{0,28},{4,24},{8,20},{12,16},{16,12},{20,8},{24,4},{28,0},{1,29},{... | collective-permute-start | bytes 196616 | tf_op jit(solution)/shard_map/ppermute | solution.py:405
  8.6 9.8 %copy-start.5 = (bf16[256,1024]{1,0:T(8,128)(2,1)S(1)}, bf16[256,1024]{1,0:T(8,128)(2,1)}, u32[]{:S(2)}) copy-start(bf16[256,1024]{1,0:T(8,128)(2,1)} %refs_0_.1) | copy-start | bytes 1572868
  8.6 10.7 %copy-start.2 = (bf16[1024,256]{1,0:T(8,128)(2,1)S(1)}, bf16[1024,256]{1,0:T(8,128)(2,1)}, u32[]{:S(2)}) copy-start(bf16[1024,256]{1,0:T(8,128)(2,1)} %refs_10_.1) | copy-start | bytes 1572868
  8.7 10.7 %copy-start.3 = (bf16[1024,256]{1,0:T(8,128)(2,1)S(1)}, bf16[1024,256]{1,0:T(8,128)(2,1)}, u32[]{:S(2)}) copy-start(bf16[1024,256]{1,0:T(8,128)(2,1)} %refs_11_.1) | copy-start | bytes 1572868
  8.7 10.7 %copy-start.4 = (bf16[1024,256]{1,0:T(8,128)(2,1)S(1)}, bf16[1024,256]{1,0:T(8,128)(2,1)}, u32[]{:S(2)}) copy-start(bf16[1024,256]{1,0:T(8,128)(2,1)} %refs_12_.1) | copy-start | bytes 1572868
  8.7 10.7 %copy-start.6 = (bf16[1024,64]{0,1:T(8,128)(2,1)S(1)}, bf16[1024,64]{0,1:T(8,128)(2,1)}, u32[]{:S(2)}) copy-start(bf16[1024,64]{0,1:T(8,128)(2,1)} %param.30) | copy-start | bytes 393220
  8.7 10.7 %copy-start.7 = (bf16[1024,64]{0,1:T(8,128)(2,1)S(1)}, bf16[1024,64]{0,1:T(8,128)(2,1)}, u32[]{:S(2)}) copy-start(bf16[1024,64]{0,1:T(8,128)(2,1)} %param.33) | copy-start | bytes 393220
  8.7 10.7 %copy-start.9 = (f32[5,1024]{1,0:T(8,128)S(1)}, f32[5,1024]{1,0:T(8,128)}, u32[]{:S(2)}) copy-start(f32[5,1024]{1,0:T(8,128)} %refs_9_.1) | copy-start | bytes 61444
  8.7 10.7 %copy-start.10 = (bf16[64,256]{1,0:T(8,128)(2,1)S(1)}, bf16[64,256]{1,0:T(8,128)(2,1)}, u32[]{:S(2)}) copy-start(bf16[64,256]{1,0:T(8,128)(2,1)} %refs_15_.1) | copy-start | bytes 98308
  8.7 10.7 %copy-start.11 = (bf16[64,256]{1,0:T(8,128)(2,1)S(1)}, bf16[64,256]{1,0:T(8,128)(2,1)}, u32[]{:S(2)}) copy-start(bf16[64,256]{1,0:T(8,128)(2,1)} %refs_16_.1) | copy-start | bytes 98308
  8.7 10.7 %copy-start.13 = (f32[1024]{0:T(1024)S(1)}, f32[1024]{0:T(1024)}, u32[]{:S(2)}) copy-start(f32[1024]{0:T(1024)} %param.24) | copy-start | bytes 12292
  8.8 10.7 %copy-start.15 = (f32[256]{0:T(256)S(1)}, f32[256]{0:T(256)}, u32[]{:S(2)}) copy-start(f32[256]{0:T(256)} %param.31) | copy-start | bytes 3076
  8.8 10.7 %copy-start.16 = (f32[256]{0:T(256)S(1)}, f32[256]{0:T(256)}, u32[]{:S(2)}) copy-start(f32[256]{0:T(256)} %param.34) | copy-start | bytes 3076
  16.3 6.7 %collective-permute-start.1 = (bf16[2,1024]{1,0:T(2,128)(2,1)S(1)}, bf16[2,1024]{1,0:T(2,128)(2,1)S(1)}, u32[]{:S(2)}, u32[]{:S(2)}) collective-permute-start(bf16[2,1024]{1,0:T(2,128)(2,1)S(1)} %bitcast.31), channel_id=1, source_target_pairs={{0,4},{4,0},{8,12},{12,8},{16,20},{20,16},{24,28},{28,24},{1,5},{5... | collective-permute-start | bytes 12296 | tf_op jit(solution)/shard_map/ppermute | solution.py:428
  17.8 5.2 %collective-permute-start.2 = (bf16[2,1024]{1,0:T(2,128)(2,1)S(1)}, bf16[2,1024]{1,0:T(2,128)(2,1)S(1)}, u32[]{:S(2)}, u32[]{:S(2)}) collective-permute-start(bf16[2,1024]{1,0:T(2,128)(2,1)S(1)} %bitcast.32), channel_id=1, source_target_pairs={{4,8},{12,16},{20,24},{8,4},{16,12},{24,20},{5,9},{13,17},{21,25},... | collective-permute-start | bytes 12296 | tf_op jit(solution)/shard_map/ppermute | solution.py:431
  18.5 17.2 %collective-permute-start.6 = (bf16[256,1024]{1,0:T(8,128)(2,1)S(1)}, bf16[256,1024]{1,0:T(8,128)(2,1)S(1)}, u32[]{:S(2)}, u32[]{:S(2)}) collective-permute-start(bf16[256,1024]{1,0:T(8,128)(2,1)S(1)} %copy-done.5), channel_id=1, source_target_pairs={{0,2},{1,3},{2,0},{3,1},{4,6},{5,7},{6,4},{7,5},{8,10},{9,11},{10,... | collective-permute-start | bytes 1572872 | tf_op jit(solution)/shard_map/ppermute | solution.py:374
  27.5 7.3 %copy-start.19 = (bf16[2,7,128,256]{3,2,1,0:T(8,128)(2,1)}, bf16[2,7,128,256]{3,2,1,0:T(8,128)(2,1)S(1)}, u32[]{:S(2)}) copy-start(bf16[2,7,128,256]{3,2,1,0:T(8,128)(2,1)S(1)} %get-tuple-element.56.sent_ref) | copy-start | bytes 2752516
  27.5 7.3 %collective-permute-start.3 = (bf16[2,128,256]{2,1,0:T(8,128)(2,1)S(1)}, bf16[2,128,256]{2,1,0:T(8,128)(2,1)S(1)}, u32[]{:S(2)}, u32[]{:S(2)}) collective-permute-start(bf16[2,128,256]{2,1,0:T(8,128)(2,1)S(1)} %get-tuple-element.51), channel_id=1, source_target_pairs={{0,4},{4,0},{8,12},{12,8},{16,20},{20,16},{24,28},{28,24},{1,5},{5... | collective-permute-start | bytes 393224 | tf_op jit(solution)/shard_map/ppermute | solution.py:374
  35.7 13.4 %collective-permute-start.7 = (bf16[256,1024]{1,0:T(8,128)(2,1)S(1)}, bf16[256,1024]{1,0:T(8,128)(2,1)S(1)}, u32[]{:S(2)}, u32[]{:S(2)}) collective-permute-start(bf16[256,1024]{1,0:T(8,128)(2,1)S(1)} %collective-permute-done.6.refs_2_), channel_id=1, source_target_pairs={{0,1},{1,0},{2,3},{3,2},{4,5},{5,4},{6,7},{7,6},{8,9},{9,8},{10,11... | collective-permute-start | bytes 1572872 | tf_op jit(solution)/shard_map/ppermute | solution.py:374
  35.7 5.9 %collective-permute-start.4 = (bf16[2,128,256]{2,1,0:T(8,128)(2,1)S(1)}, bf16[2,128,256]{2,1,0:T(8,128)(2,1)S(1)}, u32[]{:S(2)}, u32[]{:S(2)}) collective-permute-start(bf16[2,128,256]{2,1,0:T(8,128)(2,1)S(1)} %get-tuple-element.52.total_ref), channel_id=1, source_target_pairs={{0,8},{4,12},{8,0},{12,4},{16,24},{20,28},{24,16},{28,20},{1,9},{5... | collective-permute-start | bytes 393224 | tf_op jit(solution)/shard_map/ppermute | solution.py:374
  36.7 26.0 %collective-permute-start.9 = (bf16[256,1024]{1,0:T(8,128)(2,1)S(1)}, bf16[256,1024]{1,0:T(8,128)(2,1)S(1)}, u32[]{:S(2)}, u32[]{:S(2)}) collective-permute-start(bf16[256,1024]{1,0:T(8,128)(2,1)S(1)} %copy-done.5), channel_id=1, source_target_pairs={{0,1},{1,0},{2,3},{3,2},{4,5},{5,4},{6,7},{7,6},{8,9},{9,8},{10,11... | collective-permute-start | bytes 1572872 | tf_op jit(solution)/shard_map/ppermute | solution.py:374
  41.6 4.2 %copy-start.20 = (bf16[2,7,128,256]{3,2,1,0:T(8,128)(2,1)S(1)}, bf16[2,7,128,256]{3,2,1,0:T(8,128)(2,1)}, u32[]{:S(2)}) copy-start(bf16[2,7,128,256]{3,2,1,0:T(8,128)(2,1)} %copy-done.19) | copy-start | bytes 2752516
  41.6 4.2 %copy-start.22 = (bf16[2,7,128,256]{3,2,1,0:T(8,128)(2,1)S(1)}, bf16[2,7,128,256]{3,2,1,0:T(8,128)(2,1)}, u32[]{:S(2)}) copy-start(bf16[2,7,128,256]{3,2,1,0:T(8,128)(2,1)} %copy-done.21) | copy-start | bytes 2752516
  42.5 6.6 %collective-permute-start.5 = (bf16[2,64,256]{2,1,0:T(8,128)(2,1)S(1)}, bf16[2,64,256]{2,1,0:T(8,128)(2,1)S(1)}, u32[]{:S(2)}, u32[]{:S(2)}) collective-permute-start(bf16[2,64,256]{2,1,0:T(8,128)(2,1)S(1)} %get-tuple-element.53), channel_id=1, source_target_pairs={{0,16},{4,20},{8,24},{12,28},{16,0},{20,4},{24,8},{28,12},{1,17},{... | collective-permute-start | bytes 196616 | tf_op jit(solution)/shard_map/ppermute | solution.py:374
  49.1 4.5 %copy-start.17 = (f32[256]{0:T(256)S(1)}, f32[256]{0:T(256)}, u32[]{:S(2)}) copy-start(f32[256]{0:T(256)} %param.36) | copy-start | bytes 3076
  49.3 4.3 %collective-permute-start.8 = (bf16[2,64,256]{2,1,0:T(8,128)(2,1)S(1)}, bf16[2,64,256]{2,1,0:T(8,128)(2,1)S(1)}, u32[]{:S(2)}, u32[]{:S(2)}) collective-permute-start(bf16[2,64,256]{2,1,0:T(8,128)(2,1)S(1)} %shard_map.198.entry_ref), channel_id=1, source_target_pairs={{0,4},{4,0},{8,12},{12,8},{16,20},{20,16},{24,28},{28,24},{1,5},{5... | collective-permute-start | bytes 196616 | tf_op jit(solution)/shard_map/ppermute | solution.py:374
  54.6 8.2 %copy-start = (bf16[1024,1024]{1,0:T(8,128)(2,1)S(1)}, bf16[1024,1024]{1,0:T(8,128)(2,1)}, u32[]{:S(2)}) copy-start(bf16[1024,1024]{1,0:T(8,128)(2,1)} %refs_4_.3) | copy-start | bytes 6291460
  54.6 8.2 %copy-start.1 = (bf16[1024,1024]{1,0:T(8,128)(2,1)S(1)}, bf16[1024,1024]{1,0:T(8,128)(2,1)}, u32[]{:S(2)}) copy-start(bf16[1024,1024]{1,0:T(8,128)(2,1)} %refs_5_.1) | copy-start | bytes 6291460
  54.6 8.2 %copy-start.14 = (f32[1024]{0:T(1024)S(1)}, f32[1024]{0:T(1024)}, u32[]{:S(2)}) copy-start(f32[1024]{0:T(1024)} %param.25) | copy-start | bytes 12292
  64.8 1.9 %collective-permute-start.10 = (bf16[128,256]{1,0:T(8,128)(2,1)S(1)}, bf16[128,256]{1,0:T(8,128)(2,1)S(1)}, u32[]{:S(2)}, u32[]{:S(2)}) collective-permute-start(bf16[128,256]{1,0:T(8,128)(2,1)S(1)} %get-tuple-element.68), channel_id=1, source_target_pairs={{0,1},{1,0},{2,3},{3,2},{4,5},{5,4},{6,7},{7,6},{8,9},{9,8},{10,11... | collective-permute-start | bytes 196616 | tf_op jit(solution)/shard_map/ppermute | solution.py:374
  65.3 4.7 %collective-permute-start.11 = (bf16[128,256]{1,0:T(8,128)(2,1)S(1)}, bf16[128,256]{1,0:T(8,128)(2,1)S(1)}, u32[]{:S(2)}, u32[]{:S(2)}) collective-permute-start(bf16[128,256]{1,0:T(8,128)(2,1)S(1)} %get-tuple-element.69), channel_id=1, source_target_pairs={{0,2},{1,3},{2,0},{3,1},{4,6},{5,7},{6,4},{7,5},{8,10},{9,11},{10,... | collective-permute-start | bytes 196616 | tf_op jit(solution)/shard_map/ppermute | solution.py:374
  66.1 4.4 %collective-permute-start.12 = (bf16[128,256]{1,0:T(8,128)(2,1)S(1)}, bf16[128,256]{1,0:T(8,128)(2,1)S(1)}, u32[]{:S(2)}, u32[]{:S(2)}) collective-permute-start(bf16[128,256]{1,0:T(8,128)(2,1)S(1)} %get-tuple-element.70), channel_id=1, source_target_pairs={{0,3},{1,2},{2,1},{3,0},{4,7},{5,6},{6,5},{7,4},{8,11},{9,10},{10,... | collective-permute-start | bytes 196616 | tf_op jit(solution)/shard_map/ppermute | solution.py:374
  (6 other events, 4.8 us)

commit v7 on v6

--- a/solution.py
+++ b/solution.py
@@ -132,16 +132,20 @@
         edge_ref[s : s + 1, :] = values[:1]
         edge_ref[strands + s : strands + s + 1, :] = values[rows - 1 :]
 
+    step = 16
+    for s in range(strands):
+        for start in range(0, rows, step):
+            center = normed[s, pad + start : pad + start + step, :]
+            for d in range(2):
+                shift = pad + start - 1 + 2 * d
+                change = normed[s, shift : shift + step, :] - center
+                place = (d * strands + s) * rows + start
+                for index in range(mixed.shape[0]):
+                    weight = mixing_ref[index : index + 1, :]
+                    mixed[index, place : place + step, :] = (center + change * weight).astype(BF16)
+
     def mix(index):
-        weight = mixing_ref[index : index + 1, :]
-        for s in range(strands):
-            center = normed[s, pad : pad + rows, :]
-            for d in range(2):
-                shift = pad - 1 + 2 * d
-                neighbour = normed[s, shift : shift + rows, :]
-                start = (d * strands + s) * rows
-                mixed[start : start + rows, :] = (center + (neighbour - center) * weight).astype(BF16)
-        return mixed[...]
+        return mixed[index]
 
     shape = (2 * strands, rows, width)
     for out_ref, result in zip(outs, project_all(mix, params)):
@@ -279,25 +283,23 @@
     return jnp.concatenate([state, mm(across, spread(earlier[HEAD:].astype(BF16), same_head))], axis=0)
 
 
-def pair_kernel(keep_ref, from_ref, pair_ref, state_ref):
+def pair_kernel(keep_ref, from_ref, pair_ref):
     same_head = block_ones(keep_ref.shape[2])
     for s in range(keep_ref.shape[0]):
-        pair = composed(keep_ref[s], from_ref[s], same_head).astype(BF16)
-        pair_ref[s] = pair
-        state_ref[s] = pair[:HEAD]
+        pair_ref[s] = composed(keep_ref[s], from_ref[s], same_head).astype(BF16)
 
 
 def advance_kernel(has_prefix, later_ref, total_ref, from_ref, *refs):
-    *prefix_ref, wide_ref, next_ref, state_ref = refs
+    *prefix_ref, wide_ref, next_ref = refs
+    state_only = next_ref.shape[1] == HEAD
     same_head = block_ones(total_ref.shape[2])
     later = later_ref[0] == 1
     shape = total_ref.shape[1:]
     within = (ids_of(shape, 0) - HEAD) == ids_of(shape, 1) % HEAD
     for s in range(total_ref.shape[0]):
         own, other = total_ref[s], from_ref[s]
-        total = composed(jnp.where(later, own, other), jnp.where(later, other, own), same_head).astype(BF16)
-        next_ref[s] = total
-        state_ref[s] = total[:HEAD]
+        total = composed(jnp.where(later, own, other), jnp.where(later, other, own), same_head, state_only)
+        next_ref[s] = total.astype(BF16)
         ahead = jnp.where(later, other.astype(F32), within.astype(F32))
         if has_prefix:
             ahead = composed(prefix_ref[0][s], ahead, same_head)
@@ -359,7 +361,7 @@
         ref[...] = part(partial, me ^ (step + 1)).astype(BF16)
 
 
-def call(kernel, out_shape, scratch=(), mib=12, us=2, **kwargs):
+def call(kernel, out_shape, scratch=(), mib=12, us=10, **kwargs):
     return pl.pallas_call(
         kernel,
         out_shape=out_shape,
@@ -417,10 +419,10 @@
         iclr_base.reshape(1, width),
     )
     strand, other = call(
-        embed_kernel, (struct((rows, width), BF16), struct((rows, width), F32)), us=10
+        embed_kernel, (struct((rows, width), BF16), struct((rows, width), F32)), us=10, mib=4
     )(ids.reshape(1, rows), hidden_fwd, embed)
     rc_here, strand, other = lax.optimization_barrier((rc_here, strand, other))
-    local = call(strands_kernel, struct((strands, rows, width), BF16), us=10)(rc_here, strand, other)
+    local = call(strands_kernel, struct((strands, rows, width), BF16), us=10, mib=4)(rc_here, strand, other)
     whole = lax.all_gather(local, "mp", axis=2, tiled=True)
     place = lax.axis_index("seq").astype(jnp.int32)
     parity = place % 2
@@ -430,9 +432,6 @@
     bridges += [(j, i) for i, j in bridges]
     far = lax.ppermute(jnp.where(parity == 1, last, first), "seq", bridges)
     parity = parity.reshape(1)
-    w_output_held, _ = lax.optimization_barrier((w_output, whole))
-    w_across = swapped(w_output_held, "mp", 2)
-    w_beside = swapped(w_output_held, "mp", 1)
 
     groups = 2 * strands
     f32_lanes, bf16_lanes = struct((groups, rows, width), F32), struct((strands, rows, width), BF16)
@@ -444,7 +443,7 @@
         (f32_lanes,) * 5 + (struct((groups, full), F32),),
         scratch=[
             pltpu.VMEM((strands, rows + 16, full), F32),
-            pltpu.VMEM((groups * rows, full), BF16),
+            pltpu.VMEM((mixing.shape[0], groups * rows, full), BF16),
         ],
     )(whole, *params)
 
@@ -460,41 +459,47 @@
         in_specs=[SMEM_SPEC] + [VMEM_SPEC] * 6,
     )(1 - parity, *lanes, edges)
 
-    total, state = call(pair_kernel, (state_struct, entry_struct))(kept, from_partner)
-    paired = total
-    w_across, _ = lax.optimization_barrier((w_across, total))
-    w_opposite = swapped(w_across, "mp", 1)
+    total = call(pair_kernel, state_struct, mib=4, us=1)(kept, from_partner)
+    w_held, _ = lax.optimization_barrier((w_output, total))
+    w_across = swapped(w_held, "mp", 2)
+    sent_parts, kept_parts, _ = lax.optimization_barrier((sent_parts, kept_parts, total))
+    reads = call(
+        read_kernel,
+        (f32_lanes, struct(f32_lanes.shape, BF16)),
+        mib=6,
+        in_specs=[SMEM_SPEC] + [VMEM_SPEC] * 2,
+    )(parity, sent_parts, kept_parts)
     prefix = []
     bits = range(1, seq_count.bit_length() - 1)
     for bit in bits:
         later = ((place >> bit) % 2 == place % 2).astype(jnp.int32).reshape(1)
+        received = swapped(total, "seq", 1 << bit)
+        if bit == bits[0]:
+            received, reads = lax.optimization_barrier((received, reads))
         if bit == bits[-1]:
-            received = swapped(state, "seq", 1 << bit)
             break
-        arriving = swapped(total, "seq", 1 << bit)
-        wide, total, state = call(
+        wide, total = call(
             functools.partial(advance_kernel, bool(prefix)),
-            (struct(state_struct.shape, F32), state_struct, entry_struct),
+            (struct(state_struct.shape, F32), entry_struct if bit + 1 == bits[-1] else state_struct),
+            mib=4,
+            us=1,
             in_specs=[SMEM_SPEC] + [VMEM_SPEC] * (2 + len(prefix)),
-        )(later, total, arriving, *prefix)
+        )(later, total, received, *prefix)
         prefix = [wide]
-    sent_parts, kept_parts, _ = lax.optimization_barrier((sent_parts, kept_parts, paired))
-    local_out, start_map = call(
-        read_kernel,
-        (f32_lanes, struct(f32_lanes.shape, BF16)),
-        in_specs=[SMEM_SPEC] + [VMEM_SPEC] * 2,
-    )(parity, sent_parts, kept_parts)
-    received, local_out, start_map, w_opposite = lax.optimization_barrier(
-        (received, local_out, start_map, w_opposite)
-    )
+    w_held, _ = lax.optimization_barrier((w_output, total))
+    w_beside = swapped(w_held, "mp", 1)
     entry = call(
         functools.partial(entry_kernel, bool(prefix)),
         entry_struct,
+        mib=4,
+        us=1,
         in_specs=[SMEM_SPEC] + [VMEM_SPEC] * (1 + len(prefix)),
     )(later, received, *prefix)
     other = swapped(entry, "seq", 1)
-    joined = call(finish_kernel, bf16_lanes)(
-        entry, from_partner, other, local_out, start_map, group_gain.reshape(1, width)
+    w_across, other = lax.optimization_barrier((w_across, other))
+    w_opposite = swapped(w_across, "mp", 1)
+    joined = call(finish_kernel, bf16_lanes, mib=6)(
+        entry, from_partner, other, *reads, group_gain.reshape(1, width)
     )
     joined_whole = lax.all_gather(joined, "mp", axis=2, tiled=True)
 
@@ -507,7 +512,7 @@
             pltpu.VMEM((rows, full), F32),
             pltpu.VMEM((rows, full), F32),
         ],
-        mib=24,
+        mib=16,
         in_specs=[SMEM_SPEC] + [VMEM_SPEC] * (5 + mp_count),
     )(position, joined_whole, whole, *w_blocks, ffn_key, ffn_value, ln2_gain.reshape(1, full))
     merged = own

time: 71.4 us -> 67.2 us (0.941)
  Pallas kernels: 19.6 us -> 17.8 us
  local copies, waits for them, and re-layouts: 3.96 us -> 2.29 us
  waiting for transfers between devices: 11.9 us -> 10.3 us
    unnamed x52 -> x40, local copies, waits for them, and re-layouts: 3.96 us -> 2.29 us
    ppermute x10, waiting for transfers between devices: 11.9 us -> 10.3 us  [swapped(): lax.ppermute(value, axis, [(i, i ^ mask) for i in range(lax.axis_size(axi...]
  transfers between devices with their start and end apart: 13 -> 13, of which waited for: 5 -> 5; matrix products, arithmetic and copies ran while one was open for 0% -> 0% of each run, Pallas kernels for 25% -> 16%
where the time goes in v7:
time: 67.2 us; the launch traced here: 66.9 us
  starting transfers between devices  20.7 us (31%)
  Pallas kernels  17.8 us (26%)
  blocking collectives  14.7 us (22%)
  waiting for transfers between devices  10.3 us (15%)
  local copies, waits for them, and re-layouts  2.29 us (3%)
  other arithmetic  0.69 us (1%)
    ppermute x10, starting transfers between devices, swapped(): lax.ppermute(value, axis, [(i, i ^ mask) for i in range(lax.axis_size(axi...  12.5 us
    ppermute x10, waiting for transfers between devices, swapped(): lax.ppermute(value, axis, [(i, i ^ mask) for i in range(lax.axis_size(axi...  10.3 us
    all_gather x1, blocking collectives, on_device(): joined_whole = lax.all_gather(joined, 'mp', axis=2, tiled=True)  7.42 us
    all_gather x1, blocking collectives, on_device(): whole = lax.all_gather(local, 'mp', axis=2, tiled=True)  7.3 us
    ppermute x1, starting transfers between devices, on_device(): rc_here = lax.ppermute(hidden_rc, 'seq', mirror)  6 us
    pallas_call x1, Pallas kernels, on_device(): call(functools.partial(chunk_kernel, True), (state_struct, parts_struct,...  4.47 us
    pallas_call x1, Pallas kernels, on_device(): call(functools.partial(chunk_kernel, False), (state_struct, parts_struct)...  3.63 us
    pallas_call x1, Pallas kernels, on_device(): call(project_kernel, (f32_lanes,) * 5 + (struct((groups, full), F32),), s...  3.07 us
  transfers between devices with their start and end apart: 13, of which 5 were waited for; matrix products, arithmetic and copies ran while one was open for 0% of the time, Pallas kernels for 16%

profile of v7, /device:TPU:0, one launch (start us, length us, event | category | flops | bytes accessed | tf_op | source)
XLA Modules:
  0.0 66.9 jit_solution(8252528779792355320)
XLA Ops:
  0.0 6.0 %collective-permute-start = (bf16[128,256]{1,0:T(8,128)(2,1)}, bf16[128,256]{1,0:T(8,128)(2,1)S(1)}, u32[]{:S(2)}, u32[]{:S(2)}) collective-permute-start(bf16[128,256]{1,0:T(8,128)(2,1)} %param.22), channel_id=1, source_target_pairs={{0,28},{4,24},{8,20},{12,16},{16,12},{20,8},{24,4},{28,0},{1,29},{... | collective-permute-start | bytes 196616 | tf_op jit(solution)/shard_map/ppermute | solution.py:407
  6.0 0.8 %copy-done.8 = bf16[128,256]{1,0:T(8,128)(2,1)S(1)} copy-done((bf16[128,256]{1,0:T(8,128)(2,1)S(1)}, bf16[128,256]{1,0:T(8,128)(2,1)}, u32[]{:S(2)}) %copy-start.8) | copy-done | bytes 65560
  6.8 0.7 %copy-done.12 = f32[4,256]{1,0:T(4,128)S(1)} copy-done((f32[4,256]{1,0:T(4,128)S(1)}, f32[4,256]{1,0:T(4,128)}, u32[]{:S(2)}) %copy-start.12) | copy-done | bytes 4120
  7.5 0.7 copy-done.18
  8.2 0.4 shard_map.190
  8.9 7.3 %all_gather.6.x_ref = bf16[2,128,1024]{2,1,0:T(8,128)(2,1)S(1)} all-gather(bf16[2,128,256]{2,1,0:T(8,128)(2,1)S(1)} %shard_map.191), channel_id=1, replica_groups=mesh['seq'=8,'mp'=4] {'mp'}, dimensions={2}, use_global_device_ids=true | all-gather | bytes 655360 | tf_op jit(solution)/shard_map/all_gather | solution.py:426
  16.3 1.5 %collective-permute-start.1 = (bf16[2,1024]{1,0:T(2,128)(2,1)S(1)}, bf16[2,1024]{1,0:T(2,128)(2,1)S(1)}, u32[]{:S(2)}, u32[]{:S(2)}) collective-permute-start(bf16[2,1024]{1,0:T(2,128)(2,1)S(1)} %bitcast.31), channel_id=1, source_target_pairs={{0,4},{4,0},{8,12},{12,8},{16,20},{20,16},{24,28},{28,24},{1,5},{5... | collective-permute-start | bytes 12296 | tf_op jit(solution)/shard_map/ppermute | solution.py:430
  17.8 0.6 collective-permute-start.2
  18.6 3.1 %shard_map.192 = (f32[4,128,256]{2,1,0:T(8,128)S(1)}, f32[4,128,256]{2,1,0:T(8,128)S(1)}, f32[4,128,256]{2,1,0:T(8,128)S(1)}, f32[4,128,256]{2,1,0:T(8,128)S(1)}...) custom-call(bf16[2,128,1024]{2,1,0:T(8,128)(2,1)S(1)} %all_gather.6.x_ref, f32[1,1024]{1,0:T(1,128)S(1)} %bitcast.22, ...), custom_call_target="tpu_custom_call" | custom-call | flops 10000000000 | bytes 10000000 | tf_op jit(solution)/shard_map/pallas_call | solution.py:441
  21.7 4.5 %shard_map.193 = (bf16[2,128,256]{2,1,0:T(8,128)(2,1)S(1)}, bf16[2,7,128,256]{3,2,1,0:T(8,128)(2,1)S(1)}, f32[5,4,256]{2,1,0:T(4,128)S(1)}) custom-call(s32[1]{0:T(128)} %bitcast.3.direction_ref, f32[4,128,256]{2,1,0:T(8,128)S(1)} %get-tuple-element.43.refs_0_, f32[4,128,256]{2,1,0:T(8,128)S(1)} %get-tuple-element.44.refs_1_, ...), custom_call_target="tpu_custom_call" | custom-call | flops 10000000000 | bytes 10000000 | tf_op jit(solution)/shard_map/pallas_call | solution.py:450
  26.1 3.6 %collective-permute-start.3 = (bf16[2,128,256]{2,1,0:T(8,128)(2,1)S(1)}, bf16[2,128,256]{2,1,0:T(8,128)(2,1)S(1)}, u32[]{:S(2)}, u32[]{:S(2)}) collective-permute-start(bf16[2,128,256]{2,1,0:T(8,128)(2,1)S(1)} %get-tuple-element.51), channel_id=1, source_target_pairs={{0,4},{4,0},{8,12},{12,8},{16,20},{20,16},{24,28},{28,24},{1,5},{5... | collective-permute-start | bytes 393224 | tf_op jit(solution)/shard_map/ppermute | solution.py:376
  29.7 3.6 %shard_map.194 = (bf16[2,128,256]{2,1,0:T(8,128)(2,1)S(1)}, bf16[2,7,128,256]{3,2,1,0:T(8,128)(2,1)S(1)}) custom-call(s32[1]{0:T(128)S(6)} %sub.3.direction_ref, f32[4,128,256]{2,1,0:T(8,128)S(1)} %get-tuple-element.43.refs_0_, f32[4,128,256]{2,1,0:T(8,128)S(1)} %get-tuple-element.44.refs_1_, f32[4,128,256]{2,1,0:T(8,128)S(1)} %get-tuple-element.45.refs_2_, ...), custom_call_target="tpu_custom_call" | custom-call | flops 10000000000 | bytes 10000000 | tf_op jit(solution)/shard_map/pallas_call | solution.py:456
  33.4 0.2 shard_map.195.total_ref
  33.6 1.3 %collective-permute-start.4 = (bf16[2,128,256]{2,1,0:T(8,128)(2,1)S(1)}, bf16[2,128,256]{2,1,0:T(8,128)(2,1)S(1)}, u32[]{:S(2)}, u32[]{:S(2)}) collective-permute-start(bf16[2,128,256]{2,1,0:T(8,128)(2,1)S(1)} %shard_map.195.total_ref), channel_id=1, source_target_pairs={{0,8},{4,12},{8,0},{12,4},{16,24},{20,28},{24,16},{28,20},{1,9},{5... | collective-permute-start | bytes 393224 | tf_op jit(solution)/shard_map/ppermute | solution.py:376
  35.0 0.8 %collective-permute-start.6 = (bf16[256,1024]{1,0:T(8,128)(2,1)S(1)}, bf16[256,1024]{1,0:T(8,128)(2,1)S(1)}, u32[]{:S(2)}, u32[]{:S(2)}) collective-permute-start(bf16[256,1024]{1,0:T(8,128)(2,1)S(1)} %copy-done.5), channel_id=1, source_target_pairs={{0,2},{1,3},{2,0},{3,1},{4,6},{5,7},{6,4},{7,5},{8,10},{9,11},{10,... | collective-permute-start | bytes 1572872 | tf_op jit(solution)/shard_map/ppermute | solution.py:376
  35.8 2.1 %shard_map.196 = (f32[4,128,256]{2,1,0:T(8,128)S(1)}, bf16[4,128,256]{2,1,0:T(8,128)(2,1)S(1)}) custom-call(s32[1]{0:T(128)} %bitcast.3.direction_ref, bf16[2,7,128,256]{3,2,1,0:T(8,128)(2,1)S(1)} %get-tuple-element.54.sent_ref, bf16[2,7,128,256]{3,2,1,0:T(8,128)(2,1)S(1)} %get-tuple-element.55.kept_ref), custom_call_target="tpu_custom_call" | custom-call | flops 10000000000 | bytes 10000000 | tf_op jit(solution)/shard_map/pallas_call | solution.py:466
  37.9 0.8 %collective-permute-done.4.from_ref = bf16[2,128,256]{2,1,0:T(8,128)(2,1)S(1)} collective-permute-done((bf16[2,128,256]{2,1,0:T(8,128)(2,1)S(1)}, bf16[2,128,256]{2,1,0:T(8,128)(2,1)S(1)}, u32[]{:S(2)}, u32[]{:S(2)}) %collective-permute-start.4) | collective-permute-done | bytes 131104 | tf_op jit(solution)/shard_map/ppermute | solution.py:376
  38.7 0.2 shard_map.197
  38.9 3.4 %collective-permute-start.5 = (bf16[2,64,256]{2,1,0:T(8,128)(2,1)S(1)}, bf16[2,64,256]{2,1,0:T(8,128)(2,1)S(1)}, u32[]{:S(2)}, u32[]{:S(2)}) collective-permute-start(bf16[2,64,256]{2,1,0:T(8,128)(2,1)S(1)} %get-tuple-element.59), channel_id=1, source_target_pairs={{0,16},{4,20},{8,24},{12,28},{16,0},{20,4},{24,8},{28,12},{1,17},{... | collective-permute-start | bytes 196616 | tf_op jit(solution)/shard_map/ppermute | solution.py:376
  42.2 2.9 %collective-permute-done.5.from_ref = bf16[2,64,256]{2,1,0:T(8,128)(2,1)S(1)} collective-permute-done((bf16[2,64,256]{2,1,0:T(8,128)(2,1)S(1)}, bf16[2,64,256]{2,1,0:T(8,128)(2,1)S(1)}, u32[]{:S(2)}, u32[]{:S(2)}) %collective-permute-start.5) | collective-permute-done | bytes 65568 | tf_op jit(solution)/shard_map/ppermute | solution.py:376
  45.2 0.2 shard_map.198.entry_ref
  45.4 1.5 %collective-permute-start.7 = (bf16[2,64,256]{2,1,0:T(8,128)(2,1)S(1)}, bf16[2,64,256]{2,1,0:T(8,128)(2,1)S(1)}, u32[]{:S(2)}, u32[]{:S(2)}) collective-permute-start(bf16[2,64,256]{2,1,0:T(8,128)(2,1)S(1)} %shard_map.198.entry_ref), channel_id=1, source_target_pairs={{0,4},{4,0},{8,12},{12,8},{16,20},{20,16},{24,28},{28,24},{1,5},{5... | collective-permute-start | bytes 196616 | tf_op jit(solution)/shard_map/ppermute | solution.py:376
  46.8 2.9 %collective-permute-done.7.other_ref = bf16[2,64,256]{2,1,0:T(8,128)(2,1)S(1)} collective-permute-done((bf16[2,64,256]{2,1,0:T(8,128)(2,1)S(1)}, bf16[2,64,256]{2,1,0:T(8,128)(2,1)S(1)}, u32[]{:S(2)}, u32[]{:S(2)}) %collective-permute-start.7) | collective-permute-done | bytes 65568 | tf_op jit(solution)/shard_map/ppermute | solution.py:376
  49.8 1.3 %shard_map.199 = bf16[2,128,256]{2,1,0:T(8,128)(2,1)S(1)} custom-call(bf16[2,64,256]{2,1,0:T(8,128)(2,1)S(1)} %shard_map.198.entry_ref, bf16[2,128,256]{2,1,0:T(8,128)(2,1)S(1)} %collective-permute-done.3.from_ref, bf16[2,64,256]{2,1,0:T(8,128)(2,1)S(1)} %collective-permute-done.7.other_ref, f32[4,128,256]{2,1,0:T(8,128)S(1)} %get-tuple-element.63.local_ref, ...), custom_call_target="tpu_custom_call" | custom-call | flops 10000000000 | bytes 10000000 | tf_op jit(solution)/shard_map/pallas_call | solution.py:501
  51.1 7.4 %all_gather.7.joined_ref = bf16[2,128,1024]{2,1,0:T(8,128)(2,1)S(1)} all-gather(bf16[2,128,256]{2,1,0:T(8,128)(2,1)S(1)} %shard_map.199), channel_id=1, replica_groups=mesh['seq'=8,'mp'=4] {'mp'}, dimensions={2}, use_global_device_ids=true | all-gather | bytes 655360 | tf_op jit(solution)/shard_map/all_gather | solution.py:504
  58.6 2.0 %shard_map.200 = (f32[128,256]{1,0:T(8,128)S(1)}, bf16[128,256]{1,0:T(8,128)(2,1)S(1)}, bf16[128,256]{1,0:T(8,128)(2,1)S(1)}, bf16[128,256]{1,0:T(8,128)(2,1)S(1)}) custom-call(s32[1]{0:T(128)} %bitcast.index_ref, bf16[2,128,1024]{2,1,0:T(8,128)(2,1)S(1)} %all_gather.7.joined_ref, bf16[2,128,1024]{2,1,0:T(8,128)(2,1)S(1)} %all_gather.6.x_ref, ...), custom_call_target="tpu_custom_call" | custom-call | flops 10000000000 | bytes 10000000 | tf_op jit(solution)/shard_map/pallas_call | solution.py:508
  60.6 0.4 collective-permute-start.10
  61.0 0.8 %collective-permute-start.11 = (bf16[128,256]{1,0:T(8,128)(2,1)S(1)}, bf16[128,256]{1,0:T(8,128)(2,1)S(1)}, u32[]{:S(2)}, u32[]{:S(2)}) collective-permute-start(bf16[128,256]{1,0:T(8,128)(2,1)S(1)} %get-tuple-element.69), channel_id=1, source_target_pairs={{0,2},{1,3},{2,0},{3,1},{4,6},{5,7},{6,4},{7,5},{8,10},{9,11},{10,... | collective-permute-start | bytes 196616 | tf_op jit(solution)/shard_map/ppermute | solution.py:376
  61.9 0.7 %collective-permute-start.12 = (bf16[128,256]{1,0:T(8,128)(2,1)S(1)}, bf16[128,256]{1,0:T(8,128)(2,1)S(1)}, u32[]{:S(2)}, u32[]{:S(2)}) collective-permute-start(bf16[128,256]{1,0:T(8,128)(2,1)S(1)} %get-tuple-element.70), channel_id=1, source_target_pairs={{0,3},{1,2},{2,1},{3,0},{4,7},{5,6},{6,5},{7,4},{8,11},{9,10},{10,... | collective-permute-start | bytes 196616 | tf_op jit(solution)/shard_map/ppermute | solution.py:376
  62.5 3.2 %collective-permute-done.11 = bf16[128,256]{1,0:T(8,128)(2,1)S(1)} collective-permute-done((bf16[128,256]{1,0:T(8,128)(2,1)S(1)}, bf16[128,256]{1,0:T(8,128)(2,1)S(1)}, u32[]{:S(2)}, u32[]{:S(2)}) %collective-permute-start.11) | collective-permute-done | bytes 65568 | tf_op jit(solution)/shard_map/ppermute | solution.py:376
  65.7 0.5 collective-permute-done.12
  66.2 0.7 add_convert_fusion
  (49 shorter events, 0.3 us)
Async XLA Ops:
  0.0 8.6 %collective-permute-start = (bf16[128,256]{1,0:T(8,128)(2,1)}, bf16[128,256]{1,0:T(8,128)(2,1)S(1)}, u32[]{:S(2)}, u32[]{:S(2)}) collective-permute-start(bf16[128,256]{1,0:T(8,128)(2,1)} %param.22), channel_id=1, source_target_pairs={{0,28},{4,24},{8,20},{12,16},{16,12},{20,8},{24,4},{28,0},{1,29},{... | collective-permute-start | bytes 196616 | tf_op jit(solution)/shard_map/ppermute | solution.py:407
  6.0 0.8 %copy-start.8 = (bf16[128,256]{1,0:T(8,128)(2,1)S(1)}, bf16[128,256]{1,0:T(8,128)(2,1)}, u32[]{:S(2)}) copy-start(bf16[128,256]{1,0:T(8,128)(2,1)} %fwd_ref.1) | copy-start | bytes 196612
  6.8 0.7 %copy-start.12 = (f32[4,256]{1,0:T(4,128)S(1)}, f32[4,256]{1,0:T(4,128)}, u32[]{:S(2)}) copy-start(f32[4,256]{1,0:T(4,128)} %embed_ref.1) | copy-start | bytes 12292
  7.5 0.7 copy-start.18
  8.6 9.8 %copy-start.2 = (bf16[1024,256]{1,0:T(8,128)(2,1)S(1)}, bf16[1024,256]{1,0:T(8,128)(2,1)}, u32[]{:S(2)}) copy-start(bf16[1024,256]{1,0:T(8,128)(2,1)} %refs_10_.1) | copy-start | bytes 1572868
  8.7 9.8 %copy-start.3 = (bf16[1024,256]{1,0:T(8,128)(2,1)S(1)}, bf16[1024,256]{1,0:T(8,128)(2,1)}, u32[]{:S(2)}) copy-start(bf16[1024,256]{1,0:T(8,128)(2,1)} %refs_11_.1) | copy-start | bytes 1572868
  8.7 9.8 %copy-start.4 = (bf16[1024,256]{1,0:T(8,128)(2,1)S(1)}, bf16[1024,256]{1,0:T(8,128)(2,1)}, u32[]{:S(2)}) copy-start(bf16[1024,256]{1,0:T(8,128)(2,1)} %refs_12_.1) | copy-start | bytes 1572868
  8.7 9.8 %copy-start.6 = (bf16[1024,64]{0,1:T(8,128)(2,1)S(1)}, bf16[1024,64]{0,1:T(8,128)(2,1)}, u32[]{:S(2)}) copy-start(bf16[1024,64]{0,1:T(8,128)(2,1)} %param.30) | copy-start | bytes 393220
  8.7 9.8 %copy-start.7 = (bf16[1024,64]{0,1:T(8,128)(2,1)S(1)}, bf16[1024,64]{0,1:T(8,128)(2,1)}, u32[]{:S(2)}) copy-start(bf16[1024,64]{0,1:T(8,128)(2,1)} %param.33) | copy-start | bytes 393220
  8.7 9.8 %copy-start.9 = (f32[5,1024]{1,0:T(8,128)S(1)}, f32[5,1024]{1,0:T(8,128)}, u32[]{:S(2)}) copy-start(f32[5,1024]{1,0:T(8,128)} %refs_9_.1) | copy-start | bytes 61444
  8.7 9.8 %copy-start.10 = (bf16[64,256]{1,0:T(8,128)(2,1)S(1)}, bf16[64,256]{1,0:T(8,128)(2,1)}, u32[]{:S(2)}) copy-start(bf16[64,256]{1,0:T(8,128)(2,1)} %refs_15_.1) | copy-start | bytes 98308
  8.7 9.8 %copy-start.11 = (bf16[64,256]{1,0:T(8,128)(2,1)S(1)}, bf16[64,256]{1,0:T(8,128)(2,1)}, u32[]{:S(2)}) copy-start(bf16[64,256]{1,0:T(8,128)(2,1)} %refs_16_.1) | copy-start | bytes 98308
  8.7 9.8 %copy-start.13 = (f32[1024]{0:T(1024)S(1)}, f32[1024]{0:T(1024)}, u32[]{:S(2)}) copy-start(f32[1024]{0:T(1024)} %param.24) | copy-start | bytes 12292
  8.8 9.8 %copy-start.15 = (f32[256]{0:T(256)S(1)}, f32[256]{0:T(256)}, u32[]{:S(2)}) copy-start(f32[256]{0:T(256)} %param.31) | copy-start | bytes 3076
  8.8 9.8 %copy-start.16 = (f32[256]{0:T(256)S(1)}, f32[256]{0:T(256)}, u32[]{:S(2)}) copy-start(f32[256]{0:T(256)} %param.34) | copy-start | bytes 3076
  16.3 5.4 %collective-permute-start.1 = (bf16[2,1024]{1,0:T(2,128)(2,1)S(1)}, bf16[2,1024]{1,0:T(2,128)(2,1)S(1)}, u32[]{:S(2)}, u32[]{:S(2)}) collective-permute-start(bf16[2,1024]{1,0:T(2,128)(2,1)S(1)} %bitcast.31), channel_id=1, source_target_pairs={{0,4},{4,0},{8,12},{12,8},{16,20},{20,16},{24,28},{28,24},{1,5},{5... | collective-permute-start | bytes 12296 | tf_op jit(solution)/shard_map/ppermute | solution.py:430
  17.8 3.9 %collective-permute-start.2 = (bf16[2,1024]{1,0:T(2,128)(2,1)S(1)}, bf16[2,1024]{1,0:T(2,128)(2,1)S(1)}, u32[]{:S(2)}, u32[]{:S(2)}) collective-permute-start(bf16[2,1024]{1,0:T(2,128)(2,1)S(1)} %bitcast.32), channel_id=1, source_target_pairs={{4,8},{12,16},{20,24},{8,4},{16,12},{24,20},{5,9},{13,17},{21,25},... | collective-permute-start | bytes 12296 | tf_op jit(solution)/shard_map/ppermute | solution.py:433
  26.1 7.3 %collective-permute-start.3 = (bf16[2,128,256]{2,1,0:T(8,128)(2,1)S(1)}, bf16[2,128,256]{2,1,0:T(8,128)(2,1)S(1)}, u32[]{:S(2)}, u32[]{:S(2)}) collective-permute-start(bf16[2,128,256]{2,1,0:T(8,128)(2,1)S(1)} %get-tuple-element.51), channel_id=1, source_target_pairs={{0,4},{4,0},{8,12},{12,8},{16,20},{20,16},{24,28},{28,24},{1,5},{5... | collective-permute-start | bytes 393224 | tf_op jit(solution)/shard_map/ppermute | solution.py:376
  33.4 1.6 %copy-start.5 = (bf16[256,1024]{1,0:T(8,128)(2,1)S(1)}, bf16[256,1024]{1,0:T(8,128)(2,1)}, u32[]{:S(2)}) copy-start(bf16[256,1024]{1,0:T(8,128)(2,1)} %refs_0_.1) | copy-start | bytes 1572868
  33.6 5.0 %collective-permute-start.4 = (bf16[2,128,256]{2,1,0:T(8,128)(2,1)S(1)}, bf16[2,128,256]{2,1,0:T(8,128)(2,1)S(1)}, u32[]{:S(2)}, u32[]{:S(2)}) collective-permute-start(bf16[2,128,256]{2,1,0:T(8,128)(2,1)S(1)} %shard_map.195.total_ref), channel_id=1, source_target_pairs={{0,8},{4,12},{8,0},{12,4},{16,24},{20,28},{24,16},{28,20},{1,9},{5... | collective-permute-start | bytes 393224 | tf_op jit(solution)/shard_map/ppermute | solution.py:376
  35.0 14.8 %collective-permute-start.6 = (bf16[256,1024]{1,0:T(8,128)(2,1)S(1)}, bf16[256,1024]{1,0:T(8,128)(2,1)S(1)}, u32[]{:S(2)}, u32[]{:S(2)}) collective-permute-start(bf16[256,1024]{1,0:T(8,128)(2,1)S(1)} %copy-done.5), channel_id=1, source_target_pairs={{0,2},{1,3},{2,0},{3,1},{4,6},{5,7},{6,4},{7,5},{8,10},{9,11},{10,... | collective-permute-start | bytes 1572872 | tf_op jit(solution)/shard_map/ppermute | solution.py:376
  38.8 10.9 %copy-start.17 = (f32[256]{0:T(256)S(1)}, f32[256]{0:T(256)}, u32[]{:S(2)}) copy-start(f32[256]{0:T(256)} %param.36) | copy-start | bytes 3076
  38.9 6.3 %collective-permute-start.5 = (bf16[2,64,256]{2,1,0:T(8,128)(2,1)S(1)}, bf16[2,64,256]{2,1,0:T(8,128)(2,1)S(1)}, u32[]{:S(2)}, u32[]{:S(2)}) collective-permute-start(bf16[2,64,256]{2,1,0:T(8,128)(2,1)S(1)} %get-tuple-element.59), channel_id=1, source_target_pairs={{0,16},{4,20},{8,24},{12,28},{16,0},{20,4},{24,8},{28,12},{1,17},{... | collective-permute-start | bytes 196616 | tf_op jit(solution)/shard_map/ppermute | solution.py:376
  45.4 4.3 %collective-permute-start.7 = (bf16[2,64,256]{2,1,0:T(8,128)(2,1)S(1)}, bf16[2,64,256]{2,1,0:T(8,128)(2,1)S(1)}, u32[]{:S(2)}, u32[]{:S(2)}) collective-permute-start(bf16[2,64,256]{2,1,0:T(8,128)(2,1)S(1)} %shard_map.198.entry_ref), channel_id=1, source_target_pairs={{0,4},{4,0},{8,12},{12,8},{16,20},{20,16},{24,28},{28,24},{1,5},{5... | collective-permute-start | bytes 196616 | tf_op jit(solution)/shard_map/ppermute | solution.py:376
  46.8 11.7 %collective-permute-start.8 = (bf16[256,1024]{1,0:T(8,128)(2,1)S(1)}, bf16[256,1024]{1,0:T(8,128)(2,1)S(1)}, u32[]{:S(2)}, u32[]{:S(2)}) collective-permute-start(bf16[256,1024]{1,0:T(8,128)(2,1)S(1)} %copy-done.5), channel_id=1, source_target_pairs={{0,1},{1,0},{2,3},{3,2},{4,5},{5,4},{6,7},{7,6},{8,9},{9,8},{10,11... | collective-permute-start | bytes 1572872 | tf_op jit(solution)/shard_map/ppermute | solution.py:376
  49.7 8.8 %collective-permute-start.9 = (bf16[256,1024]{1,0:T(8,128)(2,1)S(1)}, bf16[256,1024]{1,0:T(8,128)(2,1)S(1)}, u32[]{:S(2)}, u32[]{:S(2)}) collective-permute-start(bf16[256,1024]{1,0:T(8,128)(2,1)S(1)} %collective-permute-done.6.refs_2_), channel_id=1, source_target_pairs={{0,1},{1,0},{2,3},{3,2},{4,5},{5,4},{6,7},{7,6},{8,9},{9,8},{10,11... | collective-permute-start | bytes 1572872 | tf_op jit(solution)/shard_map/ppermute | solution.py:376
  49.7 8.8 %copy-start = (bf16[1024,1024]{1,0:T(8,128)(2,1)S(1)}, bf16[1024,1024]{1,0:T(8,128)(2,1)}, u32[]{:S(2)}) copy-start(bf16[1024,1024]{1,0:T(8,128)(2,1)} %refs_4_.3) | copy-start | bytes 6291460
  49.7 8.8 %copy-start.1 = (bf16[1024,1024]{1,0:T(8,128)(2,1)S(1)}, bf16[1024,1024]{1,0:T(8,128)(2,1)}, u32[]{:S(2)}) copy-start(bf16[1024,1024]{1,0:T(8,128)(2,1)} %refs_5_.1) | copy-start | bytes 6291460
  49.7 8.8 %copy-start.14 = (f32[1024]{0:T(1024)S(1)}, f32[1024]{0:T(1024)}, u32[]{:S(2)}) copy-start(f32[1024]{0:T(1024)} %param.25) | copy-start | bytes 12292
  60.6 1.9 %collective-permute-start.10 = (bf16[128,256]{1,0:T(8,128)(2,1)S(1)}, bf16[128,256]{1,0:T(8,128)(2,1)S(1)}, u32[]{:S(2)}, u32[]{:S(2)}) collective-permute-start(bf16[128,256]{1,0:T(8,128)(2,1)S(1)} %get-tuple-element.68), channel_id=1, source_target_pairs={{0,1},{1,0},{2,3},{3,2},{4,5},{5,4},{6,7},{7,6},{8,9},{9,8},{10,11... | collective-permute-start | bytes 196616 | tf_op jit(solution)/shard_map/ppermute | solution.py:376
  61.0 4.7 %collective-permute-start.11 = (bf16[128,256]{1,0:T(8,128)(2,1)S(1)}, bf16[128,256]{1,0:T(8,128)(2,1)S(1)}, u32[]{:S(2)}, u32[]{:S(2)}) collective-permute-start(bf16[128,256]{1,0:T(8,128)(2,1)S(1)} %get-tuple-element.69), channel_id=1, source_target_pairs={{0,2},{1,3},{2,0},{3,1},{4,6},{5,7},{6,4},{7,5},{8,10},{9,11},{10,... | collective-permute-start | bytes 196616 | tf_op jit(solution)/shard_map/ppermute | solution.py:376
  61.9 4.4 %collective-permute-start.12 = (bf16[128,256]{1,0:T(8,128)(2,1)S(1)}, bf16[128,256]{1,0:T(8,128)(2,1)S(1)}, u32[]{:S(2)}, u32[]{:S(2)}) collective-permute-start(bf16[128,256]{1,0:T(8,128)(2,1)S(1)} %get-tuple-element.70), channel_id=1, source_target_pairs={{0,3},{1,2},{2,1},{3,0},{4,7},{5,6},{6,5},{7,4},{8,11},{9,10},{10,... | collective-permute-start | bytes 196616 | tf_op jit(solution)/shard_map/ppermute | solution.py:376

commit v8 on v7

--- a/solution.py
+++ b/solution.py
@@ -107,32 +107,56 @@
     return inverses
 
 
-def project_all(mix, params):
-    w_r, w_k, w_v, w_d1, w_c1, w_d2, w_c2, d_base, c_base = params
-    for index, weight in enumerate((w_r, w_k, w_v)):
-        yield mm(mix(index), weight[...])
-    decay_low = jnp.tanh(mm_rows(mix(3), w_d1[...])).astype(BF16)
-    yield -DECAY_SCALE * jax.nn.sigmoid(d_base[...] + mm(decay_low, w_d2[...]))
-    rate_low = mm_rows(mix(4), w_c1[...]).astype(BF16)
-    yield jax.nn.sigmoid(c_base[...] + mm(rate_low, w_c2[...]))
-
-
-def project_kernel(x_ref, *refs):
-    (gain_ref, mixing_ref), params = refs[:2], refs[2:11]
-    outs, edge_ref, (normed, mixed) = refs[11:16], refs[16], refs[17:]
+def gates(low, w_d2, w_c2, d_base, c_base):
+    rank, width = w_d2.shape
+    low = jnp.where(ids_of(low.shape, 1) < rank, jnp.tanh(low), low).astype(BF16)
+    zero = jnp.zeros((rank, width), BF16)
+    both = jnp.concatenate(
+        [jnp.concatenate([w_d2, zero], axis=1), jnp.concatenate([zero, w_c2], axis=1)], axis=0
+    )
+    result = mm(low, both)
+    log_decay = -DECAY_SCALE * jax.nn.sigmoid(d_base + result[:, :width])
+    return log_decay, jax.nn.sigmoid(c_base + result[:, width:])
+
+
+def project_kernel(x_ref, gain_ref, mixing_ref, w_k, w_v, w_d1, w_c1, w_d2, w_c2, d_base, c_base, *refs):
+    outs, (normed, low_ref, edge_ref, mixed, shifts) = refs[:4], refs[4:]
     strands, rows, _ = x_ref.shape
-    width = outs[0].shape[2]
+    shape = outs[0].shape
     pad = 8
     gain = gain_ref[...]
+    lows = [(w_d1[...].astype(F32), mixing_ref[3:4]), (w_c1[...].astype(F32), mixing_ref[4:5])]
+    parts = [weight * (1.0 - share) for weight, share in lows] + [weight * share for weight, share in lows]
+    low_ref[...] = jnp.concatenate(parts, axis=0).astype(BF16)
+    half = low_ref.shape[0] // 2
     for s in range(strands):
         values = layer_norm(x_ref[s].astype(F32), gain)
+        zero = jnp.zeros_like(values[:1])
         normed[s, pad : pad + rows, :] = values
-        normed[s, pad - 1 : pad, :] = jnp.zeros_like(values[:1])
-        normed[s, pad + rows : pad + rows + 1, :] = jnp.zeros_like(values[:1])
+        normed[s, pad - 1 : pad, :] = zero
+        normed[s, pad + rows : pad + rows + 1, :] = zero
         edge_ref[s : s + 1, :] = values[:1]
         edge_ref[strands + s : strands + s + 1, :] = values[rows - 1 :]
-
-    step = 16
+        low = mm_rows(values.astype(BF16), low_ref[...])
+        shifts[s, pad : pad + rows, :] = low[:, half:]
+        shifts[s, pad - 1 : pad, :] = zero[:, :half]
+        shifts[s, pad + rows : pad + rows + 1, :] = zero[:, :half]
+        for d in range(2):
+            shift = pad - 1 + 2 * d
+            g = d * strands + s
+            log_decay, rate = gates(
+                low[:, :half] + shifts[s, shift : shift + rows, :], w_d2[...], w_c2[...], d_base[...], c_base[...]
+            )
+            outs[2][g] = log_decay
+            outs[3][g] = rate
+    blend(normed, mixing_ref, (1, 2), rows, mixed)
+    outs[0][...] = mm(mixed[0], w_k[...]).reshape(shape)
+    outs[1][...] = mm(mixed[1], w_v[...]).reshape(shape)
+
+
+def blend(normed, mixing_ref, indices, rows, mixed):
+    strands = normed.shape[0]
+    step, pad = 16, 8
     for s in range(strands):
         for start in range(0, rows, step):
             center = normed[s, pad + start : pad + start + step, :]
@@ -140,16 +164,19 @@
                 shift = pad + start - 1 + 2 * d
                 change = normed[s, shift : shift + step, :] - center
                 place = (d * strands + s) * rows + start
-                for index in range(mixed.shape[0]):
+                for slot, index in enumerate(indices):
                     weight = mixing_ref[index : index + 1, :]
-                    mixed[index, place : place + step, :] = (center + change * weight).astype(BF16)
-
-    def mix(index):
-        return mixed[index]
-
-    shape = (2 * strands, rows, width)
-    for out_ref, result in zip(outs, project_all(mix, params)):
-        out_ref[...] = result.reshape(shape)
+                    mixed[slot, place : place + step, :] = (center + change * weight).astype(BF16)
+
+
+def receptance_kernel(normed, mixing_ref, edge_ref, w_r, out_ref, mixed):
+    groups, rows, _ = out_ref.shape
+    blend(normed, mixing_ref, (0,), rows, mixed)
+    out_ref[...] = mm(mixed[0], w_r[...]).reshape(out_ref.shape)
+    edges = mm(edge_ref[...].astype(BF16), w_r[...])
+    for g in range(groups):
+        row = 0 if g < groups // 2 else rows - 1
+        out_ref[g, row : row + 1] = edges[g : g + 1]
 
 
 def masked_heads(value, lane_head, heads):
@@ -157,11 +184,12 @@
 
 
 def chunk_kernel(first, direction_ref, *refs):
-    lanes, refs = refs[:5], refs[5:]
+    lanes, refs = refs[:4], refs[4:]
     if first:
-        partner_ref, beyond_ref, edge_ref, gain_ref, mixing_ref, *params, state_ref, parts_ref, edges_ref = refs
+        partner_ref, beyond_ref, edge_ref, low_ref, gain_ref, mixing_ref, w_k, w_v, *gate_refs = refs[:12]
+        state_ref, parts_ref, here_ref, edges_ref, read_edge_ref = refs[12:]
     else:
-        edges_ref, state_ref, parts_ref = refs
+        edges_ref, state_ref, parts_ref, here_ref = refs
     strands, _, rows, width = parts_ref.shape
     heads = width // HEAD
     d = direction_ref[0]
@@ -170,13 +198,19 @@
         near, far = partner_ref[...].astype(F32), beyond_ref[...].astype(F32)
         odd = d == 1
         halo = jnp.concatenate([jnp.where(odd, near, far), jnp.where(odd, far, near)], axis=0)
-        change = layer_norm(halo, gain_ref[...]) - center
+        halo = layer_norm(halo, gain_ref[...])
+        change = halo - center
 
         def mix(index):
             return (center + change * mixing_ref[index : index + 1, :]).astype(BF16)
 
-        for index, result in enumerate(project_all(mix, params)):
-            edges_ref[index] = result
+        edges_ref[0] = mm(mix(1), w_k[...])
+        edges_ref[1] = mm(mix(2), w_v[...])
+        low = mm_rows(jnp.concatenate([center, halo], axis=0).astype(BF16), low_ref[...])
+        half, count = low.shape[1] // 2, center.shape[0]
+        low = low[:count, :half] + low[count:, half:]
+        edges_ref[2], edges_ref[3] = gates(low, *[ref[...] for ref in gate_refs])
+        read_edge_ref[...] = center + change * mixing_ref[0:1, :]
     edge_row = d * (rows - 1)
     at_edge = ids_of((rows, width), 0) == edge_row
     order = (ids_of((rows, rows), 0) - ids_of((rows, rows), 1)) * (1 - 2 * d)
@@ -195,7 +229,7 @@
         def lane(index, ref):
             return jnp.where(at_edge, edges_ref[index, pl.ds(g, 1), :], ref[g])
 
-        receptance, key, value, log_decay, rate = [lane(index, ref) for index, ref in enumerate(lanes)]
+        key, value, log_decay, rate = [lane(index, ref) for index, ref in enumerate(lanes)]
         unit = key * lax.rsqrt(head_sum(key * key, ones) + UNIT_EPS)
         high, low = halves(log_decay)
         totals = mm(tri, high) + mm(tri, low)
@@ -203,7 +237,6 @@
         final = jnp.where(d == 0, totals[rows - 1 : rows], totals[0:1])
         there = jnp.exp(middle - totals)
         left_prev = -unit * jnp.exp(totals - log_decay - middle)
-        left_here = receptance * jnp.exp(totals - middle)
         right_insert = rate * unit * there
         right_key = key * there
         from_start = jnp.exp(middle)
@@ -220,11 +253,11 @@
             key_pulls.append(jnp.where(strict, scores[:, rows:], 0.0).astype(BF16))
         value_pull = mm(jnp.concatenate(key_pulls, axis=1), of_heads(value))
         value = value.astype(BF16)
-        parts_ref[s, 0] = left_here.astype(BF16)
-        parts_ref[s, 1] = right_insert.astype(BF16)
-        parts_ref[s, 2] = right_key.astype(BF16)
-        parts_ref[s, 3] = value
-        parts_ref[s, 6] = (left_here * from_start).astype(BF16)
+        here_ref[s, :rows] = jnp.exp(totals - middle)
+        here_ref[s, rows:] = jnp.broadcast_to(from_start, (here_ref.shape[1] - rows, width))
+        parts_ref[s, 0] = right_insert.astype(BF16)
+        parts_ref[s, 1] = right_key.astype(BF16)
+        parts_ref[s, 2] = value
         tail_insert = (right_insert * to_end).astype(BF16)
         tail_key = (right_key * to_end).astype(BF16)
         solved_for = jnp.concatenate([of_heads(value_pull), of_heads(left_prev * from_start)], axis=1)
@@ -237,8 +270,8 @@
         own = inverses[s * heads : (s + 1) * heads]
         inverse = jnp.concatenate([item.astype(BF16) for item in own], axis=1)
         solved = mm(inverse, solved_for).astype(BF16)
-        parts_ref[s, 4] = solved[:, :width]
-        parts_ref[s, 5] = solved[:, width:]
+        parts_ref[s, 3] = solved[:, :width]
+        parts_ref[s, 4] = solved[:, width:]
         added = mm_cols(tail_insert, solved)
         ends = jnp.where(same, end + added[:, :width], 0.0)
         maps = jnp.where(same, added[:, width:], 0.0)
@@ -249,16 +282,20 @@
         state_ref[s] = jnp.concatenate([end, across], axis=0).astype(BF16)
 
 
-def read_kernel(direction_ref, sent_ref, kept_ref, local_ref, map_ref):
+def read_kernel(
+    direction_ref, receptances, sent_ref, kept_ref, sent_here_ref, kept_here_ref, local_ref, map_ref
+):
     strands, _, rows, width = sent_ref.shape
     heads = width // HEAD
     lane_head = ids_of((1, width), 1) // HEAD
-    for role, parts_ref in enumerate((sent_ref, kept_ref)):
-        sign = (1 - 2 * direction_ref[0]) * (1 - 2 * role)
-        inclusive = (ids_of((rows, rows), 0) - ids_of((rows, rows), 1)) * sign >= 0
+    for role, (parts_ref, here_ref) in enumerate(((sent_ref, sent_here_ref), (kept_ref, kept_here_ref))):
+        d = (direction_ref[0] + role) % 2
+        inclusive = (ids_of((rows, rows), 0) - ids_of((rows, rows), 1)) * (1 - 2 * d) >= 0
 
         def group(s, carry):
-            here, insert, key, value, pull, start, read = [parts_ref[s, i] for i in range(7)]
+            insert, key, value, pull, start = [parts_ref[s, i] for i in range(5)]
+            left = receptances[d * strands + s] * here_ref[s, :rows]
+            here = left.astype(BF16)
             reads = []
             for source in (insert, key):
                 scores = mm_rows(here, masked_heads(source, lane_head, heads))
@@ -269,7 +306,7 @@
             ]
             g = role * strands + s
             local_ref[g] = mm(reads[0], pull) + mm(reads[1], value)
-            map_ref[g] = (read.astype(F32) + mm(reads[0], start)).astype(BF16)
+            map_ref[g] = (left * here_ref[s, rows : rows + 1] + mm(reads[0], start)).astype(BF16)
             return carry
 
         lax.fori_loop(0, strands, group, 0)
@@ -317,21 +354,29 @@
         entry_ref[s] = ahead.astype(BF16)
 
 
-def finish_kernel(entry_ref, from_ref, other_ref, local_ref, map_ref, gain_ref, out_ref):
-    strands, _, width = out_ref.shape
+def normed_heads(role, states, local_ref, map_ref):
+    strands, width = len(states), local_ref.shape[2]
     same_head = block_ones(width)
     ones = same_head.astype(F32).astype(BF16)
-    gain = gain_ref[...]
-    for s in range(strands):
-        kept = composed(from_ref[s], entry_ref[s], same_head, True).astype(BF16)
-        joined = 0.0
-        for role, state in enumerate((other_ref[s], kept)):
-            g = role * strands + s
-            wkv = local_ref[g] + mm(map_ref[g], spread(state, same_head))
-            centered = wkv - head_sum(wkv, ones) * (1.0 / HEAD)
-            variance = head_sum(centered * centered, ones) * (1.0 / HEAD)
-            joined = joined + centered * lax.rsqrt(variance + GROUP_EPS)
-        out_ref[s] = (joined * gain).astype(BF16)
+    for s, state in enumerate(states):
+        g = role * strands + s
+        wkv = local_ref[g] + mm(map_ref[g], spread(state, same_head))
+        centered = wkv - head_sum(wkv, ones) * (1.0 / HEAD)
+        variance = head_sum(centered * centered, ones) * (1.0 / HEAD)
+        yield centered * lax.rsqrt(variance + GROUP_EPS)
+
+
+def kept_kernel(entry_ref, from_ref, local_ref, map_ref, out_ref):
+    same_head = block_ones(out_ref.shape[2])
+    states = [composed(from_ref[s], entry_ref[s], same_head, True).astype(BF16) for s in range(out_ref.shape[0])]
+    for s, result in enumerate(normed_heads(1, states, local_ref, map_ref)):
+        out_ref[s] = result
+
+
+def finish_kernel(other_ref, kept_ref, local_ref, map_ref, gain_ref, out_ref):
+    states = [other_ref[s] for s in range(out_ref.shape[0])]
+    for s, result in enumerate(normed_heads(0, states, local_ref, map_ref)):
+        out_ref[s] = ((result + kept_ref[s]) * gain_ref[...]).astype(BF16)
 
 
 def mix_kernel(blocks, index_ref, joined_ref, x_ref, *refs):
@@ -408,7 +453,6 @@
     params = (
         ln1_gain.reshape(1, full),
         mixing,
-        w_receptance,
         w_key,
         w_value,
         decay_first_weight.T,
@@ -435,47 +479,55 @@
 
     groups = 2 * strands
     f32_lanes, bf16_lanes = struct((groups, rows, width), F32), struct((strands, rows, width), BF16)
-    parts_struct = struct((strands, 7, rows, width), BF16)
+    parts_struct = struct((strands, 5, rows, width), BF16)
+    here_struct = struct((strands, rows + 8, width), F32)
     state_struct = struct((strands, 2 * HEAD, width), BF16)
     entry_struct = struct((strands, HEAD, width), BF16)
-    *lanes, edge = call(
+    low_shape = (4 * decay_first_weight.shape[1], full)
+    *lanes, normed, low, edge = call(
         project_kernel,
-        (f32_lanes,) * 5 + (struct((groups, full), F32),),
+        (f32_lanes,) * 4
+        + (
+            struct((strands, rows + 16, full), F32),
+            struct(low_shape, BF16),
+            struct((groups, full), F32),
+        ),
         scratch=[
-            pltpu.VMEM((strands, rows + 16, full), F32),
-            pltpu.VMEM((mixing.shape[0], groups * rows, full), BF16),
+            pltpu.VMEM((2, groups * rows, full), BF16),
+            pltpu.VMEM((strands, rows + 16, low_shape[0] // 2), F32),
         ],
     )(whole, *params)
 
-    sent, sent_parts, edges = call(
+    sent, sent_parts, sent_here, edges, read_edge = call(
         functools.partial(chunk_kernel, True),
-        (state_struct, parts_struct, struct((5, groups, width), F32)),
-        in_specs=[SMEM_SPEC] + [VMEM_SPEC] * (8 + len(params)),
-    )(parity, *lanes, near, far, edge, *params)
+        (state_struct, parts_struct, here_struct, struct((4, groups, width), F32), struct((groups, full), F32)),
+        in_specs=[SMEM_SPEC] + [VMEM_SPEC] * 16,
+    )(parity, *lanes, near, far, edge, low, *params[:4], *params[6:])
     from_partner = swapped(sent, "seq", 1)
-    kept, kept_parts = call(
+    kept, kept_parts, kept_here = call(
         functools.partial(chunk_kernel, False),
-        (state_struct, parts_struct),
-        in_specs=[SMEM_SPEC] + [VMEM_SPEC] * 6,
+        (state_struct, parts_struct, here_struct),
+        in_specs=[SMEM_SPEC] + [VMEM_SPEC] * 5,
     )(1 - parity, *lanes, edges)
 
     total = call(pair_kernel, state_struct, mib=4, us=1)(kept, from_partner)
     w_held, _ = lax.optimization_barrier((w_output, total))
     w_across = swapped(w_held, "mp", 2)
-    sent_parts, kept_parts, _ = lax.optimization_barrier((sent_parts, kept_parts, total))
-    reads = call(
-        read_kernel,
-        (f32_lanes, struct(f32_lanes.shape, BF16)),
+    read_edge, _ = lax.optimization_barrier((read_edge, total))
+    receptances = call(
+        receptance_kernel,
+        f32_lanes,
+        scratch=[pltpu.VMEM((1, groups * rows, full), BF16)],
         mib=6,
-        in_specs=[SMEM_SPEC] + [VMEM_SPEC] * 2,
-    )(parity, sent_parts, kept_parts)
+        us=3,
+    )(normed, mixing, read_edge, w_receptance)
     prefix = []
     bits = range(1, seq_count.bit_length() - 1)
     for bit in bits:
         later = ((place >> bit) % 2 == place % 2).astype(jnp.int32).reshape(1)
         received = swapped(total, "seq", 1 << bit)
         if bit == bits[0]:
-            received, reads = lax.optimization_barrier((received, reads))
+            received, receptances = lax.optimization_barrier((received, receptances))
         if bit == bits[-1]:
             break
         wide, total = call(
@@ -488,6 +540,14 @@
         prefix = [wide]
     w_held, _ = lax.optimization_barrier((w_output, total))
     w_beside = swapped(w_held, "mp", 1)
+    sent_parts, kept_parts, _ = lax.optimization_barrier((sent_parts, kept_parts, total))
+    reads = call(
+        read_kernel,
+        (f32_lanes, struct(f32_lanes.shape, BF16)),
+        mib=6,
+        in_specs=[SMEM_SPEC] + [VMEM_SPEC] * 5,
+    )(parity, receptances, sent_parts, kept_parts, sent_here, kept_here)
+    received, reads = lax.optimization_barrier((received, reads))
     entry = call(
         functools.partial(entry_kernel, bool(prefix)),
         entry_struct,
@@ -496,11 +556,10 @@
         in_specs=[SMEM_SPEC] + [VMEM_SPEC] * (1 + len(prefix)),
     )(later, received, *prefix)
     other = swapped(entry, "seq", 1)
-    w_across, other = lax.optimization_barrier((w_across, other))
+    kept_heads = call(kept_kernel, struct(bf16_lanes.shape, F32), mib=6, us=3)(entry, from_partner, *reads)
+    w_across, other, kept_heads = lax.optimization_barrier((w_across, other, kept_heads))
     w_opposite = swapped(w_across, "mp", 1)
-    joined = call(finish_kernel, bf16_lanes, mib=6)(
-        entry, from_partner, other, *reads, group_gain.reshape(1, width)
-    )
+    joined = call(finish_kernel, bf16_lanes, mib=6)(other, kept_heads, *reads, group_gain.reshape(1, width))
     joined_whole = lax.all_gather(joined, "mp", axis=2, tiled=True)
 
     w_blocks = (w_output, w_beside, w_across, w_opposite)

time: 67.2 us -> 65.4 us (0.973)
  waiting for transfers between devices: 10.3 us -> 6.94 us
  starting transfers between devices: 20.7 us -> 22.2 us
    ppermute x10, waiting for transfers between devices: 10.3 us -> 6.93 us  [swapped(): lax.ppermute(value, axis, [(i, i ^ mask) for i in range(lax.axis_size(axi...]
    ppermute x10, starting transfers between devices: 12.5 us -> 14 us  [swapped(): lax.ppermute(value, axis, [(i, i ^ mask) for i in range(lax.axis_size(axi...]
    pallas_call x2 -> x4, Pallas kernels: 6.7 us -> 7.5 us  [the longest x1 3.6 us: on_device(): call(functools.partial(chunk_kernel, False), (state_struct, parts_struct,...]
  transfers between devices with their start and end apart: 13 -> 13, of which waited for: 5 -> 5; matrix products, arithmetic and copies ran while one was open for 0% -> 0% of each run, Pallas kernels for 16% -> 17%
where the time goes in v8:
time: 65.4 us; the launch traced here: 65.2 us
  starting transfers between devices  22.2 us (34%)
  Pallas kernels  17.8 us (27%)
  blocking collectives  14.9 us (23%)
  waiting for transfers between devices  6.94 us (11%)
  local copies, waits for them, and re-layouts  2.29 us (4%)
  other arithmetic  0.69 us (1%)
    ppermute x10, starting transfers between devices, swapped(): lax.ppermute(value, axis, [(i, i ^ mask) for i in range(lax.axis_size(axi...  14 us
    all_gather x1, blocking collectives, on_device(): joined_whole = lax.all_gather(joined, 'mp', axis=2, tiled=True)  7.56 us
    all_gather x1, blocking collectives, on_device(): whole = lax.all_gather(local, 'mp', axis=2, tiled=True)  7.3 us
    ppermute x10, waiting for transfers between devices, swapped(): lax.ppermute(value, axis, [(i, i ^ mask) for i in range(lax.axis_size(axi...  6.93 us
    ppermute x1, starting transfers between devices, on_device(): rc_here = lax.ppermute(hidden_rc, 'seq', mirror)  6 us
    pallas_call x1, Pallas kernels, on_device(): call(functools.partial(chunk_kernel, True), (state_struct, parts_struct,...  4.28 us
    pallas_call x1, Pallas kernels, on_device(): call(functools.partial(chunk_kernel, False), (state_struct, parts_struct,...  3.6 us
    unnamed x40, local copies, waits for them, and re-layouts  2.29 us
  transfers between devices with their start and end apart: 13, of which 5 were waited for; matrix products, arithmetic and copies ran while one was open for 0% of the time, Pallas kernels for 17%

profile of v8, /device:TPU:0, one launch (start us, length us, event | category | flops | bytes accessed | tf_op | source)
XLA Modules:
  0.0 65.2 jit_solution(17110829975198242140)
XLA Ops:
  0.0 6.0 %collective-permute-start = (bf16[128,256]{1,0:T(8,128)(2,1)}, bf16[128,256]{1,0:T(8,128)(2,1)S(1)}, u32[]{:S(2)}, u32[]{:S(2)}) collective-permute-start(bf16[128,256]{1,0:T(8,128)(2,1)} %param.22), channel_id=1, source_target_pairs={{0,28},{4,24},{8,20},{12,16},{16,12},{20,8},{24,4},{28,0},{1,29},{... | collective-permute-start | bytes 196616 | tf_op jit(solution)/shard_map/ppermute | solution.py:452
  6.0 0.8 %copy-done.8 = bf16[128,256]{1,0:T(8,128)(2,1)S(1)} copy-done((bf16[128,256]{1,0:T(8,128)(2,1)S(1)}, bf16[128,256]{1,0:T(8,128)(2,1)}, u32[]{:S(2)}) %copy-start.8) | copy-done | bytes 65560
  6.8 0.7 %copy-done.12 = f32[4,256]{1,0:T(4,128)S(1)} copy-done((f32[4,256]{1,0:T(4,128)S(1)}, f32[4,256]{1,0:T(4,128)}, u32[]{:S(2)}) %copy-start.12) | copy-done | bytes 4120
  7.5 0.7 %copy-done.18 = s32[128]{0:T(128)S(1)} copy-done((s32[128]{0:T(128)S(1)}, s32[128]{0:T(128)}, u32[]{:S(2)}) %copy-start.18) | copy-done | bytes 536
  8.2 0.4 shard_map.190
  8.9 7.3 %all_gather.6.x_ref = bf16[2,128,1024]{2,1,0:T(8,128)(2,1)S(1)} all-gather(bf16[2,128,256]{2,1,0:T(8,128)(2,1)S(1)} %shard_map.191), channel_id=1, replica_groups=mesh['seq'=8,'mp'=4] {'mp'}, dimensions={2}, use_global_device_ids=true | all-gather | bytes 655360 | tf_op jit(solution)/shard_map/all_gather | solution.py:470
  16.3 1.5 %collective-permute-start.1 = (bf16[2,1024]{1,0:T(2,128)(2,1)S(1)}, bf16[2,1024]{1,0:T(2,128)(2,1)S(1)}, u32[]{:S(2)}, u32[]{:S(2)}) collective-permute-start(bf16[2,1024]{1,0:T(2,128)(2,1)S(1)} %bitcast.29), channel_id=1, source_target_pairs={{0,4},{4,0},{8,12},{12,8},{16,20},{20,16},{24,28},{28,24},{1,5},{5... | collective-permute-start | bytes 12296 | tf_op jit(solution)/shard_map/ppermute | solution.py:474
  17.8 0.6 collective-permute-start.2
  18.5 2.2 %shard_map.192 = (f32[4,128,256]{2,1,0:T(8,128)S(1)}, f32[4,128,256]{2,1,0:T(8,128)S(1)}, f32[4,128,256]{2,1,0:T(8,128)S(1)}, f32[4,128,256]{2,1,0:T(8,128)S(1)}...) custom-call(bf16[2,128,1024]{2,1,0:T(8,128)(2,1)S(1)} %all_gather.6.x_ref, ...), custom_call_target="tpu_custom_call" | custom-call | flops 10000000000 | bytes 10000000 | tf_op jit(solution)/shard_map/pallas_call | solution.py:487
  20.8 4.3 %shard_map.193 = (bf16[2,128,256]{2,1,0:T(8,128)(2,1)S(1)}, bf16[2,5,128,256]{3,2,1,0:T(8,128)(2,1)S(1)}, f32[2,136,256]{2,1,0:T(8,128)S(1)}, f32[4,4,256]{2,1,0:T(4,128)S(1)}, f32[4,1024]{1,0:T(4,128)S(1)}) custom-call(s32[1]{0:T(128)} %bitcast.1.direction_ref, f32[4,128,256]{2,1,0:T(8,128)S(1)} %get-tuple-element.51.refs_0_, ...), custom_call_target="tpu_custom_call" | custom-call | flops 10000000000 | bytes 10000000 | tf_op jit(solution)/shard_map/pallas_call | solution.py:501
  25.1 4.0 %collective-permute-start.3 = (bf16[2,128,256]{2,1,0:T(8,128)(2,1)S(1)}, bf16[2,128,256]{2,1,0:T(8,128)(2,1)S(1)}, u32[]{:S(2)}, u32[]{:S(2)}) collective-permute-start(bf16[2,128,256]{2,1,0:T(8,128)(2,1)S(1)} %get-tuple-element.59), channel_id=1, source_target_pairs={{0,4},{4,0},{8,12},{12,8},{16,20},{20,16},{24,28},{28,24},{1,5},{5... | collective-permute-start | bytes 393224 | tf_op jit(solution)/shard_map/ppermute | solution.py:421
  29.1 3.6 %shard_map.194 = (bf16[2,128,256]{2,1,0:T(8,128)(2,1)S(1)}, bf16[2,5,128,256]{3,2,1,0:T(8,128)(2,1)S(1)}, f32[2,136,256]{2,1,0:T(8,128)S(1)}) custom-call(s32[1]{0:T(128)S(6)} %sub.3.direction_ref, f32[4,128,256]{2,1,0:T(8,128)S(1)} %get-tuple-element.51.refs_0_, f32[4,128,256]{2,1,0:T(8,128)S(1)} %get-tuple-element.52.refs_1_, ...), custom_call_target="tpu_custom_call" | custom-call | flops 10000000000 | bytes 10000000 | tf_op jit(solution)/shard_map/pallas_call | solution.py:507
  32.7 0.2 shard_map.195.total_ref
  33.0 1.6 %collective-permute-start.5 = (bf16[2,128,256]{2,1,0:T(8,128)(2,1)S(1)}, bf16[2,128,256]{2,1,0:T(8,128)(2,1)S(1)}, u32[]{:S(2)}, u32[]{:S(2)}) collective-permute-start(bf16[2,128,256]{2,1,0:T(8,128)(2,1)S(1)} %shard_map.195.total_ref), channel_id=1, source_target_pairs={{0,8},{4,12},{8,0},{12,4},{16,24},{20,28},{24,16},{28,20},{1,9},{5... | collective-permute-start | bytes 393224 | tf_op jit(solution)/shard_map/ppermute | solution.py:421
  34.6 0.8 %collective-permute-start.4 = (bf16[256,1024]{1,0:T(8,128)(2,1)S(1)}, bf16[256,1024]{1,0:T(8,128)(2,1)S(1)}, u32[]{:S(2)}, u32[]{:S(2)}) collective-permute-start(bf16[256,1024]{1,0:T(8,128)(2,1)S(1)} %copy-done.5), channel_id=1, source_target_pairs={{0,2},{1,3},{2,0},{3,1},{4,6},{5,7},{6,4},{7,5},{8,10},{9,11},{10,... | collective-permute-start | bytes 1572872 | tf_op jit(solution)/shard_map/ppermute | solution.py:421
  35.5 0.8 %shard_map.196.receptances = f32[4,128,256]{2,1,0:T(8,128)S(1)} custom-call(f32[2,144,1024]{2,1,0:T(8,128)S(1)} %get-tuple-element.61.normed, f32[5,1024]{1,0:T(8,128)S(1)} %copy-done.11, f32[4,1024]{1,0:T(4,128)S(1)} %get-tuple-element.63.edge_ref, bf16[1024,256]{1,0:T(8,128)(2,1)S(1)} %copy-done.4), custom_call_target="tpu_custom_call" | custom-call | flops 3000000000 | bytes 3000000 | tf_op jit(solution)/shard_map/pallas_call | solution.py:517
  36.2 1.8 %collective-permute-done.5.from_ref = bf16[2,128,256]{2,1,0:T(8,128)(2,1)S(1)} collective-permute-done((bf16[2,128,256]{2,1,0:T(8,128)(2,1)S(1)}, bf16[2,128,256]{2,1,0:T(8,128)(2,1)S(1)}, u32[]{:S(2)}, u32[]{:S(2)}) %collective-permute-start.5) | collective-permute-done | bytes 131104 | tf_op jit(solution)/shard_map/ppermute | solution.py:421
  38.0 0.2 shard_map.197
  38.2 3.2 %collective-permute-start.6 = (bf16[2,64,256]{2,1,0:T(8,128)(2,1)S(1)}, bf16[2,64,256]{2,1,0:T(8,128)(2,1)S(1)}, u32[]{:S(2)}, u32[]{:S(2)}) collective-permute-start(bf16[2,64,256]{2,1,0:T(8,128)(2,1)S(1)} %get-tuple-element.65), channel_id=1, source_target_pairs={{0,16},{4,20},{8,24},{12,28},{16,0},{20,4},{24,8},{28,12},{1,17},{... | collective-permute-start | bytes 196616 | tf_op jit(solution)/shard_map/ppermute | solution.py:421
  41.4 2.1 %shard_map.198 = (f32[4,128,256]{2,1,0:T(8,128)S(1)}, bf16[4,128,256]{2,1,0:T(8,128)(2,1)S(1)}) custom-call(s32[1]{0:T(128)} %bitcast.1.direction_ref, f32[4,128,256]{2,1,0:T(8,128)S(1)} %shard_map.196.receptances, bf16[2,5,128,256]{3,2,1,0:T(8,128)(2,1)S(1)} %get-tuple-element.69.sent_ref, bf16[2,5,128,256]{3,2,1,0:T(8,128)(2,1)S(1)} %get-tuple-element.70.kept_ref, ...), custom_call_target="tpu_custom_call" | custom-call | flops 10000000000 | bytes 10000000 | tf_op jit(solution)/shard_map/pallas_call | solution.py:544
  43.8 2.3 %collective-permute-start.7 = (bf16[2,64,256]{2,1,0:T(8,128)(2,1)S(1)}, bf16[2,64,256]{2,1,0:T(8,128)(2,1)S(1)}, u32[]{:S(2)}, u32[]{:S(2)}) collective-permute-start(bf16[2,64,256]{2,1,0:T(8,128)(2,1)S(1)} %shard_map.199.entry_ref), channel_id=1, source_target_pairs={{0,4},{4,0},{8,12},{12,8},{16,20},{20,16},{24,28},{28,24},{1,5},{5... | collective-permute-start | bytes 196616 | tf_op jit(solution)/shard_map/ppermute | solution.py:421
  46.2 0.9 %shard_map.200.kept_ref = f32[2,128,256]{2,1,0:T(8,128)S(1)} custom-call(bf16[2,64,256]{2,1,0:T(8,128)(2,1)S(1)} %shard_map.199.entry_ref, bf16[2,128,256]{2,1,0:T(8,128)(2,1)S(1)} %collective-permute-done.3.from_ref, f32[4,128,256]{2,1,0:T(8,128)S(1)} %get-tuple-element.77.local_ref, bf16[4,128,256]{2,1,0:T(8,128)(2,1)S(1)} %get-tuple-element.78.map_ref), custom_call_target="tpu_custom_call" | custom-call | flops 3000000000 | bytes 3000000 | tf_op jit(solution)/shard_map/pallas_call | solution.py:559
  47.1 1.3 %collective-permute-done.7.other_ref = bf16[2,64,256]{2,1,0:T(8,128)(2,1)S(1)} collective-permute-done((bf16[2,64,256]{2,1,0:T(8,128)(2,1)S(1)}, bf16[2,64,256]{2,1,0:T(8,128)(2,1)S(1)}, u32[]{:S(2)}, u32[]{:S(2)}) %collective-permute-start.7) | collective-permute-done | bytes 65568 | tf_op jit(solution)/shard_map/ppermute | solution.py:421
  48.5 0.7 %shard_map.201 = bf16[2,128,256]{2,1,0:T(8,128)(2,1)S(1)} custom-call(bf16[2,64,256]{2,1,0:T(8,128)(2,1)S(1)} %collective-permute-done.7.other_ref, f32[2,128,256]{2,1,0:T(8,128)S(1)} %shard_map.200.kept_ref, f32[4,128,256]{2,1,0:T(8,128)S(1)} %get-tuple-element.77.local_ref, bf16[4,128,256]{2,1,0:T(8,128)(2,1)S(1)} %get-tuple-element.78.map_ref, ...), custom_call_target="tpu_custom_call" | custom-call | flops 10000000000 | bytes 10000000 | tf_op jit(solution)/shard_map/pallas_call | solution.py:562
  49.2 7.6 %all_gather.7.joined_ref = bf16[2,128,1024]{2,1,0:T(8,128)(2,1)S(1)} all-gather(bf16[2,128,256]{2,1,0:T(8,128)(2,1)S(1)} %shard_map.201), channel_id=1, replica_groups=mesh['seq'=8,'mp'=4] {'mp'}, dimensions={2}, use_global_device_ids=true | all-gather | bytes 655360 | tf_op jit(solution)/shard_map/all_gather | solution.py:563
  56.8 2.0 %shard_map.202 = (f32[128,256]{1,0:T(8,128)S(1)}, bf16[128,256]{1,0:T(8,128)(2,1)S(1)}, bf16[128,256]{1,0:T(8,128)(2,1)S(1)}, bf16[128,256]{1,0:T(8,128)(2,1)S(1)}) custom-call(s32[1]{0:T(128)} %bitcast.index_ref, bf16[2,128,1024]{2,1,0:T(8,128)(2,1)S(1)} %all_gather.7.joined_ref, bf16[2,128,1024]{2,1,0:T(8,128)(2,1)S(1)} %all_gather.6.x_ref, ...), custom_call_target="tpu_custom_call" | custom-call | flops 10000000000 | bytes 10000000 | tf_op jit(solution)/shard_map/pallas_call | solution.py:567
  58.9 0.4 collective-permute-start.10
  59.3 0.8 %collective-permute-start.11 = (bf16[128,256]{1,0:T(8,128)(2,1)S(1)}, bf16[128,256]{1,0:T(8,128)(2,1)S(1)}, u32[]{:S(2)}, u32[]{:S(2)}) collective-permute-start(bf16[128,256]{1,0:T(8,128)(2,1)S(1)} %get-tuple-element.85), channel_id=1, source_target_pairs={{0,2},{1,3},{2,0},{3,1},{4,6},{5,7},{6,4},{7,5},{8,10},{9,11},{10,... | collective-permute-start | bytes 196616 | tf_op jit(solution)/shard_map/ppermute | solution.py:421
  60.1 0.7 %collective-permute-start.12 = (bf16[128,256]{1,0:T(8,128)(2,1)S(1)}, bf16[128,256]{1,0:T(8,128)(2,1)S(1)}, u32[]{:S(2)}, u32[]{:S(2)}) collective-permute-start(bf16[128,256]{1,0:T(8,128)(2,1)S(1)} %get-tuple-element.86), channel_id=1, source_target_pairs={{0,3},{1,2},{2,1},{3,0},{4,7},{5,6},{6,5},{7,4},{8,11},{9,10},{10,... | collective-permute-start | bytes 196616 | tf_op jit(solution)/shard_map/ppermute | solution.py:421
  60.8 3.2 %collective-permute-done.11 = bf16[128,256]{1,0:T(8,128)(2,1)S(1)} collective-permute-done((bf16[128,256]{1,0:T(8,128)(2,1)S(1)}, bf16[128,256]{1,0:T(8,128)(2,1)S(1)}, u32[]{:S(2)}, u32[]{:S(2)}) %collective-permute-start.11) | collective-permute-done | bytes 65568 | tf_op jit(solution)/shard_map/ppermute | solution.py:421
  64.0 0.5 collective-permute-done.12
  64.5 0.7 %add_convert_fusion = bf16[128,256]{1,0:T(8,128)(2,1)} fusion(bf16[128,256]{1,0:T(8,128)(2,1)S(1)} %collective-permute-done.12, bf16[128,256]{1,0:T(8,128)(2,1)S(1)} %collective-permute-done.11, f32[128,256]{1,0:T(8,128)S(1)} %get-tuple-element.83, bf16[128,256]{1,0:T(8,128)(2,1)S(1)} %collective-permute-done.10), kind=kLoop, calls=%fused_computation | loop fusion | flops 229376 | bytes 393216 | tf_op jit(solution)/shard_map/convert_element_type | solution.py:580
  (51 shorter events, 0.6 us)
Async XLA Ops:
  0.0 8.6 %collective-permute-start = (bf16[128,256]{1,0:T(8,128)(2,1)}, bf16[128,256]{1,0:T(8,128)(2,1)S(1)}, u32[]{:S(2)}, u32[]{:S(2)}) collective-permute-start(bf16[128,256]{1,0:T(8,128)(2,1)} %param.22), channel_id=1, source_target_pairs={{0,28},{4,24},{8,20},{12,16},{16,12},{20,8},{24,4},{28,0},{1,29},{... | collective-permute-start | bytes 196616 | tf_op jit(solution)/shard_map/ppermute | solution.py:452
  6.0 0.8 %copy-start.8 = (bf16[128,256]{1,0:T(8,128)(2,1)S(1)}, bf16[128,256]{1,0:T(8,128)(2,1)}, u32[]{:S(2)}) copy-start(bf16[128,256]{1,0:T(8,128)(2,1)} %fwd_ref.1) | copy-start | bytes 196612
  6.8 0.7 %copy-start.12 = (f32[4,256]{1,0:T(4,128)S(1)}, f32[4,256]{1,0:T(4,128)}, u32[]{:S(2)}) copy-start(f32[4,256]{1,0:T(4,128)} %embed_ref.1) | copy-start | bytes 12292
  7.5 0.7 %copy-start.18 = (s32[128]{0:T(128)S(1)}, s32[128]{0:T(128)}, u32[]{:S(2)}) copy-start(s32[128]{0:T(128)} %param.20) | copy-start | bytes 1540
  8.7 9.8 %copy-start.2 = (bf16[1024,256]{1,0:T(8,128)(2,1)S(1)}, bf16[1024,256]{1,0:T(8,128)(2,1)}, u32[]{:S(2)}) copy-start(bf16[1024,256]{1,0:T(8,128)(2,1)} %refs_10_.1) | copy-start | bytes 1572868
  8.7 9.8 %copy-start.3 = (bf16[1024,256]{1,0:T(8,128)(2,1)S(1)}, bf16[1024,256]{1,0:T(8,128)(2,1)}, u32[]{:S(2)}) copy-start(bf16[1024,256]{1,0:T(8,128)(2,1)} %refs_11_.1) | copy-start | bytes 1572868
  8.7 9.8 %copy-start.6 = (bf16[1024,64]{0,1:T(8,128)(2,1)S(1)}, bf16[1024,64]{0,1:T(8,128)(2,1)}, u32[]{:S(2)}) copy-start(bf16[1024,64]{0,1:T(8,128)(2,1)} %param.30) | copy-start | bytes 393220
  8.7 9.8 %copy-start.7 = (bf16[1024,64]{0,1:T(8,128)(2,1)S(1)}, bf16[1024,64]{0,1:T(8,128)(2,1)}, u32[]{:S(2)}) copy-start(bf16[1024,64]{0,1:T(8,128)(2,1)} %param.33) | copy-start | bytes 393220
  8.7 9.8 %copy-start.9 = (bf16[64,256]{1,0:T(8,128)(2,1)S(1)}, bf16[64,256]{1,0:T(8,128)(2,1)}, u32[]{:S(2)}) copy-start(bf16[64,256]{1,0:T(8,128)(2,1)} %refs_12_.1) | copy-start | bytes 98308
  8.7 9.8 %copy-start.10 = (bf16[64,256]{1,0:T(8,128)(2,1)S(1)}, bf16[64,256]{1,0:T(8,128)(2,1)}, u32[]{:S(2)}) copy-start(bf16[64,256]{1,0:T(8,128)(2,1)} %refs_13_.1) | copy-start | bytes 98308
  8.7 9.8 %copy-start.11 = (f32[5,1024]{1,0:T(8,128)S(1)}, f32[5,1024]{1,0:T(8,128)}, u32[]{:S(2)}) copy-start(f32[5,1024]{1,0:T(8,128)} %mixing_ref.3) | copy-start | bytes 61444
  8.7 9.8 %copy-start.13 = (f32[1024]{0:T(1024)S(1)}, f32[1024]{0:T(1024)}, u32[]{:S(2)}) copy-start(f32[1024]{0:T(1024)} %param.24) | copy-start | bytes 12292
  8.7 9.8 %copy-start.15 = (f32[256]{0:T(256)S(1)}, f32[256]{0:T(256)}, u32[]{:S(2)}) copy-start(f32[256]{0:T(256)} %param.31) | copy-start | bytes 3076
  8.8 9.8 %copy-start.16 = (f32[256]{0:T(256)S(1)}, f32[256]{0:T(256)}, u32[]{:S(2)}) copy-start(f32[256]{0:T(256)} %param.34) | copy-start | bytes 3076
  16.3 4.5 %collective-permute-start.1 = (bf16[2,1024]{1,0:T(2,128)(2,1)S(1)}, bf16[2,1024]{1,0:T(2,128)(2,1)S(1)}, u32[]{:S(2)}, u32[]{:S(2)}) collective-permute-start(bf16[2,1024]{1,0:T(2,128)(2,1)S(1)} %bitcast.29), channel_id=1, source_target_pairs={{0,4},{4,0},{8,12},{12,8},{16,20},{20,16},{24,28},{28,24},{1,5},{5... | collective-permute-start | bytes 12296 | tf_op jit(solution)/shard_map/ppermute | solution.py:474
  17.8 3.0 %collective-permute-start.2 = (bf16[2,1024]{1,0:T(2,128)(2,1)S(1)}, bf16[2,1024]{1,0:T(2,128)(2,1)S(1)}, u32[]{:S(2)}, u32[]{:S(2)}) collective-permute-start(bf16[2,1024]{1,0:T(2,128)(2,1)S(1)} %bitcast.30), channel_id=1, source_target_pairs={{4,8},{12,16},{20,24},{8,4},{16,12},{24,20},{5,9},{13,17},{21,25},... | collective-permute-start | bytes 12296 | tf_op jit(solution)/shard_map/ppermute | solution.py:477
  25.1 7.7 %collective-permute-start.3 = (bf16[2,128,256]{2,1,0:T(8,128)(2,1)S(1)}, bf16[2,128,256]{2,1,0:T(8,128)(2,1)S(1)}, u32[]{:S(2)}, u32[]{:S(2)}) collective-permute-start(bf16[2,128,256]{2,1,0:T(8,128)(2,1)S(1)} %get-tuple-element.59), channel_id=1, source_target_pairs={{0,4},{4,0},{8,12},{12,8},{16,20},{20,16},{24,28},{28,24},{1,5},{5... | collective-permute-start | bytes 393224 | tf_op jit(solution)/shard_map/ppermute | solution.py:421
  32.7 1.9 %copy-start.5 = (bf16[256,1024]{1,0:T(8,128)(2,1)S(1)}, bf16[256,1024]{1,0:T(8,128)(2,1)}, u32[]{:S(2)}) copy-start(bf16[256,1024]{1,0:T(8,128)(2,1)} %refs_0_.1) | copy-start | bytes 1572868
  32.7 2.7 %copy-start.4 = (bf16[1024,256]{1,0:T(8,128)(2,1)S(1)}, bf16[1024,256]{1,0:T(8,128)(2,1)}, u32[]{:S(2)}) copy-start(bf16[1024,256]{1,0:T(8,128)(2,1)} %w_r.1) | copy-start | bytes 1572868
  33.0 5.0 %collective-permute-start.5 = (bf16[2,128,256]{2,1,0:T(8,128)(2,1)S(1)}, bf16[2,128,256]{2,1,0:T(8,128)(2,1)S(1)}, u32[]{:S(2)}, u32[]{:S(2)}) collective-permute-start(bf16[2,128,256]{2,1,0:T(8,128)(2,1)S(1)} %shard_map.195.total_ref), channel_id=1, source_target_pairs={{0,8},{4,12},{8,0},{12,4},{16,24},{20,28},{24,16},{28,20},{1,9},{5... | collective-permute-start | bytes 393224 | tf_op jit(solution)/shard_map/ppermute | solution.py:421
  34.6 13.8 %collective-permute-start.4 = (bf16[256,1024]{1,0:T(8,128)(2,1)S(1)}, bf16[256,1024]{1,0:T(8,128)(2,1)S(1)}, u32[]{:S(2)}, u32[]{:S(2)}) collective-permute-start(bf16[256,1024]{1,0:T(8,128)(2,1)S(1)} %copy-done.5), channel_id=1, source_target_pairs={{0,2},{1,3},{2,0},{3,1},{4,6},{5,7},{6,4},{7,5},{8,10},{9,11},{10,... | collective-permute-start | bytes 1572872 | tf_op jit(solution)/shard_map/ppermute | solution.py:421
  38.2 5.5 %collective-permute-start.6 = (bf16[2,64,256]{2,1,0:T(8,128)(2,1)S(1)}, bf16[2,64,256]{2,1,0:T(8,128)(2,1)S(1)}, u32[]{:S(2)}, u32[]{:S(2)}) collective-permute-start(bf16[2,64,256]{2,1,0:T(8,128)(2,1)S(1)} %get-tuple-element.65), channel_id=1, source_target_pairs={{0,16},{4,20},{8,24},{12,28},{16,0},{20,4},{24,8},{28,12},{1,17},{... | collective-permute-start | bytes 196616 | tf_op jit(solution)/shard_map/ppermute | solution.py:421
  41.4 15.4 %collective-permute-start.8 = (bf16[256,1024]{1,0:T(8,128)(2,1)S(1)}, bf16[256,1024]{1,0:T(8,128)(2,1)S(1)}, u32[]{:S(2)}, u32[]{:S(2)}) collective-permute-start(bf16[256,1024]{1,0:T(8,128)(2,1)S(1)} %copy-done.5), channel_id=1, source_target_pairs={{0,1},{1,0},{2,3},{3,2},{4,5},{5,4},{6,7},{7,6},{8,9},{9,8},{10,11... | collective-permute-start | bytes 1572872 | tf_op jit(solution)/shard_map/ppermute | solution.py:421
  43.8 4.6 %copy-start.17 = (f32[256]{0:T(256)S(1)}, f32[256]{0:T(256)}, u32[]{:S(2)}) copy-start(f32[256]{0:T(256)} %param.36) | copy-start | bytes 3076
  43.8 4.6 %collective-permute-start.7 = (bf16[2,64,256]{2,1,0:T(8,128)(2,1)S(1)}, bf16[2,64,256]{2,1,0:T(8,128)(2,1)S(1)}, u32[]{:S(2)}, u32[]{:S(2)}) collective-permute-start(bf16[2,64,256]{2,1,0:T(8,128)(2,1)S(1)} %shard_map.199.entry_ref), channel_id=1, source_target_pairs={{0,4},{4,0},{8,12},{12,8},{16,20},{20,16},{24,28},{28,24},{1,5},{5... | collective-permute-start | bytes 196616 | tf_op jit(solution)/shard_map/ppermute | solution.py:421
  48.4 8.4 %collective-permute-start.9 = (bf16[256,1024]{1,0:T(8,128)(2,1)S(1)}, bf16[256,1024]{1,0:T(8,128)(2,1)S(1)}, u32[]{:S(2)}, u32[]{:S(2)}) collective-permute-start(bf16[256,1024]{1,0:T(8,128)(2,1)S(1)} %collective-permute-done.4.refs_2_), channel_id=1, source_target_pairs={{0,1},{1,0},{2,3},{3,2},{4,5},{5,4},{6,7},{7,6},{8,9},{9,8},{10,11... | collective-permute-start | bytes 1572872 | tf_op jit(solution)/shard_map/ppermute | solution.py:421
  48.4 8.4 %copy-start = (bf16[1024,1024]{1,0:T(8,128)(2,1)S(1)}, bf16[1024,1024]{1,0:T(8,128)(2,1)}, u32[]{:S(2)}) copy-start(bf16[1024,1024]{1,0:T(8,128)(2,1)} %refs_4_.1) | copy-start | bytes 6291460
  48.4 8.3 %copy-start.1 = (bf16[1024,1024]{1,0:T(8,128)(2,1)S(1)}, bf16[1024,1024]{1,0:T(8,128)(2,1)}, u32[]{:S(2)}) copy-start(bf16[1024,1024]{1,0:T(8,128)(2,1)} %refs_5_.1) | copy-start | bytes 6291460
  48.5 8.3 %copy-start.14 = (f32[1024]{0:T(1024)S(1)}, f32[1024]{0:T(1024)}, u32[]{:S(2)}) copy-start(f32[1024]{0:T(1024)} %param.25) | copy-start | bytes 12292
  58.9 1.9 %collective-permute-start.10 = (bf16[128,256]{1,0:T(8,128)(2,1)S(1)}, bf16[128,256]{1,0:T(8,128)(2,1)S(1)}, u32[]{:S(2)}, u32[]{:S(2)}) collective-permute-start(bf16[128,256]{1,0:T(8,128)(2,1)S(1)} %get-tuple-element.84), channel_id=1, source_target_pairs={{0,1},{1,0},{2,3},{3,2},{4,5},{5,4},{6,7},{7,6},{8,9},{9,8},{10,11... | collective-permute-start | bytes 196616 | tf_op jit(solution)/shard_map/ppermute | solution.py:421
  59.3 4.7 %collective-permute-start.11 = (bf16[128,256]{1,0:T(8,128)(2,1)S(1)}, bf16[128,256]{1,0:T(8,128)(2,1)S(1)}, u32[]{:S(2)}, u32[]{:S(2)}) collective-permute-start(bf16[128,256]{1,0:T(8,128)(2,1)S(1)} %get-tuple-element.85), channel_id=1, source_target_pairs={{0,2},{1,3},{2,0},{3,1},{4,6},{5,7},{6,4},{7,5},{8,10},{9,11},{10,... | collective-permute-start | bytes 196616 | tf_op jit(solution)/shard_map/ppermute | solution.py:421
  60.1 4.4 %collective-permute-start.12 = (bf16[128,256]{1,0:T(8,128)(2,1)S(1)}, bf16[128,256]{1,0:T(8,128)(2,1)S(1)}, u32[]{:S(2)}, u32[]{:S(2)}) collective-permute-start(bf16[128,256]{1,0:T(8,128)(2,1)S(1)} %get-tuple-element.86), channel_id=1, source_target_pairs={{0,3},{1,2},{2,1},{3,0},{4,7},{5,6},{6,5},{7,4},{8,11},{9,10},{10,... | collective-permute-start | bytes 196616 | tf_op jit(solution)/shard_map/ppermute | solution.py:421

commit v9 on v8

--- a/solution.py
+++ b/solution.py
@@ -169,11 +169,14 @@
                     mixed[slot, place : place + step, :] = (center + change * weight).astype(BF16)
 
 
-def receptance_kernel(normed, mixing_ref, edge_ref, w_r, out_ref, mixed):
+def receptance_kernel(direction_ref, normed, mixing_ref, sent_edge_ref, kept_edge_ref, w_r, out_ref, mixed):
     groups, rows, _ = out_ref.shape
     blend(normed, mixing_ref, (0,), rows, mixed)
     out_ref[...] = mm(mixed[0], w_r[...]).reshape(out_ref.shape)
-    edges = mm(edge_ref[...].astype(BF16), w_r[...])
+    edges = [sent_edge_ref[...], kept_edge_ref[...]]
+    swap = direction_ref[0] == 1
+    edges = [jnp.where(swap, edges[1 - d], edges[d]) for d in range(2)]
+    edges = mm(jnp.concatenate(edges, axis=0).astype(BF16), w_r[...])
     for g in range(groups):
         row = 0 if g < groups // 2 else rows - 1
         out_ref[g, row : row + 1] = edges[g : g + 1]
@@ -183,34 +186,24 @@
     return jnp.concatenate([jnp.where(lane_head == h, value, 0.0).astype(BF16) for h in range(heads)], axis=0)
 
 
-def chunk_kernel(first, direction_ref, *refs):
-    lanes, refs = refs[:4], refs[4:]
-    if first:
-        partner_ref, beyond_ref, edge_ref, low_ref, gain_ref, mixing_ref, w_k, w_v, *gate_refs = refs[:12]
-        state_ref, parts_ref, here_ref, edges_ref, read_edge_ref = refs[12:]
-    else:
-        edges_ref, state_ref, parts_ref, here_ref = refs
+def chunk_kernel(direction_ref, *refs):
+    lanes, (halo_ref, edge_ref, low_ref, gain_ref, mixing_ref, w_k, w_v, *gate_refs) = refs[:4], refs[4:15]
+    state_ref, parts_ref, here_ref, read_edge_ref = refs[15:]
     strands, _, rows, width = parts_ref.shape
     heads = width // HEAD
     d = direction_ref[0]
-    if first:
-        center = edge_ref[...]
-        near, far = partner_ref[...].astype(F32), beyond_ref[...].astype(F32)
-        odd = d == 1
-        halo = jnp.concatenate([jnp.where(odd, near, far), jnp.where(odd, far, near)], axis=0)
-        halo = layer_norm(halo, gain_ref[...])
-        change = halo - center
-
-        def mix(index):
-            return (center + change * mixing_ref[index : index + 1, :]).astype(BF16)
-
-        edges_ref[0] = mm(mix(1), w_k[...])
-        edges_ref[1] = mm(mix(2), w_v[...])
-        low = mm_rows(jnp.concatenate([center, halo], axis=0).astype(BF16), low_ref[...])
-        half, count = low.shape[1] // 2, center.shape[0]
-        low = low[:count, :half] + low[count:, half:]
-        edges_ref[2], edges_ref[3] = gates(low, *[ref[...] for ref in gate_refs])
-        read_edge_ref[...] = center + change * mixing_ref[0:1, :]
+    center = jnp.where(d == 1, edge_ref[strands:], edge_ref[:strands])
+    halo = layer_norm(halo_ref[...].astype(F32), gain_ref[...])
+    change = halo - center
+
+    def mix(index):
+        return (center + change * mixing_ref[index : index + 1, :]).astype(BF16)
+
+    low = mm_rows(jnp.concatenate([center, halo], axis=0).astype(BF16), low_ref[...])
+    half = low.shape[1] // 2
+    low = low[:strands, :half] + low[strands:, half:]
+    edges = [mm(mix(1), w_k[...]), mm(mix(2), w_v[...]), *gates(low, *[ref[...] for ref in gate_refs])]
+    read_edge_ref[...] = center + change * mixing_ref[0:1, :]
     edge_row = d * (rows - 1)
     at_edge = ids_of((rows, width), 0) == edge_row
     order = (ids_of((rows, rows), 0) - ids_of((rows, rows), 1)) * (1 - 2 * d)
@@ -227,7 +220,7 @@
         g = d * strands + s
 
         def lane(index, ref):
-            return jnp.where(at_edge, edges_ref[index, pl.ds(g, 1), :], ref[g])
+            return jnp.where(at_edge, edges[index][s : s + 1], ref[g])
 
         key, value, log_decay, rate = [lane(index, ref) for index, ref in enumerate(lanes)]
         unit = key * lax.rsqrt(head_sum(key * key, ones) + UNIT_EPS)
@@ -471,7 +464,6 @@
     place = lax.axis_index("seq").astype(jnp.int32)
     parity = place % 2
     first, last = whole[:, 0], whole[:, rows - 1]
-    near = lax.ppermute(jnp.where(parity == 1, first, last), "seq", [(i, i ^ 1) for i in range(seq_count)])
     bridges = [(i, i + 1) for i in range(1, seq_count - 1, 2)]
     bridges += [(j, i) for i, j in bridges]
     far = lax.ppermute(jnp.where(parity == 1, last, first), "seq", bridges)
@@ -498,29 +490,32 @@
         ],
     )(whole, *params)
 
-    sent, sent_parts, sent_here, edges, read_edge = call(
-        functools.partial(chunk_kernel, True),
-        (state_struct, parts_struct, here_struct, struct((4, groups, width), F32), struct((groups, full), F32)),
-        in_specs=[SMEM_SPEC] + [VMEM_SPEC] * 16,
-    )(parity, *lanes, near, far, edge, low, *params[:4], *params[6:])
+    beside, _ = lax.optimization_barrier((jnp.where(parity == 1, first, last), edge))
+    near = swapped(beside, "seq", 1)
+
+    def chunk(direction, halo):
+        return call(
+            chunk_kernel,
+            (state_struct, parts_struct, here_struct, struct((strands, full), F32)),
+            in_specs=[SMEM_SPEC] + [VMEM_SPEC] * 15,
+        )(direction, *lanes, halo, edge, low, *params[:4], *params[6:])
+
+    sent, sent_parts, sent_here, sent_edge = chunk(parity, far)
     from_partner = swapped(sent, "seq", 1)
-    kept, kept_parts, kept_here = call(
-        functools.partial(chunk_kernel, False),
-        (state_struct, parts_struct, here_struct),
-        in_specs=[SMEM_SPEC] + [VMEM_SPEC] * 5,
-    )(1 - parity, *lanes, edges)
+    kept, kept_parts, kept_here, kept_edge = chunk(1 - parity, near)
 
     total = call(pair_kernel, state_struct, mib=4, us=1)(kept, from_partner)
     w_held, _ = lax.optimization_barrier((w_output, total))
     w_across = swapped(w_held, "mp", 2)
-    read_edge, _ = lax.optimization_barrier((read_edge, total))
+    kept_edge, _ = lax.optimization_barrier((kept_edge, total))
     receptances = call(
         receptance_kernel,
         f32_lanes,
         scratch=[pltpu.VMEM((1, groups * rows, full), BF16)],
         mib=6,
         us=3,
-    )(normed, mixing, read_edge, w_receptance)
+        in_specs=[SMEM_SPEC] + [VMEM_SPEC] * 5,
+    )(parity, normed, mixing, sent_edge, kept_edge, w_receptance)
     prefix = []
     bits = range(1, seq_count.bit_length() - 1)
     for bit in bits:

time: 65.4 us -> 65.1 us (level)
  starting transfers between devices: 22.2 us -> 20.2 us
  waiting for transfers between devices: 6.94 us -> 8.29 us
    ppermute x1 -> x0, starting transfers between devices: 1.52 us -> none  [on_device(): lax.ppermute(jnp.where(parity == 1, first, last), 'seq', [(i, i ^ 1) for...]
    ppermute x10 -> x11, waiting for transfers between devices: 6.93 us -> 8.28 us  [swapped(): lax.ppermute(value, axis, [(i, i ^ mask) for i in range(lax.axis_size(axi...]
    ppermute x10 -> x11, starting transfers between devices: 14 us -> 13.5 us  [swapped(): lax.ppermute(value, axis, [(i, i ^ mask) for i in range(lax.axis_size(axi...]
  transfers between devices with their start and end apart: 13 -> 13, of which waited for: 5 -> 5; matrix products, arithmetic and copies ran while one was open for 0% -> 0% of each run, Pallas kernels for 17% -> 24%
where the time goes in v9:
time: 65.1 us; the launch traced here: 64.9 us
  starting transfers between devices  20.2 us (31%)
  Pallas kernels  18.2 us (28%)
  blocking collectives  14.9 us (23%)
  waiting for transfers between devices  8.29 us (13%)
  local copies, waits for them, and re-layouts  2.29 us (4%)
  other arithmetic  0.69 us (1%)
    ppermute x11, starting transfers between devices, swapped(): lax.ppermute(value, axis, [(i, i ^ mask) for i in range(lax.axis_size(axi...  13.5 us
    ppermute x11, waiting for transfers between devices, swapped(): lax.ppermute(value, axis, [(i, i ^ mask) for i in range(lax.axis_size(axi...  8.28 us
    pallas_call x2, Pallas kernels, chunk(): call(chunk_kernel, (state_struct, parts_struct, here_struct, struct((stra...  8.22 us
    all_gather x1, blocking collectives, on_device(): joined_whole = lax.all_gather(joined, 'mp', axis=2, tiled=True)  7.56 us
    all_gather x1, blocking collectives, on_device(): whole = lax.all_gather(local, 'mp', axis=2, tiled=True)  7.3 us
    ppermute x1, starting transfers between devices, on_device(): rc_here = lax.ppermute(hidden_rc, 'seq', mirror)  6 us
    unnamed x40, local copies, waits for them, and re-layouts  2.29 us
    pallas_call x1, Pallas kernels, on_device(): call(project_kernel, (f32_lanes,) * 4 + (struct((strands, rows + 16, full...  2.2 us
  transfers between devices with their start and end apart: 13, of which 5 were waited for; matrix products, arithmetic and copies ran while one was open for 0% of the time, Pallas kernels for 24%

profile of v9, /device:TPU:0, one launch (start us, length us, event | category | flops | bytes accessed | tf_op | source)
XLA Modules:
  0.0 64.9 jit_solution(6766193304611071348)
XLA Ops:
  0.0 6.0 %collective-permute-start = (bf16[128,256]{1,0:T(8,128)(2,1)}, bf16[128,256]{1,0:T(8,128)(2,1)S(1)}, u32[]{:S(2)}, u32[]{:S(2)}) collective-permute-start(bf16[128,256]{1,0:T(8,128)(2,1)} %param.22), channel_id=1, source_target_pairs={{0,28},{4,24},{8,20},{12,16},{16,12},{20,8},{24,4},{28,0},{1,29},{... | collective-permute-start | bytes 196616 | tf_op jit(solution)/shard_map/ppermute | solution.py:445
  6.0 0.8 %copy-done.8 = bf16[128,256]{1,0:T(8,128)(2,1)S(1)} copy-done((bf16[128,256]{1,0:T(8,128)(2,1)S(1)}, bf16[128,256]{1,0:T(8,128)(2,1)}, u32[]{:S(2)}) %copy-start.8) | copy-done | bytes 65560
  6.8 0.7 %copy-done.12 = f32[4,256]{1,0:T(4,128)S(1)} copy-done((f32[4,256]{1,0:T(4,128)S(1)}, f32[4,256]{1,0:T(4,128)}, u32[]{:S(2)}) %copy-start.12) | copy-done | bytes 4120
  7.5 0.7 %copy-done.18 = s32[128]{0:T(128)S(1)} copy-done((s32[128]{0:T(128)S(1)}, s32[128]{0:T(128)}, u32[]{:S(2)}) %copy-start.18) | copy-done | bytes 536
  8.2 0.4 shard_map.190
  8.9 7.3 %all_gather.6.x_ref = bf16[2,128,1024]{2,1,0:T(8,128)(2,1)S(1)} all-gather(bf16[2,128,256]{2,1,0:T(8,128)(2,1)S(1)} %shard_map.191), channel_id=1, replica_groups=mesh['seq'=8,'mp'=4] {'mp'}, dimensions={2}, use_global_device_ids=true | all-gather | bytes 655360 | tf_op jit(solution)/shard_map/all_gather | solution.py:463
  16.3 0.7 %collective-permute-start.2 = (bf16[2,1024]{1,0:T(2,128)(2,1)S(1)}, bf16[2,1024]{1,0:T(2,128)(2,1)S(1)}, u32[]{:S(2)}, u32[]{:S(2)}) collective-permute-start(bf16[2,1024]{1,0:T(2,128)(2,1)S(1)} %bitcast.33), channel_id=1, source_target_pairs={{4,8},{12,16},{20,24},{8,4},{16,12},{24,20},{5,9},{13,17},{21,25},... | collective-permute-start | bytes 12296 | tf_op jit(solution)/shard_map/ppermute | solution.py:469
  17.0 2.2 %shard_map.192 = (f32[4,128,256]{2,1,0:T(8,128)S(1)}, f32[4,128,256]{2,1,0:T(8,128)S(1)}, f32[4,128,256]{2,1,0:T(8,128)S(1)}, f32[4,128,256]{2,1,0:T(8,128)S(1)}...) custom-call(bf16[2,128,1024]{2,1,0:T(8,128)(2,1)S(1)} %all_gather.6.x_ref, ...), custom_call_target="tpu_custom_call" | custom-call | flops 10000000000 | bytes 10000000 | tf_op jit(solution)/shard_map/pallas_call | solution.py:479
  19.3 3.7 %collective-permute-start.1 = (bf16[2,1024]{1,0:T(2,128)(2,1)S(1)}, bf16[2,1024]{1,0:T(2,128)(2,1)S(1)}, u32[]{:S(2)}, u32[]{:S(2)}) collective-permute-start(bf16[2,1024]{1,0:T(2,128)(2,1)S(1)} %bitcast.34), channel_id=1, source_target_pairs={{0,4},{4,0},{8,12},{12,8},{16,20},{20,16},{24,28},{28,24},{1,5},{5... | collective-permute-start | bytes 12296 | tf_op jit(solution)/shard_map/ppermute | solution.py:414
  22.9 4.1 %shard_map.194 = (bf16[2,128,256]{2,1,0:T(8,128)(2,1)S(1)}, bf16[2,5,128,256]{3,2,1,0:T(8,128)(2,1)S(1)}, f32[2,136,256]{2,1,0:T(8,128)S(1)}, f32[2,1024]{1,0:T(2,128)S(1)}) custom-call(s32[1]{0:T(128)} %bitcast.1.direction_ref, f32[4,128,256]{2,1,0:T(8,128)S(1)} %get-tuple-element.52.refs_0_, f32[4,128,256]{2,1,0:T(8,128)S(1)} %get-tuple-element.53.refs_1_, ...), custom_call_target="tpu_custom_call" | custom-call | flops 10000000000 | bytes 10000000 | tf_op jit(solution)/shard_map/pallas_call | solution.py:497
  27.0 1.3 %collective-permute-start.3 = (bf16[2,128,256]{2,1,0:T(8,128)(2,1)S(1)}, bf16[2,128,256]{2,1,0:T(8,128)(2,1)S(1)}, u32[]{:S(2)}, u32[]{:S(2)}) collective-permute-start(bf16[2,128,256]{2,1,0:T(8,128)(2,1)S(1)} %get-tuple-element.60), channel_id=1, source_target_pairs={{0,4},{4,0},{8,12},{12,8},{16,20},{20,16},{24,28},{28,24},{1,5},{5... | collective-permute-start | bytes 393224 | tf_op jit(solution)/shard_map/ppermute | solution.py:414
  28.3 4.1 %shard_map.193 = (bf16[2,128,256]{2,1,0:T(8,128)(2,1)S(1)}, bf16[2,5,128,256]{3,2,1,0:T(8,128)(2,1)S(1)}, f32[2,136,256]{2,1,0:T(8,128)S(1)}, f32[2,1024]{1,0:T(2,128)S(1)}) custom-call(s32[1]{0:T(128)S(6)} %sub.3.direction_ref, f32[4,128,256]{2,1,0:T(8,128)S(1)} %get-tuple-element.52.refs_0_, f32[4,128,256]{2,1,0:T(8,128)S(1)} %get-tuple-element.53.refs_1_, ...), custom_call_target="tpu_custom_call" | custom-call | flops 10000000000 | bytes 10000000 | tf_op jit(solution)/shard_map/pallas_call | solution.py:497
  32.4 0.2 shard_map.195.total_ref
  32.7 1.5 %collective-permute-start.5 = (bf16[2,128,256]{2,1,0:T(8,128)(2,1)S(1)}, bf16[2,128,256]{2,1,0:T(8,128)(2,1)S(1)}, u32[]{:S(2)}, u32[]{:S(2)}) collective-permute-start(bf16[2,128,256]{2,1,0:T(8,128)(2,1)S(1)} %shard_map.195.total_ref), channel_id=1, source_target_pairs={{0,8},{4,12},{8,0},{12,4},{16,24},{20,28},{24,16},{28,20},{1,9},{5... | collective-permute-start | bytes 393224 | tf_op jit(solution)/shard_map/ppermute | solution.py:414
  34.1 0.8 %collective-permute-start.4 = (bf16[256,1024]{1,0:T(8,128)(2,1)S(1)}, bf16[256,1024]{1,0:T(8,128)(2,1)S(1)}, u32[]{:S(2)}, u32[]{:S(2)}) collective-permute-start(bf16[256,1024]{1,0:T(8,128)(2,1)S(1)} %copy-done.5), channel_id=1, source_target_pairs={{0,2},{1,3},{2,0},{3,1},{4,6},{5,7},{6,4},{7,5},{8,10},{9,11},{10,... | collective-permute-start | bytes 1572872 | tf_op jit(solution)/shard_map/ppermute | solution.py:414
  35.0 0.8 %shard_map.196.receptances = f32[4,128,256]{2,1,0:T(8,128)S(1)} custom-call(s32[1]{0:T(128)} %bitcast.1.direction_ref, f32[2,144,1024]{2,1,0:T(8,128)S(1)} %get-tuple-element.62.normed, f32[5,1024]{1,0:T(8,128)S(1)} %copy-done.11, f32[2,1024]{1,0:T(2,128)S(1)} %get-tuple-element.63.sent_edge_ref, f32[2,1024]{1,0:T(2,128)S(1)} %get-tuple-element.65.kept_edge_ref, ...), custom_call_target="tpu_custom_call" | custom-call | flops 3000000000 | bytes 3000000 | tf_op jit(solution)/shard_map/pallas_call | solution.py:511
  35.8 1.9 %collective-permute-done.5.from_ref = bf16[2,128,256]{2,1,0:T(8,128)(2,1)S(1)} collective-permute-done((bf16[2,128,256]{2,1,0:T(8,128)(2,1)S(1)}, bf16[2,128,256]{2,1,0:T(8,128)(2,1)S(1)}, u32[]{:S(2)}, u32[]{:S(2)}) %collective-permute-start.5) | collective-permute-done | bytes 131104 | tf_op jit(solution)/shard_map/ppermute | solution.py:414
  37.7 0.2 shard_map.197
  37.9 3.1 %collective-permute-start.6 = (bf16[2,64,256]{2,1,0:T(8,128)(2,1)S(1)}, bf16[2,64,256]{2,1,0:T(8,128)(2,1)S(1)}, u32[]{:S(2)}, u32[]{:S(2)}) collective-permute-start(bf16[2,64,256]{2,1,0:T(8,128)(2,1)S(1)} %get-tuple-element.67), channel_id=1, source_target_pairs={{0,16},{4,20},{8,24},{12,28},{16,0},{20,4},{24,8},{28,12},{1,17},{... | collective-permute-start | bytes 196616 | tf_op jit(solution)/shard_map/ppermute | solution.py:414
  41.0 2.1 %shard_map.198 = (f32[4,128,256]{2,1,0:T(8,128)S(1)}, bf16[4,128,256]{2,1,0:T(8,128)(2,1)S(1)}) custom-call(s32[1]{0:T(128)} %bitcast.1.direction_ref, f32[4,128,256]{2,1,0:T(8,128)S(1)} %shard_map.196.receptances, bf16[2,5,128,256]{3,2,1,0:T(8,128)(2,1)S(1)} %get-tuple-element.71.sent_ref, bf16[2,5,128,256]{3,2,1,0:T(8,128)(2,1)S(1)} %get-tuple-element.72.kept_ref, ...), custom_call_target="tpu_custom_call" | custom-call | flops 10000000000 | bytes 10000000 | tf_op jit(solution)/shard_map/pallas_call | solution.py:539
  43.2 0.2 shard_map.199.entry_ref
  43.4 1.1 %collective-permute-start.7 = (bf16[2,64,256]{2,1,0:T(8,128)(2,1)S(1)}, bf16[2,64,256]{2,1,0:T(8,128)(2,1)S(1)}, u32[]{:S(2)}, u32[]{:S(2)}) collective-permute-start(bf16[2,64,256]{2,1,0:T(8,128)(2,1)S(1)} %shard_map.199.entry_ref), channel_id=1, source_target_pairs={{0,4},{4,0},{8,12},{12,8},{16,20},{20,16},{24,28},{28,24},{1,5},{5... | collective-permute-start | bytes 196616 | tf_op jit(solution)/shard_map/ppermute | solution.py:414
  44.6 0.9 %shard_map.200.kept_ref = f32[2,128,256]{2,1,0:T(8,128)S(1)} custom-call(bf16[2,64,256]{2,1,0:T(8,128)(2,1)S(1)} %shard_map.199.entry_ref, bf16[2,128,256]{2,1,0:T(8,128)(2,1)S(1)} %collective-permute-done.3.from_ref, f32[4,128,256]{2,1,0:T(8,128)S(1)} %get-tuple-element.79.local_ref, bf16[4,128,256]{2,1,0:T(8,128)(2,1)S(1)} %get-tuple-element.80.map_ref), custom_call_target="tpu_custom_call" | custom-call | flops 3000000000 | bytes 3000000 | tf_op jit(solution)/shard_map/pallas_call | solution.py:554
  45.5 2.4 %collective-permute-done.7.other_ref = bf16[2,64,256]{2,1,0:T(8,128)(2,1)S(1)} collective-permute-done((bf16[2,64,256]{2,1,0:T(8,128)(2,1)S(1)}, bf16[2,64,256]{2,1,0:T(8,128)(2,1)S(1)}, u32[]{:S(2)}, u32[]{:S(2)}) %collective-permute-start.7) | collective-permute-done | bytes 65568 | tf_op jit(solution)/shard_map/ppermute | solution.py:414
  47.9 0.7 %shard_map.201 = bf16[2,128,256]{2,1,0:T(8,128)(2,1)S(1)} custom-call(bf16[2,64,256]{2,1,0:T(8,128)(2,1)S(1)} %collective-permute-done.7.other_ref, f32[2,128,256]{2,1,0:T(8,128)S(1)} %shard_map.200.kept_ref, f32[4,128,256]{2,1,0:T(8,128)S(1)} %get-tuple-element.79.local_ref, bf16[4,128,256]{2,1,0:T(8,128)(2,1)S(1)} %get-tuple-element.80.map_ref, ...), custom_call_target="tpu_custom_call" | custom-call | flops 10000000000 | bytes 10000000 | tf_op jit(solution)/shard_map/pallas_call | solution.py:557
  48.7 7.6 %all_gather.7.joined_ref = bf16[2,128,1024]{2,1,0:T(8,128)(2,1)S(1)} all-gather(bf16[2,128,256]{2,1,0:T(8,128)(2,1)S(1)} %shard_map.201), channel_id=1, replica_groups=mesh['seq'=8,'mp'=4] {'mp'}, dimensions={2}, use_global_device_ids=true | all-gather | bytes 655360 | tf_op jit(solution)/shard_map/all_gather | solution.py:558
  56.3 2.0 %shard_map.202 = (f32[128,256]{1,0:T(8,128)S(1)}, bf16[128,256]{1,0:T(8,128)(2,1)S(1)}, bf16[128,256]{1,0:T(8,128)(2,1)S(1)}, bf16[128,256]{1,0:T(8,128)(2,1)S(1)}) custom-call(s32[1]{0:T(128)} %bitcast.index_ref, bf16[2,128,1024]{2,1,0:T(8,128)(2,1)S(1)} %all_gather.7.joined_ref, bf16[2,128,1024]{2,1,0:T(8,128)(2,1)S(1)} %all_gather.6.x_ref, ...), custom_call_target="tpu_custom_call" | custom-call | flops 10000000000 | bytes 10000000 | tf_op jit(solution)/shard_map/pallas_call | solution.py:562
  58.3 0.8 %collective-permute-start.12 = (bf16[128,256]{1,0:T(8,128)(2,1)S(1)}, bf16[128,256]{1,0:T(8,128)(2,1)S(1)}, u32[]{:S(2)}, u32[]{:S(2)}) collective-permute-start(bf16[128,256]{1,0:T(8,128)(2,1)S(1)} %get-tuple-element.88), channel_id=1, source_target_pairs={{0,3},{1,2},{2,1},{3,0},{4,7},{5,6},{6,5},{7,4},{8,11},{9,10},{10,... | collective-permute-start | bytes 196616 | tf_op jit(solution)/shard_map/ppermute | solution.py:414
  59.2 1.2 %collective-permute-start.11 = (bf16[128,256]{1,0:T(8,128)(2,1)S(1)}, bf16[128,256]{1,0:T(8,128)(2,1)S(1)}, u32[]{:S(2)}, u32[]{:S(2)}) collective-permute-start(bf16[128,256]{1,0:T(8,128)(2,1)S(1)} %get-tuple-element.87), channel_id=1, source_target_pairs={{0,2},{1,3},{2,0},{3,1},{4,6},{5,7},{6,4},{7,5},{8,10},{9,11},{10,... | collective-permute-start | bytes 196616 | tf_op jit(solution)/shard_map/ppermute | solution.py:414
  60.4 1.9 %collective-permute-done.12 = bf16[128,256]{1,0:T(8,128)(2,1)S(1)} collective-permute-done((bf16[128,256]{1,0:T(8,128)(2,1)S(1)}, bf16[128,256]{1,0:T(8,128)(2,1)S(1)}, u32[]{:S(2)}, u32[]{:S(2)}) %collective-permute-start.12) | collective-permute-done | bytes 65568 | tf_op jit(solution)/shard_map/ppermute | solution.py:414
  62.3 1.9 %collective-permute-done.11 = bf16[128,256]{1,0:T(8,128)(2,1)S(1)} collective-permute-done((bf16[128,256]{1,0:T(8,128)(2,1)S(1)}, bf16[128,256]{1,0:T(8,128)(2,1)S(1)}, u32[]{:S(2)}, u32[]{:S(2)}) %collective-permute-start.11) | collective-permute-done | bytes 65568 | tf_op jit(solution)/shard_map/ppermute | solution.py:414
  64.2 0.7 %add_convert_fusion = bf16[128,256]{1,0:T(8,128)(2,1)} fusion(bf16[128,256]{1,0:T(8,128)(2,1)S(1)} %collective-permute-done.12, bf16[128,256]{1,0:T(8,128)(2,1)S(1)} %collective-permute-done.11, f32[128,256]{1,0:T(8,128)S(1)} %get-tuple-element.85, bf16[128,256]{1,0:T(8,128)(2,1)S(1)} %collective-permute-done.10), kind=kLoop, calls=%fused_computation | loop fusion | flops 229376 | bytes 393216 | tf_op jit(solution)/shard_map/convert_element_type | solution.py:575
  (51 shorter events, 0.4 us)
Async XLA Ops:
  0.0 8.6 %collective-permute-start = (bf16[128,256]{1,0:T(8,128)(2,1)}, bf16[128,256]{1,0:T(8,128)(2,1)S(1)}, u32[]{:S(2)}, u32[]{:S(2)}) collective-permute-start(bf16[128,256]{1,0:T(8,128)(2,1)} %param.22), channel_id=1, source_target_pairs={{0,28},{4,24},{8,20},{12,16},{16,12},{20,8},{24,4},{28,0},{1,29},{... | collective-permute-start | bytes 196616 | tf_op jit(solution)/shard_map/ppermute | solution.py:445
  6.0 0.8 %copy-start.8 = (bf16[128,256]{1,0:T(8,128)(2,1)S(1)}, bf16[128,256]{1,0:T(8,128)(2,1)}, u32[]{:S(2)}) copy-start(bf16[128,256]{1,0:T(8,128)(2,1)} %fwd_ref.1) | copy-start | bytes 196612
  6.8 0.7 %copy-start.12 = (f32[4,256]{1,0:T(4,128)S(1)}, f32[4,256]{1,0:T(4,128)}, u32[]{:S(2)}) copy-start(f32[4,256]{1,0:T(4,128)} %embed_ref.1) | copy-start | bytes 12292
  7.5 0.7 %copy-start.18 = (s32[128]{0:T(128)S(1)}, s32[128]{0:T(128)}, u32[]{:S(2)}) copy-start(s32[128]{0:T(128)} %param.20) | copy-start | bytes 1540
  8.7 8.3 %copy-start.2 = (bf16[1024,256]{1,0:T(8,128)(2,1)S(1)}, bf16[1024,256]{1,0:T(8,128)(2,1)}, u32[]{:S(2)}) copy-start(bf16[1024,256]{1,0:T(8,128)(2,1)} %refs_9_.3) | copy-start | bytes 1572868
  8.7 8.3 %copy-start.3 = (bf16[1024,256]{1,0:T(8,128)(2,1)S(1)}, bf16[1024,256]{1,0:T(8,128)(2,1)}, u32[]{:S(2)}) copy-start(bf16[1024,256]{1,0:T(8,128)(2,1)} %refs_10_.3) | copy-start | bytes 1572868
  8.7 8.3 %copy-start.6 = (bf16[1024,64]{0,1:T(8,128)(2,1)S(1)}, bf16[1024,64]{0,1:T(8,128)(2,1)}, u32[]{:S(2)}) copy-start(bf16[1024,64]{0,1:T(8,128)(2,1)} %param.30) | copy-start | bytes 393220
  8.7 8.3 %copy-start.7 = (bf16[1024,64]{0,1:T(8,128)(2,1)S(1)}, bf16[1024,64]{0,1:T(8,128)(2,1)}, u32[]{:S(2)}) copy-start(bf16[1024,64]{0,1:T(8,128)(2,1)} %param.33) | copy-start | bytes 393220
  8.7 8.3 %copy-start.9 = (bf16[64,256]{1,0:T(8,128)(2,1)S(1)}, bf16[64,256]{1,0:T(8,128)(2,1)}, u32[]{:S(2)}) copy-start(bf16[64,256]{1,0:T(8,128)(2,1)} %refs_11_.3) | copy-start | bytes 98308
  8.7 8.3 %copy-start.10 = (bf16[64,256]{1,0:T(8,128)(2,1)S(1)}, bf16[64,256]{1,0:T(8,128)(2,1)}, u32[]{:S(2)}) copy-start(bf16[64,256]{1,0:T(8,128)(2,1)} %refs_12_.3) | copy-start | bytes 98308
  8.7 8.3 %copy-start.11 = (f32[5,1024]{1,0:T(8,128)S(1)}, f32[5,1024]{1,0:T(8,128)}, u32[]{:S(2)}) copy-start(f32[5,1024]{1,0:T(8,128)} %mixing_ref.3) | copy-start | bytes 61444
  8.7 8.3 %copy-start.13 = (f32[1024]{0:T(1024)S(1)}, f32[1024]{0:T(1024)}, u32[]{:S(2)}) copy-start(f32[1024]{0:T(1024)} %param.24) | copy-start | bytes 12292
  8.8 8.3 %copy-start.15 = (f32[256]{0:T(256)S(1)}, f32[256]{0:T(256)}, u32[]{:S(2)}) copy-start(f32[256]{0:T(256)} %param.31) | copy-start | bytes 3076
  8.8 8.3 %copy-start.16 = (f32[256]{0:T(256)S(1)}, f32[256]{0:T(256)}, u32[]{:S(2)}) copy-start(f32[256]{0:T(256)} %param.34) | copy-start | bytes 3076
  16.3 6.6 %collective-permute-start.2 = (bf16[2,1024]{1,0:T(2,128)(2,1)S(1)}, bf16[2,1024]{1,0:T(2,128)(2,1)S(1)}, u32[]{:S(2)}, u32[]{:S(2)}) collective-permute-start(bf16[2,1024]{1,0:T(2,128)(2,1)S(1)} %bitcast.33), channel_id=1, source_target_pairs={{4,8},{12,16},{20,24},{8,4},{16,12},{24,20},{5,9},{13,17},{21,25},... | collective-permute-start | bytes 12296 | tf_op jit(solution)/shard_map/ppermute | solution.py:469
  19.3 9.0 %collective-permute-start.1 = (bf16[2,1024]{1,0:T(2,128)(2,1)S(1)}, bf16[2,1024]{1,0:T(2,128)(2,1)S(1)}, u32[]{:S(2)}, u32[]{:S(2)}) collective-permute-start(bf16[2,1024]{1,0:T(2,128)(2,1)S(1)} %bitcast.34), channel_id=1, source_target_pairs={{0,4},{4,0},{8,12},{12,8},{16,20},{20,16},{24,28},{28,24},{1,5},{5... | collective-permute-start | bytes 12296 | tf_op jit(solution)/shard_map/ppermute | solution.py:414
  27.0 5.4 %collective-permute-start.3 = (bf16[2,128,256]{2,1,0:T(8,128)(2,1)S(1)}, bf16[2,128,256]{2,1,0:T(8,128)(2,1)S(1)}, u32[]{:S(2)}, u32[]{:S(2)}) collective-permute-start(bf16[2,128,256]{2,1,0:T(8,128)(2,1)S(1)} %get-tuple-element.60), channel_id=1, source_target_pairs={{0,4},{4,0},{8,12},{12,8},{16,20},{20,16},{24,28},{28,24},{1,5},{5... | collective-permute-start | bytes 393224 | tf_op jit(solution)/shard_map/ppermute | solution.py:414
  32.4 1.7 %copy-start.5 = (bf16[256,1024]{1,0:T(8,128)(2,1)S(1)}, bf16[256,1024]{1,0:T(8,128)(2,1)}, u32[]{:S(2)}) copy-start(bf16[256,1024]{1,0:T(8,128)(2,1)} %refs_0_.1) | copy-start | bytes 1572868
  32.4 2.5 %copy-start.4 = (bf16[1024,256]{1,0:T(8,128)(2,1)S(1)}, bf16[1024,256]{1,0:T(8,128)(2,1)}, u32[]{:S(2)}) copy-start(bf16[1024,256]{1,0:T(8,128)(2,1)} %w_r.1) | copy-start | bytes 1572868
  32.7 5.0 %collective-permute-start.5 = (bf16[2,128,256]{2,1,0:T(8,128)(2,1)S(1)}, bf16[2,128,256]{2,1,0:T(8,128)(2,1)S(1)}, u32[]{:S(2)}, u32[]{:S(2)}) collective-permute-start(bf16[2,128,256]{2,1,0:T(8,128)(2,1)S(1)} %shard_map.195.total_ref), channel_id=1, source_target_pairs={{0,8},{4,12},{8,0},{12,4},{16,24},{20,28},{24,16},{28,20},{1,9},{5... | collective-permute-start | bytes 393224 | tf_op jit(solution)/shard_map/ppermute | solution.py:414
  34.1 13.8 %collective-permute-start.4 = (bf16[256,1024]{1,0:T(8,128)(2,1)S(1)}, bf16[256,1024]{1,0:T(8,128)(2,1)S(1)}, u32[]{:S(2)}, u32[]{:S(2)}) collective-permute-start(bf16[256,1024]{1,0:T(8,128)(2,1)S(1)} %copy-done.5), channel_id=1, source_target_pairs={{0,2},{1,3},{2,0},{3,1},{4,6},{5,7},{6,4},{7,5},{8,10},{9,11},{10,... | collective-permute-start | bytes 1572872 | tf_op jit(solution)/shard_map/ppermute | solution.py:414
  37.9 5.4 %collective-permute-start.6 = (bf16[2,64,256]{2,1,0:T(8,128)(2,1)S(1)}, bf16[2,64,256]{2,1,0:T(8,128)(2,1)S(1)}, u32[]{:S(2)}, u32[]{:S(2)}) collective-permute-start(bf16[2,64,256]{2,1,0:T(8,128)(2,1)S(1)} %get-tuple-element.67), channel_id=1, source_target_pairs={{0,16},{4,20},{8,24},{12,28},{16,0},{20,4},{24,8},{28,12},{1,17},{... | collective-permute-start | bytes 196616 | tf_op jit(solution)/shard_map/ppermute | solution.py:414
  41.0 15.3 %collective-permute-start.8 = (bf16[256,1024]{1,0:T(8,128)(2,1)S(1)}, bf16[256,1024]{1,0:T(8,128)(2,1)S(1)}, u32[]{:S(2)}, u32[]{:S(2)}) collective-permute-start(bf16[256,1024]{1,0:T(8,128)(2,1)S(1)} %copy-done.5), channel_id=1, source_target_pairs={{0,1},{1,0},{2,3},{3,2},{4,5},{5,4},{6,7},{7,6},{8,9},{9,8},{10,11... | collective-permute-start | bytes 1572872 | tf_op jit(solution)/shard_map/ppermute | solution.py:414
  43.4 4.5 %copy-start.17 = (f32[256]{0:T(256)S(1)}, f32[256]{0:T(256)}, u32[]{:S(2)}) copy-start(f32[256]{0:T(256)} %param.36) | copy-start | bytes 3076
  43.4 4.5 %collective-permute-start.7 = (bf16[2,64,256]{2,1,0:T(8,128)(2,1)S(1)}, bf16[2,64,256]{2,1,0:T(8,128)(2,1)S(1)}, u32[]{:S(2)}, u32[]{:S(2)}) collective-permute-start(bf16[2,64,256]{2,1,0:T(8,128)(2,1)S(1)} %shard_map.199.entry_ref), channel_id=1, source_target_pairs={{0,4},{4,0},{8,12},{12,8},{16,20},{20,16},{24,28},{28,24},{1,5},{5... | collective-permute-start | bytes 196616 | tf_op jit(solution)/shard_map/ppermute | solution.py:414
  47.9 8.4 %collective-permute-start.9 = (bf16[256,1024]{1,0:T(8,128)(2,1)S(1)}, bf16[256,1024]{1,0:T(8,128)(2,1)S(1)}, u32[]{:S(2)}, u32[]{:S(2)}) collective-permute-start(bf16[256,1024]{1,0:T(8,128)(2,1)S(1)} %collective-permute-done.4.refs_2_), channel_id=1, source_target_pairs={{0,1},{1,0},{2,3},{3,2},{4,5},{5,4},{6,7},{7,6},{8,9},{9,8},{10,11... | collective-permute-start | bytes 1572872 | tf_op jit(solution)/shard_map/ppermute | solution.py:414
  47.9 8.4 %copy-start = (bf16[1024,1024]{1,0:T(8,128)(2,1)S(1)}, bf16[1024,1024]{1,0:T(8,128)(2,1)}, u32[]{:S(2)}) copy-start(bf16[1024,1024]{1,0:T(8,128)(2,1)} %refs_4_.1) | copy-start | bytes 6291460
  47.9 8.3 %copy-start.1 = (bf16[1024,1024]{1,0:T(8,128)(2,1)S(1)}, bf16[1024,1024]{1,0:T(8,128)(2,1)}, u32[]{:S(2)}) copy-start(bf16[1024,1024]{1,0:T(8,128)(2,1)} %refs_5_.1) | copy-start | bytes 6291460
  47.9 8.3 %copy-start.14 = (f32[1024]{0:T(1024)S(1)}, f32[1024]{0:T(1024)}, u32[]{:S(2)}) copy-start(f32[1024]{0:T(1024)} %param.25) | copy-start | bytes 12292
  58.3 4.0 %collective-permute-start.12 = (bf16[128,256]{1,0:T(8,128)(2,1)S(1)}, bf16[128,256]{1,0:T(8,128)(2,1)S(1)}, u32[]{:S(2)}, u32[]{:S(2)}) collective-permute-start(bf16[128,256]{1,0:T(8,128)(2,1)S(1)} %get-tuple-element.88), channel_id=1, source_target_pairs={{0,3},{1,2},{2,1},{3,0},{4,7},{5,6},{6,5},{7,4},{8,11},{9,10},{10,... | collective-permute-start | bytes 196616 | tf_op jit(solution)/shard_map/ppermute | solution.py:414
  59.2 5.0 %collective-permute-start.11 = (bf16[128,256]{1,0:T(8,128)(2,1)S(1)}, bf16[128,256]{1,0:T(8,128)(2,1)S(1)}, u32[]{:S(2)}, u32[]{:S(2)}) collective-permute-start(bf16[128,256]{1,0:T(8,128)(2,1)S(1)} %get-tuple-element.87), channel_id=1, source_target_pairs={{0,2},{1,3},{2,0},{3,1},{4,6},{5,7},{6,4},{7,5},{8,10},{9,11},{10,... | collective-permute-start | bytes 196616 | tf_op jit(solution)/shard_map/ppermute | solution.py:414
  60.4 3.8 %collective-permute-start.10 = (bf16[128,256]{1,0:T(8,128)(2,1)S(1)}, bf16[128,256]{1,0:T(8,128)(2,1)S(1)}, u32[]{:S(2)}, u32[]{:S(2)}) collective-permute-start(bf16[128,256]{1,0:T(8,128)(2,1)S(1)} %get-tuple-element.86), channel_id=1, source_target_pairs={{0,1},{1,0},{2,3},{3,2},{4,5},{5,4},{6,7},{7,6},{8,9},{9,8},{10,11... | collective-permute-start | bytes 196616 | tf_op jit(solution)/shard_map/ppermute | solution.py:414

commit v10 on v9

--- a/solution.py
+++ b/solution.py
@@ -299,7 +299,7 @@
             ]
             g = role * strands + s
             local_ref[g] = mm(reads[0], pull) + mm(reads[1], value)
-            map_ref[g] = (left * here_ref[s, rows : rows + 1] + mm(reads[0], start)).astype(BF16)
+            map_ref[g] = left * here_ref[s, rows : rows + 1] + mm(reads[0], start)
             return carry
 
         lax.fori_loop(0, strands, group, 0)
@@ -353,7 +353,9 @@
     ones = same_head.astype(F32).astype(BF16)
     for s, state in enumerate(states):
         g = role * strands + s
-        wkv = local_ref[g] + mm(map_ref[g], spread(state, same_head))
+        high, low = halves(map_ref[g])
+        held, rest = [spread(item, same_head) for item in halves(state.astype(F32))]
+        wkv = local_ref[g] + mm(high, held) + (mm(low, held) + mm(high, rest))
         centered = wkv - head_sum(wkv, ones) * (1.0 / HEAD)
         variance = head_sum(centered * centered, ones) * (1.0 / HEAD)
         yield centered * lax.rsqrt(variance + GROUP_EPS)
@@ -361,7 +363,7 @@
 
 def kept_kernel(entry_ref, from_ref, local_ref, map_ref, out_ref):
     same_head = block_ones(out_ref.shape[2])
-    states = [composed(from_ref[s], entry_ref[s], same_head, True).astype(BF16) for s in range(out_ref.shape[0])]
+    states = [composed(from_ref[s], entry_ref[s], same_head, True) for s in range(out_ref.shape[0])]
     for s, result in enumerate(normed_heads(1, states, local_ref, map_ref)):
         out_ref[s] = result
 
@@ -538,7 +540,7 @@
     sent_parts, kept_parts, _ = lax.optimization_barrier((sent_parts, kept_parts, total))
     reads = call(
         read_kernel,
-        (f32_lanes, struct(f32_lanes.shape, BF16)),
+        (f32_lanes, f32_lanes),
         mib=6,
         in_specs=[SMEM_SPEC] + [VMEM_SPEC] * 5,
     )(parity, receptances, sent_parts, kept_parts, sent_here, kept_here)

time: 65.1 us -> 65.1 us (level)
  no operation moved by 1% of the time
where the time goes in v10:
time: 65.1 us; the launch traced here: 64.9 us
  starting transfers between devices  20.2 us (31%)
  Pallas kernels  18.3 us (28%)
  blocking collectives  14.9 us (23%)
  waiting for transfers between devices  8.23 us (13%)
  local copies, waits for them, and re-layouts  2.29 us (4%)
  other arithmetic  0.69 us (1%)
    ppermute x11, starting transfers between devices, swapped(): lax.ppermute(value, axis, [(i, i ^ mask) for i in range(lax.axis_size(axi...  13.5 us
    ppermute x11, waiting for transfers between devices, swapped(): lax.ppermute(value, axis, [(i, i ^ mask) for i in range(lax.axis_size(axi...  8.23 us
    pallas_call x2, Pallas kernels, chunk(): call(chunk_kernel, (state_struct, parts_struct, here_struct, struct((stra...  8.22 us
    all_gather x1, blocking collectives, on_device(): joined_whole = lax.all_gather(joined, 'mp', axis=2, tiled=True)  7.55 us
    all_gather x1, blocking collectives, on_device(): whole = lax.all_gather(local, 'mp', axis=2, tiled=True)  7.3 us
    ppermute x1, starting transfers between devices, on_device(): rc_here = lax.ppermute(hidden_rc, 'seq', mirror)  6 us
    unnamed x40, local copies, waits for them, and re-layouts  2.29 us
    pallas_call x1, Pallas kernels, on_device(): call(project_kernel, (f32_lanes,) * 4 + (struct((strands, rows + 16, full...  2.2 us
  transfers between devices with their start and end apart: 13, of which 5 were waited for; matrix products, arithmetic and copies ran while one was open for 0% of the time, Pallas kernels for 24%

profile of v10, /device:TPU:0, one launch (start us, length us, event | category | flops | bytes accessed | tf_op | source)
XLA Modules:
  0.0 64.9 jit_solution(1046093280767256210)
XLA Ops:
  0.0 6.0 %collective-permute-start = (bf16[128,256]{1,0:T(8,128)(2,1)}, bf16[128,256]{1,0:T(8,128)(2,1)S(1)}, u32[]{:S(2)}, u32[]{:S(2)}) collective-permute-start(bf16[128,256]{1,0:T(8,128)(2,1)} %param.22), channel_id=1, source_target_pairs={{0,28},{4,24},{8,20},{12,16},{16,12},{20,8},{24,4},{28,0},{1,29},{... | collective-permute-start | bytes 196616 | tf_op jit(solution)/shard_map/ppermute | solution.py:447
  6.0 0.8 %copy-done.8 = bf16[128,256]{1,0:T(8,128)(2,1)S(1)} copy-done((bf16[128,256]{1,0:T(8,128)(2,1)S(1)}, bf16[128,256]{1,0:T(8,128)(2,1)}, u32[]{:S(2)}) %copy-start.8) | copy-done | bytes 65560
  6.8 0.7 %copy-done.12 = f32[4,256]{1,0:T(4,128)S(1)} copy-done((f32[4,256]{1,0:T(4,128)S(1)}, f32[4,256]{1,0:T(4,128)}, u32[]{:S(2)}) %copy-start.12) | copy-done | bytes 4120
  7.5 0.7 %copy-done.18 = s32[128]{0:T(128)S(1)} copy-done((s32[128]{0:T(128)S(1)}, s32[128]{0:T(128)}, u32[]{:S(2)}) %copy-start.18) | copy-done | bytes 536
  8.2 0.4 shard_map.190
  8.9 7.3 %all_gather.6.x_ref = bf16[2,128,1024]{2,1,0:T(8,128)(2,1)S(1)} all-gather(bf16[2,128,256]{2,1,0:T(8,128)(2,1)S(1)} %shard_map.191), channel_id=1, replica_groups=mesh['seq'=8,'mp'=4] {'mp'}, dimensions={2}, use_global_device_ids=true | all-gather | bytes 655360 | tf_op jit(solution)/shard_map/all_gather | solution.py:465
  16.3 0.7 %collective-permute-start.2 = (bf16[2,1024]{1,0:T(2,128)(2,1)S(1)}, bf16[2,1024]{1,0:T(2,128)(2,1)S(1)}, u32[]{:S(2)}, u32[]{:S(2)}) collective-permute-start(bf16[2,1024]{1,0:T(2,128)(2,1)S(1)} %bitcast.33), channel_id=1, source_target_pairs={{4,8},{12,16},{20,24},{8,4},{16,12},{24,20},{5,9},{13,17},{21,25},... | collective-permute-start | bytes 12296 | tf_op jit(solution)/shard_map/ppermute | solution.py:471
  17.0 2.2 %shard_map.192 = (f32[4,128,256]{2,1,0:T(8,128)S(1)}, f32[4,128,256]{2,1,0:T(8,128)S(1)}, f32[4,128,256]{2,1,0:T(8,128)S(1)}, f32[4,128,256]{2,1,0:T(8,128)S(1)}...) custom-call(bf16[2,128,1024]{2,1,0:T(8,128)(2,1)S(1)} %all_gather.6.x_ref, ...), custom_call_target="tpu_custom_call" | custom-call | flops 10000000000 | bytes 10000000 | tf_op jit(solution)/shard_map/pallas_call | solution.py:481
  19.3 3.7 %collective-permute-start.1 = (bf16[2,1024]{1,0:T(2,128)(2,1)S(1)}, bf16[2,1024]{1,0:T(2,128)(2,1)S(1)}, u32[]{:S(2)}, u32[]{:S(2)}) collective-permute-start(bf16[2,1024]{1,0:T(2,128)(2,1)S(1)} %bitcast.34), channel_id=1, source_target_pairs={{0,4},{4,0},{8,12},{12,8},{16,20},{20,16},{24,28},{28,24},{1,5},{5... | collective-permute-start | bytes 12296 | tf_op jit(solution)/shard_map/ppermute | solution.py:416
  22.9 4.1 %shard_map.194 = (bf16[2,128,256]{2,1,0:T(8,128)(2,1)S(1)}, bf16[2,5,128,256]{3,2,1,0:T(8,128)(2,1)S(1)}, f32[2,136,256]{2,1,0:T(8,128)S(1)}, f32[2,1024]{1,0:T(2,128)S(1)}) custom-call(s32[1]{0:T(128)} %bitcast.1.direction_ref, f32[4,128,256]{2,1,0:T(8,128)S(1)} %get-tuple-element.52.refs_0_, f32[4,128,256]{2,1,0:T(8,128)S(1)} %get-tuple-element.53.refs_1_, ...), custom_call_target="tpu_custom_call" | custom-call | flops 10000000000 | bytes 10000000 | tf_op jit(solution)/shard_map/pallas_call | solution.py:499
  27.0 1.3 %collective-permute-start.3 = (bf16[2,128,256]{2,1,0:T(8,128)(2,1)S(1)}, bf16[2,128,256]{2,1,0:T(8,128)(2,1)S(1)}, u32[]{:S(2)}, u32[]{:S(2)}) collective-permute-start(bf16[2,128,256]{2,1,0:T(8,128)(2,1)S(1)} %get-tuple-element.60), channel_id=1, source_target_pairs={{0,4},{4,0},{8,12},{12,8},{16,20},{20,16},{24,28},{28,24},{1,5},{5... | collective-permute-start | bytes 393224 | tf_op jit(solution)/shard_map/ppermute | solution.py:416
  28.3 4.1 %shard_map.193 = (bf16[2,128,256]{2,1,0:T(8,128)(2,1)S(1)}, bf16[2,5,128,256]{3,2,1,0:T(8,128)(2,1)S(1)}, f32[2,136,256]{2,1,0:T(8,128)S(1)}, f32[2,1024]{1,0:T(2,128)S(1)}) custom-call(s32[1]{0:T(128)S(6)} %sub.3.direction_ref, f32[4,128,256]{2,1,0:T(8,128)S(1)} %get-tuple-element.52.refs_0_, f32[4,128,256]{2,1,0:T(8,128)S(1)} %get-tuple-element.53.refs_1_, ...), custom_call_target="tpu_custom_call" | custom-call | flops 10000000000 | bytes 10000000 | tf_op jit(solution)/shard_map/pallas_call | solution.py:499
  32.4 0.2 shard_map.195.total_ref
  32.7 1.5 %collective-permute-start.5 = (bf16[2,128,256]{2,1,0:T(8,128)(2,1)S(1)}, bf16[2,128,256]{2,1,0:T(8,128)(2,1)S(1)}, u32[]{:S(2)}, u32[]{:S(2)}) collective-permute-start(bf16[2,128,256]{2,1,0:T(8,128)(2,1)S(1)} %shard_map.195.total_ref), channel_id=1, source_target_pairs={{0,8},{4,12},{8,0},{12,4},{16,24},{20,28},{24,16},{28,20},{1,9},{5... | collective-permute-start | bytes 393224 | tf_op jit(solution)/shard_map/ppermute | solution.py:416
  34.1 0.8 %collective-permute-start.4 = (bf16[256,1024]{1,0:T(8,128)(2,1)S(1)}, bf16[256,1024]{1,0:T(8,128)(2,1)S(1)}, u32[]{:S(2)}, u32[]{:S(2)}) collective-permute-start(bf16[256,1024]{1,0:T(8,128)(2,1)S(1)} %copy-done.5), channel_id=1, source_target_pairs={{0,2},{1,3},{2,0},{3,1},{4,6},{5,7},{6,4},{7,5},{8,10},{9,11},{10,... | collective-permute-start | bytes 1572872 | tf_op jit(solution)/shard_map/ppermute | solution.py:416
  35.0 0.8 %shard_map.196.receptances = f32[4,128,256]{2,1,0:T(8,128)S(1)} custom-call(s32[1]{0:T(128)} %bitcast.1.direction_ref, f32[2,144,1024]{2,1,0:T(8,128)S(1)} %get-tuple-element.62.normed, f32[5,1024]{1,0:T(8,128)S(1)} %copy-done.11, f32[2,1024]{1,0:T(2,128)S(1)} %get-tuple-element.63.sent_edge_ref, f32[2,1024]{1,0:T(2,128)S(1)} %get-tuple-element.65.kept_edge_ref, ...), custom_call_target="tpu_custom_call" | custom-call | flops 3000000000 | bytes 3000000 | tf_op jit(solution)/shard_map/pallas_call | solution.py:513
  35.8 1.9 %collective-permute-done.5.from_ref = bf16[2,128,256]{2,1,0:T(8,128)(2,1)S(1)} collective-permute-done((bf16[2,128,256]{2,1,0:T(8,128)(2,1)S(1)}, bf16[2,128,256]{2,1,0:T(8,128)(2,1)S(1)}, u32[]{:S(2)}, u32[]{:S(2)}) %collective-permute-start.5) | collective-permute-done | bytes 131104 | tf_op jit(solution)/shard_map/ppermute | solution.py:416
  37.7 0.2 shard_map.197
  37.9 3.1 %collective-permute-start.6 = (bf16[2,64,256]{2,1,0:T(8,128)(2,1)S(1)}, bf16[2,64,256]{2,1,0:T(8,128)(2,1)S(1)}, u32[]{:S(2)}, u32[]{:S(2)}) collective-permute-start(bf16[2,64,256]{2,1,0:T(8,128)(2,1)S(1)} %get-tuple-element.67), channel_id=1, source_target_pairs={{0,16},{4,20},{8,24},{12,28},{16,0},{20,4},{24,8},{28,12},{1,17},{... | collective-permute-start | bytes 196616 | tf_op jit(solution)/shard_map/ppermute | solution.py:416
  41.0 2.1 %shard_map.198 = (f32[4,128,256]{2,1,0:T(8,128)S(1)}, f32[4,128,256]{2,1,0:T(8,128)S(1)}) custom-call(s32[1]{0:T(128)} %bitcast.1.direction_ref, f32[4,128,256]{2,1,0:T(8,128)S(1)} %shard_map.196.receptances, bf16[2,5,128,256]{3,2,1,0:T(8,128)(2,1)S(1)} %get-tuple-element.71.sent_ref, bf16[2,5,128,256]{3,2,1,0:T(8,128)(2,1)S(1)} %get-tuple-element.72.kept_ref, ...), custom_call_target="tpu_custom_call" | custom-call | flops 10000000000 | bytes 10000000 | tf_op jit(solution)/shard_map/pallas_call | solution.py:541
  43.2 0.2 shard_map.199.entry_ref
  43.4 1.1 %collective-permute-start.7 = (bf16[2,64,256]{2,1,0:T(8,128)(2,1)S(1)}, bf16[2,64,256]{2,1,0:T(8,128)(2,1)S(1)}, u32[]{:S(2)}, u32[]{:S(2)}) collective-permute-start(bf16[2,64,256]{2,1,0:T(8,128)(2,1)S(1)} %shard_map.199.entry_ref), channel_id=1, source_target_pairs={{0,4},{4,0},{8,12},{12,8},{16,20},{20,16},{24,28},{28,24},{1,5},{5... | collective-permute-start | bytes 196616 | tf_op jit(solution)/shard_map/ppermute | solution.py:416
  44.6 1.0 %shard_map.200.kept_ref = f32[2,128,256]{2,1,0:T(8,128)S(1)} custom-call(bf16[2,64,256]{2,1,0:T(8,128)(2,1)S(1)} %shard_map.199.entry_ref, bf16[2,128,256]{2,1,0:T(8,128)(2,1)S(1)} %collective-permute-done.3.from_ref, f32[4,128,256]{2,1,0:T(8,128)S(1)} %get-tuple-element.79.local_ref, f32[4,128,256]{2,1,0:T(8,128)S(1)} %get-tuple-element.80.map_ref), custom_call_target="tpu_custom_call" | custom-call | flops 3000000000 | bytes 3000000 | tf_op jit(solution)/shard_map/pallas_call | solution.py:556
  45.6 2.3 %collective-permute-done.7.other_ref = bf16[2,64,256]{2,1,0:T(8,128)(2,1)S(1)} collective-permute-done((bf16[2,64,256]{2,1,0:T(8,128)(2,1)S(1)}, bf16[2,64,256]{2,1,0:T(8,128)(2,1)S(1)}, u32[]{:S(2)}, u32[]{:S(2)}) %collective-permute-start.7) | collective-permute-done | bytes 65568 | tf_op jit(solution)/shard_map/ppermute | solution.py:416
  47.9 0.8 %shard_map.201 = bf16[2,128,256]{2,1,0:T(8,128)(2,1)S(1)} custom-call(bf16[2,64,256]{2,1,0:T(8,128)(2,1)S(1)} %collective-permute-done.7.other_ref, f32[2,128,256]{2,1,0:T(8,128)S(1)} %shard_map.200.kept_ref, f32[4,128,256]{2,1,0:T(8,128)S(1)} %get-tuple-element.79.local_ref, f32[4,128,256]{2,1,0:T(8,128)S(1)} %get-tuple-element.80.map_ref, ...), custom_call_target="tpu_custom_call" | custom-call | flops 10000000000 | bytes 10000000 | tf_op jit(solution)/shard_map/pallas_call | solution.py:559
  48.7 7.6 %all_gather.7.joined_ref = bf16[2,128,1024]{2,1,0:T(8,128)(2,1)S(1)} all-gather(bf16[2,128,256]{2,1,0:T(8,128)(2,1)S(1)} %shard_map.201), channel_id=1, replica_groups=mesh['seq'=8,'mp'=4] {'mp'}, dimensions={2}, use_global_device_ids=true | all-gather | bytes 655360 | tf_op jit(solution)/shard_map/all_gather | solution.py:560
  56.3 2.0 %shard_map.202 = (f32[128,256]{1,0:T(8,128)S(1)}, bf16[128,256]{1,0:T(8,128)(2,1)S(1)}, bf16[128,256]{1,0:T(8,128)(2,1)S(1)}, bf16[128,256]{1,0:T(8,128)(2,1)S(1)}) custom-call(s32[1]{0:T(128)} %bitcast.index_ref, bf16[2,128,1024]{2,1,0:T(8,128)(2,1)S(1)} %all_gather.7.joined_ref, bf16[2,128,1024]{2,1,0:T(8,128)(2,1)S(1)} %all_gather.6.x_ref, ...), custom_call_target="tpu_custom_call" | custom-call | flops 10000000000 | bytes 10000000 | tf_op jit(solution)/shard_map/pallas_call | solution.py:564
  58.4 0.8 %collective-permute-start.12 = (bf16[128,256]{1,0:T(8,128)(2,1)S(1)}, bf16[128,256]{1,0:T(8,128)(2,1)S(1)}, u32[]{:S(2)}, u32[]{:S(2)}) collective-permute-start(bf16[128,256]{1,0:T(8,128)(2,1)S(1)} %get-tuple-element.88), channel_id=1, source_target_pairs={{0,3},{1,2},{2,1},{3,0},{4,7},{5,6},{6,5},{7,4},{8,11},{9,10},{10,... | collective-permute-start | bytes 196616 | tf_op jit(solution)/shard_map/ppermute | solution.py:416
  59.2 1.2 %collective-permute-start.11 = (bf16[128,256]{1,0:T(8,128)(2,1)S(1)}, bf16[128,256]{1,0:T(8,128)(2,1)S(1)}, u32[]{:S(2)}, u32[]{:S(2)}) collective-permute-start(bf16[128,256]{1,0:T(8,128)(2,1)S(1)} %get-tuple-element.87), channel_id=1, source_target_pairs={{0,2},{1,3},{2,0},{3,1},{4,6},{5,7},{6,4},{7,5},{8,10},{9,11},{10,... | collective-permute-start | bytes 196616 | tf_op jit(solution)/shard_map/ppermute | solution.py:416
  60.4 1.9 %collective-permute-done.12 = bf16[128,256]{1,0:T(8,128)(2,1)S(1)} collective-permute-done((bf16[128,256]{1,0:T(8,128)(2,1)S(1)}, bf16[128,256]{1,0:T(8,128)(2,1)S(1)}, u32[]{:S(2)}, u32[]{:S(2)}) %collective-permute-start.12) | collective-permute-done | bytes 65568 | tf_op jit(solution)/shard_map/ppermute | solution.py:416
  62.4 1.9 %collective-permute-done.11 = bf16[128,256]{1,0:T(8,128)(2,1)S(1)} collective-permute-done((bf16[128,256]{1,0:T(8,128)(2,1)S(1)}, bf16[128,256]{1,0:T(8,128)(2,1)S(1)}, u32[]{:S(2)}, u32[]{:S(2)}) %collective-permute-start.11) | collective-permute-done | bytes 65568 | tf_op jit(solution)/shard_map/ppermute | solution.py:416
  64.2 0.7 %add_convert_fusion = bf16[128,256]{1,0:T(8,128)(2,1)} fusion(bf16[128,256]{1,0:T(8,128)(2,1)S(1)} %collective-permute-done.12, bf16[128,256]{1,0:T(8,128)(2,1)S(1)} %collective-permute-done.11, f32[128,256]{1,0:T(8,128)S(1)} %get-tuple-element.85, bf16[128,256]{1,0:T(8,128)(2,1)S(1)} %collective-permute-done.10), kind=kLoop, calls=%fused_computation | loop fusion | flops 229376 | bytes 393216 | tf_op jit(solution)/shard_map/convert_element_type | solution.py:577
  (51 shorter events, 0.5 us)
Async XLA Ops:
  0.0 8.6 %collective-permute-start = (bf16[128,256]{1,0:T(8,128)(2,1)}, bf16[128,256]{1,0:T(8,128)(2,1)S(1)}, u32[]{:S(2)}, u32[]{:S(2)}) collective-permute-start(bf16[128,256]{1,0:T(8,128)(2,1)} %param.22), channel_id=1, source_target_pairs={{0,28},{4,24},{8,20},{12,16},{16,12},{20,8},{24,4},{28,0},{1,29},{... | collective-permute-start | bytes 196616 | tf_op jit(solution)/shard_map/ppermute | solution.py:447
  6.0 0.8 %copy-start.8 = (bf16[128,256]{1,0:T(8,128)(2,1)S(1)}, bf16[128,256]{1,0:T(8,128)(2,1)}, u32[]{:S(2)}) copy-start(bf16[128,256]{1,0:T(8,128)(2,1)} %fwd_ref.1) | copy-start | bytes 196612
  6.8 0.7 %copy-start.12 = (f32[4,256]{1,0:T(4,128)S(1)}, f32[4,256]{1,0:T(4,128)}, u32[]{:S(2)}) copy-start(f32[4,256]{1,0:T(4,128)} %embed_ref.1) | copy-start | bytes 12292
  7.5 0.7 %copy-start.18 = (s32[128]{0:T(128)S(1)}, s32[128]{0:T(128)}, u32[]{:S(2)}) copy-start(s32[128]{0:T(128)} %param.20) | copy-start | bytes 1540
  8.7 8.3 %copy-start.2 = (bf16[1024,256]{1,0:T(8,128)(2,1)S(1)}, bf16[1024,256]{1,0:T(8,128)(2,1)}, u32[]{:S(2)}) copy-start(bf16[1024,256]{1,0:T(8,128)(2,1)} %refs_9_.3) | copy-start | bytes 1572868
  8.7 8.3 %copy-start.3 = (bf16[1024,256]{1,0:T(8,128)(2,1)S(1)}, bf16[1024,256]{1,0:T(8,128)(2,1)}, u32[]{:S(2)}) copy-start(bf16[1024,256]{1,0:T(8,128)(2,1)} %refs_10_.3) | copy-start | bytes 1572868
  8.7 8.3 %copy-start.6 = (bf16[1024,64]{0,1:T(8,128)(2,1)S(1)}, bf16[1024,64]{0,1:T(8,128)(2,1)}, u32[]{:S(2)}) copy-start(bf16[1024,64]{0,1:T(8,128)(2,1)} %param.30) | copy-start | bytes 393220
  8.7 8.3 %copy-start.7 = (bf16[1024,64]{0,1:T(8,128)(2,1)S(1)}, bf16[1024,64]{0,1:T(8,128)(2,1)}, u32[]{:S(2)}) copy-start(bf16[1024,64]{0,1:T(8,128)(2,1)} %param.33) | copy-start | bytes 393220
  8.7 8.3 %copy-start.9 = (bf16[64,256]{1,0:T(8,128)(2,1)S(1)}, bf16[64,256]{1,0:T(8,128)(2,1)}, u32[]{:S(2)}) copy-start(bf16[64,256]{1,0:T(8,128)(2,1)} %refs_11_.3) | copy-start | bytes 98308
  8.7 8.3 %copy-start.10 = (bf16[64,256]{1,0:T(8,128)(2,1)S(1)}, bf16[64,256]{1,0:T(8,128)(2,1)}, u32[]{:S(2)}) copy-start(bf16[64,256]{1,0:T(8,128)(2,1)} %refs_12_.3) | copy-start | bytes 98308
  8.7 8.3 %copy-start.11 = (f32[5,1024]{1,0:T(8,128)S(1)}, f32[5,1024]{1,0:T(8,128)}, u32[]{:S(2)}) copy-start(f32[5,1024]{1,0:T(8,128)} %mixing_ref.3) | copy-start | bytes 61444
  8.7 8.3 %copy-start.13 = (f32[1024]{0:T(1024)S(1)}, f32[1024]{0:T(1024)}, u32[]{:S(2)}) copy-start(f32[1024]{0:T(1024)} %param.24) | copy-start | bytes 12292
  8.8 8.3 %copy-start.15 = (f32[256]{0:T(256)S(1)}, f32[256]{0:T(256)}, u32[]{:S(2)}) copy-start(f32[256]{0:T(256)} %param.31) | copy-start | bytes 3076
  8.8 8.3 %copy-start.16 = (f32[256]{0:T(256)S(1)}, f32[256]{0:T(256)}, u32[]{:S(2)}) copy-start(f32[256]{0:T(256)} %param.34) | copy-start | bytes 3076
  16.3 6.6 %collective-permute-start.2 = (bf16[2,1024]{1,0:T(2,128)(2,1)S(1)}, bf16[2,1024]{1,0:T(2,128)(2,1)S(1)}, u32[]{:S(2)}, u32[]{:S(2)}) collective-permute-start(bf16[2,1024]{1,0:T(2,128)(2,1)S(1)} %bitcast.33), channel_id=1, source_target_pairs={{4,8},{12,16},{20,24},{8,4},{16,12},{24,20},{5,9},{13,17},{21,25},... | collective-permute-start | bytes 12296 | tf_op jit(solution)/shard_map/ppermute | solution.py:471
  19.3 9.0 %collective-permute-start.1 = (bf16[2,1024]{1,0:T(2,128)(2,1)S(1)}, bf16[2,1024]{1,0:T(2,128)(2,1)S(1)}, u32[]{:S(2)}, u32[]{:S(2)}) collective-permute-start(bf16[2,1024]{1,0:T(2,128)(2,1)S(1)} %bitcast.34), channel_id=1, source_target_pairs={{0,4},{4,0},{8,12},{12,8},{16,20},{20,16},{24,28},{28,24},{1,5},{5... | collective-permute-start | bytes 12296 | tf_op jit(solution)/shard_map/ppermute | solution.py:416
  27.0 5.4 %collective-permute-start.3 = (bf16[2,128,256]{2,1,0:T(8,128)(2,1)S(1)}, bf16[2,128,256]{2,1,0:T(8,128)(2,1)S(1)}, u32[]{:S(2)}, u32[]{:S(2)}) collective-permute-start(bf16[2,128,256]{2,1,0:T(8,128)(2,1)S(1)} %get-tuple-element.60), channel_id=1, source_target_pairs={{0,4},{4,0},{8,12},{12,8},{16,20},{20,16},{24,28},{28,24},{1,5},{5... | collective-permute-start | bytes 393224 | tf_op jit(solution)/shard_map/ppermute | solution.py:416
  32.4 1.7 %copy-start.5 = (bf16[256,1024]{1,0:T(8,128)(2,1)S(1)}, bf16[256,1024]{1,0:T(8,128)(2,1)}, u32[]{:S(2)}) copy-start(bf16[256,1024]{1,0:T(8,128)(2,1)} %refs_0_.1) | copy-start | bytes 1572868
  32.4 2.5 %copy-start.4 = (bf16[1024,256]{1,0:T(8,128)(2,1)S(1)}, bf16[1024,256]{1,0:T(8,128)(2,1)}, u32[]{:S(2)}) copy-start(bf16[1024,256]{1,0:T(8,128)(2,1)} %w_r.1) | copy-start | bytes 1572868
  32.7 5.0 %collective-permute-start.5 = (bf16[2,128,256]{2,1,0:T(8,128)(2,1)S(1)}, bf16[2,128,256]{2,1,0:T(8,128)(2,1)S(1)}, u32[]{:S(2)}, u32[]{:S(2)}) collective-permute-start(bf16[2,128,256]{2,1,0:T(8,128)(2,1)S(1)} %shard_map.195.total_ref), channel_id=1, source_target_pairs={{0,8},{4,12},{8,0},{12,4},{16,24},{20,28},{24,16},{28,20},{1,9},{5... | collective-permute-start | bytes 393224 | tf_op jit(solution)/shard_map/ppermute | solution.py:416
  34.1 13.8 %collective-permute-start.4 = (bf16[256,1024]{1,0:T(8,128)(2,1)S(1)}, bf16[256,1024]{1,0:T(8,128)(2,1)S(1)}, u32[]{:S(2)}, u32[]{:S(2)}) collective-permute-start(bf16[256,1024]{1,0:T(8,128)(2,1)S(1)} %copy-done.5), channel_id=1, source_target_pairs={{0,2},{1,3},{2,0},{3,1},{4,6},{5,7},{6,4},{7,5},{8,10},{9,11},{10,... | collective-permute-start | bytes 1572872 | tf_op jit(solution)/shard_map/ppermute | solution.py:416
  37.9 5.4 %collective-permute-start.6 = (bf16[2,64,256]{2,1,0:T(8,128)(2,1)S(1)}, bf16[2,64,256]{2,1,0:T(8,128)(2,1)S(1)}, u32[]{:S(2)}, u32[]{:S(2)}) collective-permute-start(bf16[2,64,256]{2,1,0:T(8,128)(2,1)S(1)} %get-tuple-element.67), channel_id=1, source_target_pairs={{0,16},{4,20},{8,24},{12,28},{16,0},{20,4},{24,8},{28,12},{1,17},{... | collective-permute-start | bytes 196616 | tf_op jit(solution)/shard_map/ppermute | solution.py:416
  41.0 15.3 %collective-permute-start.8 = (bf16[256,1024]{1,0:T(8,128)(2,1)S(1)}, bf16[256,1024]{1,0:T(8,128)(2,1)S(1)}, u32[]{:S(2)}, u32[]{:S(2)}) collective-permute-start(bf16[256,1024]{1,0:T(8,128)(2,1)S(1)} %copy-done.5), channel_id=1, source_target_pairs={{0,1},{1,0},{2,3},{3,2},{4,5},{5,4},{6,7},{7,6},{8,9},{9,8},{10,11... | collective-permute-start | bytes 1572872 | tf_op jit(solution)/shard_map/ppermute | solution.py:416
  43.4 4.5 %copy-start.17 = (f32[256]{0:T(256)S(1)}, f32[256]{0:T(256)}, u32[]{:S(2)}) copy-start(f32[256]{0:T(256)} %param.36) | copy-start | bytes 3076
  43.4 4.4 %collective-permute-start.7 = (bf16[2,64,256]{2,1,0:T(8,128)(2,1)S(1)}, bf16[2,64,256]{2,1,0:T(8,128)(2,1)S(1)}, u32[]{:S(2)}, u32[]{:S(2)}) collective-permute-start(bf16[2,64,256]{2,1,0:T(8,128)(2,1)S(1)} %shard_map.199.entry_ref), channel_id=1, source_target_pairs={{0,4},{4,0},{8,12},{12,8},{16,20},{20,16},{24,28},{28,24},{1,5},{5... | collective-permute-start | bytes 196616 | tf_op jit(solution)/shard_map/ppermute | solution.py:416
  47.9 8.4 %collective-permute-start.9 = (bf16[256,1024]{1,0:T(8,128)(2,1)S(1)}, bf16[256,1024]{1,0:T(8,128)(2,1)S(1)}, u32[]{:S(2)}, u32[]{:S(2)}) collective-permute-start(bf16[256,1024]{1,0:T(8,128)(2,1)S(1)} %collective-permute-done.4.refs_2_), channel_id=1, source_target_pairs={{0,1},{1,0},{2,3},{3,2},{4,5},{5,4},{6,7},{7,6},{8,9},{9,8},{10,11... | collective-permute-start | bytes 1572872 | tf_op jit(solution)/shard_map/ppermute | solution.py:416
  47.9 8.4 %copy-start = (bf16[1024,1024]{1,0:T(8,128)(2,1)S(1)}, bf16[1024,1024]{1,0:T(8,128)(2,1)}, u32[]{:S(2)}) copy-start(bf16[1024,1024]{1,0:T(8,128)(2,1)} %refs_4_.1) | copy-start | bytes 6291460
  47.9 8.4 %copy-start.1 = (bf16[1024,1024]{1,0:T(8,128)(2,1)S(1)}, bf16[1024,1024]{1,0:T(8,128)(2,1)}, u32[]{:S(2)}) copy-start(bf16[1024,1024]{1,0:T(8,128)(2,1)} %refs_5_.1) | copy-start | bytes 6291460
  47.9 8.4 %copy-start.14 = (f32[1024]{0:T(1024)S(1)}, f32[1024]{0:T(1024)}, u32[]{:S(2)}) copy-start(f32[1024]{0:T(1024)} %param.25) | copy-start | bytes 12292
  58.4 4.0 %collective-permute-start.12 = (bf16[128,256]{1,0:T(8,128)(2,1)S(1)}, bf16[128,256]{1,0:T(8,128)(2,1)S(1)}, u32[]{:S(2)}, u32[]{:S(2)}) collective-permute-start(bf16[128,256]{1,0:T(8,128)(2,1)S(1)} %get-tuple-element.88), channel_id=1, source_target_pairs={{0,3},{1,2},{2,1},{3,0},{4,7},{5,6},{6,5},{7,4},{8,11},{9,10},{10,... | collective-permute-start | bytes 196616 | tf_op jit(solution)/shard_map/ppermute | solution.py:416
  59.2 5.0 %collective-permute-start.11 = (bf16[128,256]{1,0:T(8,128)(2,1)S(1)}, bf16[128,256]{1,0:T(8,128)(2,1)S(1)}, u32[]{:S(2)}, u32[]{:S(2)}) collective-permute-start(bf16[128,256]{1,0:T(8,128)(2,1)S(1)} %get-tuple-element.87), channel_id=1, source_target_pairs={{0,2},{1,3},{2,0},{3,1},{4,6},{5,7},{6,4},{7,5},{8,10},{9,11},{10,... | collective-permute-start | bytes 196616 | tf_op jit(solution)/shard_map/ppermute | solution.py:416
  60.4 3.8 %collective-permute-start.10 = (bf16[128,256]{1,0:T(8,128)(2,1)S(1)}, bf16[128,256]{1,0:T(8,128)(2,1)S(1)}, u32[]{:S(2)}, u32[]{:S(2)}) collective-permute-start(bf16[128,256]{1,0:T(8,128)(2,1)S(1)} %get-tuple-element.86), channel_id=1, source_target_pairs={{0,1},{1,0},{2,3},{3,2},{4,5},{5,4},{6,7},{7,6},{8,9},{9,8},{10,11... | collective-permute-start | bytes 196616 | tf_op jit(solution)/shard_map/ppermute | solution.py:416

commit v11 on v10

--- a/solution.py
+++ b/solution.py
@@ -120,7 +120,8 @@
 
 
 def project_kernel(x_ref, gain_ref, mixing_ref, w_k, w_v, w_d1, w_c1, w_d2, w_c2, d_base, c_base, *refs):
-    outs, (normed, low_ref, edge_ref, mixed, shifts) = refs[:4], refs[4:]
+    outs, (rows_ref, normed, low_ref, edge_ref, mixed, shifts) = refs[:5], refs[5:]
+    prev_ref, insert_ref, key_ref, value_ref, here_ref = outs
     strands, rows, _ = x_ref.shape
     shape = outs[0].shape
     pad = 8
@@ -129,6 +130,7 @@
     parts = [weight * (1.0 - share) for weight, share in lows] + [weight * share for weight, share in lows]
     low_ref[...] = jnp.concatenate(parts, axis=0).astype(BF16)
     half = low_ref.shape[0] // 2
+    gated = {}
     for s in range(strands):
         values = layer_norm(x_ref[s].astype(F32), gain)
         zero = jnp.zeros_like(values[:1])
@@ -144,14 +146,35 @@
         for d in range(2):
             shift = pad - 1 + 2 * d
             g = d * strands + s
-            log_decay, rate = gates(
+            gated[g] = gates(
                 low[:, :half] + shifts[s, shift : shift + rows, :], w_d2[...], w_c2[...], d_base[...], c_base[...]
             )
-            outs[2][g] = log_decay
-            outs[3][g] = rate
     blend(normed, mixing_ref, (1, 2), rows, mixed)
-    outs[0][...] = mm(mixed[0], w_k[...]).reshape(shape)
-    outs[1][...] = mm(mixed[1], w_v[...]).reshape(shape)
+    keys = mm(mixed[0], w_k[...])
+    value_ref[...] = mm(mixed[1], w_v[...]).reshape(shape)
+    ones = block_ones(shape[2]).astype(F32).astype(BF16)
+    order = ids_of((rows, rows), 0) - ids_of((rows, rows), 1)
+    row_ids = ids_of(shape[1:], 0)
+    for g in range(shape[0]):
+        d = g // strands
+        edge = d * (rows - 1)
+        key = keys[g * rows : (g + 1) * rows]
+        log_decay, rate = gated[g]
+        unit = key * lax.rsqrt(head_sum(key * key, ones) + UNIT_EPS)
+        log_decay = jnp.where(row_ids == edge, 0.0, log_decay)
+        tri = ((order if d == 0 else -order) >= 0).astype(F32).astype(BF16)
+        high, low = halves(log_decay)
+        totals = mm(tri, high) + mm(tri, low)
+        middle = totals[rows // 2 : rows // 2 + 1]
+        there = jnp.exp(middle - totals)
+        prev_ref[g] = -unit * jnp.exp(totals - log_decay - middle)
+        insert_ref[g] = rate * unit * there
+        key_ref[g] = key * there
+        here_ref[g] = jnp.exp(totals - middle)
+        final = rows - 1 - edge
+        rows_ref[g, 0:1] = there[edge : edge + 1]
+        rows_ref[g, 1:2] = middle
+        rows_ref[g, 2:3] = totals[final : final + 1]
 
 
 def blend(normed, mixing_ref, indices, rows, mixed):
@@ -187,8 +210,9 @@
 
 
 def chunk_kernel(direction_ref, *refs):
-    lanes, (halo_ref, edge_ref, low_ref, gain_ref, mixing_ref, w_k, w_v, *gate_refs) = refs[:4], refs[4:15]
-    state_ref, parts_ref, here_ref, read_edge_ref = refs[15:]
+    prev_ref, insert_ref, key_ref, value_ref, rows_ref = refs[:5]
+    halo_ref, edge_ref, low_ref, gain_ref, mixing_ref, w_k, w_v, *gate_refs = refs[5:16]
+    state_ref, parts_ref, start_ref, read_edge_ref = refs[16:]
     strands, _, rows, width = parts_ref.shape
     heads = width // HEAD
     d = direction_ref[0]
@@ -202,16 +226,17 @@
     low = mm_rows(jnp.concatenate([center, halo], axis=0).astype(BF16), low_ref[...])
     half = low.shape[1] // 2
     low = low[:strands, :half] + low[strands:, half:]
-    edges = [mm(mix(1), w_k[...]), mm(mix(2), w_v[...]), *gates(low, *[ref[...] for ref in gate_refs])]
+    edge_key, edge_value = mm(mix(1), w_k[...]), mm(mix(2), w_v[...])
+    edge_decay, edge_rate = gates(low, *[ref[...] for ref in gate_refs])
     read_edge_ref[...] = center + change * mixing_ref[0:1, :]
     edge_row = d * (rows - 1)
     at_edge = ids_of((rows, width), 0) == edge_row
     order = (ids_of((rows, rows), 0) - ids_of((rows, rows), 1)) * (1 - 2 * d)
-    strict, inclusive = order > 0, order >= 0
+    strict = order > 0
     same = block_ones(width)
     ones = same.astype(F32).astype(BF16)
     lane_head = ids_of((1, width), 1) // HEAD
-    tri = inclusive.astype(F32).astype(BF16)
+    edge_unit = edge_key * lax.rsqrt(head_sum(edge_key * edge_key, ones) + UNIT_EPS)
 
     def of_heads(value):
         return masked_heads(value, lane_head, heads)
@@ -219,21 +244,18 @@
     def prepared(s):
         g = d * strands + s
 
-        def lane(index, ref):
-            return jnp.where(at_edge, edges[index][s : s + 1], ref[g])
-
-        key, value, log_decay, rate = [lane(index, ref) for index, ref in enumerate(lanes)]
-        unit = key * lax.rsqrt(head_sum(key * key, ones) + UNIT_EPS)
-        high, low = halves(log_decay)
-        totals = mm(tri, high) + mm(tri, low)
-        middle = totals[rows // 2 : rows // 2 + 1]
-        final = jnp.where(d == 0, totals[rows - 1 : rows], totals[0:1])
-        there = jnp.exp(middle - totals)
-        left_prev = -unit * jnp.exp(totals - log_decay - middle)
-        right_insert = rate * unit * there
-        right_key = key * there
-        from_start = jnp.exp(middle)
+        def patched(ref, row):
+            return jnp.where(at_edge, row, ref[g])
+
+        one = slice(s, s + 1)
+        there, middle, final = [rows_ref[g, i : i + 1] for i in range(3)]
+        from_start = jnp.exp(middle + edge_decay[one])
         to_end = jnp.exp(final - middle)
+        final = final + edge_decay[one]
+        left_prev = patched(prev_ref, -edge_unit[one] * jnp.exp(-middle - edge_decay[one]))
+        right_insert = patched(insert_ref, edge_rate[one] * edge_unit[one] * there)
+        right_key = patched(key_ref, edge_key[one] * there)
+        value = patched(value_ref, edge_value[one])
         left = left_prev.astype(BF16)
         insert_pulls, key_pulls = [], []
         for h in range(heads):
@@ -246,8 +268,7 @@
             key_pulls.append(jnp.where(strict, scores[:, rows:], 0.0).astype(BF16))
         value_pull = mm(jnp.concatenate(key_pulls, axis=1), of_heads(value))
         value = value.astype(BF16)
-        here_ref[s, :rows] = jnp.exp(totals - middle)
-        here_ref[s, rows:] = jnp.broadcast_to(from_start, (here_ref.shape[1] - rows, width))
+        start_ref[s] = jnp.broadcast_to(from_start, start_ref.shape[1:])
         parts_ref[s, 0] = right_insert.astype(BF16)
         parts_ref[s, 1] = right_key.astype(BF16)
         parts_ref[s, 2] = value
@@ -276,18 +297,18 @@
 
 
 def read_kernel(
-    direction_ref, receptances, sent_ref, kept_ref, sent_here_ref, kept_here_ref, local_ref, map_ref
+    direction_ref, receptances, here_ref, sent_ref, kept_ref, sent_start_ref, kept_start_ref, local_ref, map_ref
 ):
     strands, _, rows, width = sent_ref.shape
     heads = width // HEAD
     lane_head = ids_of((1, width), 1) // HEAD
-    for role, (parts_ref, here_ref) in enumerate(((sent_ref, sent_here_ref), (kept_ref, kept_here_ref))):
+    for role, (parts_ref, start_ref) in enumerate(((sent_ref, sent_start_ref), (kept_ref, kept_start_ref))):
         d = (direction_ref[0] + role) % 2
         inclusive = (ids_of((rows, rows), 0) - ids_of((rows, rows), 1)) * (1 - 2 * d) >= 0
 
         def group(s, carry):
             insert, key, value, pull, start = [parts_ref[s, i] for i in range(5)]
-            left = receptances[d * strands + s] * here_ref[s, :rows]
+            left = receptances[d * strands + s] * here_ref[d * strands + s]
             here = left.astype(BF16)
             reads = []
             for source in (insert, key):
@@ -299,7 +320,7 @@
             ]
             g = role * strands + s
             local_ref[g] = mm(reads[0], pull) + mm(reads[1], value)
-            map_ref[g] = left * here_ref[s, rows : rows + 1] + mm(reads[0], start)
+            map_ref[g] = left * start_ref[s, 0:1] + mm(reads[0], start)
             return carry
 
         lax.fori_loop(0, strands, group, 0)
@@ -474,14 +495,15 @@
     groups = 2 * strands
     f32_lanes, bf16_lanes = struct((groups, rows, width), F32), struct((strands, rows, width), BF16)
     parts_struct = struct((strands, 5, rows, width), BF16)
-    here_struct = struct((strands, rows + 8, width), F32)
+    start_struct = struct((strands, 8, width), F32)
     state_struct = struct((strands, 2 * HEAD, width), BF16)
     entry_struct = struct((strands, HEAD, width), BF16)
     low_shape = (4 * decay_first_weight.shape[1], full)
-    *lanes, normed, low, edge = call(
+    *lanes, here, spans, normed, low, edge = call(
         project_kernel,
-        (f32_lanes,) * 4
+        (f32_lanes,) * 5
         + (
+            struct((groups, 8, width), F32),
             struct((strands, rows + 16, full), F32),
             struct(low_shape, BF16),
             struct((groups, full), F32),
@@ -498,13 +520,13 @@
     def chunk(direction, halo):
         return call(
             chunk_kernel,
-            (state_struct, parts_struct, here_struct, struct((strands, full), F32)),
-            in_specs=[SMEM_SPEC] + [VMEM_SPEC] * 15,
-        )(direction, *lanes, halo, edge, low, *params[:4], *params[6:])
-
-    sent, sent_parts, sent_here, sent_edge = chunk(parity, far)
+            (state_struct, parts_struct, start_struct, struct((strands, full), F32)),
+            in_specs=[SMEM_SPEC] + [VMEM_SPEC] * 16,
+        )(direction, *lanes, spans, halo, edge, low, *params[:4], *params[6:])
+
+    sent, sent_parts, sent_start, sent_edge = chunk(parity, far)
     from_partner = swapped(sent, "seq", 1)
-    kept, kept_parts, kept_here, kept_edge = chunk(1 - parity, near)
+    kept, kept_parts, kept_start, kept_edge = chunk(1 - parity, near)
 
     total = call(pair_kernel, state_struct, mib=4, us=1)(kept, from_partner)
     w_held, _ = lax.optimization_barrier((w_output, total))
@@ -542,8 +564,8 @@
         read_kernel,
         (f32_lanes, f32_lanes),
         mib=6,
-        in_specs=[SMEM_SPEC] + [VMEM_SPEC] * 5,
-    )(parity, receptances, sent_parts, kept_parts, sent_here, kept_here)
+        in_specs=[SMEM_SPEC] + [VMEM_SPEC] * 6,
+    )(parity, receptances, here, sent_parts, kept_parts, sent_start, kept_start)
     received, reads = lax.optimization_barrier((received, reads))
     entry = call(
         functools.partial(entry_kernel, bool(prefix)),

time: 65.1 us -> 65.6 us (level)
  waiting for transfers between devices: 8.23 us -> 10.9 us
  starting transfers between devices: 20.2 us -> 18.6 us
    ppermute x11, waiting for transfers between devices: 8.23 us -> 10.9 us  [swapped(): lax.ppermute(value, axis, [(i, i ^ mask) for i in range(lax.axis_size(axi...]
    ppermute x11, starting transfers between devices: 13.5 us -> 11.9 us  [swapped(): lax.ppermute(value, axis, [(i, i ^ mask) for i in range(lax.axis_size(axi...]
  transfers between devices with their start and end apart: 13 -> 13, of which waited for: 5 -> 6; matrix products, arithmetic and copies ran while one was open for 0% -> 0% of each run, Pallas kernels for 24% -> 23%
where the time goes in v11:
time: 65.6 us; the launch traced here: 65.4 us
  starting transfers between devices  18.6 us (28%)
  Pallas kernels  17.7 us (27%)
  blocking collectives  14.9 us (23%)
  waiting for transfers between devices  10.9 us (17%)
  local copies, waits for them, and re-layouts  2.29 us (3%)
  other arithmetic  0.69 us (1%)
    ppermute x11, starting transfers between devices, swapped(): lax.ppermute(value, axis, [(i, i ^ mask) for i in range(lax.axis_size(axi...  11.9 us
    ppermute x11, waiting for transfers between devices, swapped(): lax.ppermute(value, axis, [(i, i ^ mask) for i in range(lax.axis_size(axi...  10.9 us
    all_gather x1, blocking collectives, on_device(): joined_whole = lax.all_gather(joined, 'mp', axis=2, tiled=True)  7.55 us
    all_gather x1, blocking collectives, on_device(): whole = lax.all_gather(local, 'mp', axis=2, tiled=True)  7.3 us
    pallas_call x2, Pallas kernels, chunk(): call(chunk_kernel, (state_struct, parts_struct, start_struct, struct((str...  7.24 us
    ppermute x1, starting transfers between devices, on_device(): rc_here = lax.ppermute(hidden_rc, 'seq', mirror)  6 us
    pallas_call x1, Pallas kernels, on_device(): call(project_kernel, (f32_lanes,) * 5 + (struct((groups, 8, width), F32),...  2.58 us
    unnamed x40, local copies, waits for them, and re-layouts  2.29 us
  transfers between devices with their start and end apart: 13, of which 6 were waited for; matrix products, arithmetic and copies ran while one was open for 0% of the time, Pallas kernels for 23%

profile of v11, /device:TPU:0, one launch (start us, length us, event | category | flops | bytes accessed | tf_op | source)
XLA Modules:
  0.0 65.4 jit_solution(9208246626272118990)
XLA Ops:
  0.0 6.0 %collective-permute-start = (bf16[128,256]{1,0:T(8,128)(2,1)}, bf16[128,256]{1,0:T(8,128)(2,1)S(1)}, u32[]{:S(2)}, u32[]{:S(2)}) collective-permute-start(bf16[128,256]{1,0:T(8,128)(2,1)} %param.22), channel_id=1, source_target_pairs={{0,28},{4,24},{8,20},{12,16},{16,12},{20,8},{24,4},{28,0},{1,29},{... | collective-permute-start | bytes 196616 | tf_op jit(solution)/shard_map/ppermute | solution.py:468
  6.0 0.8 %copy-done.8 = bf16[128,256]{1,0:T(8,128)(2,1)S(1)} copy-done((bf16[128,256]{1,0:T(8,128)(2,1)S(1)}, bf16[128,256]{1,0:T(8,128)(2,1)}, u32[]{:S(2)}) %copy-start.8) | copy-done | bytes 65560
  6.8 0.7 %copy-done.12 = f32[4,256]{1,0:T(4,128)S(1)} copy-done((f32[4,256]{1,0:T(4,128)S(1)}, f32[4,256]{1,0:T(4,128)}, u32[]{:S(2)}) %copy-start.12) | copy-done | bytes 4120
  7.5 0.7 copy-done.18
  8.2 0.4 shard_map.190
  8.9 7.3 %all_gather.6.x_ref = bf16[2,128,1024]{2,1,0:T(8,128)(2,1)S(1)} all-gather(bf16[2,128,256]{2,1,0:T(8,128)(2,1)S(1)} %shard_map.191), channel_id=1, replica_groups=mesh['seq'=8,'mp'=4] {'mp'}, dimensions={2}, use_global_device_ids=true | all-gather | bytes 655360 | tf_op jit(solution)/shard_map/all_gather | solution.py:486
  16.3 0.7 %collective-permute-start.2 = (bf16[2,1024]{1,0:T(2,128)(2,1)S(1)}, bf16[2,1024]{1,0:T(2,128)(2,1)S(1)}, u32[]{:S(2)}, u32[]{:S(2)}) collective-permute-start(bf16[2,1024]{1,0:T(2,128)(2,1)S(1)} %bitcast.33), channel_id=1, source_target_pairs={{4,8},{12,16},{20,24},{8,4},{16,12},{24,20},{5,9},{13,17},{21,25},... | collective-permute-start | bytes 12296 | tf_op jit(solution)/shard_map/ppermute | solution.py:492
  17.0 2.6 %shard_map.192 = (f32[4,128,256]{2,1,0:T(8,128)S(1)}, f32[4,128,256]{2,1,0:T(8,128)S(1)}, f32[4,128,256]{2,1,0:T(8,128)S(1)}, f32[4,128,256]{2,1,0:T(8,128)S(1)}...) custom-call(bf16[2,128,1024]{2,1,0:T(8,128)(2,1)S(1)} %all_gather.6., ...), custom_call_target="tpu_custom_call" | custom-call | flops 10000000000 | bytes 10000000 | tf_op jit(solution)/shard_map/pallas_call | solution.py:502
  19.6 3.7 %collective-permute-start.1 = (bf16[2,1024]{1,0:T(2,128)(2,1)S(1)}, bf16[2,1024]{1,0:T(2,128)(2,1)S(1)}, u32[]{:S(2)}, u32[]{:S(2)}) collective-permute-start(bf16[2,1024]{1,0:T(2,128)(2,1)S(1)} %bitcast.34), channel_id=1, source_target_pairs={{0,4},{4,0},{8,12},{12,8},{16,20},{20,16},{24,28},{28,24},{1,5},{5... | collective-permute-start | bytes 12296 | tf_op jit(solution)/shard_map/ppermute | solution.py:437
  23.3 3.6 %shard_map.194 = (bf16[2,128,256]{2,1,0:T(8,128)(2,1)S(1)}, bf16[2,5,128,256]{3,2,1,0:T(8,128)(2,1)S(1)}, f32[2,8,256]{2,1,0:T(8,128)S(1)}, f32[2,1024]{1,0:T(2,128)S(1)}) custom-call(s32[1]{0:T(128)} %bitcast.1.direction_ref, f32[4,128,256]{2,1,0:T(8,128)S(1)} %get-tuple-element.54.refs_0_, f32[4,128,256]{2,1,0:T(8,128)S(1)} %get-tuple-element.55.refs_1_, ...), custom_call_target="tpu_custom_call" | custom-call | flops 10000000000 | bytes 10000000 | tf_op jit(solution)/shard_map/pallas_call | solution.py:521
  26.9 0.9 %collective-permute-start.3 = (bf16[2,128,256]{2,1,0:T(8,128)(2,1)S(1)}, bf16[2,128,256]{2,1,0:T(8,128)(2,1)S(1)}, u32[]{:S(2)}, u32[]{:S(2)}) collective-permute-start(bf16[2,128,256]{2,1,0:T(8,128)(2,1)S(1)} %get-tuple-element.63), channel_id=1, source_target_pairs={{0,4},{4,0},{8,12},{12,8},{16,20},{20,16},{24,28},{28,24},{1,5},{5... | collective-permute-start | bytes 393224 | tf_op jit(solution)/shard_map/ppermute | solution.py:437
  27.8 3.6 %shard_map.193 = (bf16[2,128,256]{2,1,0:T(8,128)(2,1)S(1)}, bf16[2,5,128,256]{3,2,1,0:T(8,128)(2,1)S(1)}, f32[2,8,256]{2,1,0:T(8,128)S(1)}, f32[2,1024]{1,0:T(2,128)S(1)}) custom-call(s32[1]{0:T(128)S(6)} %sub.3.direction_ref, f32[4,128,256]{2,1,0:T(8,128)S(1)} %get-tuple-element.54.refs_0_, f32[4,128,256]{2,1,0:T(8,128)S(1)} %get-tuple-element.55.refs_1_, ...), custom_call_target="tpu_custom_call" | custom-call | flops 10000000000 | bytes 10000000 | tf_op jit(solution)/shard_map/pallas_call | solution.py:521
  31.5 0.7 %collective-permute-done.3.from_ref = bf16[2,128,256]{2,1,0:T(8,128)(2,1)S(1)} collective-permute-done((bf16[2,128,256]{2,1,0:T(8,128)(2,1)S(1)}, bf16[2,128,256]{2,1,0:T(8,128)(2,1)S(1)}, u32[]{:S(2)}, u32[]{:S(2)}) %collective-permute-start.3) | collective-permute-done | bytes 131104 | tf_op jit(solution)/shard_map/ppermute | solution.py:437
  32.2 0.2 shard_map.195.total_ref
  32.4 1.1 %collective-permute-start.5 = (bf16[2,128,256]{2,1,0:T(8,128)(2,1)S(1)}, bf16[2,128,256]{2,1,0:T(8,128)(2,1)S(1)}, u32[]{:S(2)}, u32[]{:S(2)}) collective-permute-start(bf16[2,128,256]{2,1,0:T(8,128)(2,1)S(1)} %shard_map.195.total_ref), channel_id=1, source_target_pairs={{0,8},{4,12},{8,0},{12,4},{16,24},{20,28},{24,16},{28,20},{1,9},{5... | collective-permute-start | bytes 393224 | tf_op jit(solution)/shard_map/ppermute | solution.py:437
  33.5 0.8 %collective-permute-start.4 = (bf16[256,1024]{1,0:T(8,128)(2,1)S(1)}, bf16[256,1024]{1,0:T(8,128)(2,1)S(1)}, u32[]{:S(2)}, u32[]{:S(2)}) collective-permute-start(bf16[256,1024]{1,0:T(8,128)(2,1)S(1)} %copy-done.5), channel_id=1, source_target_pairs={{0,2},{1,3},{2,0},{3,1},{4,6},{5,7},{6,4},{7,5},{8,10},{9,11},{10,... | collective-permute-start | bytes 1572872 | tf_op jit(solution)/shard_map/ppermute | solution.py:437
  34.4 0.8 %shard_map.196.receptances = f32[4,128,256]{2,1,0:T(8,128)S(1)} custom-call(s32[1]{0:T(128)} %bitcast.1.direction_ref, f32[2,144,1024]{2,1,0:T(8,128)S(1)} %get-tuple-element.65.normed, f32[5,1024]{1,0:T(8,128)S(1)} %copy-done.11, f32[2,1024]{1,0:T(2,128)S(1)} %get-tuple-element.66.sent_edge_ref, f32[2,1024]{1,0:T(2,128)S(1)} %get-tuple-element.68.kept_edge_ref, ...), custom_call_target="tpu_custom_call" | custom-call | flops 3000000000 | bytes 3000000 | tf_op jit(solution)/shard_map/pallas_call | solution.py:535
  35.2 2.3 %collective-permute-done.5.from_ref = bf16[2,128,256]{2,1,0:T(8,128)(2,1)S(1)} collective-permute-done((bf16[2,128,256]{2,1,0:T(8,128)(2,1)S(1)}, bf16[2,128,256]{2,1,0:T(8,128)(2,1)S(1)}, u32[]{:S(2)}, u32[]{:S(2)}) %collective-permute-start.5) | collective-permute-done | bytes 131104 | tf_op jit(solution)/shard_map/ppermute | solution.py:437
  37.4 0.2 shard_map.197
  37.6 3.3 %collective-permute-start.6 = (bf16[2,64,256]{2,1,0:T(8,128)(2,1)S(1)}, bf16[2,64,256]{2,1,0:T(8,128)(2,1)S(1)}, u32[]{:S(2)}, u32[]{:S(2)}) collective-permute-start(bf16[2,64,256]{2,1,0:T(8,128)(2,1)S(1)} %get-tuple-element.70), channel_id=1, source_target_pairs={{0,16},{4,20},{8,24},{12,28},{16,0},{20,4},{24,8},{28,12},{1,17},{... | collective-permute-start | bytes 196616 | tf_op jit(solution)/shard_map/ppermute | solution.py:437
  40.9 2.1 %shard_map.198 = (f32[4,128,256]{2,1,0:T(8,128)S(1)}, f32[4,128,256]{2,1,0:T(8,128)S(1)}) custom-call(s32[1]{0:T(128)} %bitcast.1.direction_ref, f32[4,128,256]{2,1,0:T(8,128)S(1)} %shard_map.196.receptances, f32[4,128,256]{2,1,0:T(8,128)S(1)} %get-tuple-element.72.here_ref, bf16[2,5,128,256]{3,2,1,0:T(8,128)(2,1)S(1)} %get-tuple-element.75.sent_ref, ...), custom_call_target="tpu_custom_call" | custom-call | flops 10000000000 | bytes 10000000 | tf_op jit(solution)/shard_map/pallas_call | solution.py:563
  43.0 0.8 %collective-permute-done.6.from_ref = bf16[2,64,256]{2,1,0:T(8,128)(2,1)S(1)} collective-permute-done((bf16[2,64,256]{2,1,0:T(8,128)(2,1)S(1)}, bf16[2,64,256]{2,1,0:T(8,128)(2,1)S(1)}, u32[]{:S(2)}, u32[]{:S(2)}) %collective-permute-start.6) | collective-permute-done | bytes 65568 | tf_op jit(solution)/shard_map/ppermute | solution.py:437
  44.1 1.0 %shard_map.200.kept_ref = f32[2,128,256]{2,1,0:T(8,128)S(1)} custom-call(bf16[2,64,256]{2,1,0:T(8,128)(2,1)S(1)} %shard_map.199.entry_ref, bf16[2,128,256]{2,1,0:T(8,128)(2,1)S(1)} %collective-permute-done.3.from_ref, f32[4,128,256]{2,1,0:T(8,128)S(1)} %get-tuple-element.83.local_ref, f32[4,128,256]{2,1,0:T(8,128)S(1)} %get-tuple-element.84.map_ref), custom_call_target="tpu_custom_call" | custom-call | flops 3000000000 | bytes 3000000 | tf_op jit(solution)/shard_map/pallas_call | solution.py:578
  45.1 3.3 %collective-permute-done.7.other_ref = bf16[2,64,256]{2,1,0:T(8,128)(2,1)S(1)} collective-permute-done((bf16[2,64,256]{2,1,0:T(8,128)(2,1)S(1)}, bf16[2,64,256]{2,1,0:T(8,128)(2,1)S(1)}, u32[]{:S(2)}, u32[]{:S(2)}) %collective-permute-start.7) | collective-permute-done | bytes 65568 | tf_op jit(solution)/shard_map/ppermute | solution.py:437
  48.4 0.8 %shard_map.201 = bf16[2,128,256]{2,1,0:T(8,128)(2,1)S(1)} custom-call(bf16[2,64,256]{2,1,0:T(8,128)(2,1)S(1)} %collective-permute-done.7.other_ref, f32[2,128,256]{2,1,0:T(8,128)S(1)} %shard_map.200.kept_ref, f32[4,128,256]{2,1,0:T(8,128)S(1)} %get-tuple-element.83.local_ref, f32[4,128,256]{2,1,0:T(8,128)S(1)} %get-tuple-element.84.map_ref, ...), custom_call_target="tpu_custom_call" | custom-call | flops 10000000000 | bytes 10000000 | tf_op jit(solution)/shard_map/pallas_call | solution.py:581
  49.2 7.6 %all_gather.7.joined_ref = bf16[2,128,1024]{2,1,0:T(8,128)(2,1)S(1)} all-gather(bf16[2,128,256]{2,1,0:T(8,128)(2,1)S(1)} %shard_map.201), channel_id=1, replica_groups=mesh['seq'=8,'mp'=4] {'mp'}, dimensions={2}, use_global_device_ids=true | all-gather | bytes 655360 | tf_op jit(solution)/shard_map/all_gather | solution.py:582
  56.8 2.0 %shard_map.202 = (f32[128,256]{1,0:T(8,128)S(1)}, bf16[128,256]{1,0:T(8,128)(2,1)S(1)}, bf16[128,256]{1,0:T(8,128)(2,1)S(1)}, bf16[128,256]{1,0:T(8,128)(2,1)S(1)}) custom-call(s32[1]{0:T(128)} %bitcast.index_ref, bf16[2,128,1024]{2,1,0:T(8,128)(2,1)S(1)} %all_gather.7.joined_ref, bf16[2,128,1024]{2,1,0:T(8,128)(2,1)S(1)} %all_gather.6.x_ref, ...), custom_call_target="tpu_custom_call" | custom-call | flops 10000000000 | bytes 10000000 | tf_op jit(solution)/shard_map/pallas_call | solution.py:586
  58.9 0.8 %collective-permute-start.12 = (bf16[128,256]{1,0:T(8,128)(2,1)S(1)}, bf16[128,256]{1,0:T(8,128)(2,1)S(1)}, u32[]{:S(2)}, u32[]{:S(2)}) collective-permute-start(bf16[128,256]{1,0:T(8,128)(2,1)S(1)} %get-tuple-element.92), channel_id=1, source_target_pairs={{0,3},{1,2},{2,1},{3,0},{4,7},{5,6},{6,5},{7,4},{8,11},{9,10},{10,... | collective-permute-start | bytes 196616 | tf_op jit(solution)/shard_map/ppermute | solution.py:437
  59.7 1.2 %collective-permute-start.11 = (bf16[128,256]{1,0:T(8,128)(2,1)S(1)}, bf16[128,256]{1,0:T(8,128)(2,1)S(1)}, u32[]{:S(2)}, u32[]{:S(2)}) collective-permute-start(bf16[128,256]{1,0:T(8,128)(2,1)S(1)} %get-tuple-element.91), channel_id=1, source_target_pairs={{0,2},{1,3},{2,0},{3,1},{4,6},{5,7},{6,4},{7,5},{8,10},{9,11},{10,... | collective-permute-start | bytes 196616 | tf_op jit(solution)/shard_map/ppermute | solution.py:437
  60.9 1.9 %collective-permute-done.12 = bf16[128,256]{1,0:T(8,128)(2,1)S(1)} collective-permute-done((bf16[128,256]{1,0:T(8,128)(2,1)S(1)}, bf16[128,256]{1,0:T(8,128)(2,1)S(1)}, u32[]{:S(2)}, u32[]{:S(2)}) %collective-permute-start.12) | collective-permute-done | bytes 65568 | tf_op jit(solution)/shard_map/ppermute | solution.py:437
  62.8 1.9 %collective-permute-done.11 = bf16[128,256]{1,0:T(8,128)(2,1)S(1)} collective-permute-done((bf16[128,256]{1,0:T(8,128)(2,1)S(1)}, bf16[128,256]{1,0:T(8,128)(2,1)S(1)}, u32[]{:S(2)}, u32[]{:S(2)}) %collective-permute-start.11) | collective-permute-done | bytes 65568 | tf_op jit(solution)/shard_map/ppermute | solution.py:437
  64.7 0.7 %add_convert_fusion = bf16[128,256]{1,0:T(8,128)(2,1)} fusion(bf16[128,256]{1,0:T(8,128)(2,1)S(1)} %collective-permute-done.12, bf16[128,256]{1,0:T(8,128)(2,1)S(1)} %collective-permute-done.11, f32[128,256]{1,0:T(8,128)S(1)} %get-tuple-element.89, bf16[128,256]{1,0:T(8,128)(2,1)S(1)} %collective-permute-done.10), kind=kLoop, calls=%fused_computation | loop fusion | flops 229376 | bytes 393216 | tf_op jit(solution)/shard_map/convert_element_type | solution.py:599
  (51 shorter events, 0.6 us)
Async XLA Ops:
  0.0 8.6 %collective-permute-start = (bf16[128,256]{1,0:T(8,128)(2,1)}, bf16[128,256]{1,0:T(8,128)(2,1)S(1)}, u32[]{:S(2)}, u32[]{:S(2)}) collective-permute-start(bf16[128,256]{1,0:T(8,128)(2,1)} %param.22), channel_id=1, source_target_pairs={{0,28},{4,24},{8,20},{12,16},{16,12},{20,8},{24,4},{28,0},{1,29},{... | collective-permute-start | bytes 196616 | tf_op jit(solution)/shard_map/ppermute | solution.py:468
  6.0 0.8 %copy-start.8 = (bf16[128,256]{1,0:T(8,128)(2,1)S(1)}, bf16[128,256]{1,0:T(8,128)(2,1)}, u32[]{:S(2)}) copy-start(bf16[128,256]{1,0:T(8,128)(2,1)} %fwd_ref.1) | copy-start | bytes 196612
  6.8 0.7 %copy-start.12 = (f32[4,256]{1,0:T(4,128)S(1)}, f32[4,256]{1,0:T(4,128)}, u32[]{:S(2)}) copy-start(f32[4,256]{1,0:T(4,128)} %embed_ref.1) | copy-start | bytes 12292
  7.5 0.7 %copy-start.18 = (s32[128]{0:T(128)S(1)}, s32[128]{0:T(128)}, u32[]{:S(2)}) copy-start(s32[128]{0:T(128)} %param.20) | copy-start | bytes 1540
  8.7 8.3 %copy-start.2 = (bf16[1024,256]{1,0:T(8,128)(2,1)S(1)}, bf16[1024,256]{1,0:T(8,128)(2,1)}, u32[]{:S(2)}) copy-start(bf16[1024,256]{1,0:T(8,128)(2,1)} %refs_10_.3) | copy-start | bytes 1572868
  8.7 8.3 %copy-start.3 = (bf16[1024,256]{1,0:T(8,128)(2,1)S(1)}, bf16[1024,256]{1,0:T(8,128)(2,1)}, u32[]{:S(2)}) copy-start(bf16[1024,256]{1,0:T(8,128)(2,1)} %refs_11_.3) | copy-start | bytes 1572868
  8.7 8.3 %copy-start.6 = (bf16[1024,64]{0,1:T(8,128)(2,1)S(1)}, bf16[1024,64]{0,1:T(8,128)(2,1)}, u32[]{:S(2)}) copy-start(bf16[1024,64]{0,1:T(8,128)(2,1)} %param.30) | copy-start | bytes 393220
  8.7 8.3 %copy-start.7 = (bf16[1024,64]{0,1:T(8,128)(2,1)S(1)}, bf16[1024,64]{0,1:T(8,128)(2,1)}, u32[]{:S(2)}) copy-start(bf16[1024,64]{0,1:T(8,128)(2,1)} %param.33) | copy-start | bytes 393220
  8.7 8.3 %copy-start.9 = (bf16[64,256]{1,0:T(8,128)(2,1)S(1)}, bf16[64,256]{1,0:T(8,128)(2,1)}, u32[]{:S(2)}) copy-start(bf16[64,256]{1,0:T(8,128)(2,1)} %refs_12_.3) | copy-start | bytes 98308
  8.7 8.3 %copy-start.10 = (bf16[64,256]{1,0:T(8,128)(2,1)S(1)}, bf16[64,256]{1,0:T(8,128)(2,1)}, u32[]{:S(2)}) copy-start(bf16[64,256]{1,0:T(8,128)(2,1)} %refs_13_.3) | copy-start | bytes 98308
  8.7 8.3 %copy-start.11 = (f32[5,1024]{1,0:T(8,128)S(1)}, f32[5,1024]{1,0:T(8,128)}, u32[]{:S(2)}) copy-start(f32[5,1024]{1,0:T(8,128)} %mixing_ref.3) | copy-start | bytes 61444
  8.7 8.3 %copy-start.13 = (f32[1024]{0:T(1024)S(1)}, f32[1024]{0:T(1024)}, u32[]{:S(2)}) copy-start(f32[1024]{0:T(1024)} %param.24) | copy-start | bytes 12292
  8.8 8.3 %copy-start.15 = (f32[256]{0:T(256)S(1)}, f32[256]{0:T(256)}, u32[]{:S(2)}) copy-start(f32[256]{0:T(256)} %param.31) | copy-start | bytes 3076
  8.8 8.3 %copy-start.16 = (f32[256]{0:T(256)S(1)}, f32[256]{0:T(256)}, u32[]{:S(2)}) copy-start(f32[256]{0:T(256)} %param.34) | copy-start | bytes 3076
  16.3 7.0 %collective-permute-start.2 = (bf16[2,1024]{1,0:T(2,128)(2,1)S(1)}, bf16[2,1024]{1,0:T(2,128)(2,1)S(1)}, u32[]{:S(2)}, u32[]{:S(2)}) collective-permute-start(bf16[2,1024]{1,0:T(2,128)(2,1)S(1)} %bitcast.33), channel_id=1, source_target_pairs={{4,8},{12,16},{20,24},{8,4},{16,12},{24,20},{5,9},{13,17},{21,25},... | collective-permute-start | bytes 12296 | tf_op jit(solution)/shard_map/ppermute | solution.py:492
  19.6 8.2 %collective-permute-start.1 = (bf16[2,1024]{1,0:T(2,128)(2,1)S(1)}, bf16[2,1024]{1,0:T(2,128)(2,1)S(1)}, u32[]{:S(2)}, u32[]{:S(2)}) collective-permute-start(bf16[2,1024]{1,0:T(2,128)(2,1)S(1)} %bitcast.34), channel_id=1, source_target_pairs={{0,4},{4,0},{8,12},{12,8},{16,20},{20,16},{24,28},{28,24},{1,5},{5... | collective-permute-start | bytes 12296 | tf_op jit(solution)/shard_map/ppermute | solution.py:437
  26.9 5.3 %collective-permute-start.3 = (bf16[2,128,256]{2,1,0:T(8,128)(2,1)S(1)}, bf16[2,128,256]{2,1,0:T(8,128)(2,1)S(1)}, u32[]{:S(2)}, u32[]{:S(2)}) collective-permute-start(bf16[2,128,256]{2,1,0:T(8,128)(2,1)S(1)} %get-tuple-element.63), channel_id=1, source_target_pairs={{0,4},{4,0},{8,12},{12,8},{16,20},{20,16},{24,28},{28,24},{1,5},{5... | collective-permute-start | bytes 393224 | tf_op jit(solution)/shard_map/ppermute | solution.py:437
  31.4 2.1 %copy-start.5 = (bf16[256,1024]{1,0:T(8,128)(2,1)S(1)}, bf16[256,1024]{1,0:T(8,128)(2,1)}, u32[]{:S(2)}) copy-start(bf16[256,1024]{1,0:T(8,128)(2,1)} %refs_0_.1) | copy-start | bytes 1572868
  31.4 2.9 %copy-start.4 = (bf16[1024,256]{1,0:T(8,128)(2,1)S(1)}, bf16[1024,256]{1,0:T(8,128)(2,1)}, u32[]{:S(2)}) copy-start(bf16[1024,256]{1,0:T(8,128)(2,1)} %w_r.1) | copy-start | bytes 1572868
  32.4 5.0 %collective-permute-start.5 = (bf16[2,128,256]{2,1,0:T(8,128)(2,1)S(1)}, bf16[2,128,256]{2,1,0:T(8,128)(2,1)S(1)}, u32[]{:S(2)}, u32[]{:S(2)}) collective-permute-start(bf16[2,128,256]{2,1,0:T(8,128)(2,1)S(1)} %shard_map.195.total_ref), channel_id=1, source_target_pairs={{0,8},{4,12},{8,0},{12,4},{16,24},{20,28},{24,16},{28,20},{1,9},{5... | collective-permute-start | bytes 393224 | tf_op jit(solution)/shard_map/ppermute | solution.py:437
  33.5 14.8 %collective-permute-start.4 = (bf16[256,1024]{1,0:T(8,128)(2,1)S(1)}, bf16[256,1024]{1,0:T(8,128)(2,1)S(1)}, u32[]{:S(2)}, u32[]{:S(2)}) collective-permute-start(bf16[256,1024]{1,0:T(8,128)(2,1)S(1)} %copy-done.5), channel_id=1, source_target_pairs={{0,2},{1,3},{2,0},{3,1},{4,6},{5,7},{6,4},{7,5},{8,10},{9,11},{10,... | collective-permute-start | bytes 1572872 | tf_op jit(solution)/shard_map/ppermute | solution.py:437
  37.6 6.2 %collective-permute-start.6 = (bf16[2,64,256]{2,1,0:T(8,128)(2,1)S(1)}, bf16[2,64,256]{2,1,0:T(8,128)(2,1)S(1)}, u32[]{:S(2)}, u32[]{:S(2)}) collective-permute-start(bf16[2,64,256]{2,1,0:T(8,128)(2,1)S(1)} %get-tuple-element.70), channel_id=1, source_target_pairs={{0,16},{4,20},{8,24},{12,28},{16,0},{20,4},{24,8},{28,12},{1,17},{... | collective-permute-start | bytes 196616 | tf_op jit(solution)/shard_map/ppermute | solution.py:437
  40.9 15.9 %collective-permute-start.8 = (bf16[256,1024]{1,0:T(8,128)(2,1)S(1)}, bf16[256,1024]{1,0:T(8,128)(2,1)S(1)}, u32[]{:S(2)}, u32[]{:S(2)}) collective-permute-start(bf16[256,1024]{1,0:T(8,128)(2,1)S(1)} %copy-done.5), channel_id=1, source_target_pairs={{0,1},{1,0},{2,3},{3,2},{4,5},{5,4},{6,7},{7,6},{8,9},{9,8},{10,11... | collective-permute-start | bytes 1572872 | tf_op jit(solution)/shard_map/ppermute | solution.py:437
  44.0 4.4 %copy-start.17 = (f32[256]{0:T(256)S(1)}, f32[256]{0:T(256)}, u32[]{:S(2)}) copy-start(f32[256]{0:T(256)} %param.36) | copy-start | bytes 3076
  44.0 4.3 %collective-permute-start.7 = (bf16[2,64,256]{2,1,0:T(8,128)(2,1)S(1)}, bf16[2,64,256]{2,1,0:T(8,128)(2,1)S(1)}, u32[]{:S(2)}, u32[]{:S(2)}) collective-permute-start(bf16[2,64,256]{2,1,0:T(8,128)(2,1)S(1)} %shard_map.199.entry_ref), channel_id=1, source_target_pairs={{0,4},{4,0},{8,12},{12,8},{16,20},{20,16},{24,28},{28,24},{1,5},{5... | collective-permute-start | bytes 196616 | tf_op jit(solution)/shard_map/ppermute | solution.py:437
  48.4 8.4 %collective-permute-start.9 = (bf16[256,1024]{1,0:T(8,128)(2,1)S(1)}, bf16[256,1024]{1,0:T(8,128)(2,1)S(1)}, u32[]{:S(2)}, u32[]{:S(2)}) collective-permute-start(bf16[256,1024]{1,0:T(8,128)(2,1)S(1)} %collective-permute-done.4.refs_2_), channel_id=1, source_target_pairs={{0,1},{1,0},{2,3},{3,2},{4,5},{5,4},{6,7},{7,6},{8,9},{9,8},{10,11... | collective-permute-start | bytes 1572872 | tf_op jit(solution)/shard_map/ppermute | solution.py:437
  48.4 8.4 %copy-start = (bf16[1024,1024]{1,0:T(8,128)(2,1)S(1)}, bf16[1024,1024]{1,0:T(8,128)(2,1)}, u32[]{:S(2)}) copy-start(bf16[1024,1024]{1,0:T(8,128)(2,1)} %refs_4_.1) | copy-start | bytes 6291460
  48.4 8.4 %copy-start.1 = (bf16[1024,1024]{1,0:T(8,128)(2,1)S(1)}, bf16[1024,1024]{1,0:T(8,128)(2,1)}, u32[]{:S(2)}) copy-start(bf16[1024,1024]{1,0:T(8,128)(2,1)} %refs_5_.1) | copy-start | bytes 6291460
  48.4 8.4 %copy-start.14 = (f32[1024]{0:T(1024)S(1)}, f32[1024]{0:T(1024)}, u32[]{:S(2)}) copy-start(f32[1024]{0:T(1024)} %param.25) | copy-start | bytes 12292
  58.9 4.0 %collective-permute-start.12 = (bf16[128,256]{1,0:T(8,128)(2,1)S(1)}, bf16[128,256]{1,0:T(8,128)(2,1)S(1)}, u32[]{:S(2)}, u32[]{:S(2)}) collective-permute-start(bf16[128,256]{1,0:T(8,128)(2,1)S(1)} %get-tuple-element.92), channel_id=1, source_target_pairs={{0,3},{1,2},{2,1},{3,0},{4,7},{5,6},{6,5},{7,4},{8,11},{9,10},{10,... | collective-permute-start | bytes 196616 | tf_op jit(solution)/shard_map/ppermute | solution.py:437
  59.7 5.0 %collective-permute-start.11 = (bf16[128,256]{1,0:T(8,128)(2,1)S(1)}, bf16[128,256]{1,0:T(8,128)(2,1)S(1)}, u32[]{:S(2)}, u32[]{:S(2)}) collective-permute-start(bf16[128,256]{1,0:T(8,128)(2,1)S(1)} %get-tuple-element.91), channel_id=1, source_target_pairs={{0,2},{1,3},{2,0},{3,1},{4,6},{5,7},{6,4},{7,5},{8,10},{9,11},{10,... | collective-permute-start | bytes 196616 | tf_op jit(solution)/shard_map/ppermute | solution.py:437
  60.9 3.8 %collective-permute-start.10 = (bf16[128,256]{1,0:T(8,128)(2,1)S(1)}, bf16[128,256]{1,0:T(8,128)(2,1)S(1)}, u32[]{:S(2)}, u32[]{:S(2)}) collective-permute-start(bf16[128,256]{1,0:T(8,128)(2,1)S(1)} %get-tuple-element.90), channel_id=1, source_target_pairs={{0,1},{1,0},{2,3},{3,2},{4,5},{5,4},{6,7},{7,6},{8,9},{9,8},{10,11... | collective-permute-start | bytes 196616 | tf_op jit(solution)/shard_map/ppermute | solution.py:437

commit v12 on v11

--- a/solution.py
+++ b/solution.py
@@ -514,7 +514,8 @@
         ],
     )(whole, *params)
 
-    beside, _ = lax.optimization_barrier((jnp.where(parity == 1, first, last), edge))
+    beside, w_held, _ = lax.optimization_barrier((jnp.where(parity == 1, first, last), w_output, edge))
+    w_across = swapped(w_held, "mp", 2)
     near = swapped(beside, "seq", 1)
 
     def chunk(direction, halo):
@@ -529,8 +530,6 @@
     kept, kept_parts, kept_start, kept_edge = chunk(1 - parity, near)
 
     total = call(pair_kernel, state_struct, mib=4, us=1)(kept, from_partner)
-    w_held, _ = lax.optimization_barrier((w_output, total))
-    w_across = swapped(w_held, "mp", 2)
     kept_edge, _ = lax.optimization_barrier((kept_edge, total))
     receptances = call(
         receptance_kernel,
@@ -557,9 +556,10 @@
             in_specs=[SMEM_SPEC] + [VMEM_SPEC] * (2 + len(prefix)),
         )(later, total, received, *prefix)
         prefix = [wide]
-    w_held, _ = lax.optimization_barrier((w_output, total))
-    w_beside = swapped(w_held, "mp", 1)
-    sent_parts, kept_parts, _ = lax.optimization_barrier((sent_parts, kept_parts, total))
+    sent_parts, kept_parts, w_across, w_held, _ = lax.optimization_barrier(
+        (sent_parts, kept_parts, w_across, w_output, total)
+    )
+    w_beside, w_opposite = swapped(w_held, "mp", 1), swapped(w_across, "mp", 1)
     reads = call(
         read_kernel,
         (f32_lanes, f32_lanes),
@@ -576,8 +576,7 @@
     )(later, received, *prefix)
     other = swapped(entry, "seq", 1)
     kept_heads = call(kept_kernel, struct(bf16_lanes.shape, F32), mib=6, us=3)(entry, from_partner, *reads)
-    w_across, other, kept_heads = lax.optimization_barrier((w_across, other, kept_heads))
-    w_opposite = swapped(w_across, "mp", 1)
+    w_beside, w_opposite, other, kept_heads = lax.optimization_barrier((w_beside, w_opposite, other, kept_heads))
     joined = call(finish_kernel, bf16_lanes, mib=6)(other, kept_heads, *reads, group_gain.reshape(1, width))
     joined_whole = lax.all_gather(joined, "mp", axis=2, tiled=True)
 

time: 65.6 us -> 65.5 us (level)
  transfers between devices with their start and end apart: 13 -> 13, of which waited for: 6 -> 6; matrix products, arithmetic and copies ran while one was open for 0% -> 0% of each run, Pallas kernels for 23% -> 22%
where the time goes in v12:
time: 65.5 us; the launch traced here: 65.2 us
  starting transfers between devices  18.8 us (29%)
  Pallas kernels  17.6 us (27%)
  blocking collectives  14.3 us (22%)
  waiting for transfers between devices  11.1 us (17%)
  local copies, waits for them, and re-layouts  2.29 us (3%)
  other arithmetic  0.69 us (1%)
    ppermute x11, starting transfers between devices, swapped(): lax.ppermute(value, axis, [(i, i ^ mask) for i in range(lax.axis_size(axi...  12.2 us
    ppermute x11, waiting for transfers between devices, swapped(): lax.ppermute(value, axis, [(i, i ^ mask) for i in range(lax.axis_size(axi...  11.1 us
    all_gather x1, blocking collectives, on_device(): whole = lax.all_gather(local, 'mp', axis=2, tiled=True)  7.3 us
    pallas_call x2, Pallas kernels, chunk(): call(chunk_kernel, (state_struct, parts_struct, start_struct, struct((str...  7.24 us
    all_gather x1, blocking collectives, on_device(): joined_whole = lax.all_gather(joined, 'mp', axis=2, tiled=True)  7.01 us
    ppermute x1, starting transfers between devices, on_device(): rc_here = lax.ppermute(hidden_rc, 'seq', mirror)  6 us
    pallas_call x1, Pallas kernels, on_device(): call(project_kernel, (f32_lanes,) * 5 + (struct((groups, 8, width), F32),...  2.58 us
    unnamed x40, local copies, waits for them, and re-layouts  2.29 us
  transfers between devices with their start and end apart: 13, of which 6 were waited for; matrix products, arithmetic and copies ran while one was open for 0% of the time, Pallas kernels for 22%

profile of v12, /device:TPU:0, one launch (start us, length us, event | category | flops | bytes accessed | tf_op | source)
XLA Modules:
  0.0 65.2 jit_solution(4664250936097933650)
XLA Ops:
  0.0 6.0 %collective-permute-start = (bf16[128,256]{1,0:T(8,128)(2,1)}, bf16[128,256]{1,0:T(8,128)(2,1)S(1)}, u32[]{:S(2)}, u32[]{:S(2)}) collective-permute-start(bf16[128,256]{1,0:T(8,128)(2,1)} %param.22), channel_id=1, source_target_pairs={{0,28},{4,24},{8,20},{12,16},{16,12},{20,8},{24,4},{28,0},{1,29},{... | collective-permute-start | bytes 196616 | tf_op jit(solution)/shard_map/ppermute | solution.py:468
  6.0 0.8 %copy-done.8 = bf16[128,256]{1,0:T(8,128)(2,1)S(1)} copy-done((bf16[128,256]{1,0:T(8,128)(2,1)S(1)}, bf16[128,256]{1,0:T(8,128)(2,1)}, u32[]{:S(2)}) %copy-start.8) | copy-done | bytes 65560
  6.8 0.7 %copy-done.12 = f32[4,256]{1,0:T(4,128)S(1)} copy-done((f32[4,256]{1,0:T(4,128)S(1)}, f32[4,256]{1,0:T(4,128)}, u32[]{:S(2)}) %copy-start.12) | copy-done | bytes 4120
  7.5 0.7 %copy-done.18 = s32[128]{0:T(128)S(1)} copy-done((s32[128]{0:T(128)S(1)}, s32[128]{0:T(128)}, u32[]{:S(2)}) %copy-start.18) | copy-done | bytes 536
  8.2 0.4 shard_map.190
  8.9 7.3 %all_gather.6.x_ref = bf16[2,128,1024]{2,1,0:T(8,128)(2,1)S(1)} all-gather(bf16[2,128,256]{2,1,0:T(8,128)(2,1)S(1)} %shard_map.191), channel_id=1, replica_groups=mesh['seq'=8,'mp'=4] {'mp'}, dimensions={2}, use_global_device_ids=true | all-gather | bytes 655360 | tf_op jit(solution)/shard_map/all_gather | solution.py:486
  16.3 0.7 %collective-permute-start.1 = (bf16[2,1024]{1,0:T(2,128)(2,1)S(1)}, bf16[2,1024]{1,0:T(2,128)(2,1)S(1)}, u32[]{:S(2)}, u32[]{:S(2)}) collective-permute-start(bf16[2,1024]{1,0:T(2,128)(2,1)S(1)} %bitcast.33), channel_id=1, source_target_pairs={{4,8},{12,16},{20,24},{8,4},{16,12},{24,20},{5,9},{13,17},{21,25},... | collective-permute-start | bytes 12296 | tf_op jit(solution)/shard_map/ppermute | solution.py:492
  17.1 2.6 %shard_map.192 = (f32[4,128,256]{2,1,0:T(8,128)S(1)}, f32[4,128,256]{2,1,0:T(8,128)S(1)}, f32[4,128,256]{2,1,0:T(8,128)S(1)}, f32[4,128,256]{2,1,0:T(8,128)S(1)}...) custom-call(bf16[2,128,1024]{2,1,0:T(8,128)(2,1)S(1)} %all_gather.6., ...), custom_call_target="tpu_custom_call" | custom-call | flops 10000000000 | bytes 10000000 | tf_op jit(solution)/shard_map/pallas_call | solution.py:502
  19.7 3.7 %collective-permute-start.2 = (bf16[2,1024]{1,0:T(2,128)(2,1)S(1)}, bf16[2,1024]{1,0:T(2,128)(2,1)S(1)}, u32[]{:S(2)}, u32[]{:S(2)}) collective-permute-start(bf16[2,1024]{1,0:T(2,128)(2,1)S(1)} %bitcast.34), channel_id=1, source_target_pairs={{0,4},{4,0},{8,12},{12,8},{16,20},{20,16},{24,28},{28,24},{1,5},{5... | collective-permute-start | bytes 12296 | tf_op jit(solution)/shard_map/ppermute | solution.py:437
  23.3 0.8 %collective-permute-start.3 = (bf16[256,1024]{1,0:T(8,128)(2,1)S(1)}, bf16[256,1024]{1,0:T(8,128)(2,1)S(1)}, u32[]{:S(2)}, u32[]{:S(2)}) collective-permute-start(bf16[256,1024]{1,0:T(8,128)(2,1)S(1)} %copy-done.5), channel_id=1, source_target_pairs={{0,2},{1,3},{2,0},{3,1},{4,6},{5,7},{6,4},{7,5},{8,10},{9,11},{10,... | collective-permute-start | bytes 1572872 | tf_op jit(solution)/shard_map/ppermute | solution.py:437
  24.1 3.6 %shard_map.193 = (bf16[2,128,256]{2,1,0:T(8,128)(2,1)S(1)}, bf16[2,5,128,256]{3,2,1,0:T(8,128)(2,1)S(1)}, f32[2,8,256]{2,1,0:T(8,128)S(1)}, f32[2,1024]{1,0:T(2,128)S(1)}) custom-call(s32[1]{0:T(128)} %bitcast.1.direction_ref, f32[4,128,256]{2,1,0:T(8,128)S(1)} %get-tuple-element.56.refs_0_, f32[4,128,256]{2,1,0:T(8,128)S(1)} %get-tuple-element.57.refs_1_, ...), custom_call_target="tpu_custom_call" | custom-call | flops 10000000000 | bytes 10000000 | tf_op jit(solution)/shard_map/pallas_call | solution.py:522
  27.9 3.6 %shard_map.194 = (bf16[2,128,256]{2,1,0:T(8,128)(2,1)S(1)}, bf16[2,5,128,256]{3,2,1,0:T(8,128)(2,1)S(1)}, f32[2,8,256]{2,1,0:T(8,128)S(1)}, f32[2,1024]{1,0:T(2,128)S(1)}) custom-call(s32[1]{0:T(128)S(6)} %sub.3.direction_ref, f32[4,128,256]{2,1,0:T(8,128)S(1)} %get-tuple-element.56.refs_0_, f32[4,128,256]{2,1,0:T(8,128)S(1)} %get-tuple-element.57.refs_1_, ...), custom_call_target="tpu_custom_call" | custom-call | flops 10000000000 | bytes 10000000 | tf_op jit(solution)/shard_map/pallas_call | solution.py:522
  31.6 1.2 %collective-permute-done.4.from_ref = bf16[2,128,256]{2,1,0:T(8,128)(2,1)S(1)} collective-permute-done((bf16[2,128,256]{2,1,0:T(8,128)(2,1)S(1)}, bf16[2,128,256]{2,1,0:T(8,128)(2,1)S(1)}, u32[]{:S(2)}, u32[]{:S(2)}) %collective-permute-start.4) | collective-permute-done | bytes 131104 | tf_op jit(solution)/shard_map/ppermute | solution.py:437
  33.0 1.3 %collective-permute-start.5 = (bf16[2,128,256]{2,1,0:T(8,128)(2,1)S(1)}, bf16[2,128,256]{2,1,0:T(8,128)(2,1)S(1)}, u32[]{:S(2)}, u32[]{:S(2)}) collective-permute-start(bf16[2,128,256]{2,1,0:T(8,128)(2,1)S(1)} %shard_map.195.total_ref), channel_id=1, source_target_pairs={{0,8},{4,12},{8,0},{12,4},{16,24},{20,28},{24,16},{28,20},{1,9},{5... | collective-permute-start | bytes 393224 | tf_op jit(solution)/shard_map/ppermute | solution.py:437
  34.4 0.8 %shard_map.196.receptances = f32[4,128,256]{2,1,0:T(8,128)S(1)} custom-call(s32[1]{0:T(128)} %bitcast.1.direction_ref, f32[2,144,1024]{2,1,0:T(8,128)S(1)} %get-tuple-element.69.normed, f32[5,1024]{1,0:T(8,128)S(1)} %copy-done.11, f32[2,1024]{1,0:T(2,128)S(1)} %get-tuple-element.70.sent_edge_ref, f32[2,1024]{1,0:T(2,128)S(1)} %get-tuple-element.72.kept_edge_ref, ...), custom_call_target="tpu_custom_call" | custom-call | flops 3000000000 | bytes 3000000 | tf_op jit(solution)/shard_map/pallas_call | solution.py:534
  35.2 2.9 %collective-permute-done.5.from_ref = bf16[2,128,256]{2,1,0:T(8,128)(2,1)S(1)} collective-permute-done((bf16[2,128,256]{2,1,0:T(8,128)(2,1)S(1)}, bf16[2,128,256]{2,1,0:T(8,128)(2,1)S(1)}, u32[]{:S(2)}, u32[]{:S(2)}) %collective-permute-start.5) | collective-permute-done | bytes 131104 | tf_op jit(solution)/shard_map/ppermute | solution.py:437
  38.2 3.3 %collective-permute-start.8 = (bf16[2,64,256]{2,1,0:T(8,128)(2,1)S(1)}, bf16[2,64,256]{2,1,0:T(8,128)(2,1)S(1)}, u32[]{:S(2)}, u32[]{:S(2)}) collective-permute-start(bf16[2,64,256]{2,1,0:T(8,128)(2,1)S(1)} %get-tuple-element.74), channel_id=1, source_target_pairs={{0,16},{4,20},{8,24},{12,28},{16,0},{20,4},{24,8},{28,12},{1,17},{... | collective-permute-start | bytes 196616 | tf_op jit(solution)/shard_map/ppermute | solution.py:437
  41.5 0.5 collective-permute-start.7
  42.0 2.1 %shard_map.198 = (f32[4,128,256]{2,1,0:T(8,128)S(1)}, f32[4,128,256]{2,1,0:T(8,128)S(1)}) custom-call(s32[1]{0:T(128)} %bitcast.1.direction_ref, f32[4,128,256]{2,1,0:T(8,128)S(1)} %shard_map.196.receptances, f32[4,128,256]{2,1,0:T(8,128)S(1)} %get-tuple-element.78.here_ref, bf16[2,5,128,256]{3,2,1,0:T(8,128)(2,1)S(1)} %get-tuple-element.79.sent_ref, ...), custom_call_target="tpu_custom_call" | custom-call | flops 10000000000 | bytes 10000000 | tf_op jit(solution)/shard_map/pallas_call | solution.py:563
  44.1 0.3 collective-permute-done.8.from_ref
  44.7 0.5 collective-permute-start.9
  45.1 1.0 %shard_map.200.kept_ref = f32[2,128,256]{2,1,0:T(8,128)S(1)} custom-call(bf16[2,64,256]{2,1,0:T(8,128)(2,1)S(1)} %shard_map.199.entry_ref, bf16[2,128,256]{2,1,0:T(8,128)(2,1)S(1)} %collective-permute-done.4.from_ref, f32[4,128,256]{2,1,0:T(8,128)S(1)} %get-tuple-element.87.local_ref, f32[4,128,256]{2,1,0:T(8,128)S(1)} %get-tuple-element.88.map_ref), custom_call_target="tpu_custom_call" | custom-call | flops 3000000000 | bytes 3000000 | tf_op jit(solution)/shard_map/pallas_call | solution.py:578
  46.1 2.9 %collective-permute-done.9.other_ref = bf16[2,64,256]{2,1,0:T(8,128)(2,1)S(1)} collective-permute-done((bf16[2,64,256]{2,1,0:T(8,128)(2,1)S(1)}, bf16[2,64,256]{2,1,0:T(8,128)(2,1)S(1)}, u32[]{:S(2)}, u32[]{:S(2)}) %collective-permute-start.9) | collective-permute-done | bytes 65568 | tf_op jit(solution)/shard_map/ppermute | solution.py:437
  49.0 0.8 %shard_map.201 = bf16[2,128,256]{2,1,0:T(8,128)(2,1)S(1)} custom-call(bf16[2,64,256]{2,1,0:T(8,128)(2,1)S(1)} %collective-permute-done.9.other_ref, f32[2,128,256]{2,1,0:T(8,128)S(1)} %shard_map.200.kept_ref, f32[4,128,256]{2,1,0:T(8,128)S(1)} %get-tuple-element.87.local_ref, f32[4,128,256]{2,1,0:T(8,128)S(1)} %get-tuple-element.88.map_ref, ...), custom_call_target="tpu_custom_call" | custom-call | flops 10000000000 | bytes 10000000 | tf_op jit(solution)/shard_map/pallas_call | solution.py:580
  49.8 7.0 %all_gather.7.joined_ref = bf16[2,128,1024]{2,1,0:T(8,128)(2,1)S(1)} all-gather(bf16[2,128,256]{2,1,0:T(8,128)(2,1)S(1)} %shard_map.201), channel_id=1, replica_groups=mesh['seq'=8,'mp'=4] {'mp'}, dimensions={2}, use_global_device_ids=true | all-gather | bytes 655360 | tf_op jit(solution)/shard_map/all_gather | solution.py:581
  56.9 2.0 %shard_map.202 = (f32[128,256]{1,0:T(8,128)S(1)}, bf16[128,256]{1,0:T(8,128)(2,1)S(1)}, bf16[128,256]{1,0:T(8,128)(2,1)S(1)}, bf16[128,256]{1,0:T(8,128)(2,1)S(1)}) custom-call(s32[1]{0:T(128)} %bitcast.index_ref, bf16[2,128,1024]{2,1,0:T(8,128)(2,1)S(1)} %all_gather.7.joined_ref, bf16[2,128,1024]{2,1,0:T(8,128)(2,1)S(1)} %all_gather.6.x_ref, ...), custom_call_target="tpu_custom_call" | custom-call | flops 10000000000 | bytes 10000000 | tf_op jit(solution)/shard_map/pallas_call | solution.py:585
  58.9 0.4 collective-permute-start.10
  59.3 0.8 %collective-permute-start.11 = (bf16[128,256]{1,0:T(8,128)(2,1)S(1)}, bf16[128,256]{1,0:T(8,128)(2,1)S(1)}, u32[]{:S(2)}, u32[]{:S(2)}) collective-permute-start(bf16[128,256]{1,0:T(8,128)(2,1)S(1)} %get-tuple-element.95), channel_id=1, source_target_pairs={{0,2},{1,3},{2,0},{3,1},{4,6},{5,7},{6,4},{7,5},{8,10},{9,11},{10,... | collective-permute-start | bytes 196616 | tf_op jit(solution)/shard_map/ppermute | solution.py:437
  60.2 0.7 %collective-permute-start.12 = (bf16[128,256]{1,0:T(8,128)(2,1)S(1)}, bf16[128,256]{1,0:T(8,128)(2,1)S(1)}, u32[]{:S(2)}, u32[]{:S(2)}) collective-permute-start(bf16[128,256]{1,0:T(8,128)(2,1)S(1)} %get-tuple-element.96), channel_id=1, source_target_pairs={{0,3},{1,2},{2,1},{3,0},{4,7},{5,6},{6,5},{7,4},{8,11},{9,10},{10,... | collective-permute-start | bytes 196616 | tf_op jit(solution)/shard_map/ppermute | solution.py:437
  60.8 3.2 %collective-permute-done.11 = bf16[128,256]{1,0:T(8,128)(2,1)S(1)} collective-permute-done((bf16[128,256]{1,0:T(8,128)(2,1)S(1)}, bf16[128,256]{1,0:T(8,128)(2,1)S(1)}, u32[]{:S(2)}, u32[]{:S(2)}) %collective-permute-start.11) | collective-permute-done | bytes 65568 | tf_op jit(solution)/shard_map/ppermute | solution.py:437
  64.0 0.5 collective-permute-done.12
  64.5 0.7 %add_convert_fusion = bf16[128,256]{1,0:T(8,128)(2,1)} fusion(bf16[128,256]{1,0:T(8,128)(2,1)S(1)} %collective-permute-done.12, bf16[128,256]{1,0:T(8,128)(2,1)S(1)} %collective-permute-done.11, f32[128,256]{1,0:T(8,128)S(1)} %get-tuple-element.93, bf16[128,256]{1,0:T(8,128)(2,1)S(1)} %collective-permute-done.10), kind=kLoop, calls=%fused_computation | loop fusion | flops 229376 | bytes 393216 | tf_op jit(solution)/shard_map/convert_element_type | solution.py:598
  (51 shorter events, 1.0 us)
Async XLA Ops:
  0.0 8.6 %collective-permute-start = (bf16[128,256]{1,0:T(8,128)(2,1)}, bf16[128,256]{1,0:T(8,128)(2,1)S(1)}, u32[]{:S(2)}, u32[]{:S(2)}) collective-permute-start(bf16[128,256]{1,0:T(8,128)(2,1)} %param.22), channel_id=1, source_target_pairs={{0,28},{4,24},{8,20},{12,16},{16,12},{20,8},{24,4},{28,0},{1,29},{... | collective-permute-start | bytes 196616 | tf_op jit(solution)/shard_map/ppermute | solution.py:468
  6.0 0.8 %copy-start.8 = (bf16[128,256]{1,0:T(8,128)(2,1)S(1)}, bf16[128,256]{1,0:T(8,128)(2,1)}, u32[]{:S(2)}) copy-start(bf16[128,256]{1,0:T(8,128)(2,1)} %fwd_ref.1) | copy-start | bytes 196612
  6.8 0.7 %copy-start.12 = (f32[4,256]{1,0:T(4,128)S(1)}, f32[4,256]{1,0:T(4,128)}, u32[]{:S(2)}) copy-start(f32[4,256]{1,0:T(4,128)} %embed_ref.1) | copy-start | bytes 12292
  7.5 0.7 %copy-start.18 = (s32[128]{0:T(128)S(1)}, s32[128]{0:T(128)}, u32[]{:S(2)}) copy-start(s32[128]{0:T(128)} %param.20) | copy-start | bytes 1540
  8.7 8.3 %copy-start.2 = (bf16[1024,256]{1,0:T(8,128)(2,1)S(1)}, bf16[1024,256]{1,0:T(8,128)(2,1)}, u32[]{:S(2)}) copy-start(bf16[1024,256]{1,0:T(8,128)(2,1)} %refs_10_.3) | copy-start | bytes 1572868
  8.7 8.3 %copy-start.3 = (bf16[1024,256]{1,0:T(8,128)(2,1)S(1)}, bf16[1024,256]{1,0:T(8,128)(2,1)}, u32[]{:S(2)}) copy-start(bf16[1024,256]{1,0:T(8,128)(2,1)} %refs_11_.3) | copy-start | bytes 1572868
  8.7 8.3 %copy-start.6 = (bf16[1024,64]{0,1:T(8,128)(2,1)S(1)}, bf16[1024,64]{0,1:T(8,128)(2,1)}, u32[]{:S(2)}) copy-start(bf16[1024,64]{0,1:T(8,128)(2,1)} %param.30) | copy-start | bytes 393220
  8.7 8.3 %copy-start.7 = (bf16[1024,64]{0,1:T(8,128)(2,1)S(1)}, bf16[1024,64]{0,1:T(8,128)(2,1)}, u32[]{:S(2)}) copy-start(bf16[1024,64]{0,1:T(8,128)(2,1)} %param.33) | copy-start | bytes 393220
  8.7 8.3 %copy-start.9 = (bf16[64,256]{1,0:T(8,128)(2,1)S(1)}, bf16[64,256]{1,0:T(8,128)(2,1)}, u32[]{:S(2)}) copy-start(bf16[64,256]{1,0:T(8,128)(2,1)} %refs_12_.3) | copy-start | bytes 98308
  8.7 8.3 %copy-start.10 = (bf16[64,256]{1,0:T(8,128)(2,1)S(1)}, bf16[64,256]{1,0:T(8,128)(2,1)}, u32[]{:S(2)}) copy-start(bf16[64,256]{1,0:T(8,128)(2,1)} %refs_13_.3) | copy-start | bytes 98308
  8.7 8.3 %copy-start.11 = (f32[5,1024]{1,0:T(8,128)S(1)}, f32[5,1024]{1,0:T(8,128)}, u32[]{:S(2)}) copy-start(f32[5,1024]{1,0:T(8,128)} %mixing_ref.3) | copy-start | bytes 61444
  8.7 8.3 %copy-start.13 = (f32[1024]{0:T(1024)S(1)}, f32[1024]{0:T(1024)}, u32[]{:S(2)}) copy-start(f32[1024]{0:T(1024)} %param.24) | copy-start | bytes 12292
  8.8 8.3 %copy-start.15 = (f32[256]{0:T(256)S(1)}, f32[256]{0:T(256)}, u32[]{:S(2)}) copy-start(f32[256]{0:T(256)} %param.31) | copy-start | bytes 3076
  8.8 8.3 %copy-start.16 = (f32[256]{0:T(256)S(1)}, f32[256]{0:T(256)}, u32[]{:S(2)}) copy-start(f32[256]{0:T(256)} %param.34) | copy-start | bytes 3076
  16.3 7.9 %collective-permute-start.1 = (bf16[2,1024]{1,0:T(2,128)(2,1)S(1)}, bf16[2,1024]{1,0:T(2,128)(2,1)S(1)}, u32[]{:S(2)}, u32[]{:S(2)}) collective-permute-start(bf16[2,1024]{1,0:T(2,128)(2,1)S(1)} %bitcast.33), channel_id=1, source_target_pairs={{4,8},{12,16},{20,24},{8,4},{16,12},{24,20},{5,9},{13,17},{21,25},... | collective-permute-start | bytes 12296 | tf_op jit(solution)/shard_map/ppermute | solution.py:492
  17.0 6.3 %copy-start.5 = (bf16[256,1024]{1,0:T(8,128)(2,1)S(1)}, bf16[256,1024]{1,0:T(8,128)(2,1)}, u32[]{:S(2)}) copy-start(bf16[256,1024]{1,0:T(8,128)(2,1)} %refs_0_.1) | copy-start | bytes 1572868
  19.7 8.3 %collective-permute-start.2 = (bf16[2,1024]{1,0:T(2,128)(2,1)S(1)}, bf16[2,1024]{1,0:T(2,128)(2,1)S(1)}, u32[]{:S(2)}, u32[]{:S(2)}) collective-permute-start(bf16[2,1024]{1,0:T(2,128)(2,1)S(1)} %bitcast.34), channel_id=1, source_target_pairs={{0,4},{4,0},{8,12},{12,8},{16,20},{20,16},{24,28},{28,24},{1,5},{5... | collective-permute-start | bytes 12296 | tf_op jit(solution)/shard_map/ppermute | solution.py:437
  23.3 18.2 %collective-permute-start.3 = (bf16[256,1024]{1,0:T(8,128)(2,1)S(1)}, bf16[256,1024]{1,0:T(8,128)(2,1)S(1)}, u32[]{:S(2)}, u32[]{:S(2)}) collective-permute-start(bf16[256,1024]{1,0:T(8,128)(2,1)S(1)} %copy-done.5), channel_id=1, source_target_pairs={{0,2},{1,3},{2,0},{3,1},{4,6},{5,7},{6,4},{7,5},{8,10},{9,11},{10,... | collective-permute-start | bytes 1572872 | tf_op jit(solution)/shard_map/ppermute | solution.py:437
  27.8 5.0 %collective-permute-start.4 = (bf16[2,128,256]{2,1,0:T(8,128)(2,1)S(1)}, bf16[2,128,256]{2,1,0:T(8,128)(2,1)S(1)}, u32[]{:S(2)}, u32[]{:S(2)}) collective-permute-start(bf16[2,128,256]{2,1,0:T(8,128)(2,1)S(1)} %get-tuple-element.68), channel_id=1, source_target_pairs={{0,4},{4,0},{8,12},{12,8},{16,20},{20,16},{24,28},{28,24},{1,5},{5... | collective-permute-start | bytes 393224 | tf_op jit(solution)/shard_map/ppermute | solution.py:437
  31.5 2.8 %copy-start.4 = (bf16[1024,256]{1,0:T(8,128)(2,1)S(1)}, bf16[1024,256]{1,0:T(8,128)(2,1)}, u32[]{:S(2)}) copy-start(bf16[1024,256]{1,0:T(8,128)(2,1)} %w_r.1) | copy-start | bytes 1572868
  33.0 5.0 %collective-permute-start.5 = (bf16[2,128,256]{2,1,0:T(8,128)(2,1)S(1)}, bf16[2,128,256]{2,1,0:T(8,128)(2,1)S(1)}, u32[]{:S(2)}, u32[]{:S(2)}) collective-permute-start(bf16[2,128,256]{2,1,0:T(8,128)(2,1)S(1)} %shard_map.195.total_ref), channel_id=1, source_target_pairs={{0,8},{4,12},{8,0},{12,4},{16,24},{20,28},{24,16},{28,20},{1,9},{5... | collective-permute-start | bytes 393224 | tf_op jit(solution)/shard_map/ppermute | solution.py:437
  38.2 6.2 %collective-permute-start.8 = (bf16[2,64,256]{2,1,0:T(8,128)(2,1)S(1)}, bf16[2,64,256]{2,1,0:T(8,128)(2,1)S(1)}, u32[]{:S(2)}, u32[]{:S(2)}) collective-permute-start(bf16[2,64,256]{2,1,0:T(8,128)(2,1)S(1)} %get-tuple-element.74), channel_id=1, source_target_pairs={{0,16},{4,20},{8,24},{12,28},{16,0},{20,4},{24,8},{28,12},{1,17},{... | collective-permute-start | bytes 196616 | tf_op jit(solution)/shard_map/ppermute | solution.py:437
  41.5 7.5 %collective-permute-start.6 = (bf16[256,1024]{1,0:T(8,128)(2,1)S(1)}, bf16[256,1024]{1,0:T(8,128)(2,1)S(1)}, u32[]{:S(2)}, u32[]{:S(2)}) collective-permute-start(bf16[256,1024]{1,0:T(8,128)(2,1)S(1)} %copy-done.5), channel_id=1, source_target_pairs={{0,1},{1,0},{2,3},{3,2},{4,5},{5,4},{6,7},{7,6},{8,9},{9,8},{10,11... | collective-permute-start | bytes 1572872 | tf_op jit(solution)/shard_map/ppermute | solution.py:437
  41.5 7.5 %collective-permute-start.7 = (bf16[256,1024]{1,0:T(8,128)(2,1)S(1)}, bf16[256,1024]{1,0:T(8,128)(2,1)S(1)}, u32[]{:S(2)}, u32[]{:S(2)}) collective-permute-start(bf16[256,1024]{1,0:T(8,128)(2,1)S(1)} %collective-permute-done.3.refs_2_), channel_id=1, source_target_pairs={{0,1},{1,0},{2,3},{3,2},{4,5},{5,4},{6,7},{7,6},{8,9},{9,8},{10,11... | collective-permute-start | bytes 1572872 | tf_op jit(solution)/shard_map/ppermute | solution.py:437
  44.6 4.4 %copy-start.17 = (f32[256]{0:T(256)S(1)}, f32[256]{0:T(256)}, u32[]{:S(2)}) copy-start(f32[256]{0:T(256)} %param.36) | copy-start | bytes 3076
  44.7 4.3 %collective-permute-start.9 = (bf16[2,64,256]{2,1,0:T(8,128)(2,1)S(1)}, bf16[2,64,256]{2,1,0:T(8,128)(2,1)S(1)}, u32[]{:S(2)}, u32[]{:S(2)}) collective-permute-start(bf16[2,64,256]{2,1,0:T(8,128)(2,1)S(1)} %shard_map.199.entry_ref), channel_id=1, source_target_pairs={{0,4},{4,0},{8,12},{12,8},{16,20},{20,16},{24,28},{28,24},{1,5},{5... | collective-permute-start | bytes 196616 | tf_op jit(solution)/shard_map/ppermute | solution.py:437
  49.0 7.8 %copy-start = (bf16[1024,1024]{1,0:T(8,128)(2,1)S(1)}, bf16[1024,1024]{1,0:T(8,128)(2,1)}, u32[]{:S(2)}) copy-start(bf16[1024,1024]{1,0:T(8,128)(2,1)} %refs_4_.1) | copy-start | bytes 6291460
  49.0 7.8 %copy-start.1 = (bf16[1024,1024]{1,0:T(8,128)(2,1)S(1)}, bf16[1024,1024]{1,0:T(8,128)(2,1)}, u32[]{:S(2)}) copy-start(bf16[1024,1024]{1,0:T(8,128)(2,1)} %refs_5_.1) | copy-start | bytes 6291460
  49.0 7.8 %copy-start.14 = (f32[1024]{0:T(1024)S(1)}, f32[1024]{0:T(1024)}, u32[]{:S(2)}) copy-start(f32[1024]{0:T(1024)} %param.25) | copy-start | bytes 12292
  58.9 1.9 %collective-permute-start.10 = (bf16[128,256]{1,0:T(8,128)(2,1)S(1)}, bf16[128,256]{1,0:T(8,128)(2,1)S(1)}, u32[]{:S(2)}, u32[]{:S(2)}) collective-permute-start(bf16[128,256]{1,0:T(8,128)(2,1)S(1)} %get-tuple-element.94), channel_id=1, source_target_pairs={{0,1},{1,0},{2,3},{3,2},{4,5},{5,4},{6,7},{7,6},{8,9},{9,8},{10,11... | collective-permute-start | bytes 196616 | tf_op jit(solution)/shard_map/ppermute | solution.py:437
  59.3 4.7 %collective-permute-start.11 = (bf16[128,256]{1,0:T(8,128)(2,1)S(1)}, bf16[128,256]{1,0:T(8,128)(2,1)S(1)}, u32[]{:S(2)}, u32[]{:S(2)}) collective-permute-start(bf16[128,256]{1,0:T(8,128)(2,1)S(1)} %get-tuple-element.95), channel_id=1, source_target_pairs={{0,2},{1,3},{2,0},{3,1},{4,6},{5,7},{6,4},{7,5},{8,10},{9,11},{10,... | collective-permute-start | bytes 196616 | tf_op jit(solution)/shard_map/ppermute | solution.py:437
  60.2 4.4 %collective-permute-start.12 = (bf16[128,256]{1,0:T(8,128)(2,1)S(1)}, bf16[128,256]{1,0:T(8,128)(2,1)S(1)}, u32[]{:S(2)}, u32[]{:S(2)}) collective-permute-start(bf16[128,256]{1,0:T(8,128)(2,1)S(1)} %get-tuple-element.96), channel_id=1, source_target_pairs={{0,3},{1,2},{2,1},{3,0},{4,7},{5,6},{6,5},{7,4},{8,11},{9,10},{10,... | collective-permute-start | bytes 196616 | tf_op jit(solution)/shard_map/ppermute | solution.py:437

commit v13 on v10

--- a/solution.py
+++ b/solution.py
@@ -376,7 +376,7 @@
 
 def mix_kernel(blocks, index_ref, joined_ref, x_ref, *refs):
     w_refs, (up_ref, down_ref, gain_ref, own_ref) = refs[:blocks], refs[blocks : blocks + 4]
-    *sent_refs, partial, total = refs[blocks + 4 :]
+    added_ref, *sent_refs, total = refs[blocks + 4 :]
     strands, rows, _ = x_ref.shape
     width = own_ref.shape[1]
     gain = gain_ref[...]
@@ -390,15 +390,23 @@
     inner = jnp.concatenate([layer_norm(item, gain).astype(BF16) for item in residuals], axis=0)
     active = jnp.square(jnp.maximum(mm(inner, up_ref[...]), 0.0)).astype(BF16).astype(F32)
     added = sum(active[s * rows : (s + 1) * rows] for s in range(strands)).astype(BF16)
-    partial[...] = mm(added, down_ref[...])
+    added_ref[...] = added
+    for mask, ref in enumerate(sent_refs, blocks - len(sent_refs)):
+        ref[...] = mm(added, columns_of(down_ref, me ^ mask, width)).astype(BF16)
     total[...] = sum(residuals)
-
-    def part(ref, which):
-        return ref[:, pl.ds(pl.multiple_of(which * width, width), width)]
-
-    own_ref[...] = part(total, me) + part(partial, me)
-    for step, ref in enumerate(sent_refs):
-        ref[...] = part(partial, me ^ (step + 1)).astype(BF16)
+    own_ref[...] = columns_of(total, me, width)
+
+
+def columns_of(ref, which, width):
+    return ref[:, pl.ds(pl.multiple_of(which * width, width), width)]
+
+
+def near_kernel(index_ref, added_ref, held_ref, down_ref, own_ref, *sent_refs):
+    me, width = index_ref[0], own_ref.shape[1]
+    added = added_ref[...]
+    for mask, ref in enumerate(sent_refs, 1):
+        ref[...] = mm(added, columns_of(down_ref, me ^ mask, width)).astype(BF16)
+    own_ref[...] = held_ref[...] + mm(added, columns_of(down_ref, me, width))
 
 
 def call(kernel, out_shape, scratch=(), mib=12, us=10, **kwargs):
@@ -561,19 +569,27 @@
 
     w_blocks = (w_output, w_beside, w_across, w_opposite)
     position = lax.axis_index("mp").astype(jnp.int32).reshape(1)
-    own, *sent = call(
+    near_count = mp_count // 2
+    own_struct, sent_struct = struct((rows, width), F32), struct((rows, width), BF16)
+    held, added, *far_parts = call(
         functools.partial(mix_kernel, mp_count),
-        (struct((rows, width), F32),) + (struct((rows, width), BF16),) * (mp_count - 1),
-        scratch=[
-            pltpu.VMEM((rows, full), F32),
-            pltpu.VMEM((rows, full), F32),
-        ],
+        (own_struct, struct((rows, ffn_key.shape[1]), BF16)) + (sent_struct,) * near_count,
+        scratch=[pltpu.VMEM((rows, full), F32)],
         mib=16,
         in_specs=[SMEM_SPEC] + [VMEM_SPEC] * (5 + mp_count),
     )(position, joined_whole, whole, *w_blocks, ffn_key, ffn_value, ln2_gain.reshape(1, full))
+    arrivals = [swapped(item, "mp", mask) for mask, item in enumerate(far_parts, near_count)]
+    own, *near_parts = call(
+        near_kernel,
+        (own_struct,) + (sent_struct,) * (near_count - 1),
+        mib=6,
+        us=1,
+        in_specs=[SMEM_SPEC] + [VMEM_SPEC] * 3,
+    )(position, added, held, ffn_value)
+    arrivals += [swapped(item, "mp", mask) for mask, item in enumerate(near_parts, 1)]
     merged = own
-    for step, item in enumerate(sent):
-        merged = merged + swapped(item, "mp", step + 1).astype(F32)
+    for item in reversed(arrivals):
+        merged = merged + item.astype(F32)
     return merged.astype(BF16)
 
 

time: 65.1 us -> 64.4 us (0.989)
  waiting for transfers between devices: 8.23 us -> 7.1 us
    ppermute x11, waiting for transfers between devices: 8.23 us -> 7.1 us  [swapped(): lax.ppermute(value, axis, [(i, i ^ mask) for i in range(lax.axis_size(axi...]
    pallas_call x1 -> x2, Pallas kernels: 2.05 us -> 2.21 us  [the longest x1 1.89 us: on_device(): call(functools.partial(mix_kernel, mp_count), (own_struct, struct((rows,...]
  transfers between devices with their start and end apart: 13 -> 13, of which waited for: 5 -> 5; matrix products, arithmetic and copies ran while one was open for 0% -> 0% of each run, Pallas kernels for 24% -> 25%
where the time goes in v13:
time: 64.4 us; the launch traced here: 64.2 us
  starting transfers between devices  20.4 us (32%)
  Pallas kernels  18.4 us (29%)
  blocking collectives  14.9 us (23%)
  waiting for transfers between devices  7.1 us (11%)
  local copies, waits for them, and re-layouts  2.29 us (4%)
  other arithmetic  0.69 us (1%)
    ppermute x11, starting transfers between devices, swapped(): lax.ppermute(value, axis, [(i, i ^ mask) for i in range(lax.axis_size(axi...  13.7 us
    pallas_call x2, Pallas kernels, chunk(): call(chunk_kernel, (state_struct, parts_struct, here_struct, struct((stra...  8.22 us
    all_gather x1, blocking collectives, on_device(): joined_whole = lax.all_gather(joined, 'mp', axis=2, tiled=True)  7.55 us
    all_gather x1, blocking collectives, on_device(): whole = lax.all_gather(local, 'mp', axis=2, tiled=True)  7.3 us
    ppermute x11, waiting for transfers between devices, swapped(): lax.ppermute(value, axis, [(i, i ^ mask) for i in range(lax.axis_size(axi...  7.1 us
    ppermute x1, starting transfers between devices, on_device(): rc_here = lax.ppermute(hidden_rc, 'seq', mirror)  6 us
    unnamed x40, local copies, waits for them, and re-layouts  2.29 us
    pallas_call x1, Pallas kernels, on_device(): call(project_kernel, (f32_lanes,) * 4 + (struct((strands, rows + 16, full...  2.2 us
  transfers between devices with their start and end apart: 13, of which 5 were waited for; matrix products, arithmetic and copies ran while one was open for 0% of the time, Pallas kernels for 25%

profile of v13, /device:TPU:0, one launch (start us, length us, event | category | flops | bytes accessed | tf_op | source)
XLA Modules:
  0.0 64.2 jit_solution(11752199538791384480)
XLA Ops:
  0.0 6.0 %collective-permute-start = (bf16[128,256]{1,0:T(8,128)(2,1)}, bf16[128,256]{1,0:T(8,128)(2,1)S(1)}, u32[]{:S(2)}, u32[]{:S(2)}) collective-permute-start(bf16[128,256]{1,0:T(8,128)(2,1)} %param.22), channel_id=1, source_target_pairs={{0,28},{4,24},{8,20},{12,16},{16,12},{20,8},{24,4},{28,0},{1,29},{... | collective-permute-start | bytes 196616 | tf_op jit(solution)/shard_map/ppermute | solution.py:455
  6.0 0.8 %copy-done.8 = bf16[128,256]{1,0:T(8,128)(2,1)S(1)} copy-done((bf16[128,256]{1,0:T(8,128)(2,1)S(1)}, bf16[128,256]{1,0:T(8,128)(2,1)}, u32[]{:S(2)}) %copy-start.8) | copy-done | bytes 65560
  6.8 0.7 %copy-done.12 = f32[4,256]{1,0:T(4,128)S(1)} copy-done((f32[4,256]{1,0:T(4,128)S(1)}, f32[4,256]{1,0:T(4,128)}, u32[]{:S(2)}) %copy-start.12) | copy-done | bytes 4120
  7.5 0.7 %copy-done.18 = s32[128]{0:T(128)S(1)} copy-done((s32[128]{0:T(128)S(1)}, s32[128]{0:T(128)}, u32[]{:S(2)}) %copy-start.18) | copy-done | bytes 536
  8.2 0.4 shard_map.190
  8.9 7.3 %all_gather.6.x_ref = bf16[2,128,1024]{2,1,0:T(8,128)(2,1)S(1)} all-gather(bf16[2,128,256]{2,1,0:T(8,128)(2,1)S(1)} %shard_map.191), channel_id=1, replica_groups=mesh['seq'=8,'mp'=4] {'mp'}, dimensions={2}, use_global_device_ids=true | all-gather | bytes 655360 | tf_op jit(solution)/shard_map/all_gather | solution.py:473
  16.3 0.7 %collective-permute-start.2 = (bf16[2,1024]{1,0:T(2,128)(2,1)S(1)}, bf16[2,1024]{1,0:T(2,128)(2,1)S(1)}, u32[]{:S(2)}, u32[]{:S(2)}) collective-permute-start(bf16[2,1024]{1,0:T(2,128)(2,1)S(1)} %bitcast.33), channel_id=1, source_target_pairs={{4,8},{12,16},{20,24},{8,4},{16,12},{24,20},{5,9},{13,17},{21,25},... | collective-permute-start | bytes 12296 | tf_op jit(solution)/shard_map/ppermute | solution.py:479
  17.0 2.2 %shard_map.192 = (f32[4,128,256]{2,1,0:T(8,128)S(1)}, f32[4,128,256]{2,1,0:T(8,128)S(1)}, f32[4,128,256]{2,1,0:T(8,128)S(1)}, f32[4,128,256]{2,1,0:T(8,128)S(1)}...) custom-call(bf16[2,128,1024]{2,1,0:T(8,128)(2,1)S(1)} %all_gather.6.x_ref, ...), custom_call_target="tpu_custom_call" | custom-call | flops 10000000000 | bytes 10000000 | tf_op jit(solution)/shard_map/pallas_call | solution.py:489
  19.3 3.7 %collective-permute-start.1 = (bf16[2,1024]{1,0:T(2,128)(2,1)S(1)}, bf16[2,1024]{1,0:T(2,128)(2,1)S(1)}, u32[]{:S(2)}, u32[]{:S(2)}) collective-permute-start(bf16[2,1024]{1,0:T(2,128)(2,1)S(1)} %bitcast.34), channel_id=1, source_target_pairs={{0,4},{4,0},{8,12},{12,8},{16,20},{20,16},{24,28},{28,24},{1,5},{5... | collective-permute-start | bytes 12296 | tf_op jit(solution)/shard_map/ppermute | solution.py:424
  22.9 4.1 %shard_map.194 = (bf16[2,128,256]{2,1,0:T(8,128)(2,1)S(1)}, bf16[2,5,128,256]{3,2,1,0:T(8,128)(2,1)S(1)}, f32[2,136,256]{2,1,0:T(8,128)S(1)}, f32[2,1024]{1,0:T(2,128)S(1)}) custom-call(s32[1]{0:T(128)} %bitcast.1.direction_ref, f32[4,128,256]{2,1,0:T(8,128)S(1)} %get-tuple-element.54.refs_0_, f32[4,128,256]{2,1,0:T(8,128)S(1)} %get-tuple-element.55.refs_1_, ...), custom_call_target="tpu_custom_call" | custom-call | flops 10000000000 | bytes 10000000 | tf_op jit(solution)/shard_map/pallas_call | solution.py:507
  27.0 1.3 %collective-permute-start.3 = (bf16[2,128,256]{2,1,0:T(8,128)(2,1)S(1)}, bf16[2,128,256]{2,1,0:T(8,128)(2,1)S(1)}, u32[]{:S(2)}, u32[]{:S(2)}) collective-permute-start(bf16[2,128,256]{2,1,0:T(8,128)(2,1)S(1)} %get-tuple-element.62), channel_id=1, source_target_pairs={{0,4},{4,0},{8,12},{12,8},{16,20},{20,16},{24,28},{28,24},{1,5},{5... | collective-permute-start | bytes 393224 | tf_op jit(solution)/shard_map/ppermute | solution.py:424
  28.3 4.1 %shard_map.193 = (bf16[2,128,256]{2,1,0:T(8,128)(2,1)S(1)}, bf16[2,5,128,256]{3,2,1,0:T(8,128)(2,1)S(1)}, f32[2,136,256]{2,1,0:T(8,128)S(1)}, f32[2,1024]{1,0:T(2,128)S(1)}) custom-call(s32[1]{0:T(128)S(6)} %sub.3.direction_ref, f32[4,128,256]{2,1,0:T(8,128)S(1)} %get-tuple-element.54.refs_0_, f32[4,128,256]{2,1,0:T(8,128)S(1)} %get-tuple-element.55.refs_1_, ...), custom_call_target="tpu_custom_call" | custom-call | flops 10000000000 | bytes 10000000 | tf_op jit(solution)/shard_map/pallas_call | solution.py:507
  32.4 0.2 shard_map.195.total_ref
  32.7 1.5 %collective-permute-start.5 = (bf16[2,128,256]{2,1,0:T(8,128)(2,1)S(1)}, bf16[2,128,256]{2,1,0:T(8,128)(2,1)S(1)}, u32[]{:S(2)}, u32[]{:S(2)}) collective-permute-start(bf16[2,128,256]{2,1,0:T(8,128)(2,1)S(1)} %shard_map.195.total_ref), channel_id=1, source_target_pairs={{0,8},{4,12},{8,0},{12,4},{16,24},{20,28},{24,16},{28,20},{1,9},{5... | collective-permute-start | bytes 393224 | tf_op jit(solution)/shard_map/ppermute | solution.py:424
  34.1 0.8 %collective-permute-start.4 = (bf16[256,1024]{1,0:T(8,128)(2,1)S(1)}, bf16[256,1024]{1,0:T(8,128)(2,1)S(1)}, u32[]{:S(2)}, u32[]{:S(2)}) collective-permute-start(bf16[256,1024]{1,0:T(8,128)(2,1)S(1)} %copy-done.5), channel_id=1, source_target_pairs={{0,2},{1,3},{2,0},{3,1},{4,6},{5,7},{6,4},{7,5},{8,10},{9,11},{10,... | collective-permute-start | bytes 1572872 | tf_op jit(solution)/shard_map/ppermute | solution.py:424
  35.0 0.8 %shard_map.196.receptances = f32[4,128,256]{2,1,0:T(8,128)S(1)} custom-call(s32[1]{0:T(128)} %bitcast.1.direction_ref, f32[2,144,1024]{2,1,0:T(8,128)S(1)} %get-tuple-element.64.normed, f32[5,1024]{1,0:T(8,128)S(1)} %copy-done.11, f32[2,1024]{1,0:T(2,128)S(1)} %get-tuple-element.65.sent_edge_ref, f32[2,1024]{1,0:T(2,128)S(1)} %get-tuple-element.67.kept_edge_ref, ...), custom_call_target="tpu_custom_call" | custom-call | flops 3000000000 | bytes 3000000 | tf_op jit(solution)/shard_map/pallas_call | solution.py:521
  35.8 1.9 %collective-permute-done.5.from_ref = bf16[2,128,256]{2,1,0:T(8,128)(2,1)S(1)} collective-permute-done((bf16[2,128,256]{2,1,0:T(8,128)(2,1)S(1)}, bf16[2,128,256]{2,1,0:T(8,128)(2,1)S(1)}, u32[]{:S(2)}, u32[]{:S(2)}) %collective-permute-start.5) | collective-permute-done | bytes 131104 | tf_op jit(solution)/shard_map/ppermute | solution.py:424
  37.9 3.1 %collective-permute-start.6 = (bf16[2,64,256]{2,1,0:T(8,128)(2,1)S(1)}, bf16[2,64,256]{2,1,0:T(8,128)(2,1)S(1)}, u32[]{:S(2)}, u32[]{:S(2)}) collective-permute-start(bf16[2,64,256]{2,1,0:T(8,128)(2,1)S(1)} %get-tuple-element.69), channel_id=1, source_target_pairs={{0,16},{4,20},{8,24},{12,28},{16,0},{20,4},{24,8},{28,12},{1,17},{... | collective-permute-start | bytes 196616 | tf_op jit(solution)/shard_map/ppermute | solution.py:424
  41.0 2.1 %shard_map.198 = (f32[4,128,256]{2,1,0:T(8,128)S(1)}, f32[4,128,256]{2,1,0:T(8,128)S(1)}) custom-call(s32[1]{0:T(128)} %bitcast.1.direction_ref, f32[4,128,256]{2,1,0:T(8,128)S(1)} %shard_map.196.receptances, bf16[2,5,128,256]{3,2,1,0:T(8,128)(2,1)S(1)} %get-tuple-element.73.sent_ref, bf16[2,5,128,256]{3,2,1,0:T(8,128)(2,1)S(1)} %get-tuple-element.74.kept_ref, ...), custom_call_target="tpu_custom_call" | custom-call | flops 10000000000 | bytes 10000000 | tf_op jit(solution)/shard_map/pallas_call | solution.py:549
  43.4 1.1 %collective-permute-start.7 = (bf16[2,64,256]{2,1,0:T(8,128)(2,1)S(1)}, bf16[2,64,256]{2,1,0:T(8,128)(2,1)S(1)}, u32[]{:S(2)}, u32[]{:S(2)}) collective-permute-start(bf16[2,64,256]{2,1,0:T(8,128)(2,1)S(1)} %shard_map.199.entry_ref), channel_id=1, source_target_pairs={{0,4},{4,0},{8,12},{12,8},{16,20},{20,16},{24,28},{28,24},{1,5},{5... | collective-permute-start | bytes 196616 | tf_op jit(solution)/shard_map/ppermute | solution.py:424
  44.6 1.0 %shard_map.200.kept_ref = f32[2,128,256]{2,1,0:T(8,128)S(1)} custom-call(bf16[2,64,256]{2,1,0:T(8,128)(2,1)S(1)} %shard_map.199.entry_ref, bf16[2,128,256]{2,1,0:T(8,128)(2,1)S(1)} %collective-permute-done.3.from_ref, f32[4,128,256]{2,1,0:T(8,128)S(1)} %get-tuple-element.81.local_ref, f32[4,128,256]{2,1,0:T(8,128)S(1)} %get-tuple-element.82.map_ref), custom_call_target="tpu_custom_call" | custom-call | flops 3000000000 | bytes 3000000 | tf_op jit(solution)/shard_map/pallas_call | solution.py:564
  45.6 2.3 %collective-permute-done.7.other_ref = bf16[2,64,256]{2,1,0:T(8,128)(2,1)S(1)} collective-permute-done((bf16[2,64,256]{2,1,0:T(8,128)(2,1)S(1)}, bf16[2,64,256]{2,1,0:T(8,128)(2,1)S(1)}, u32[]{:S(2)}, u32[]{:S(2)}) %collective-permute-start.7) | collective-permute-done | bytes 65568 | tf_op jit(solution)/shard_map/ppermute | solution.py:424
  47.9 0.8 %shard_map.201 = bf16[2,128,256]{2,1,0:T(8,128)(2,1)S(1)} custom-call(bf16[2,64,256]{2,1,0:T(8,128)(2,1)S(1)} %collective-permute-done.7.other_ref, f32[2,128,256]{2,1,0:T(8,128)S(1)} %shard_map.200.kept_ref, f32[4,128,256]{2,1,0:T(8,128)S(1)} %get-tuple-element.81.local_ref, f32[4,128,256]{2,1,0:T(8,128)S(1)} %get-tuple-element.82.map_ref, ...), custom_call_target="tpu_custom_call" | custom-call | flops 10000000000 | bytes 10000000 | tf_op jit(solution)/shard_map/pallas_call | solution.py:567
  48.7 7.6 %all_gather.7.joined_ref = bf16[2,128,1024]{2,1,0:T(8,128)(2,1)S(1)} all-gather(bf16[2,128,256]{2,1,0:T(8,128)(2,1)S(1)} %shard_map.201), channel_id=1, replica_groups=mesh['seq'=8,'mp'=4] {'mp'}, dimensions={2}, use_global_device_ids=true | all-gather | bytes 655360 | tf_op jit(solution)/shard_map/all_gather | solution.py:568
  56.3 1.9 %shard_map.202 = (f32[128,256]{1,0:T(8,128)S(1)}, bf16[128,1024]{1,0:T(8,128)(2,1)S(1)}, bf16[128,256]{1,0:T(8,128)(2,1)S(1)}, bf16[128,256]{1,0:T(8,128)(2,1)S(1)}) custom-call(s32[1]{0:T(128)} %bitcast.index_ref, bf16[2,128,1024]{2,1,0:T(8,128)(2,1)S(1)} %all_gather.7.joined_ref, bf16[2,128,1024]{2,1,0:T(8,128)(2,1)S(1)} %all_gather.6.x_ref, ...), custom_call_target="tpu_custom_call" | custom-call | flops 10000000000 | bytes 10000000 | tf_op jit(solution)/shard_map/pallas_call | solution.py:574
  58.2 0.9 %collective-permute-start.12 = (bf16[128,256]{1,0:T(8,128)(2,1)S(1)}, bf16[128,256]{1,0:T(8,128)(2,1)S(1)}, u32[]{:S(2)}, u32[]{:S(2)}) collective-permute-start(bf16[128,256]{1,0:T(8,128)(2,1)S(1)} %get-tuple-element.92), channel_id=1, source_target_pairs={{0,2},{1,3},{2,0},{3,1},{4,6},{5,7},{6,4},{7,5},{8,10},{9,11},{10,... | collective-permute-start | bytes 196616 | tf_op jit(solution)/shard_map/ppermute | solution.py:424
  59.1 0.9 %collective-permute-start.11 = (bf16[128,256]{1,0:T(8,128)(2,1)S(1)}, bf16[128,256]{1,0:T(8,128)(2,1)S(1)}, u32[]{:S(2)}, u32[]{:S(2)}) collective-permute-start(bf16[128,256]{1,0:T(8,128)(2,1)S(1)} %get-tuple-element.91), channel_id=1, source_target_pairs={{0,3},{1,2},{2,1},{3,0},{4,7},{5,6},{6,5},{7,4},{8,11},{9,10},{10,... | collective-permute-start | bytes 196616 | tf_op jit(solution)/shard_map/ppermute | solution.py:424
  60.0 0.3 shard_map.203
  60.3 0.5 collective-permute-start.10
  60.8 2.3 %collective-permute-done.12 = bf16[128,256]{1,0:T(8,128)(2,1)S(1)} collective-permute-done((bf16[128,256]{1,0:T(8,128)(2,1)S(1)}, bf16[128,256]{1,0:T(8,128)(2,1)S(1)}, u32[]{:S(2)}, u32[]{:S(2)}) %collective-permute-start.12) | collective-permute-done | bytes 65568 | tf_op jit(solution)/shard_map/ppermute | solution.py:424
  63.1 0.4 collective-permute-done.11
  63.5 0.7 %add_convert_fusion = bf16[128,256]{1,0:T(8,128)(2,1)} fusion(bf16[128,256]{1,0:T(8,128)(2,1)S(1)} %collective-permute-done.12, bf16[128,256]{1,0:T(8,128)(2,1)S(1)} %collective-permute-done.11, f32[128,256]{1,0:T(8,128)S(1)} %get-tuple-element.89, bf16[128,256]{1,0:T(8,128)(2,1)S(1)} %collective-permute-done.10), kind=kLoop, calls=%fused_computation | loop fusion | flops 229376 | bytes 393216 | tf_op jit(solution)/shard_map/convert_element_type | solution.py:593
  (52 shorter events, 0.8 us)
Async XLA Ops:
  0.0 8.6 %collective-permute-start = (bf16[128,256]{1,0:T(8,128)(2,1)}, bf16[128,256]{1,0:T(8,128)(2,1)S(1)}, u32[]{:S(2)}, u32[]{:S(2)}) collective-permute-start(bf16[128,256]{1,0:T(8,128)(2,1)} %param.22), channel_id=1, source_target_pairs={{0,28},{4,24},{8,20},{12,16},{16,12},{20,8},{24,4},{28,0},{1,29},{... | collective-permute-start | bytes 196616 | tf_op jit(solution)/shard_map/ppermute | solution.py:455
  6.0 0.8 %copy-start.8 = (bf16[128,256]{1,0:T(8,128)(2,1)S(1)}, bf16[128,256]{1,0:T(8,128)(2,1)}, u32[]{:S(2)}) copy-start(bf16[128,256]{1,0:T(8,128)(2,1)} %fwd_ref.1) | copy-start | bytes 196612
  6.8 0.7 %copy-start.12 = (f32[4,256]{1,0:T(4,128)S(1)}, f32[4,256]{1,0:T(4,128)}, u32[]{:S(2)}) copy-start(f32[4,256]{1,0:T(4,128)} %embed_ref.1) | copy-start | bytes 12292
  7.5 0.7 %copy-start.18 = (s32[128]{0:T(128)S(1)}, s32[128]{0:T(128)}, u32[]{:S(2)}) copy-start(s32[128]{0:T(128)} %param.20) | copy-start | bytes 1540
  8.7 8.3 %copy-start.2 = (bf16[1024,256]{1,0:T(8,128)(2,1)S(1)}, bf16[1024,256]{1,0:T(8,128)(2,1)}, u32[]{:S(2)}) copy-start(bf16[1024,256]{1,0:T(8,128)(2,1)} %refs_9_.3) | copy-start | bytes 1572868
  8.7 8.3 %copy-start.3 = (bf16[1024,256]{1,0:T(8,128)(2,1)S(1)}, bf16[1024,256]{1,0:T(8,128)(2,1)}, u32[]{:S(2)}) copy-start(bf16[1024,256]{1,0:T(8,128)(2,1)} %refs_10_.3) | copy-start | bytes 1572868
  8.7 8.3 %copy-start.6 = (bf16[1024,64]{0,1:T(8,128)(2,1)S(1)}, bf16[1024,64]{0,1:T(8,128)(2,1)}, u32[]{:S(2)}) copy-start(bf16[1024,64]{0,1:T(8,128)(2,1)} %param.30) | copy-start | bytes 393220
  8.7 8.3 %copy-start.7 = (bf16[1024,64]{0,1:T(8,128)(2,1)S(1)}, bf16[1024,64]{0,1:T(8,128)(2,1)}, u32[]{:S(2)}) copy-start(bf16[1024,64]{0,1:T(8,128)(2,1)} %param.33) | copy-start | bytes 393220
  8.7 8.3 %copy-start.9 = (bf16[64,256]{1,0:T(8,128)(2,1)S(1)}, bf16[64,256]{1,0:T(8,128)(2,1)}, u32[]{:S(2)}) copy-start(bf16[64,256]{1,0:T(8,128)(2,1)} %refs_11_.3) | copy-start | bytes 98308
  8.7 8.3 %copy-start.10 = (bf16[64,256]{1,0:T(8,128)(2,1)S(1)}, bf16[64,256]{1,0:T(8,128)(2,1)}, u32[]{:S(2)}) copy-start(bf16[64,256]{1,0:T(8,128)(2,1)} %refs_12_.3) | copy-start | bytes 98308
  8.7 8.3 %copy-start.11 = (f32[5,1024]{1,0:T(8,128)S(1)}, f32[5,1024]{1,0:T(8,128)}, u32[]{:S(2)}) copy-start(f32[5,1024]{1,0:T(8,128)} %mixing_ref.3) | copy-start | bytes 61444
  8.7 8.3 %copy-start.13 = (f32[1024]{0:T(1024)S(1)}, f32[1024]{0:T(1024)}, u32[]{:S(2)}) copy-start(f32[1024]{0:T(1024)} %param.24) | copy-start | bytes 12292
  8.8 8.3 %copy-start.15 = (f32[256]{0:T(256)S(1)}, f32[256]{0:T(256)}, u32[]{:S(2)}) copy-start(f32[256]{0:T(256)} %param.31) | copy-start | bytes 3076
  8.8 8.3 %copy-start.16 = (f32[256]{0:T(256)S(1)}, f32[256]{0:T(256)}, u32[]{:S(2)}) copy-start(f32[256]{0:T(256)} %param.34) | copy-start | bytes 3076
  16.3 6.6 %collective-permute-start.2 = (bf16[2,1024]{1,0:T(2,128)(2,1)S(1)}, bf16[2,1024]{1,0:T(2,128)(2,1)S(1)}, u32[]{:S(2)}, u32[]{:S(2)}) collective-permute-start(bf16[2,1024]{1,0:T(2,128)(2,1)S(1)} %bitcast.33), channel_id=1, source_target_pairs={{4,8},{12,16},{20,24},{8,4},{16,12},{24,20},{5,9},{13,17},{21,25},... | collective-permute-start | bytes 12296 | tf_op jit(solution)/shard_map/ppermute | solution.py:479
  19.3 9.0 %collective-permute-start.1 = (bf16[2,1024]{1,0:T(2,128)(2,1)S(1)}, bf16[2,1024]{1,0:T(2,128)(2,1)S(1)}, u32[]{:S(2)}, u32[]{:S(2)}) collective-permute-start(bf16[2,1024]{1,0:T(2,128)(2,1)S(1)} %bitcast.34), channel_id=1, source_target_pairs={{0,4},{4,0},{8,12},{12,8},{16,20},{20,16},{24,28},{28,24},{1,5},{5... | collective-permute-start | bytes 12296 | tf_op jit(solution)/shard_map/ppermute | solution.py:424
  27.0 5.4 %collective-permute-start.3 = (bf16[2,128,256]{2,1,0:T(8,128)(2,1)S(1)}, bf16[2,128,256]{2,1,0:T(8,128)(2,1)S(1)}, u32[]{:S(2)}, u32[]{:S(2)}) collective-permute-start(bf16[2,128,256]{2,1,0:T(8,128)(2,1)S(1)} %get-tuple-element.62), channel_id=1, source_target_pairs={{0,4},{4,0},{8,12},{12,8},{16,20},{20,16},{24,28},{28,24},{1,5},{5... | collective-permute-start | bytes 393224 | tf_op jit(solution)/shard_map/ppermute | solution.py:424
  32.4 1.7 %copy-start.5 = (bf16[256,1024]{1,0:T(8,128)(2,1)S(1)}, bf16[256,1024]{1,0:T(8,128)(2,1)}, u32[]{:S(2)}) copy-start(bf16[256,1024]{1,0:T(8,128)(2,1)} %refs_0_.1) | copy-start | bytes 1572868
  32.4 2.5 %copy-start.4 = (bf16[1024,256]{1,0:T(8,128)(2,1)S(1)}, bf16[1024,256]{1,0:T(8,128)(2,1)}, u32[]{:S(2)}) copy-start(bf16[1024,256]{1,0:T(8,128)(2,1)} %w_r.1) | copy-start | bytes 1572868
  32.7 5.0 %collective-permute-start.5 = (bf16[2,128,256]{2,1,0:T(8,128)(2,1)S(1)}, bf16[2,128,256]{2,1,0:T(8,128)(2,1)S(1)}, u32[]{:S(2)}, u32[]{:S(2)}) collective-permute-start(bf16[2,128,256]{2,1,0:T(8,128)(2,1)S(1)} %shard_map.195.total_ref), channel_id=1, source_target_pairs={{0,8},{4,12},{8,0},{12,4},{16,24},{20,28},{24,16},{28,20},{1,9},{5... | collective-permute-start | bytes 393224 | tf_op jit(solution)/shard_map/ppermute | solution.py:424
  34.1 13.8 %collective-permute-start.4 = (bf16[256,1024]{1,0:T(8,128)(2,1)S(1)}, bf16[256,1024]{1,0:T(8,128)(2,1)S(1)}, u32[]{:S(2)}, u32[]{:S(2)}) collective-permute-start(bf16[256,1024]{1,0:T(8,128)(2,1)S(1)} %copy-done.5), channel_id=1, source_target_pairs={{0,2},{1,3},{2,0},{3,1},{4,6},{5,7},{6,4},{7,5},{8,10},{9,11},{10,... | collective-permute-start | bytes 1572872 | tf_op jit(solution)/shard_map/ppermute | solution.py:424
  37.9 5.4 %collective-permute-start.6 = (bf16[2,64,256]{2,1,0:T(8,128)(2,1)S(1)}, bf16[2,64,256]{2,1,0:T(8,128)(2,1)S(1)}, u32[]{:S(2)}, u32[]{:S(2)}) collective-permute-start(bf16[2,64,256]{2,1,0:T(8,128)(2,1)S(1)} %get-tuple-element.69), channel_id=1, source_target_pairs={{0,16},{4,20},{8,24},{12,28},{16,0},{20,4},{24,8},{28,12},{1,17},{... | collective-permute-start | bytes 196616 | tf_op jit(solution)/shard_map/ppermute | solution.py:424
  41.0 15.3 %collective-permute-start.8 = (bf16[256,1024]{1,0:T(8,128)(2,1)S(1)}, bf16[256,1024]{1,0:T(8,128)(2,1)S(1)}, u32[]{:S(2)}, u32[]{:S(2)}) collective-permute-start(bf16[256,1024]{1,0:T(8,128)(2,1)S(1)} %copy-done.5), channel_id=1, source_target_pairs={{0,1},{1,0},{2,3},{3,2},{4,5},{5,4},{6,7},{7,6},{8,9},{9,8},{10,11... | collective-permute-start | bytes 1572872 | tf_op jit(solution)/shard_map/ppermute | solution.py:424
  43.4 4.5 %copy-start.17 = (f32[256]{0:T(256)S(1)}, f32[256]{0:T(256)}, u32[]{:S(2)}) copy-start(f32[256]{0:T(256)} %param.36) | copy-start | bytes 3076
  43.4 4.4 %collective-permute-start.7 = (bf16[2,64,256]{2,1,0:T(8,128)(2,1)S(1)}, bf16[2,64,256]{2,1,0:T(8,128)(2,1)S(1)}, u32[]{:S(2)}, u32[]{:S(2)}) collective-permute-start(bf16[2,64,256]{2,1,0:T(8,128)(2,1)S(1)} %shard_map.199.entry_ref), channel_id=1, source_target_pairs={{0,4},{4,0},{8,12},{12,8},{16,20},{20,16},{24,28},{28,24},{1,5},{5... | collective-permute-start | bytes 196616 | tf_op jit(solution)/shard_map/ppermute | solution.py:424
  47.9 8.4 %collective-permute-start.9 = (bf16[256,1024]{1,0:T(8,128)(2,1)S(1)}, bf16[256,1024]{1,0:T(8,128)(2,1)S(1)}, u32[]{:S(2)}, u32[]{:S(2)}) collective-permute-start(bf16[256,1024]{1,0:T(8,128)(2,1)S(1)} %collective-permute-done.4.refs_2_), channel_id=1, source_target_pairs={{0,1},{1,0},{2,3},{3,2},{4,5},{5,4},{6,7},{7,6},{8,9},{9,8},{10,11... | collective-permute-start | bytes 1572872 | tf_op jit(solution)/shard_map/ppermute | solution.py:424
  47.9 8.4 %copy-start = (bf16[1024,1024]{1,0:T(8,128)(2,1)S(1)}, bf16[1024,1024]{1,0:T(8,128)(2,1)}, u32[]{:S(2)}) copy-start(bf16[1024,1024]{1,0:T(8,128)(2,1)} %refs_4_.1) | copy-start | bytes 6291460
  47.9 8.4 %copy-start.1 = (bf16[1024,1024]{1,0:T(8,128)(2,1)S(1)}, bf16[1024,1024]{1,0:T(8,128)(2,1)}, u32[]{:S(2)}) copy-start(bf16[1024,1024]{1,0:T(8,128)(2,1)} %down_ref.1) | copy-start | bytes 6291460
  47.9 8.4 %copy-start.14 = (f32[1024]{0:T(1024)S(1)}, f32[1024]{0:T(1024)}, u32[]{:S(2)}) copy-start(f32[1024]{0:T(1024)} %param.25) | copy-start | bytes 12292
  58.2 4.9 %collective-permute-start.12 = (bf16[128,256]{1,0:T(8,128)(2,1)S(1)}, bf16[128,256]{1,0:T(8,128)(2,1)S(1)}, u32[]{:S(2)}, u32[]{:S(2)}) collective-permute-start(bf16[128,256]{1,0:T(8,128)(2,1)S(1)} %get-tuple-element.92), channel_id=1, source_target_pairs={{0,2},{1,3},{2,0},{3,1},{4,6},{5,7},{6,4},{7,5},{8,10},{9,11},{10,... | collective-permute-start | bytes 196616 | tf_op jit(solution)/shard_map/ppermute | solution.py:424
  59.1 4.4 %collective-permute-start.11 = (bf16[128,256]{1,0:T(8,128)(2,1)S(1)}, bf16[128,256]{1,0:T(8,128)(2,1)S(1)}, u32[]{:S(2)}, u32[]{:S(2)}) collective-permute-start(bf16[128,256]{1,0:T(8,128)(2,1)S(1)} %get-tuple-element.91), channel_id=1, source_target_pairs={{0,3},{1,2},{2,1},{3,0},{4,7},{5,6},{6,5},{7,4},{8,11},{9,10},{10,... | collective-permute-start | bytes 196616 | tf_op jit(solution)/shard_map/ppermute | solution.py:424
  60.3 3.2 %collective-permute-start.10 = (bf16[128,256]{1,0:T(8,128)(2,1)S(1)}, bf16[128,256]{1,0:T(8,128)(2,1)S(1)}, u32[]{:S(2)}, u32[]{:S(2)}) collective-permute-start(bf16[128,256]{1,0:T(8,128)(2,1)S(1)} %get-tuple-element.90), channel_id=1, source_target_pairs={{0,1},{1,0},{2,3},{3,2},{4,5},{5,4},{6,7},{7,6},{8,9},{9,8},{10,11... | collective-permute-start | bytes 196616 | tf_op jit(solution)/shard_map/ppermute | solution.py:424

commit v14 on v11

--- a/solution.py
+++ b/solution.py
@@ -397,7 +397,7 @@
 
 def mix_kernel(blocks, index_ref, joined_ref, x_ref, *refs):
     w_refs, (up_ref, down_ref, gain_ref, own_ref) = refs[:blocks], refs[blocks : blocks + 4]
-    *sent_refs, partial, total = refs[blocks + 4 :]
+    added_ref, *sent_refs, total = refs[blocks + 4 :]
     strands, rows, _ = x_ref.shape
     width = own_ref.shape[1]
     gain = gain_ref[...]
@@ -411,15 +411,23 @@
     inner = jnp.concatenate([layer_norm(item, gain).astype(BF16) for item in residuals], axis=0)
     active = jnp.square(jnp.maximum(mm(inner, up_ref[...]), 0.0)).astype(BF16).astype(F32)
     added = sum(active[s * rows : (s + 1) * rows] for s in range(strands)).astype(BF16)
-    partial[...] = mm(added, down_ref[...])
+    added_ref[...] = added
+    for mask, ref in enumerate(sent_refs, blocks - len(sent_refs)):
+        ref[...] = mm(added, columns_of(down_ref, me ^ mask, width)).astype(BF16)
     total[...] = sum(residuals)
-
-    def part(ref, which):
-        return ref[:, pl.ds(pl.multiple_of(which * width, width), width)]
-
-    own_ref[...] = part(total, me) + part(partial, me)
-    for step, ref in enumerate(sent_refs):
-        ref[...] = part(partial, me ^ (step + 1)).astype(BF16)
+    own_ref[...] = columns_of(total, me, width)
+
+
+def columns_of(ref, which, width):
+    return ref[:, pl.ds(pl.multiple_of(which * width, width), width)]
+
+
+def near_kernel(index_ref, added_ref, held_ref, down_ref, own_ref, *sent_refs):
+    me, width = index_ref[0], own_ref.shape[1]
+    added = added_ref[...]
+    for mask, ref in enumerate(sent_refs, 1):
+        ref[...] = mm(added, columns_of(down_ref, me ^ mask, width)).astype(BF16)
+    own_ref[...] = held_ref[...] + mm(added, columns_of(down_ref, me, width))
 
 
 def call(kernel, out_shape, scratch=(), mib=12, us=10, **kwargs):
@@ -583,19 +591,27 @@
 
     w_blocks = (w_output, w_beside, w_across, w_opposite)
     position = lax.axis_index("mp").astype(jnp.int32).reshape(1)
-    own, *sent = call(
+    near_count = mp_count // 2
+    own_struct, sent_struct = struct((rows, width), F32), struct((rows, width), BF16)
+    held, added, *far_parts = call(
         functools.partial(mix_kernel, mp_count),
-        (struct((rows, width), F32),) + (struct((rows, width), BF16),) * (mp_count - 1),
-        scratch=[
-            pltpu.VMEM((rows, full), F32),
-            pltpu.VMEM((rows, full), F32),
-        ],
+        (own_struct, struct((rows, ffn_key.shape[1]), BF16)) + (sent_struct,) * near_count,
+        scratch=[pltpu.VMEM((rows, full), F32)],
         mib=16,
         in_specs=[SMEM_SPEC] + [VMEM_SPEC] * (5 + mp_count),
     )(position, joined_whole, whole, *w_blocks, ffn_key, ffn_value, ln2_gain.reshape(1, full))
+    arrivals = [swapped(item, "mp", mask) for mask, item in enumerate(far_parts, near_count)]
+    own, *near_parts = call(
+        near_kernel,
+        (own_struct,) + (sent_struct,) * (near_count - 1),
+        mib=6,
+        us=1,
+        in_specs=[SMEM_SPEC] + [VMEM_SPEC] * 3,
+    )(position, added, held, ffn_value)
+    arrivals += [swapped(item, "mp", mask) for mask, item in enumerate(near_parts, 1)]
     merged = own
-    for step, item in enumerate(sent):
-        merged = merged + swapped(item, "mp", step + 1).astype(F32)
+    for item in reversed(arrivals):
+        merged = merged + item.astype(F32)
     return merged.astype(BF16)
 
 

time: 65.6 us -> 64.9 us (0.989)
  waiting for transfers between devices: 10.9 us -> 9.78 us
    ppermute x11, waiting for transfers between devices: 10.9 us -> 9.77 us  [swapped(): lax.ppermute(value, axis, [(i, i ^ mask) for i in range(lax.axis_size(axi...]
    pallas_call x1 -> x2, Pallas kernels: 2.04 us -> 2.21 us  [the longest x1 1.89 us: on_device(): call(functools.partial(mix_kernel, mp_count), (own_struct, struct((rows,...]
  transfers between devices with their start and end apart: 13 -> 13, of which waited for: 6 -> 6; matrix products, arithmetic and copies ran while one was open for 0% -> 0% of each run, Pallas kernels for 23% -> 24%
where the time goes in v14:
time: 64.9 us; the launch traced here: 64.6 us
  starting transfers between devices  18.8 us (29%)
  Pallas kernels  17.8 us (27%)
  blocking collectives  14.9 us (23%)
  waiting for transfers between devices  9.78 us (15%)
  local copies, waits for them, and re-layouts  2.29 us (4%)
  other arithmetic  0.69 us (1%)
    ppermute x11, starting transfers between devices, swapped(): lax.ppermute(value, axis, [(i, i ^ mask) for i in range(lax.axis_size(axi...  12.1 us
    ppermute x11, waiting for transfers between devices, swapped(): lax.ppermute(value, axis, [(i, i ^ mask) for i in range(lax.axis_size(axi...  9.77 us
    all_gather x1, blocking collectives, on_device(): joined_whole = lax.all_gather(joined, 'mp', axis=2, tiled=True)  7.55 us
    all_gather x1, blocking collectives, on_device(): whole = lax.all_gather(local, 'mp', axis=2, tiled=True)  7.3 us
    pallas_call x2, Pallas kernels, chunk(): call(chunk_kernel, (state_struct, parts_struct, start_struct, struct((str...  7.24 us
    ppermute x1, starting transfers between devices, on_device(): rc_here = lax.ppermute(hidden_rc, 'seq', mirror)  6 us
    pallas_call x1, Pallas kernels, on_device(): call(project_kernel, (f32_lanes,) * 5 + (struct((groups, 8, width), F32),...  2.58 us
    unnamed x40, local copies, waits for them, and re-layouts  2.29 us
  transfers between devices with their start and end apart: 13, of which 6 were waited for; matrix products, arithmetic and copies ran while one was open for 0% of the time, Pallas kernels for 24%

profile of v14, /device:TPU:0, one launch (start us, length us, event | category | flops | bytes accessed | tf_op | source)
XLA Modules:
  0.0 64.6 jit_solution(5670710983815993405)
XLA Ops:
  0.0 6.0 %collective-permute-start = (bf16[128,256]{1,0:T(8,128)(2,1)}, bf16[128,256]{1,0:T(8,128)(2,1)S(1)}, u32[]{:S(2)}, u32[]{:S(2)}) collective-permute-start(bf16[128,256]{1,0:T(8,128)(2,1)} %param.22), channel_id=1, source_target_pairs={{0,28},{4,24},{8,20},{12,16},{16,12},{20,8},{24,4},{28,0},{1,29},{... | collective-permute-start | bytes 196616 | tf_op jit(solution)/shard_map/ppermute | solution.py:476
  6.0 0.8 %copy-done.8 = bf16[128,256]{1,0:T(8,128)(2,1)S(1)} copy-done((bf16[128,256]{1,0:T(8,128)(2,1)S(1)}, bf16[128,256]{1,0:T(8,128)(2,1)}, u32[]{:S(2)}) %copy-start.8) | copy-done | bytes 65560
  6.8 0.7 %copy-done.12 = f32[4,256]{1,0:T(4,128)S(1)} copy-done((f32[4,256]{1,0:T(4,128)S(1)}, f32[4,256]{1,0:T(4,128)}, u32[]{:S(2)}) %copy-start.12) | copy-done | bytes 4120
  7.5 0.7 %copy-done.18 = s32[128]{0:T(128)S(1)} copy-done((s32[128]{0:T(128)S(1)}, s32[128]{0:T(128)}, u32[]{:S(2)}) %copy-start.18) | copy-done | bytes 536
  8.2 0.4 shard_map.190
  8.9 7.3 %all_gather.6.x_ref = bf16[2,128,1024]{2,1,0:T(8,128)(2,1)S(1)} all-gather(bf16[2,128,256]{2,1,0:T(8,128)(2,1)S(1)} %shard_map.191), channel_id=1, replica_groups=mesh['seq'=8,'mp'=4] {'mp'}, dimensions={2}, use_global_device_ids=true | all-gather | bytes 655360 | tf_op jit(solution)/shard_map/all_gather | solution.py:494
  16.3 0.7 %collective-permute-start.2 = (bf16[2,1024]{1,0:T(2,128)(2,1)S(1)}, bf16[2,1024]{1,0:T(2,128)(2,1)S(1)}, u32[]{:S(2)}, u32[]{:S(2)}) collective-permute-start(bf16[2,1024]{1,0:T(2,128)(2,1)S(1)} %bitcast.33), channel_id=1, source_target_pairs={{4,8},{12,16},{20,24},{8,4},{16,12},{24,20},{5,9},{13,17},{21,25},... | collective-permute-start | bytes 12296 | tf_op jit(solution)/shard_map/ppermute | solution.py:500
  17.0 2.6 %shard_map.192 = (f32[4,128,256]{2,1,0:T(8,128)S(1)}, f32[4,128,256]{2,1,0:T(8,128)S(1)}, f32[4,128,256]{2,1,0:T(8,128)S(1)}, f32[4,128,256]{2,1,0:T(8,128)S(1)}...) custom-call(bf16[2,128,1024]{2,1,0:T(8,128)(2,1)S(1)} %all_gather.6., ...), custom_call_target="tpu_custom_call" | custom-call | flops 10000000000 | bytes 10000000 | tf_op jit(solution)/shard_map/pallas_call | solution.py:510
  19.6 3.7 %collective-permute-start.1 = (bf16[2,1024]{1,0:T(2,128)(2,1)S(1)}, bf16[2,1024]{1,0:T(2,128)(2,1)S(1)}, u32[]{:S(2)}, u32[]{:S(2)}) collective-permute-start(bf16[2,1024]{1,0:T(2,128)(2,1)S(1)} %bitcast.34), channel_id=1, source_target_pairs={{0,4},{4,0},{8,12},{12,8},{16,20},{20,16},{24,28},{28,24},{1,5},{5... | collective-permute-start | bytes 12296 | tf_op jit(solution)/shard_map/ppermute | solution.py:445
  23.3 3.6 %shard_map.194 = (bf16[2,128,256]{2,1,0:T(8,128)(2,1)S(1)}, bf16[2,5,128,256]{3,2,1,0:T(8,128)(2,1)S(1)}, f32[2,8,256]{2,1,0:T(8,128)S(1)}, f32[2,1024]{1,0:T(2,128)S(1)}) custom-call(s32[1]{0:T(128)} %bitcast.1.direction_ref, f32[4,128,256]{2,1,0:T(8,128)S(1)} %get-tuple-element.56.refs_0_, f32[4,128,256]{2,1,0:T(8,128)S(1)} %get-tuple-element.57.refs_1_, ...), custom_call_target="tpu_custom_call" | custom-call | flops 10000000000 | bytes 10000000 | tf_op jit(solution)/shard_map/pallas_call | solution.py:529
  26.9 0.9 %collective-permute-start.3 = (bf16[2,128,256]{2,1,0:T(8,128)(2,1)S(1)}, bf16[2,128,256]{2,1,0:T(8,128)(2,1)S(1)}, u32[]{:S(2)}, u32[]{:S(2)}) collective-permute-start(bf16[2,128,256]{2,1,0:T(8,128)(2,1)S(1)} %get-tuple-element.65), channel_id=1, source_target_pairs={{0,4},{4,0},{8,12},{12,8},{16,20},{20,16},{24,28},{28,24},{1,5},{5... | collective-permute-start | bytes 393224 | tf_op jit(solution)/shard_map/ppermute | solution.py:445
  27.8 3.6 %shard_map.193 = (bf16[2,128,256]{2,1,0:T(8,128)(2,1)S(1)}, bf16[2,5,128,256]{3,2,1,0:T(8,128)(2,1)S(1)}, f32[2,8,256]{2,1,0:T(8,128)S(1)}, f32[2,1024]{1,0:T(2,128)S(1)}) custom-call(s32[1]{0:T(128)S(6)} %sub.3.direction_ref, f32[4,128,256]{2,1,0:T(8,128)S(1)} %get-tuple-element.56.refs_0_, f32[4,128,256]{2,1,0:T(8,128)S(1)} %get-tuple-element.57.refs_1_, ...), custom_call_target="tpu_custom_call" | custom-call | flops 10000000000 | bytes 10000000 | tf_op jit(solution)/shard_map/pallas_call | solution.py:529
  31.5 0.7 %collective-permute-done.3.from_ref = bf16[2,128,256]{2,1,0:T(8,128)(2,1)S(1)} collective-permute-done((bf16[2,128,256]{2,1,0:T(8,128)(2,1)S(1)}, bf16[2,128,256]{2,1,0:T(8,128)(2,1)S(1)}, u32[]{:S(2)}, u32[]{:S(2)}) %collective-permute-start.3) | collective-permute-done | bytes 131104 | tf_op jit(solution)/shard_map/ppermute | solution.py:445
  32.4 1.1 %collective-permute-start.5 = (bf16[2,128,256]{2,1,0:T(8,128)(2,1)S(1)}, bf16[2,128,256]{2,1,0:T(8,128)(2,1)S(1)}, u32[]{:S(2)}, u32[]{:S(2)}) collective-permute-start(bf16[2,128,256]{2,1,0:T(8,128)(2,1)S(1)} %shard_map.195.total_ref), channel_id=1, source_target_pairs={{0,8},{4,12},{8,0},{12,4},{16,24},{20,28},{24,16},{28,20},{1,9},{5... | collective-permute-start | bytes 393224 | tf_op jit(solution)/shard_map/ppermute | solution.py:445
  33.5 0.8 %collective-permute-start.4 = (bf16[256,1024]{1,0:T(8,128)(2,1)S(1)}, bf16[256,1024]{1,0:T(8,128)(2,1)S(1)}, u32[]{:S(2)}, u32[]{:S(2)}) collective-permute-start(bf16[256,1024]{1,0:T(8,128)(2,1)S(1)} %copy-done.5), channel_id=1, source_target_pairs={{0,2},{1,3},{2,0},{3,1},{4,6},{5,7},{6,4},{7,5},{8,10},{9,11},{10,... | collective-permute-start | bytes 1572872 | tf_op jit(solution)/shard_map/ppermute | solution.py:445
  34.4 0.8 %shard_map.196.receptances = f32[4,128,256]{2,1,0:T(8,128)S(1)} custom-call(s32[1]{0:T(128)} %bitcast.1.direction_ref, f32[2,144,1024]{2,1,0:T(8,128)S(1)} %get-tuple-element.67.normed, f32[5,1024]{1,0:T(8,128)S(1)} %copy-done.11, f32[2,1024]{1,0:T(2,128)S(1)} %get-tuple-element.68.sent_edge_ref, f32[2,1024]{1,0:T(2,128)S(1)} %get-tuple-element.70.kept_edge_ref, ...), custom_call_target="tpu_custom_call" | custom-call | flops 3000000000 | bytes 3000000 | tf_op jit(solution)/shard_map/pallas_call | solution.py:543
  35.2 2.3 %collective-permute-done.5.from_ref = bf16[2,128,256]{2,1,0:T(8,128)(2,1)S(1)} collective-permute-done((bf16[2,128,256]{2,1,0:T(8,128)(2,1)S(1)}, bf16[2,128,256]{2,1,0:T(8,128)(2,1)S(1)}, u32[]{:S(2)}, u32[]{:S(2)}) %collective-permute-start.5) | collective-permute-done | bytes 131104 | tf_op jit(solution)/shard_map/ppermute | solution.py:445
  37.6 3.3 %collective-permute-start.6 = (bf16[2,64,256]{2,1,0:T(8,128)(2,1)S(1)}, bf16[2,64,256]{2,1,0:T(8,128)(2,1)S(1)}, u32[]{:S(2)}, u32[]{:S(2)}) collective-permute-start(bf16[2,64,256]{2,1,0:T(8,128)(2,1)S(1)} %get-tuple-element.72), channel_id=1, source_target_pairs={{0,16},{4,20},{8,24},{12,28},{16,0},{20,4},{24,8},{28,12},{1,17},{... | collective-permute-start | bytes 196616 | tf_op jit(solution)/shard_map/ppermute | solution.py:445
  40.9 2.1 %shard_map.198 = (f32[4,128,256]{2,1,0:T(8,128)S(1)}, f32[4,128,256]{2,1,0:T(8,128)S(1)}) custom-call(s32[1]{0:T(128)} %bitcast.1.direction_ref, f32[4,128,256]{2,1,0:T(8,128)S(1)} %shard_map.196.receptances, f32[4,128,256]{2,1,0:T(8,128)S(1)} %get-tuple-element.74.here_ref, bf16[2,5,128,256]{3,2,1,0:T(8,128)(2,1)S(1)} %get-tuple-element.77.sent_ref, ...), custom_call_target="tpu_custom_call" | custom-call | flops 10000000000 | bytes 10000000 | tf_op jit(solution)/shard_map/pallas_call | solution.py:571
  43.0 0.8 %collective-permute-done.6.from_ref = bf16[2,64,256]{2,1,0:T(8,128)(2,1)S(1)} collective-permute-done((bf16[2,64,256]{2,1,0:T(8,128)(2,1)S(1)}, bf16[2,64,256]{2,1,0:T(8,128)(2,1)S(1)}, u32[]{:S(2)}, u32[]{:S(2)}) %collective-permute-start.6) | collective-permute-done | bytes 65568 | tf_op jit(solution)/shard_map/ppermute | solution.py:445
  44.1 1.0 %shard_map.200.kept_ref = f32[2,128,256]{2,1,0:T(8,128)S(1)} custom-call(bf16[2,64,256]{2,1,0:T(8,128)(2,1)S(1)} %shard_map.199.entry_ref, bf16[2,128,256]{2,1,0:T(8,128)(2,1)S(1)} %collective-permute-done.3.from_ref, f32[4,128,256]{2,1,0:T(8,128)S(1)} %get-tuple-element.85.local_ref, f32[4,128,256]{2,1,0:T(8,128)S(1)} %get-tuple-element.86.map_ref), custom_call_target="tpu_custom_call" | custom-call | flops 3000000000 | bytes 3000000 | tf_op jit(solution)/shard_map/pallas_call | solution.py:586
  45.1 3.3 %collective-permute-done.7.other_ref = bf16[2,64,256]{2,1,0:T(8,128)(2,1)S(1)} collective-permute-done((bf16[2,64,256]{2,1,0:T(8,128)(2,1)S(1)}, bf16[2,64,256]{2,1,0:T(8,128)(2,1)S(1)}, u32[]{:S(2)}, u32[]{:S(2)}) %collective-permute-start.7) | collective-permute-done | bytes 65568 | tf_op jit(solution)/shard_map/ppermute | solution.py:445
  48.4 0.8 %shard_map.201 = bf16[2,128,256]{2,1,0:T(8,128)(2,1)S(1)} custom-call(bf16[2,64,256]{2,1,0:T(8,128)(2,1)S(1)} %collective-permute-done.7.other_ref, f32[2,128,256]{2,1,0:T(8,128)S(1)} %shard_map.200.kept_ref, f32[4,128,256]{2,1,0:T(8,128)S(1)} %get-tuple-element.85.local_ref, f32[4,128,256]{2,1,0:T(8,128)S(1)} %get-tuple-element.86.map_ref, ...), custom_call_target="tpu_custom_call" | custom-call | flops 10000000000 | bytes 10000000 | tf_op jit(solution)/shard_map/pallas_call | solution.py:589
  49.2 7.6 %all_gather.7.joined_ref = bf16[2,128,1024]{2,1,0:T(8,128)(2,1)S(1)} all-gather(bf16[2,128,256]{2,1,0:T(8,128)(2,1)S(1)} %shard_map.201), channel_id=1, replica_groups=mesh['seq'=8,'mp'=4] {'mp'}, dimensions={2}, use_global_device_ids=true | all-gather | bytes 655360 | tf_op jit(solution)/shard_map/all_gather | solution.py:590
  56.8 1.9 %shard_map.202 = (f32[128,256]{1,0:T(8,128)S(1)}, bf16[128,1024]{1,0:T(8,128)(2,1)S(1)}, bf16[128,256]{1,0:T(8,128)(2,1)S(1)}, bf16[128,256]{1,0:T(8,128)(2,1)S(1)}) custom-call(s32[1]{0:T(128)} %bitcast.index_ref, bf16[2,128,1024]{2,1,0:T(8,128)(2,1)S(1)} %all_gather.7.joined_ref, bf16[2,128,1024]{2,1,0:T(8,128)(2,1)S(1)} %all_gather.6.x_ref, ...), custom_call_target="tpu_custom_call" | custom-call | flops 10000000000 | bytes 10000000 | tf_op jit(solution)/shard_map/pallas_call | solution.py:596
  58.7 0.9 %collective-permute-start.12 = (bf16[128,256]{1,0:T(8,128)(2,1)S(1)}, bf16[128,256]{1,0:T(8,128)(2,1)S(1)}, u32[]{:S(2)}, u32[]{:S(2)}) collective-permute-start(bf16[128,256]{1,0:T(8,128)(2,1)S(1)} %get-tuple-element.96), channel_id=1, source_target_pairs={{0,2},{1,3},{2,0},{3,1},{4,6},{5,7},{6,4},{7,5},{8,10},{9,11},{10,... | collective-permute-start | bytes 196616 | tf_op jit(solution)/shard_map/ppermute | solution.py:445
  59.6 0.9 %collective-permute-start.11 = (bf16[128,256]{1,0:T(8,128)(2,1)S(1)}, bf16[128,256]{1,0:T(8,128)(2,1)S(1)}, u32[]{:S(2)}, u32[]{:S(2)}) collective-permute-start(bf16[128,256]{1,0:T(8,128)(2,1)S(1)} %get-tuple-element.95), channel_id=1, source_target_pairs={{0,3},{1,2},{2,1},{3,0},{4,7},{5,6},{6,5},{7,4},{8,11},{9,10},{10,... | collective-permute-start | bytes 196616 | tf_op jit(solution)/shard_map/ppermute | solution.py:445
  60.5 0.3 shard_map.203
  60.8 0.5 collective-permute-start.10
  61.3 2.3 %collective-permute-done.12 = bf16[128,256]{1,0:T(8,128)(2,1)S(1)} collective-permute-done((bf16[128,256]{1,0:T(8,128)(2,1)S(1)}, bf16[128,256]{1,0:T(8,128)(2,1)S(1)}, u32[]{:S(2)}, u32[]{:S(2)}) %collective-permute-start.12) | collective-permute-done | bytes 65568 | tf_op jit(solution)/shard_map/ppermute | solution.py:445
  63.6 0.4 collective-permute-done.11
  64.0 0.7 %add_convert_fusion = bf16[128,256]{1,0:T(8,128)(2,1)} fusion(bf16[128,256]{1,0:T(8,128)(2,1)S(1)} %collective-permute-done.12, bf16[128,256]{1,0:T(8,128)(2,1)S(1)} %collective-permute-done.11, f32[128,256]{1,0:T(8,128)S(1)} %get-tuple-element.93, bf16[128,256]{1,0:T(8,128)(2,1)S(1)} %collective-permute-done.10), kind=kLoop, calls=%fused_computation | loop fusion | flops 229376 | bytes 393216 | tf_op jit(solution)/shard_map/convert_element_type | solution.py:615
  (52 shorter events, 1.0 us)
Async XLA Ops:
  0.0 8.6 %collective-permute-start = (bf16[128,256]{1,0:T(8,128)(2,1)}, bf16[128,256]{1,0:T(8,128)(2,1)S(1)}, u32[]{:S(2)}, u32[]{:S(2)}) collective-permute-start(bf16[128,256]{1,0:T(8,128)(2,1)} %param.22), channel_id=1, source_target_pairs={{0,28},{4,24},{8,20},{12,16},{16,12},{20,8},{24,4},{28,0},{1,29},{... | collective-permute-start | bytes 196616 | tf_op jit(solution)/shard_map/ppermute | solution.py:476
  6.0 0.8 %copy-start.8 = (bf16[128,256]{1,0:T(8,128)(2,1)S(1)}, bf16[128,256]{1,0:T(8,128)(2,1)}, u32[]{:S(2)}) copy-start(bf16[128,256]{1,0:T(8,128)(2,1)} %fwd_ref.1) | copy-start | bytes 196612
  6.8 0.7 %copy-start.12 = (f32[4,256]{1,0:T(4,128)S(1)}, f32[4,256]{1,0:T(4,128)}, u32[]{:S(2)}) copy-start(f32[4,256]{1,0:T(4,128)} %embed_ref.1) | copy-start | bytes 12292
  7.5 0.7 %copy-start.18 = (s32[128]{0:T(128)S(1)}, s32[128]{0:T(128)}, u32[]{:S(2)}) copy-start(s32[128]{0:T(128)} %param.20) | copy-start | bytes 1540
  8.7 8.3 %copy-start.2 = (bf16[1024,256]{1,0:T(8,128)(2,1)S(1)}, bf16[1024,256]{1,0:T(8,128)(2,1)}, u32[]{:S(2)}) copy-start(bf16[1024,256]{1,0:T(8,128)(2,1)} %refs_10_.3) | copy-start | bytes 1572868
  8.7 8.3 %copy-start.3 = (bf16[1024,256]{1,0:T(8,128)(2,1)S(1)}, bf16[1024,256]{1,0:T(8,128)(2,1)}, u32[]{:S(2)}) copy-start(bf16[1024,256]{1,0:T(8,128)(2,1)} %refs_11_.3) | copy-start | bytes 1572868
  8.7 8.3 %copy-start.6 = (bf16[1024,64]{0,1:T(8,128)(2,1)S(1)}, bf16[1024,64]{0,1:T(8,128)(2,1)}, u32[]{:S(2)}) copy-start(bf16[1024,64]{0,1:T(8,128)(2,1)} %param.30) | copy-start | bytes 393220
  8.7 8.3 %copy-start.7 = (bf16[1024,64]{0,1:T(8,128)(2,1)S(1)}, bf16[1024,64]{0,1:T(8,128)(2,1)}, u32[]{:S(2)}) copy-start(bf16[1024,64]{0,1:T(8,128)(2,1)} %param.33) | copy-start | bytes 393220
  8.7 8.3 %copy-start.9 = (bf16[64,256]{1,0:T(8,128)(2,1)S(1)}, bf16[64,256]{1,0:T(8,128)(2,1)}, u32[]{:S(2)}) copy-start(bf16[64,256]{1,0:T(8,128)(2,1)} %refs_12_.3) | copy-start | bytes 98308
  8.7 8.3 %copy-start.10 = (bf16[64,256]{1,0:T(8,128)(2,1)S(1)}, bf16[64,256]{1,0:T(8,128)(2,1)}, u32[]{:S(2)}) copy-start(bf16[64,256]{1,0:T(8,128)(2,1)} %refs_13_.3) | copy-start | bytes 98308
  8.7 8.3 %copy-start.11 = (f32[5,1024]{1,0:T(8,128)S(1)}, f32[5,1024]{1,0:T(8,128)}, u32[]{:S(2)}) copy-start(f32[5,1024]{1,0:T(8,128)} %mixing_ref.3) | copy-start | bytes 61444
  8.7 8.3 %copy-start.13 = (f32[1024]{0:T(1024)S(1)}, f32[1024]{0:T(1024)}, u32[]{:S(2)}) copy-start(f32[1024]{0:T(1024)} %param.24) | copy-start | bytes 12292
  8.8 8.3 %copy-start.15 = (f32[256]{0:T(256)S(1)}, f32[256]{0:T(256)}, u32[]{:S(2)}) copy-start(f32[256]{0:T(256)} %param.31) | copy-start | bytes 3076
  8.8 8.3 %copy-start.16 = (f32[256]{0:T(256)S(1)}, f32[256]{0:T(256)}, u32[]{:S(2)}) copy-start(f32[256]{0:T(256)} %param.34) | copy-start | bytes 3076
  16.3 7.0 %collective-permute-start.2 = (bf16[2,1024]{1,0:T(2,128)(2,1)S(1)}, bf16[2,1024]{1,0:T(2,128)(2,1)S(1)}, u32[]{:S(2)}, u32[]{:S(2)}) collective-permute-start(bf16[2,1024]{1,0:T(2,128)(2,1)S(1)} %bitcast.33), channel_id=1, source_target_pairs={{4,8},{12,16},{20,24},{8,4},{16,12},{24,20},{5,9},{13,17},{21,25},... | collective-permute-start | bytes 12296 | tf_op jit(solution)/shard_map/ppermute | solution.py:500
  19.6 8.2 %collective-permute-start.1 = (bf16[2,1024]{1,0:T(2,128)(2,1)S(1)}, bf16[2,1024]{1,0:T(2,128)(2,1)S(1)}, u32[]{:S(2)}, u32[]{:S(2)}) collective-permute-start(bf16[2,1024]{1,0:T(2,128)(2,1)S(1)} %bitcast.34), channel_id=1, source_target_pairs={{0,4},{4,0},{8,12},{12,8},{16,20},{20,16},{24,28},{28,24},{1,5},{5... | collective-permute-start | bytes 12296 | tf_op jit(solution)/shard_map/ppermute | solution.py:445
  26.9 5.3 %collective-permute-start.3 = (bf16[2,128,256]{2,1,0:T(8,128)(2,1)S(1)}, bf16[2,128,256]{2,1,0:T(8,128)(2,1)S(1)}, u32[]{:S(2)}, u32[]{:S(2)}) collective-permute-start(bf16[2,128,256]{2,1,0:T(8,128)(2,1)S(1)} %get-tuple-element.65), channel_id=1, source_target_pairs={{0,4},{4,0},{8,12},{12,8},{16,20},{20,16},{24,28},{28,24},{1,5},{5... | collective-permute-start | bytes 393224 | tf_op jit(solution)/shard_map/ppermute | solution.py:445
  31.4 2.1 %copy-start.5 = (bf16[256,1024]{1,0:T(8,128)(2,1)S(1)}, bf16[256,1024]{1,0:T(8,128)(2,1)}, u32[]{:S(2)}) copy-start(bf16[256,1024]{1,0:T(8,128)(2,1)} %refs_0_.1) | copy-start | bytes 1572868
  31.4 2.9 %copy-start.4 = (bf16[1024,256]{1,0:T(8,128)(2,1)S(1)}, bf16[1024,256]{1,0:T(8,128)(2,1)}, u32[]{:S(2)}) copy-start(bf16[1024,256]{1,0:T(8,128)(2,1)} %w_r.1) | copy-start | bytes 1572868
  32.4 5.0 %collective-permute-start.5 = (bf16[2,128,256]{2,1,0:T(8,128)(2,1)S(1)}, bf16[2,128,256]{2,1,0:T(8,128)(2,1)S(1)}, u32[]{:S(2)}, u32[]{:S(2)}) collective-permute-start(bf16[2,128,256]{2,1,0:T(8,128)(2,1)S(1)} %shard_map.195.total_ref), channel_id=1, source_target_pairs={{0,8},{4,12},{8,0},{12,4},{16,24},{20,28},{24,16},{28,20},{1,9},{5... | collective-permute-start | bytes 393224 | tf_op jit(solution)/shard_map/ppermute | solution.py:445
  33.5 14.8 %collective-permute-start.4 = (bf16[256,1024]{1,0:T(8,128)(2,1)S(1)}, bf16[256,1024]{1,0:T(8,128)(2,1)S(1)}, u32[]{:S(2)}, u32[]{:S(2)}) collective-permute-start(bf16[256,1024]{1,0:T(8,128)(2,1)S(1)} %copy-done.5), channel_id=1, source_target_pairs={{0,2},{1,3},{2,0},{3,1},{4,6},{5,7},{6,4},{7,5},{8,10},{9,11},{10,... | collective-permute-start | bytes 1572872 | tf_op jit(solution)/shard_map/ppermute | solution.py:445
  37.6 6.2 %collective-permute-start.6 = (bf16[2,64,256]{2,1,0:T(8,128)(2,1)S(1)}, bf16[2,64,256]{2,1,0:T(8,128)(2,1)S(1)}, u32[]{:S(2)}, u32[]{:S(2)}) collective-permute-start(bf16[2,64,256]{2,1,0:T(8,128)(2,1)S(1)} %get-tuple-element.72), channel_id=1, source_target_pairs={{0,16},{4,20},{8,24},{12,28},{16,0},{20,4},{24,8},{28,12},{1,17},{... | collective-permute-start | bytes 196616 | tf_op jit(solution)/shard_map/ppermute | solution.py:445
  40.9 15.9 %collective-permute-start.8 = (bf16[256,1024]{1,0:T(8,128)(2,1)S(1)}, bf16[256,1024]{1,0:T(8,128)(2,1)S(1)}, u32[]{:S(2)}, u32[]{:S(2)}) collective-permute-start(bf16[256,1024]{1,0:T(8,128)(2,1)S(1)} %copy-done.5), channel_id=1, source_target_pairs={{0,1},{1,0},{2,3},{3,2},{4,5},{5,4},{6,7},{7,6},{8,9},{9,8},{10,11... | collective-permute-start | bytes 1572872 | tf_op jit(solution)/shard_map/ppermute | solution.py:445
  44.0 4.4 %copy-start.17 = (f32[256]{0:T(256)S(1)}, f32[256]{0:T(256)}, u32[]{:S(2)}) copy-start(f32[256]{0:T(256)} %param.36) | copy-start | bytes 3076
  44.0 4.3 %collective-permute-start.7 = (bf16[2,64,256]{2,1,0:T(8,128)(2,1)S(1)}, bf16[2,64,256]{2,1,0:T(8,128)(2,1)S(1)}, u32[]{:S(2)}, u32[]{:S(2)}) collective-permute-start(bf16[2,64,256]{2,1,0:T(8,128)(2,1)S(1)} %shard_map.199.entry_ref), channel_id=1, source_target_pairs={{0,4},{4,0},{8,12},{12,8},{16,20},{20,16},{24,28},{28,24},{1,5},{5... | collective-permute-start | bytes 196616 | tf_op jit(solution)/shard_map/ppermute | solution.py:445
  48.4 8.4 %collective-permute-start.9 = (bf16[256,1024]{1,0:T(8,128)(2,1)S(1)}, bf16[256,1024]{1,0:T(8,128)(2,1)S(1)}, u32[]{:S(2)}, u32[]{:S(2)}) collective-permute-start(bf16[256,1024]{1,0:T(8,128)(2,1)S(1)} %collective-permute-done.4.refs_2_), channel_id=1, source_target_pairs={{0,1},{1,0},{2,3},{3,2},{4,5},{5,4},{6,7},{7,6},{8,9},{9,8},{10,11... | collective-permute-start | bytes 1572872 | tf_op jit(solution)/shard_map/ppermute | solution.py:445
  48.4 8.4 %copy-start = (bf16[1024,1024]{1,0:T(8,128)(2,1)S(1)}, bf16[1024,1024]{1,0:T(8,128)(2,1)}, u32[]{:S(2)}) copy-start(bf16[1024,1024]{1,0:T(8,128)(2,1)} %refs_4_.1) | copy-start | bytes 6291460
  48.4 8.4 %copy-start.1 = (bf16[1024,1024]{1,0:T(8,128)(2,1)S(1)}, bf16[1024,1024]{1,0:T(8,128)(2,1)}, u32[]{:S(2)}) copy-start(bf16[1024,1024]{1,0:T(8,128)(2,1)} %down_ref.1) | copy-start | bytes 6291460
  48.4 8.4 %copy-start.14 = (f32[1024]{0:T(1024)S(1)}, f32[1024]{0:T(1024)}, u32[]{:S(2)}) copy-start(f32[1024]{0:T(1024)} %param.25) | copy-start | bytes 12292
  58.7 4.9 %collective-permute-start.12 = (bf16[128,256]{1,0:T(8,128)(2,1)S(1)}, bf16[128,256]{1,0:T(8,128)(2,1)S(1)}, u32[]{:S(2)}, u32[]{:S(2)}) collective-permute-start(bf16[128,256]{1,0:T(8,128)(2,1)S(1)} %get-tuple-element.96), channel_id=1, source_target_pairs={{0,2},{1,3},{2,0},{3,1},{4,6},{5,7},{6,4},{7,5},{8,10},{9,11},{10,... | collective-permute-start | bytes 196616 | tf_op jit(solution)/shard_map/ppermute | solution.py:445
  59.6 4.4 %collective-permute-start.11 = (bf16[128,256]{1,0:T(8,128)(2,1)S(1)}, bf16[128,256]{1,0:T(8,128)(2,1)S(1)}, u32[]{:S(2)}, u32[]{:S(2)}) collective-permute-start(bf16[128,256]{1,0:T(8,128)(2,1)S(1)} %get-tuple-element.95), channel_id=1, source_target_pairs={{0,3},{1,2},{2,1},{3,0},{4,7},{5,6},{6,5},{7,4},{8,11},{9,10},{10,... | collective-permute-start | bytes 196616 | tf_op jit(solution)/shard_map/ppermute | solution.py:445
  60.8 3.2 %collective-permute-start.10 = (bf16[128,256]{1,0:T(8,128)(2,1)S(1)}, bf16[128,256]{1,0:T(8,128)(2,1)S(1)}, u32[]{:S(2)}, u32[]{:S(2)}) collective-permute-start(bf16[128,256]{1,0:T(8,128)(2,1)S(1)} %get-tuple-element.94), channel_id=1, source_target_pairs={{0,1},{1,0},{2,3},{3,2},{4,5},{5,4},{6,7},{7,6},{8,9},{9,8},{10,11... | collective-permute-start | bytes 196616 | tf_op jit(solution)/shard_map/ppermute | solution.py:445
